TPU v7x, 32 devices: a whole 2x2x4 slice. The times are simulated.
32 devices in a mesh: group: 2 (over x), seq: 16 (over z, y, core).
Axes of the slice: x: 2, y: 2, z: 4, core: 2. Of those that a mesh axis runs over, the one named last changes fastest.
Arguments:
- query_rows: bfloat16 [8192, 1536], P(('group', 'seq')), parts along dimension 0, may hold values from -120 to 120
- key_rows: bfloat16 [8192, 1536], P(('group', 'seq')), parts along dimension 0, may hold values from -6.6 to 6.6
- value_rows: bfloat16 [8192, 1536], P(('group', 'seq')), parts along dimension 0, may hold values from -60 to 60
- block_list: int32 [64, 27], P(('group', 'seq')), parts along dimension 0, may hold values from -1 to 31, as said below
- out_weight: bfloat16 [1536, 3072], P('seq'), may hold values from -4 to 4
Outputs:
- projected: bfloat16 [8192, 3072], P(('group', 'seq')), parts along dimension 0
There are 2 independent parts, one for each index of `group`. A program takes and returns all parts, laid end to end along the dimension named above; an argument that names none is the same for every part. Nothing has to cross between parts.
Inputs may be any that keep to these rules, and one draw needn't show every extreme that they name: `block_list`: tile t lies at grid row (t // 2) // 8, grid column (t // 2) % 8 and frame group t % 2. Row t lists distinct key tiles whose grid row, grid column and frame group each differ from t's by at most one; every such tile that shares t's grid row or grid column is listed, t itself among them; the other slots hold -1.
All inputs are finite; a program needn't handle non-finite values.
Results may differ from a plain program's by a relative error of at most 0.0056.
Values may be sent and summed in bfloat16 or wider, within the bound.
No kernel may reach another device: no remote copies, remote signals or barrier semaphores. Data moves between devices by JAX's collectives and lax.ppermute only.
A program may use at most 128 MiB of HBM per device.

v0:
```python
import math

import jax
import jax.numpy as jnp
from jax import lax
from jax.sharding import PartitionSpec as P

HD = 128
FRAMES = 2
GRID_COLS = 8


def shifted(value, axis, steps):
    count = lax.axis_size(axis)
    first, last = (max(0, -steps), min(count, count - steps))
    return lax.ppermute(value, axis, [(source, source + steps) for source in range(first, last)])


def body(query_rows, key_rows, value_rows, block_list, out_weight):
    row_count, features = query_rows.shape
    tile_rows = row_count // FRAMES
    head_count = features // HD
    scale = HD ** (-0.5)
    devices = lax.axis_size("seq")
    position = lax.axis_index("seq")
    columns_count = GRID_COLS
    key_value = jnp.stack([key_rows, value_rows])
    ordering = [
        -(columns_count + 1),
        -columns_count,
        -(columns_count - 1),
        -1,
        0,
        1,
        columns_count - 1,
        columns_count,
        columns_count + 1,
    ]
    received = {0: key_value}
    for offset in ordering:
        if offset != 0:
            received[offset] = shifted(key_value, "seq", offset)
    sources = position - jnp.array(ordering, dtype=jnp.int32)
    inside = (sources >= 0) & (sources < devices)
    tile_ids = sources[:, None] * FRAMES + jnp.arange(FRAMES, dtype=jnp.int32)[None, :]
    tile_ids = jnp.where(inside[:, None], tile_ids, -2).reshape(-1)
    member = jnp.any(block_list[:, :, None] == tile_ids[None, None, :], axis=1)
    allowed = jnp.repeat(jnp.repeat(member, tile_rows, axis=0), tile_rows, axis=1)
    per_block = math.gcd(head_count, 2)
    width = per_block * HD
    outputs = []
    for block in range(head_count // per_block):
        lower = block * width
        queries_here = query_rows[:, lower : lower + width].reshape(row_count, per_block, HD)
        keys_here = jnp.concatenate(
            [received[shift_by][0, :, lower : lower + width] for shift_by in ordering], axis=0
        )
        keys_here = keys_here.reshape(-1, per_block, HD)
        values_here = jnp.concatenate(
            [received[shift_by][1, :, lower : lower + width] for shift_by in ordering], axis=0
        )
        values_here = values_here.reshape(-1, per_block, HD)
        scores = (
            jnp.einsum("qhd,khd->hqk", queries_here, keys_here, preferred_element_type=jnp.float32)
            * scale
        )
        scores = jnp.where(allowed[None, :, :], scores, -jnp.inf)
        peak = jnp.max(scores, axis=-1, keepdims=True)
        weights = jnp.exp(scores - peak)
        totals = jnp.sum(weights, axis=-1, keepdims=True)
        probs = weights.astype(jnp.bfloat16)
        mixed = jnp.einsum("hqk,khd->qhd", probs, values_here, preferred_element_type=jnp.float32)
        mixed = mixed / jnp.transpose(totals, (1, 0, 2))
        outputs.append(mixed.astype(jnp.bfloat16).reshape(row_count, width))
    attention = jnp.concatenate(outputs, axis=1)
    summed = jnp.dot(
        attention,
        lax.all_gather(out_weight, "seq", axis=0, tiled=True),
        preferred_element_type=jnp.float32,
    )
    return summed.astype(jnp.bfloat16)


def solution(mesh):
    placed = (
        P(("group", "seq"), None),
        P(("group", "seq"), None),
        P(("group", "seq"), None),
        P(("group", "seq"), None),
        P("seq", None),
    )
    return jax.shard_map(
        body, mesh=mesh, in_specs=placed, out_specs=P(("group", "seq"), None), check_vma=False
    )
```

profile of v0, /device:TPU:27, one launch (start us, length us, event | category | flops | bytes accessed | tf_op | source)
XLA Modules:
  0.0 405.7 jit_solution(7567085291168828110)
XLA Ops:
  6.5 1.5 copy.142
  8.5 3.7 collective-permute-start
  12.2 2.4 collective-permute-start.1
  14.6 2.5 collective-permute-start.2
  17.1 2.6 collective-permute-start.3
  19.7 3.0 collective-permute-start.4
  24.2 0.8 fusion.104
  25.1 1.7 copy.148
  26.8 1.6 copy.228
  29.5 1.7 copy.229
  37.2 18.8 %collective-permute-done = bf16[2,256,1536]{1,2,0:T(8,128)(2,1)} collective-permute-done((bf16[2,256,1536]{1,2,0:T(8,128)(2,1)S(1)}, bf16[2,256,1536]{1,2,0:T(8,128)(2,1)}, u32[]{:S(2)}, u32[]{:S(2)}) %collective-permute-start) | collective-permute-done | bytes 1572896 | tf_op jit(solution)/shard_map/ppermute | solution.py:16
  56.0 1.3 collective-permute-start.5
  57.3 0.8 fusion.106
  58.1 38.9 %collective-permute-done.1 = bf16[2,256,1536]{1,2,0:T(8,128)(2,1)} collective-permute-done((bf16[2,256,1536]{1,2,0:T(8,128)(2,1)S(1)}, bf16[2,256,1536]{1,2,0:T(8,128)(2,1)}, u32[]{:S(2)}, u32[]{:S(2)}) %collective-permute-start.1) | collective-permute-done | bytes 1572896 | tf_op jit(solution)/shard_map/ppermute | solution.py:16
  97.1 1.3 collective-permute-start.6
  98.4 2.6 fusion.103
  101.0 29.8 %collective-permute-done.2 = bf16[2,256,1536]{1,2,0:T(8,128)(2,1)} collective-permute-done((bf16[2,256,1536]{1,2,0:T(8,128)(2,1)S(1)}, bf16[2,256,1536]{1,2,0:T(8,128)(2,1)}, u32[]{:S(2)}, u32[]{:S(2)}) %collective-permute-start.2) | collective-permute-done | bytes 1572896 | tf_op jit(solution)/shard_map/ppermute | solution.py:16
  130.8 1.5 collective-permute-start.7
  132.2 2.6 fusion.102
  134.9 1.6 copy.144
  136.5 1.7 copy.145
  138.2 2.6 fusion.101
  140.8 1.7 copy.146
  142.4 2.6 fusion.100
  145.0 1.7 copy.147
  146.7 2.6 fusion.99
  149.2 1.7 copy.149
  151.0 2.6 fusion.98
  153.6 1.7 copy.150
  155.2 2.6 fusion.97
  157.8 1.6 copy.151
  159.5 1.6 constant_dynamic-update-slice_fusion.8
  161.1 1.6 constant_dynamic-update-slice_fusion.17
  162.6 166.3 %collective-permute-done.7 = bf16[2,256,1536]{1,2,0:T(8,128)(2,1)S(1)} collective-permute-done((bf16[2,256,1536]{1,2,0:T(8,128)(2,1)S(1)}, bf16[2,256,1536]{1,2,0:T(8,128)(2,1)S(1)}, u32[]{:S(2)}, u32[]{:S(2)}) %collective-permute-start.7) | collective-permute-done | bytes 1572896 | tf_op jit(solution)/shard_map/ppermute | solution.py:16
  328.9 0.9 fusion.96
  332.9 1.7 copy.159
  355.1 1.7 copy.200
  362.2 1.0 copy.212
  367.0 1.0 fusion.93
  371.0 0.8 fusion.108
  372.5 0.9 fusion.90
  375.5 0.8 fusion.109
  376.3 0.9 fusion.16
  377.1 0.9 fusion.87
  381.6 0.9 fusion.84
  386.0 0.9 fusion.81
  390.4 0.9 fusion.78
  391.4 7.5 %convolution_convert_fusion = bf16[256,3072]{1,0:T(8,128)(2,1)} fusion(bf16[256,1536]{0,1:T(8,128)(2,1)S(1)} %constant_dynamic-update-slice_fusion.108, bf16[1536,3072]{1,0:T(8,128)(2,1)} %all-gather.2.cloned.1.call-done), kind=kOutput, calls=%fused_computation.36 | convolution fusion | flops 2416705536 | bytes 11796480 | tf_op jit(solution)/shard_map/dot_general | solution.py:76
  (484 shorter events, 56.5 us)
Async XLA Ops:
  6.5 384.9 %all-gather.2.cloned.1.call-start = ((), (), s32[]{:S(2)}) async-start(), calls=%async_computation | async-start | bytes 10027008 | tf_op jit(solution)/shard_map/all_gather | solution.py:78
  8.3 14.4 %copy-start.147 = (s32[9]{0:T(128)S(1)}, s32[9]{0:T(128)}, u32[]{:S(2)}) copy-start(s32[9]{0:T(128)} %constant.24) | copy-start | bytes 112
  8.5 47.5 %collective-permute-start = (bf16[2,256,1536]{1,2,0:T(8,128)(2,1)S(1)}, bf16[2,256,1536]{1,2,0:T(8,128)(2,1)}, u32[]{:S(2)}, u32[]{:S(2)}) collective-permute-start(bf16[2,256,1536]{1,2,0:T(8,128)(2,1)S(1)} %pad_maximum_fusion), channel_id=1, source_target_pairs={{9,0},{10,1},{11,2},{12,3},{13,4},{14,5},{15,6},{25,16},{26,17},{2... | collective-permute-start | bytes 4718600 | tf_op jit(solution)/shard_map/ppermute | solution.py:16
  12.2 84.9 %collective-permute-start.1 = (bf16[2,256,1536]{1,2,0:T(8,128)(2,1)S(1)}, bf16[2,256,1536]{1,2,0:T(8,128)(2,1)}, u32[]{:S(2)}, u32[]{:S(2)}) collective-permute-start(bf16[2,256,1536]{1,2,0:T(8,128)(2,1)S(1)} %pad_maximum_fusion), channel_id=1, source_target_pairs={{8,0},{9,1},{10,2},{11,3},{12,4},{13,5},{14,6},{15,7},{24,16},{25,... | collective-permute-start | bytes 4718600 | tf_op jit(solution)/shard_map/ppermute | solution.py:16
  14.6 116.1 %collective-permute-start.2 = (bf16[2,256,1536]{1,2,0:T(8,128)(2,1)S(1)}, bf16[2,256,1536]{1,2,0:T(8,128)(2,1)}, u32[]{:S(2)}, u32[]{:S(2)}) collective-permute-start(bf16[2,256,1536]{1,2,0:T(8,128)(2,1)S(1)} %pad_maximum_fusion), channel_id=1, source_target_pairs={{7,0},{8,1},{9,2},{10,3},{11,4},{12,5},{13,6},{14,7},{15,8},{23,16... | collective-permute-start | bytes 4718600 | tf_op jit(solution)/shard_map/ppermute | solution.py:16
  17.1 125.3 %collective-permute-start.3 = (bf16[2,256,1536]{1,2,0:T(8,128)(2,1)S(1)}, bf16[2,256,1536]{1,2,0:T(8,128)(2,1)}, u32[]{:S(2)}, u32[]{:S(2)}) collective-permute-start(bf16[2,256,1536]{1,2,0:T(8,128)(2,1)S(1)} %pad_maximum_fusion), channel_id=1, source_target_pairs={{1,0},{2,1},{3,2},{4,3},{5,4},{6,5},{7,6},{8,7},{9,8},{10,9},{11,1... | collective-permute-start | bytes 4718600 | tf_op jit(solution)/shard_map/ppermute | solution.py:16
  19.7 127.0 %collective-permute-start.4 = (bf16[2,256,1536]{1,2,0:T(8,128)(2,1)S(1)}, bf16[2,256,1536]{1,2,0:T(8,128)(2,1)}, u32[]{:S(2)}, u32[]{:S(2)}) collective-permute-start(bf16[2,256,1536]{1,2,0:T(8,128)(2,1)S(1)} %pad_maximum_fusion), channel_id=1, source_target_pairs={{0,1},{1,2},{2,3},{3,4},{4,5},{5,6},{6,7},{7,8},{8,9},{9,10},{10,1... | collective-permute-start | bytes 4718600 | tf_op jit(solution)/shard_map/ppermute | solution.py:16
  24.2 7.0 %copy-start.84 = (bf16[1,256,256]{1,2,0:T(8,128)(2,1)S(1)}, bf16[1,256,256]{1,2,0:T(8,128)(2,1)}, u32[]{:S(2)}) copy-start(bf16[1,256,256]{1,2,0:T(8,128)(2,1)} %get-tuple-element.110) | copy-start | bytes 393220
  56.0 95.0 %collective-permute-start.5 = (bf16[2,256,1536]{1,2,0:T(8,128)(2,1)S(1)}, bf16[2,256,1536]{1,2,0:T(8,128)(2,1)}, u32[]{:S(2)}, u32[]{:S(2)}) collective-permute-start(bf16[2,256,1536]{1,2,0:T(8,128)(2,1)S(1)} %pad_maximum_fusion), channel_id=1, source_target_pairs={{0,7},{1,8},{2,9},{3,10},{4,11},{5,12},{6,13},{7,14},{8,15},{16,23... | collective-permute-start | bytes 4718600 | tf_op jit(solution)/shard_map/ppermute | solution.py:16
  97.1 58.1 %collective-permute-start.6 = (bf16[2,256,1536]{1,2,0:T(8,128)(2,1)S(1)}, bf16[2,256,1536]{1,2,0:T(8,128)(2,1)}, u32[]{:S(2)}, u32[]{:S(2)}) collective-permute-start(bf16[2,256,1536]{1,2,0:T(8,128)(2,1)S(1)} %pad_maximum_fusion), channel_id=1, source_target_pairs={{0,8},{1,9},{2,10},{3,11},{4,12},{5,13},{6,14},{7,15},{16,24},{17,... | collective-permute-start | bytes 4718600 | tf_op jit(solution)/shard_map/ppermute | solution.py:16
  130.8 198.2 %collective-permute-start.7 = (bf16[2,256,1536]{1,2,0:T(8,128)(2,1)S(1)}, bf16[2,256,1536]{1,2,0:T(8,128)(2,1)S(1)}, u32[]{:S(2)}, u32[]{:S(2)}) collective-permute-start(bf16[2,256,1536]{1,2,0:T(8,128)(2,1)S(1)} %pad_maximum_fusion), channel_id=1, source_target_pairs={{0,9},{1,10},{2,11},{3,12},{4,13},{5,14},{6,15},{16,25},{17,26},{1... | collective-permute-start | bytes 4718600 | tf_op jit(solution)/shard_map/ppermute | solution.py:16
  329.9 5.5 %copy-start.79 = (bf16[1,256,256]{1,2,0:T(8,128)(2,1)S(1)}, bf16[1,256,256]{1,2,0:T(8,128)(2,1)}, u32[]{:S(2)}) copy-start(bf16[1,256,256]{1,2,0:T(8,128)(2,1)} %get-tuple-element.37) | copy-start | bytes 393220
  329.9 6.3 %copy-start.82 = (bf16[1,256,256]{1,2,0:T(8,128)(2,1)S(1)}, bf16[1,256,256]{1,2,0:T(8,128)(2,1)}, u32[]{:S(2)}) copy-start(bf16[1,256,256]{1,2,0:T(8,128)(2,1)} %get-tuple-element.25) | copy-start | bytes 393220
  329.9 7.0 %copy-start.86 = (bf16[1,256,256]{1,2,0:T(8,128)(2,1)S(1)}, bf16[1,256,256]{1,2,0:T(8,128)(2,1)}, u32[]{:S(2)}) copy-start(bf16[1,256,256]{1,2,0:T(8,128)(2,1)} %get-tuple-element.13) | copy-start | bytes 393220
  329.9 7.8 %copy-start.50 = (bf16[1,256,256]{1,2,0:T(8,128)(2,1)S(1)}, bf16[1,256,256]{1,2,0:T(8,128)(2,1)}, u32[]{:S(2)}) copy-start(bf16[1,256,256]{1,2,0:T(8,128)(2,1)} %get-tuple-element.95) | copy-start | bytes 393220
  330.7 7.8 %copy-start.56 = (bf16[1,256,256]{1,2,0:T(8,128)(2,1)S(1)}, bf16[1,256,256]{1,2,0:T(8,128)(2,1)}, u32[]{:S(2)}) copy-start(bf16[1,256,256]{1,2,0:T(8,128)(2,1)} %get-tuple-element.83) | copy-start | bytes 393220
  331.4 7.8 %copy-start.62 = (bf16[1,256,256]{1,2,0:T(8,128)(2,1)S(1)}, bf16[1,256,256]{1,2,0:T(8,128)(2,1)}, u32[]{:S(2)}) copy-start(bf16[1,256,256]{1,2,0:T(8,128)(2,1)} %get-tuple-element.71) | copy-start | bytes 393220
  332.2 7.8 %copy-start.68 = (bf16[1,256,256]{1,2,0:T(8,128)(2,1)S(1)}, bf16[1,256,256]{1,2,0:T(8,128)(2,1)}, u32[]{:S(2)}) copy-start(bf16[1,256,256]{1,2,0:T(8,128)(2,1)} %get-tuple-element.59) | copy-start | bytes 393220
  332.9 7.8 %copy-start.73 = (bf16[1,256,256]{1,2,0:T(8,128)(2,1)S(1)}, bf16[1,256,256]{1,2,0:T(8,128)(2,1)}, u32[]{:S(2)}) copy-start(bf16[1,256,256]{1,2,0:T(8,128)(2,1)} %get-tuple-element.47) | copy-start | bytes 393220
  334.6 6.8 %copy-start.77 = (bf16[1,256,256]{1,2,0:T(8,128)(2,1)S(1)}, bf16[1,256,256]{1,2,0:T(8,128)(2,1)}, u32[]{:S(2)}) copy-start(bf16[1,256,256]{1,2,0:T(8,128)(2,1)} %get-tuple-element.35) | copy-start | bytes 393220
  335.4 6.8 %copy-start.80 = (bf16[1,256,256]{1,2,0:T(8,128)(2,1)S(1)}, bf16[1,256,256]{1,2,0:T(8,128)(2,1)}, u32[]{:S(2)}) copy-start(bf16[1,256,256]{1,2,0:T(8,128)(2,1)} %get-tuple-element.23) | copy-start | bytes 393220
  336.1 6.8 %copy-start.83 = (bf16[1,256,256]{1,2,0:T(8,128)(2,1)S(1)}, bf16[1,256,256]{1,2,0:T(8,128)(2,1)}, u32[]{:S(2)}) copy-start(bf16[1,256,256]{1,2,0:T(8,128)(2,1)} %get-tuple-element.11) | copy-start | bytes 393220
  336.9 6.8 %copy-start.46 = (bf16[1,256,256]{1,2,0:T(8,128)(2,1)S(1)}, bf16[1,256,256]{1,2,0:T(8,128)(2,1)}, u32[]{:S(2)}) copy-start(bf16[1,256,256]{1,2,0:T(8,128)(2,1)} %get-tuple-element.93) | copy-start | bytes 393220
  337.7 6.8 %copy-start.51 = (bf16[1,256,256]{1,2,0:T(8,128)(2,1)S(1)}, bf16[1,256,256]{1,2,0:T(8,128)(2,1)}, u32[]{:S(2)}) copy-start(bf16[1,256,256]{1,2,0:T(8,128)(2,1)} %get-tuple-element.81) | copy-start | bytes 393220
  338.4 6.8 %copy-start.57 = (bf16[1,256,256]{1,2,0:T(8,128)(2,1)S(1)}, bf16[1,256,256]{1,2,0:T(8,128)(2,1)}, u32[]{:S(2)}) copy-start(bf16[1,256,256]{1,2,0:T(8,128)(2,1)} %get-tuple-element.69) | copy-start | bytes 393220
  339.2 6.8 %copy-start.63 = (bf16[1,256,256]{1,2,0:T(8,128)(2,1)S(1)}, bf16[1,256,256]{1,2,0:T(8,128)(2,1)}, u32[]{:S(2)}) copy-start(bf16[1,256,256]{1,2,0:T(8,128)(2,1)} %get-tuple-element.57) | copy-start | bytes 393220
  339.9 6.8 %copy-start.69 = (bf16[1,256,256]{1,2,0:T(8,128)(2,1)S(1)}, bf16[1,256,256]{1,2,0:T(8,128)(2,1)}, u32[]{:S(2)}) copy-start(bf16[1,256,256]{1,2,0:T(8,128)(2,1)} %get-tuple-element.45) | copy-start | bytes 393220
  340.7 6.8 %copy-start.74 = (bf16[1,256,256]{1,2,0:T(8,128)(2,1)S(1)}, bf16[1,256,256]{1,2,0:T(8,128)(2,1)}, u32[]{:S(2)}) copy-start(bf16[1,256,256]{1,2,0:T(8,128)(2,1)} %get-tuple-element.33) | copy-start | bytes 393220
  341.5 6.8 %copy-start.78 = (bf16[1,256,256]{1,2,0:T(8,128)(2,1)S(1)}, bf16[1,256,256]{1,2,0:T(8,128)(2,1)}, u32[]{:S(2)}) copy-start(bf16[1,256,256]{1,2,0:T(8,128)(2,1)} %get-tuple-element.21) | copy-start | bytes 393220
  342.2 6.8 %copy-start.81 = (bf16[1,256,256]{1,2,0:T(8,128)(2,1)S(1)}, bf16[1,256,256]{1,2,0:T(8,128)(2,1)}, u32[]{:S(2)}) copy-start(bf16[1,256,256]{1,2,0:T(8,128)(2,1)} %get-tuple-element.9) | copy-start | bytes 393220
  343.0 6.8 %copy-start.43 = (bf16[1,256,256]{1,2,0:T(8,128)(2,1)S(1)}, bf16[1,256,256]{1,2,0:T(8,128)(2,1)}, u32[]{:S(2)}) copy-start(bf16[1,256,256]{1,2,0:T(8,128)(2,1)} %get-tuple-element.91) | copy-start | bytes 393220
  343.7 6.8 %copy-start.47 = (bf16[1,256,256]{1,2,0:T(8,128)(2,1)S(1)}, bf16[1,256,256]{1,2,0:T(8,128)(2,1)}, u32[]{:S(2)}) copy-start(bf16[1,256,256]{1,2,0:T(8,128)(2,1)} %get-tuple-element.79) | copy-start | bytes 393220
  344.5 6.8 %copy-start.52 = (bf16[1,256,256]{1,2,0:T(8,128)(2,1)S(1)}, bf16[1,256,256]{1,2,0:T(8,128)(2,1)}, u32[]{:S(2)}) copy-start(bf16[1,256,256]{1,2,0:T(8,128)(2,1)} %get-tuple-element.67) | copy-start | bytes 393220
  345.2 6.8 %copy-start.59 = (bf16[1,256,256]{1,2,0:T(8,128)(2,1)S(1)}, bf16[1,256,256]{1,2,0:T(8,128)(2,1)}, u32[]{:S(2)}) copy-start(bf16[1,256,256]{1,2,0:T(8,128)(2,1)} %get-tuple-element.55) | copy-start | bytes 393220
  346.0 6.8 %copy-start.65 = (bf16[1,256,256]{1,2,0:T(8,128)(2,1)S(1)}, bf16[1,256,256]{1,2,0:T(8,128)(2,1)}, u32[]{:S(2)}) copy-start(bf16[1,256,256]{1,2,0:T(8,128)(2,1)} %get-tuple-element.43) | copy-start | bytes 393220
  346.8 6.8 %copy-start.70 = (bf16[1,256,256]{1,2,0:T(8,128)(2,1)S(1)}, bf16[1,256,256]{1,2,0:T(8,128)(2,1)}, u32[]{:S(2)}) copy-start(bf16[1,256,256]{1,2,0:T(8,128)(2,1)} %get-tuple-element.31) | copy-start | bytes 393220
  347.5 6.8 %copy-start.75 = (bf16[1,256,256]{1,2,0:T(8,128)(2,1)S(1)}, bf16[1,256,256]{1,2,0:T(8,128)(2,1)}, u32[]{:S(2)}) copy-start(bf16[1,256,256]{1,2,0:T(8,128)(2,1)} %get-tuple-element.19) | copy-start | bytes 393220
  349.0 7.8 %copy-start.41 = (bf16[1,256,256]{1,2,0:T(8,128)(2,1)S(1)}, bf16[1,256,256]{1,2,0:T(8,128)(2,1)}, u32[]{:S(2)}) copy-start(bf16[1,256,256]{1,2,0:T(8,128)(2,1)} %get-tuple-element.89) | copy-start | bytes 393220
  349.8 7.8 %copy-start.44 = (bf16[1,256,256]{1,2,0:T(8,128)(2,1)S(1)}, bf16[1,256,256]{1,2,0:T(8,128)(2,1)}, u32[]{:S(2)}) copy-start(bf16[1,256,256]{1,2,0:T(8,128)(2,1)} %get-tuple-element.77) | copy-start | bytes 393220
  350.6 7.8 %copy-start.48 = (bf16[1,256,256]{1,2,0:T(8,128)(2,1)S(1)}, bf16[1,256,256]{1,2,0:T(8,128)(2,1)}, u32[]{:S(2)}) copy-start(bf16[1,256,256]{1,2,0:T(8,128)(2,1)} %get-tuple-element.65) | copy-start | bytes 393220
  351.3 7.8 %copy-start.54 = (bf16[1,256,256]{1,2,0:T(8,128)(2,1)S(1)}, bf16[1,256,256]{1,2,0:T(8,128)(2,1)}, u32[]{:S(2)}) copy-start(bf16[1,256,256]{1,2,0:T(8,128)(2,1)} %get-tuple-element.53) | copy-start | bytes 393220
  352.1 7.8 %copy-start.60 = (bf16[1,256,256]{1,2,0:T(8,128)(2,1)S(1)}, bf16[1,256,256]{1,2,0:T(8,128)(2,1)}, u32[]{:S(2)}) copy-start(bf16[1,256,256]{1,2,0:T(8,128)(2,1)} %get-tuple-element.41) | copy-start | bytes 393220
  352.8 7.8 %copy-start.66 = (bf16[1,256,256]{1,2,0:T(8,128)(2,1)S(1)}, bf16[1,256,256]{1,2,0:T(8,128)(2,1)}, u32[]{:S(2)}) copy-start(bf16[1,256,256]{1,2,0:T(8,128)(2,1)} %get-tuple-element.29) | copy-start | bytes 393220
  353.6 7.8 %copy-start.71 = (bf16[1,256,256]{1,2,0:T(8,128)(2,1)S(1)}, bf16[1,256,256]{1,2,0:T(8,128)(2,1)}, u32[]{:S(2)}) copy-start(bf16[1,256,256]{1,2,0:T(8,128)(2,1)} %get-tuple-element.17) | copy-start | bytes 393220
  355.1 8.1 %copy-start = (bf16[2304,2,128]{0,2,1:T(8,128)(2,1)S(1)}, bf16[2304,2,128]{0,2,1:T(8,128)(2,1)}, u32[]{:S(2)}) copy-start(bf16[2304,2,128]{0,2,1:T(8,128)(2,1)} %constant_dynamic-update-slice_fusion.8) | copy-start | bytes 3538948
  355.1 8.1 %copy-start.42 = (bf16[1,256,256]{1,2,0:T(8,128)(2,1)S(1)}, bf16[1,256,256]{1,2,0:T(8,128)(2,1)}, u32[]{:S(2)}) copy-start(bf16[1,256,256]{1,2,0:T(8,128)(2,1)} %get-tuple-element.88) | copy-start | bytes 393220
  356.9 6.4 %copy-start.45 = (bf16[1,256,256]{1,2,0:T(8,128)(2,1)S(1)}, bf16[1,256,256]{1,2,0:T(8,128)(2,1)}, u32[]{:S(2)}) copy-start(bf16[1,256,256]{1,2,0:T(8,128)(2,1)} %get-tuple-element.76) | copy-start | bytes 393220
  357.6 5.7 %copy-start.49 = (bf16[1,256,256]{1,2,0:T(8,128)(2,1)S(1)}, bf16[1,256,256]{1,2,0:T(8,128)(2,1)}, u32[]{:S(2)}) copy-start(bf16[1,256,256]{1,2,0:T(8,128)(2,1)} %get-tuple-element.64) | copy-start | bytes 393220
  (109 other events, 139.3 us)
Sparse Core Ops, SparseCore 0:
  22.8 199.3 all-gather.1
where the time goes:
time: 407 us; the launch traced here: 406 us
  waiting for transfers between devices  254 us (62%)
  local copies, waits for them, and re-layouts  96.1 us (24%)
  starting transfers between devices  18.2 us (4%)
  matrix products  17.8 us (4%)
  between operations  15.2 us (4%)
  other arithmetic  4.45 us (1%)
    ppermute x8, waiting for transfers between devices, shifted(): lax.ppermute(value, axis, [(source, source + steps) for source in range(f...  254 us
    concatenate x60, local copies, waits for them, and re-layouts, body(): jnp.concatenate([received[shift_by][0, :, lower:lower + width] for shift_...  50.3 us
    unnamed x408, local copies, waits for them, and re-layouts  24 us
    slice x9, local copies, waits for them, and re-layouts, body(): received[shift_by][0, :, lower:lower + width]  19.9 us
    ppermute x8, starting transfers between devices, shifted(): lax.ppermute(value, axis, [(source, source + steps) for source in range(f...  18.2 us
  transfers between devices with their start and end apart: 9, of which 4 were waited for; matrix products, arithmetic and copies ran while one was open for 24% of the time, Pallas kernels for 0%

commit v1 on v0

v1 whole, which is shorter than its diff:
```python
import functools
import math

import jax
import jax.numpy as jnp
from jax import lax
from jax.experimental import pallas as pl
from jax.experimental.pallas import tpu as pltpu
from jax.sharding import PartitionSpec as P

HD = 128
FRAMES = 2
GRID_COLS = 8
EXTRA = 16
PIECES = 3
LOG2E = math.log2(math.e)
VMEM_BYTES = 48 * 1024 * 1024


def swap_bit(value, bit):
    count = lax.axis_size("seq")
    return lax.ppermute(value, "seq", [(s, s ^ bit) for s in range(count)])


def swap_group(value, groups):
    return lax.ppermute(value, "group", [(s, s ^ 1) for s in range(groups)])


def column_shift(value, steps):
    count = lax.axis_size("seq")
    pairs = [(s, s + steps) for s in range(count) if 0 <= s % GRID_COLS + steps < GRID_COLS]
    return lax.ppermute(value, "seq", pairs)


def row_pairs(parity):
    count = lax.axis_size("seq")
    rows = count // GRID_COLS
    pairs = []
    for s in range(count):
        row = s // GRID_COLS
        other = row + 1 if row % 2 == parity else row - 1
        if 0 <= other < rows:
            pairs.append((s, s + (other - row) * GRID_COLS))
    return pairs


def attend_kernel(rows, per_block, bias_ref, q_ref, k0, ka, kb, v0, va, vb, out_ref):
    factor = HD ** (-0.5) * LOG2E
    tile = rows // FRAMES
    nt = (((1,), (1,)), ((), ()))
    lse = jnp.zeros((rows, HD), jnp.float32)
    lane = lax.broadcasted_iota(jnp.int32, (rows, HD), 1)
    for head in range(per_block):
        cols = slice(head * HD, (head + 1) * HD)
        keys = [k0[:, cols], ka[0, :, cols], kb[0, :, cols]]
        values = [v0[:, cols], va[0, :, cols], vb[0, :, cols]]
        parts = []
        for frame in range(FRAMES):
            here = slice(frame * tile, (frame + 1) * tile)
            q = q_ref[here, cols]
            bias = bias_ref[frame : frame + 1, :].astype(jnp.float32)
            scores = [
                lax.dot_general(q, key, nt, preferred_element_type=jnp.float32)
                + bias[:, i * rows : (i + 1) * rows]
                for i, key in enumerate(keys)
            ]
            peak = functools.reduce(jnp.maximum, scores)
            peak = jnp.max(peak, axis=1, keepdims=True)
            weights = [jnp.exp2((s - peak) * factor) for s in scores]
            total = jnp.sum(functools.reduce(jnp.add, weights), axis=1, keepdims=True)
            mixed = functools.reduce(
                jnp.add,
                [
                    jnp.dot(w.astype(jnp.bfloat16), v, preferred_element_type=jnp.float32)
                    for w, v in zip(weights, values)
                ],
            )
            out_ref[here, cols] = (mixed / total).astype(out_ref.dtype)
            parts.append(peak * factor + jnp.log2(total))
        lse = jnp.where(lane == head, jnp.concatenate(parts, axis=0), lse)
    turned = jnp.transpose(lse)
    stats = []
    for head in range(per_block):
        rest = turned[head : head + 1, :]
        for _ in range(PIECES):
            piece = rest.astype(out_ref.dtype)
            stats.append(piece.astype(jnp.float32))
            rest = rest - stats[-1]
    stats.append(jnp.zeros((EXTRA - len(stats), rows), jnp.float32))
    out_ref[rows:, :] = jnp.concatenate(stats, axis=0).astype(out_ref.dtype)


def attend(bias, q, q_first, heads, keys, values, kv_up, kv_down, first, kind):
    rows = keys.shape[0]
    per_block = rows // HD
    width = per_block * HD
    lo, q_lo = first * HD // width, q_first * HD // width
    here = pl.BlockSpec((rows, width), lambda i: (0, lo + i))
    key_spec = pl.BlockSpec((1, rows, width), lambda i: (0, 0, lo + i))
    value_spec = pl.BlockSpec((1, rows, width), lambda i: (1, 0, lo + i))
    span = 3 * rows
    return pl.pallas_call(
        functools.partial(attend_kernel, rows, per_block),
        grid=(heads // per_block,),
        in_specs=[
            pl.BlockSpec(bias.shape, lambda i: (0, 0)),
            pl.BlockSpec((rows, width), lambda i: (0, q_lo + i)),
            here,
            key_spec,
            key_spec,
            here,
            value_spec,
            value_spec,
        ],
        out_specs=pl.BlockSpec((rows + EXTRA, width), lambda i: (0, i)),
        out_shape=jax.ShapeDtypeStruct((rows + EXTRA, heads * HD), kind),
        compiler_params=pltpu.CompilerParams(vmem_limit_bytes=VMEM_BYTES),
        cost_estimate=pl.CostEstimate(
            flops=4 * heads * rows * span * HD,
            bytes_accessed=heads * HD * 2 * (2 * span + 2 * rows),
            transcendentals=heads * rows * span,
        ),
    )(bias, q, keys, kv_up, kv_down, values, kv_up, kv_down)


def project_kernel(rows, plan, chunk_counts, *refs):
    sources = len(plan)
    weights = refs[:sources]
    partner_ref = refs[sources]
    cursor = sources + 1
    own = refs[cursor]
    cursor += 1
    others = []
    for count in chunk_counts:
        others.append(refs[cursor : cursor + count])
        cursor += count
    out_ref, held, attention, sems = refs[cursor:]
    copies = []
    for source, moves in zip(weights, plan):
        for from_row, count, place in moves:
            into = pl.multiple_of(place(), 16)
            copy = pltpu.make_async_copy(
                source.at[pl.ds(from_row, count), :],
                held.at[pl.ds(into, count), :],
                sems.at[len(copies)],
            )
            copy.start()
            copies.append(copy)
    per_block = rows // HD
    width = per_block * HD
    features = own.shape[1]
    for block in range(features // width):
        cols = slice(block * width, (block + 1) * width)
        tiles = [own[:, cols].astype(jnp.float32)]
        for number, chunks in enumerate(others):
            chunk_width = chunks[0].shape[1]
            index, offset = divmod(block * width, chunk_width)
            tiles.append(chunks[index][:, offset : offset + width].astype(jnp.float32))
        shares = []
        for head in range(per_block):
            lses = []
            for number, t in enumerate(tiles):
                row = rows + PIECES * head
                lse = functools.reduce(
                    jnp.add, [t[row + i : row + i + 1, :] for i in range(PIECES)]
                )
                if number:
                    lse = jnp.where(partner_ref[number - 1] == 1, lse, -jnp.inf)
                lses.append(lse)
            top = functools.reduce(jnp.maximum, lses)
            raw = [jnp.exp2(lse - top) for lse in lses]
            total = functools.reduce(jnp.add, raw)
            shares.extend(r / total for r in raw)
        shares.append(jnp.zeros((HD - len(shares), rows), jnp.float32))
        turned = jnp.transpose(jnp.concatenate(shares, axis=0))
        for head in range(per_block):
            inner = slice(head * HD, (head + 1) * HD)
            mixed = functools.reduce(
                jnp.add,
                [
                    t[:rows, inner] * turned[:, head * len(tiles) + n : head * len(tiles) + n + 1]
                    for n, t in enumerate(tiles)
                ],
            )
            start = block * width + head * HD
            attention[:, start : start + HD] = mixed.astype(jnp.bfloat16)
    for copy in copies:
        copy.wait()
    columns = out_ref.shape[1]
    step = math.gcd(columns, 512)

    @pl.loop(0, columns // step)
    def _(i):
        there = pl.ds(pl.multiple_of(i * step, step), step)
        out_ref[:, there] = jnp.dot(
            attention[...], held[:, there], preferred_element_type=jnp.float32
        ).astype(out_ref.dtype)


def project(pieces, partner, own, others):
    arrays = [array for array, _ in pieces]
    plan = [moves for _, moves in pieces]
    rows, features = own.shape[0] - EXTRA, own.shape[1]
    columns = arrays[0].shape[1]
    flat = [chunk for chunks in others for chunk in chunks]
    vmem = pl.BlockSpec(memory_space=pltpu.VMEM)
    return pl.pallas_call(
        functools.partial(project_kernel, rows, plan, [len(c) for c in others]),
        in_specs=[pl.BlockSpec(memory_space=pl.ANY)] * len(arrays)
        + [pl.BlockSpec(memory_space=pltpu.SMEM)]
        + [vmem] * (1 + len(flat)),
        out_specs=vmem,
        out_shape=jax.ShapeDtypeStruct((rows, columns), jnp.bfloat16),
        scratch_shapes=[
            pltpu.VMEM((features, columns), jnp.bfloat16),
            pltpu.VMEM((rows, features), jnp.bfloat16),
            pltpu.SemaphoreType.DMA((sum(len(m) for m in plan),)),
        ],
        compiler_params=pltpu.CompilerParams(vmem_limit_bytes=VMEM_BYTES),
        cost_estimate=pl.CostEstimate(
            flops=2 * rows * features * columns,
            bytes_accessed=2 * features * columns,
            transcendentals=0,
        ),
    )(*arrays, partner, own, *flat)


def gather_weight(out_weight, groups, devices):
    shard = out_weight.shape[0]
    if devices != 16 or groups != 2 or shard % 32:
        whole = lax.all_gather(out_weight, "seq", axis=0, tiled=True)
        return [(whole, [(0, whole.shape[0], lambda: 0)])]
    half = shard // 2

    def full(*bits):
        def at(bit):
            return lambda: (lax.axis_index("seq") ^ bit) * shard

        return [(i * shard, shard, at(bit)) for i, bit in enumerate(bits)]

    def halves(*bits):
        def at(bit, turn):
            return lambda: (lax.axis_index("seq") ^ bit) * shard + (
                lax.axis_index("group") ^ turn
            ) * half

        return [(i * half, half, at(bit, turn)) for i, (bit, turn) in enumerate(bits)]

    mine = lax.dynamic_slice_in_dim(out_weight, lax.axis_index("group") * half, half, 0)
    c0 = swap_bit(mine, 8)
    wz = swap_bit(out_weight, 4)
    cz = swap_bit(c0, 4)
    near = jnp.concatenate([out_weight, wz], axis=0)
    wy = swap_bit(near, 2)
    far = jnp.concatenate([c0, cz], axis=0)
    cy = swap_bit(far, 2)
    quad = jnp.concatenate([near, wy], axis=0)
    wc = swap_bit(quad, 1)
    four = jnp.concatenate([far, cy], axis=0)
    cx = swap_group(four, groups)
    eight = jnp.concatenate([four, cx], axis=0)
    cc = swap_bit(eight, 1)
    return [
        (quad, full(0, 4, 2, 6)),
        (wc, full(1, 5, 3, 7)),
        (eight, halves((8, 0), (12, 0), (10, 0), (14, 0), (8, 1), (12, 1), (10, 1), (14, 1))),
        (cc, halves((9, 0), (13, 0), (11, 0), (15, 0), (9, 1), (13, 1), (11, 1), (15, 1))),
    ]


def body(groups, query_rows, key_rows, value_rows, block_list, out_weight):
    rows, features = query_rows.shape
    heads = features // HD
    devices = lax.axis_size("seq")
    grid_rows = devices // GRID_COLS
    position = lax.axis_index("seq")
    row = position // GRID_COLS
    tile = rows // FRAMES
    chunk_heads = heads // 2
    chunk = chunk_heads * HD

    def bias_for(there):
        centre = there * GRID_COLS + position % GRID_COLS
        places = centre + jnp.array([0, -1, 1], jnp.int32)
        ids = (places[:, None] * FRAMES + jnp.arange(FRAMES, dtype=jnp.int32)[None, :]).reshape(-1)
        ids = jnp.where(ids >= 0, ids, -2)
        member = jnp.any(block_list[:, :, None] == ids[None, None, :], axis=1)
        return jnp.repeat(jnp.where(member, 0.0, -jnp.inf), tile, axis=1)

    kv = jnp.stack([key_rows, value_rows])
    pieces = gather_weight(out_weight, groups, devices)
    phases = [parity for parity in range(2) if parity + 1 < grid_rows]
    sent = []
    for parity in phases:
        there = jnp.where(row % 2 == parity, row + 1, row - 1)
        bias = bias_for(there).reshape(-1).astype(jnp.bfloat16)
        bias = jnp.pad(bias, (0, EXTRA * chunk - bias.shape[0])).reshape(EXTRA, chunk)
        pairs = row_pairs(parity)
        first = jnp.concatenate([query_rows[:, :chunk], bias], axis=0)
        sent.append(
            [
                lax.ppermute(first, "seq", pairs),
                lax.ppermute(query_rows[:, chunk:], "seq", pairs),
            ]
        )
    kv_up = column_shift(kv, 1)
    kv_down = column_shift(kv, -1)
    common = (key_rows, value_rows, kv_up, kv_down)
    others = []
    for parity, asked in zip(phases, sent):
        bias = asked[0][rows:, :].reshape(-1)[: FRAMES * 3 * rows].reshape(FRAMES, 3 * rows)
        pairs = row_pairs(parity)
        back = []
        for number, q in enumerate(asked):
            part = attend(bias, q, 0, chunk_heads, *common, number * chunk_heads, jnp.bfloat16)
            back.append(lax.ppermute(part, "seq", pairs))
        others.append(back)
    own = attend(bias_for(row), query_rows, 0, heads, *common, 0, jnp.float32)
    partner = jnp.stack(
        [
            jnp.where(row % 2 == parity, row + 1 < grid_rows, row > 0).astype(jnp.int32)
            for parity in phases
        ]
        or [jnp.int32(0)]
    )
    return project(pieces, partner, own, others)


def solution(mesh):
    placed = (
        P(("group", "seq"), None),
        P(("group", "seq"), None),
        P(("group", "seq"), None),
        P(("group", "seq"), None),
        P("seq", None),
    )
    return jax.shard_map(
        functools.partial(body, mesh.shape["group"]),
        mesh=mesh,
        in_specs=placed,
        out_specs=P(("group", "seq"), None),
        check_vma=False,
    )
```

time: 407 us -> 198 us (0.49)
  the two profiles are of different devices: /device:TPU:27 before, /device:TPU:0 now
where the time goes in v1:
time: 198 us
  waiting for transfers between devices  106 us (54%)
  starting transfers between devices  39.4 us (20%)
  Pallas kernels  31 us (16%)
  local copies, waits for them, and re-layouts  16.8 us (8%)
  other arithmetic  4.44 us (2%)
    ppermute x7, waiting for transfers between devices, swap_bit(): return lax.ppermute(value, 'seq', [(s, s ^ bit) for s in range(count)])  48.6 us
    ppermute x7, starting transfers between devices, swap_bit(): return lax.ppermute(value, 'seq', [(s, s ^ bit) for s in range(count)])  29.2 us
    pallas_call x3, Pallas kernels, attend(): pl.pallas_call(functools.partial(attend_kernel, rows, per_block), grid=(h...  21.4 us
    ppermute x1, waiting for transfers between devices, body(): lax.ppermute(first, 'seq', pairs)  20.7 us
    ppermute x1, waiting for transfers between devices, body(): lax.ppermute(query_rows[:, chunk:], 'seq', pairs)  19.4 us
    ppermute x2, waiting for transfers between devices, body(): back.append(lax.ppermute(part, 'seq', pairs))  16.5 us
    unnamed x23, local copies, waits for them, and re-layouts  11.2 us
    pallas_call x1, Pallas kernels, project(): pl.pallas_call(functools.partial(project_kernel, rows, plan, [len(c) for...  9.61 us
  transfers between devices with their start and end apart: 14, of which 9 were waited for; matrix products, arithmetic and copies ran while one was open for 7% of the time, Pallas kernels for 11%

profile of v1, /device:TPU:0, one launch (start us, length us, event | category | flops | bytes accessed | tf_op | source)
XLA Modules:
  0.0 197.9 jit_solution(10997757872825532031)
XLA Ops:
  0.0 2.7 %pad_maximum_fusion = bf16[2,256,1536]{2,1,0:T(8,128)(2,1)} fusion(bf16[1,256,1536]{2,1,0:T(8,128)(2,1)} %bitcast.9, bf16[1,256,1536]{2,1,0:T(8,128)(2,1)} %bitcast.8), kind=kLoop, calls=%fused_computation | loop fusion | flops 786432 | bytes 3145728 | tf_op jit(solution)/shard_map/stack | solution.py:290
  2.7 1.3 collective-permute-start.9
  4.0 3.1 %collective-permute-start.8 = (bf16[2,256,1536]{2,1,0:T(8,128)(2,1)}, bf16[2,256,1536]{2,1,0:T(8,128)(2,1)S(1)}, u32[]{:S(2)}, u32[]{:S(2)}) collective-permute-start(bf16[2,256,1536]{2,1,0:T(8,128)(2,1)} %pad_maximum_fusion), channel_id=1, source_target_pairs={{0,1},{1,2},{2,3},{3,4},{4,5},{5,6},{6,7},{8,9},{9,10},{10,11},{11... | collective-permute-start | bytes 4718600 | tf_op jit(solution)/shard_map/ppermute | solution.py:32
  7.1 3.3 %collective-permute-start = (bf16[96,3072]{1,0:T(8,128)(2,1)}, bf16[96,3072]{1,0:T(8,128)(2,1)}, u32[]{:S(2)}, u32[]{:S(2)}) collective-permute-start(bf16[96,3072]{1,0:T(8,128)(2,1)} %param.11), channel_id=1, source_target_pairs={{0,4},{1,5},{2,6},{3,7},{4,0},{5,1},{6,2},{7,3},{8,12},{9,13},{10,... | collective-permute-start | bytes 1769480 | tf_op jit(solution)/shard_map/ppermute | solution.py:22
  10.4 1.7 constant_dynamic-slice_fusion
  12.2 2.6 %collective-permute-start.3 = (bf16[48,3072]{1,0:T(8,128)(2,1)}, bf16[48,3072]{1,0:T(8,128)(2,1)S(1)}, u32[]{:S(2)}, u32[]{:S(2)}) collective-permute-start(bf16[48,3072]{1,0:T(8,128)(2,1)} %constant_dynamic-slice_fusion), channel_id=1, source_target_pairs={{0,8},{1,9},{2,10},{3,11},{4,12},{5,13},{6,14},{7,15},{8,0},{9,1},... | collective-permute-start | bytes 884744 | tf_op jit(solution)/shard_map/ppermute | solution.py:22
  14.8 0.1 iota_add_fusion
  14.8 0.1 add.97
  14.9 0.1 add.90
  15.0 15.6 %collective-permute-done.3 = bf16[48,3072]{1,0:T(8,128)(2,1)S(1)} collective-permute-done((bf16[48,3072]{1,0:T(8,128)(2,1)}, bf16[48,3072]{1,0:T(8,128)(2,1)S(1)}, u32[]{:S(2)}, u32[]{:S(2)}) %collective-permute-start.3) | collective-permute-done | bytes 294944 | tf_op jit(solution)/shard_map/ppermute | solution.py:22
  30.6 21.1 %collective-permute-start.4 = (bf16[48,3072]{1,0:T(8,128)(2,1)S(1)}, bf16[48,3072]{1,0:T(8,128)(2,1)S(1)}, u32[]{:S(2)}, u32[]{:S(2)}) collective-permute-start(bf16[48,3072]{1,0:T(8,128)(2,1)S(1)} %collective-permute-done.3), channel_id=1, source_target_pairs={{0,4},{1,5},{2,6},{3,7},{4,0},{5,1},{6,2},{7,3},{8,12},{9,13},{10,... | collective-permute-start | bytes 884744 | tf_op jit(solution)/shard_map/ppermute | solution.py:22
  51.7 2.0 constant_dynamic-update-slice_fusion.2
  53.7 2.7 %collective-permute-done.4 = bf16[48,3072]{1,0:T(8,128)(2,1)S(1)} collective-permute-done((bf16[48,3072]{1,0:T(8,128)(2,1)S(1)}, bf16[48,3072]{1,0:T(8,128)(2,1)S(1)}, u32[]{:S(2)}, u32[]{:S(2)}) %collective-permute-start.4) | collective-permute-done | bytes 294944 | tf_op jit(solution)/shard_map/ppermute | solution.py:22
  56.5 0.1 collective-permute-start.5
  56.6 0.7 constant_dynamic-update-slice_fusion.6
  57.3 0.0 collective-permute-done
  57.3 1.3 pad_maximum_fusion.1
  58.6 2.1 %collective-permute-start.1 = (bf16[192,3072]{1,0:T(8,128)(2,1)S(1)}, bf16[192,3072]{1,0:T(8,128)(2,1)S(1)}, u32[]{:S(2)}, u32[]{:S(2)}) collective-permute-start(bf16[192,3072]{1,0:T(8,128)(2,1)S(1)} %pad_maximum_fusion.1), channel_id=1, source_target_pairs={{0,2},{1,3},{2,0},{3,1},{4,6},{5,7},{6,4},{7,5},{8,10},{9,11},{10,... | collective-permute-start | bytes 3538952 | tf_op jit(solution)/shard_map/ppermute | solution.py:22
  60.7 12.1 %collective-permute-done.5 = bf16[96,3072]{1,0:T(8,128)(2,1)S(1)} collective-permute-done((bf16[96,3072]{1,0:T(8,128)(2,1)S(1)}, bf16[96,3072]{1,0:T(8,128)(2,1)S(1)}, u32[]{:S(2)}, u32[]{:S(2)}) %collective-permute-start.5) | collective-permute-done | bytes 589856 | tf_op jit(solution)/shard_map/ppermute | solution.py:22
  72.8 0.1 pad_maximum_fusion.2
  72.9 1.6 collective-permute-start.6
  74.5 0.7 constant_dynamic-update-slice_fusion.5
  75.2 1.9 constant_dynamic-update-slice_fusion.1
  77.1 0.9 constant_dynamic-update-slice_fusion.4
  78.0 18.1 %collective-permute-done.1 = bf16[192,3072]{1,0:T(8,128)(2,1)S(1)} collective-permute-done((bf16[192,3072]{1,0:T(8,128)(2,1)S(1)}, bf16[192,3072]{1,0:T(8,128)(2,1)S(1)}, u32[]{:S(2)}, u32[]{:S(2)}) %collective-permute-start.1) | collective-permute-done | bytes 1179680 | tf_op jit(solution)/shard_map/ppermute | solution.py:22
  96.2 1.1 constant_dynamic-update-slice_fusion.refs_0_
  97.3 0.9 collective-permute-done.6
  98.2 1.2 constant_dynamic-update-slice_fusion.3.refs_2_
  99.4 0.2 compare_reduce_fusion
  99.6 0.1 broadcast_in_dim.33
  99.7 0.0 copy-start
  99.8 0.0 copy-start.2
  99.8 1.3 fusion
  101.1 1.3 collective-permute-start.10
  102.4 20.7 %collective-permute-done.10.q_ref = bf16[272,768]{1,0:T(8,128)(2,1)S(1)} collective-permute-done((bf16[272,768]{1,0:T(8,128)(2,1)S(1)}, bf16[272,768]{1,0:T(8,128)(2,1)S(1)}, u32[]{:S(2)}, u32[]{:S(2)}) %collective-permute-start.10) | collective-permute-done | bytes 417824 | tf_op jit(solution)/shard_map/ppermute | solution.py:302
  123.1 19.4 %collective-permute-done.12.q_ref = bf16[256,768]{1,0:T(8,128)(2,1)S(1)} collective-permute-done((bf16[256,768]{1,0:T(8,128)(2,1)S(1)}, bf16[256,768]{1,0:T(8,128)(2,1)S(1)}, u32[]{:S(2)}, u32[]{:S(2)}) %collective-permute-start.12) | collective-permute-done | bytes 393248 | tf_op jit(solution)/shard_map/ppermute | solution.py:303
  142.5 5.5 %shard_map.75 = bf16[272,768]{1,0:T(8,128)(2,1)} custom-call(bf16[2,768]{1,0:T(2,128)(2,1)S(1)} %slice.15.bias_ref, bf16[256,768]{1,0:T(8,128)(2,1)S(1)} %collective-permute-done.12.q_ref, bf16[256,1536]{1,0:T(8,128)(2,1)S(1)} %copy-done, bf16[2,256,1536]{2,1,0:T(8,128)(2,1)S(1)} %collective-permute-done.8.ka.va, ...), custom_call_target="tpu_custom_call" | custom-call | flops 603979776 | bytes 3145728 | tf_op jit(solution)/shard_map/pallas_call | solution.py:102
  148.0 5.4 %shard_map.74 = bf16[272,768]{1,0:T(8,128)(2,1)} custom-call(bf16[2,768]{1,0:T(2,128)(2,1)S(1)} %slice.15.bias_ref, bf16[272,768]{1,0:T(8,128)(2,1)S(1)} %collective-permute-done.10.q_ref, bf16[256,1536]{1,0:T(8,128)(2,1)S(1)} %copy-done, bf16[2,256,1536]{2,1,0:T(8,128)(2,1)S(1)} %collective-permute-done.8.ka.va, ...), custom_call_target="tpu_custom_call" | custom-call | flops 603979776 | bytes 3145728 | tf_op jit(solution)/shard_map/pallas_call | solution.py:102
  153.4 2.9 %collective-permute-start.11 = (bf16[272,768]{1,0:T(8,128)(2,1)}, bf16[272,768]{1,0:T(8,128)(2,1)}, u32[]{:S(2)}, u32[]{:S(2)}) collective-permute-start(bf16[272,768]{1,0:T(8,128)(2,1)} %shard_map.74), channel_id=1, source_target_pairs={{0,8},{1,9},{2,10},{3,11},{4,12},{5,13},{6,14},{7,15},{8,0},{9,1},... | collective-permute-start | bytes 1253384 | tf_op jit(solution)/shard_map/ppermute | solution.py:316
  156.3 0.1 broadcast_bitcast_fusion
  156.4 1.1 copy-done.1
  157.6 1.1 copy-done.3
  158.7 1.1 copy-done.5
  159.8 10.5 %shard_map.73.refs_5_ = f32[272,1536]{1,0:T(8,128)} custom-call(f32[2,768]{1,0:T(2,128)S(1)} %bitcast.10, bf16[256,1536]{1,0:T(8,128)(2,1)S(1)} %copy-done.5, bf16[256,1536]{1,0:T(8,128)(2,1)S(1)} %copy-done.1, bf16[2,256,1536]{2,1,0:T(8,128)(2,1)S(1)} %collective-permute-done.8.ka.va, bf16[2,256,1536]{2,1,0:T(8,128)(2,1)S(1)} %collective-permute-done.9.kb.vb, ...), custom_call_target="tpu_custom_call" | custom-call | flops 1207959552 | bytes 6291456 | tf_op jit(solution)/shard_map/pallas_call | solution.py:102
  170.3 7.7 %collective-permute-done.13.refs_7_ = bf16[272,768]{1,0:T(8,128)(2,1)} collective-permute-done((bf16[272,768]{1,0:T(8,128)(2,1)}, bf16[272,768]{1,0:T(8,128)(2,1)}, u32[]{:S(2)}, u32[]{:S(2)}) %collective-permute-start.13) | collective-permute-done | bytes 417824 | tf_op jit(solution)/shard_map/ppermute | solution.py:316
  178.0 8.9 %collective-permute-done.11.refs_6_ = bf16[272,768]{1,0:T(8,128)(2,1)} collective-permute-done((bf16[272,768]{1,0:T(8,128)(2,1)}, bf16[272,768]{1,0:T(8,128)(2,1)}, u32[]{:S(2)}, u32[]{:S(2)}) %collective-permute-start.11) | collective-permute-done | bytes 417824 | tf_op jit(solution)/shard_map/ppermute | solution.py:316
  186.9 1.4 copy-done.4
  188.3 9.6 %shard_map.76 = bf16[256,3072]{1,0:T(8,128)(2,1)} custom-call(bf16[384,3072]{1,0:T(8,128)(2,1)} %constant_dynamic-update-slice_fusion.refs_0_, bf16[384,3072]{1,0:T(8,128)(2,1)} %collective-permute-done.2.refs_1_, bf16[384,3072]{1,0:T(8,128)(2,1)} %constant_dynamic-update-slice_fusion.3.refs_2_, bf16[384,3072]{1,0:T(8,128)(2,1)} %collective-permute-done.7.refs_3_, ...), custom_call_target="tpu_custom_call" | custom-call | flops 2415919104 | bytes 9437184 | tf_op jit(solution)/shard_map/pallas_call | solution.py:207
  (30 shorter events, 0.2 us)
Async XLA Ops:
  0.0 14.7 %copy-start.7 = (s32[3]{0:T(128)S(1)}, s32[3]{0:T(128)}, u32[]{:S(2)}) copy-start(s32[3]{0:T(128)} %constant.69.clone) | copy-start | bytes 40
  2.7 139.8 %collective-permute-start.9 = (bf16[2,256,1536]{2,1,0:T(8,128)(2,1)}, bf16[2,256,1536]{2,1,0:T(8,128)(2,1)S(1)}, u32[]{:S(2)}, u32[]{:S(2)}) collective-permute-start(bf16[2,256,1536]{2,1,0:T(8,128)(2,1)} %pad_maximum_fusion), channel_id=1, source_target_pairs={{1,0},{2,1},{3,2},{4,3},{5,4},{6,5},{7,6},{9,8},{10,9},{11,10},{12... | collective-permute-start | bytes 4718600 | tf_op jit(solution)/shard_map/ppermute | solution.py:32
  4.0 138.5 %collective-permute-start.8 = (bf16[2,256,1536]{2,1,0:T(8,128)(2,1)}, bf16[2,256,1536]{2,1,0:T(8,128)(2,1)S(1)}, u32[]{:S(2)}, u32[]{:S(2)}) collective-permute-start(bf16[2,256,1536]{2,1,0:T(8,128)(2,1)} %pad_maximum_fusion), channel_id=1, source_target_pairs={{0,1},{1,2},{2,3},{3,4},{4,5},{5,6},{6,7},{8,9},{9,10},{10,11},{11... | collective-permute-start | bytes 4718600 | tf_op jit(solution)/shard_map/ppermute | solution.py:32
  7.1 50.2 %collective-permute-start = (bf16[96,3072]{1,0:T(8,128)(2,1)}, bf16[96,3072]{1,0:T(8,128)(2,1)}, u32[]{:S(2)}, u32[]{:S(2)}) collective-permute-start(bf16[96,3072]{1,0:T(8,128)(2,1)} %param.11), channel_id=1, source_target_pairs={{0,4},{1,5},{2,6},{3,7},{4,0},{5,1},{6,2},{7,3},{8,12},{9,13},{10,... | collective-permute-start | bytes 1769480 | tf_op jit(solution)/shard_map/ppermute | solution.py:22
  12.2 18.5 %collective-permute-start.3 = (bf16[48,3072]{1,0:T(8,128)(2,1)}, bf16[48,3072]{1,0:T(8,128)(2,1)S(1)}, u32[]{:S(2)}, u32[]{:S(2)}) collective-permute-start(bf16[48,3072]{1,0:T(8,128)(2,1)} %constant_dynamic-slice_fusion), channel_id=1, source_target_pairs={{0,8},{1,9},{2,10},{3,11},{4,12},{5,13},{6,14},{7,15},{8,0},{9,1},... | collective-permute-start | bytes 884744 | tf_op jit(solution)/shard_map/ppermute | solution.py:22
  30.6 25.8 %collective-permute-start.4 = (bf16[48,3072]{1,0:T(8,128)(2,1)S(1)}, bf16[48,3072]{1,0:T(8,128)(2,1)S(1)}, u32[]{:S(2)}, u32[]{:S(2)}) collective-permute-start(bf16[48,3072]{1,0:T(8,128)(2,1)S(1)} %collective-permute-done.3), channel_id=1, source_target_pairs={{0,4},{1,5},{2,6},{3,7},{4,0},{5,1},{6,2},{7,3},{8,12},{9,13},{10,... | collective-permute-start | bytes 884744 | tf_op jit(solution)/shard_map/ppermute | solution.py:22
  56.5 16.3 %collective-permute-start.5 = (bf16[96,3072]{1,0:T(8,128)(2,1)S(1)}, bf16[96,3072]{1,0:T(8,128)(2,1)S(1)}, u32[]{:S(2)}, u32[]{:S(2)}) collective-permute-start(bf16[96,3072]{1,0:T(8,128)(2,1)S(1)} %pad_maximum_fusion.3), channel_id=1, source_target_pairs={{0,2},{1,3},{2,0},{3,1},{4,6},{5,7},{6,4},{7,5},{8,10},{9,11},{10,... | collective-permute-start | bytes 1769480 | tf_op jit(solution)/shard_map/ppermute | solution.py:22
  58.6 37.6 %collective-permute-start.1 = (bf16[192,3072]{1,0:T(8,128)(2,1)S(1)}, bf16[192,3072]{1,0:T(8,128)(2,1)S(1)}, u32[]{:S(2)}, u32[]{:S(2)}) collective-permute-start(bf16[192,3072]{1,0:T(8,128)(2,1)S(1)} %pad_maximum_fusion.1), channel_id=1, source_target_pairs={{0,2},{1,3},{2,0},{3,1},{4,6},{5,7},{6,4},{7,5},{8,10},{9,11},{10,... | collective-permute-start | bytes 3538952 | tf_op jit(solution)/shard_map/ppermute | solution.py:22
  72.9 25.3 %collective-permute-start.6 = (bf16[192,3072]{1,0:T(8,128)(2,1)S(1)}, bf16[192,3072]{1,0:T(8,128)(2,1)S(1)}, u32[]{:S(2)}, u32[]{:S(2)}) collective-permute-start(bf16[192,3072]{1,0:T(8,128)(2,1)S(1)} %pad_maximum_fusion.2), channel_id=1, source_target_pairs={{0,16},{16,0},{1,17},{17,1},{2,18},{18,2},{3,19},{19,3},{4,20},{20... | collective-permute-start | bytes 3538952 | tf_op jit(solution)/shard_map/ppermute | solution.py:26
  78.0 21.3 %copy-start.6 = (s32[2,27]{1,0:T(2,128)S(1)}, s32[2,27]{1,0:T(2,128)}, u32[]{:S(2)}) copy-start(s32[2,27]{1,0:T(2,128)} %param.10) | copy-start | bytes 652
  97.3 89.6 %collective-permute-start.2 = (bf16[384,3072]{1,0:T(8,128)(2,1)}, bf16[384,3072]{1,0:T(8,128)(2,1)}, u32[]{:S(2)}, u32[]{:S(2)}) collective-permute-start(bf16[384,3072]{1,0:T(8,128)(2,1)} %constant_dynamic-update-slice_fusion.refs_0_), channel_id=1, source_target_pairs={{0,1},{1,0},{2,3},{3,2},{4,5},{5,4},{6,7},{7,6},{8,9},{9,8},{10,11... | collective-permute-start | bytes 7077896 | tf_op jit(solution)/shard_map/ppermute | solution.py:22
  99.4 87.5 %collective-permute-start.7 = (bf16[384,3072]{1,0:T(8,128)(2,1)}, bf16[384,3072]{1,0:T(8,128)(2,1)}, u32[]{:S(2)}, u32[]{:S(2)}) collective-permute-start(bf16[384,3072]{1,0:T(8,128)(2,1)} %constant_dynamic-update-slice_fusion.3.refs_2_), channel_id=1, source_target_pairs={{0,1},{1,0},{2,3},{3,2},{4,5},{5,4},{6,7},{7,6},{8,9},{9,8},{10,11... | collective-permute-start | bytes 7077896 | tf_op jit(solution)/shard_map/ppermute | solution.py:22
  99.7 42.7 %copy-start = (bf16[256,1536]{1,0:T(8,128)(2,1)S(1)}, bf16[256,1536]{1,0:T(8,128)(2,1)}, u32[]{:S(2)}) copy-start(bf16[256,1536]{1,0:T(8,128)(2,1)} %k0.5) | copy-start | bytes 2359300
  99.8 42.7 %copy-start.2 = (bf16[256,1536]{1,0:T(8,128)(2,1)S(1)}, bf16[256,1536]{1,0:T(8,128)(2,1)}, u32[]{:S(2)}) copy-start(bf16[256,1536]{1,0:T(8,128)(2,1)} %v0.5) | copy-start | bytes 2359300
  101.1 22.0 %collective-permute-start.10 = (bf16[272,768]{1,0:T(8,128)(2,1)S(1)}, bf16[272,768]{1,0:T(8,128)(2,1)S(1)}, u32[]{:S(2)}, u32[]{:S(2)}) collective-permute-start(bf16[272,768]{1,0:T(8,128)(2,1)S(1)} %pad_maximum_fusion.4), channel_id=1, source_target_pairs={{0,8},{1,9},{2,10},{3,11},{4,12},{5,13},{6,14},{7,15},{8,0},{9,1},... | collective-permute-start | bytes 1253384 | tf_op jit(solution)/shard_map/ppermute | solution.py:302
  123.1 19.4 %collective-permute-start.12 = (bf16[256,768]{1,0:T(8,128)(2,1)S(1)}, bf16[256,768]{1,0:T(8,128)(2,1)S(1)}, u32[]{:S(2)}, u32[]{:S(2)}) collective-permute-start(bf16[256,768]{1,0:T(8,128)(2,1)S(1)} %get-tuple-element.7), channel_id=1, source_target_pairs={{0,8},{1,9},{2,10},{3,11},{4,12},{5,13},{6,14},{7,15},{8,0},{9,1},... | collective-permute-start | bytes 1179656 | tf_op jit(solution)/shard_map/ppermute | solution.py:303
  148.0 30.0 %collective-permute-start.13 = (bf16[272,768]{1,0:T(8,128)(2,1)}, bf16[272,768]{1,0:T(8,128)(2,1)}, u32[]{:S(2)}, u32[]{:S(2)}) collective-permute-start(bf16[272,768]{1,0:T(8,128)(2,1)} %shard_map.75), channel_id=1, source_target_pairs={{0,8},{1,9},{2,10},{3,11},{4,12},{5,13},{6,14},{7,15},{8,0},{9,1},... | collective-permute-start | bytes 1253384 | tf_op jit(solution)/shard_map/ppermute | solution.py:316
  153.4 33.4 %collective-permute-start.11 = (bf16[272,768]{1,0:T(8,128)(2,1)}, bf16[272,768]{1,0:T(8,128)(2,1)}, u32[]{:S(2)}, u32[]{:S(2)}) collective-permute-start(bf16[272,768]{1,0:T(8,128)(2,1)} %shard_map.74), channel_id=1, source_target_pairs={{0,8},{1,9},{2,10},{3,11},{4,12},{5,13},{6,14},{7,15},{8,0},{9,1},... | collective-permute-start | bytes 1253384 | tf_op jit(solution)/shard_map/ppermute | solution.py:316
  156.4 1.1 copy-start.1
  157.6 1.1 copy-start.3
  158.7 1.1 copy-start.5
  186.8 1.4 copy-start.4

commit v2 on v1

--- a/solution.py
+++ b/solution.py
@@ -15,6 +15,7 @@
 PIECES = 3
 LOG2E = math.log2(math.e)
 VMEM_BYTES = 48 * 1024 * 1024
+WEIGHTY = 10**12
 
 
 def swap_bit(value, bit):
@@ -90,7 +91,7 @@
     out_ref[rows:, :] = jnp.concatenate(stats, axis=0).astype(out_ref.dtype)
 
 
-def attend(bias, q, q_first, heads, keys, values, kv_up, kv_down, first, kind):
+def attend(bias, q, q_first, heads, keys, values, kv_up, kv_down, first, kind, cost=WEIGHTY):
     rows = keys.shape[0]
     per_block = rows // HD
     width = per_block * HD
@@ -116,46 +117,28 @@
         out_shape=jax.ShapeDtypeStruct((rows + EXTRA, heads * HD), kind),
         compiler_params=pltpu.CompilerParams(vmem_limit_bytes=VMEM_BYTES),
         cost_estimate=pl.CostEstimate(
-            flops=4 * heads * rows * span * HD,
-            bytes_accessed=heads * HD * 2 * (2 * span + 2 * rows),
-            transcendentals=heads * rows * span,
+            flops=cost, bytes_accessed=0, transcendentals=0
         ),
     )(bias, q, keys, kv_up, kv_down, values, kv_up, kv_down)
 
 
-def project_kernel(rows, plan, chunk_counts, *refs):
-    sources = len(plan)
-    weights = refs[:sources]
-    partner_ref = refs[sources]
-    cursor = sources + 1
-    own = refs[cursor]
-    cursor += 1
-    others = []
+def merge_kernel(rows, chunk_counts, partner_ref, *refs):
+    parts, cursor = [], 0
     for count in chunk_counts:
-        others.append(refs[cursor : cursor + count])
+        parts.append(refs[cursor : cursor + count])
         cursor += count
-    out_ref, held, attention, sems = refs[cursor:]
-    copies = []
-    for source, moves in zip(weights, plan):
-        for from_row, count, place in moves:
-            into = pl.multiple_of(place(), 16)
-            copy = pltpu.make_async_copy(
-                source.at[pl.ds(from_row, count), :],
-                held.at[pl.ds(into, count), :],
-                sems.at[len(copies)],
-            )
-            copy.start()
-            copies.append(copy)
+    attention = refs[cursor]
     per_block = rows // HD
     width = per_block * HD
-    features = own.shape[1]
-    for block in range(features // width):
-        cols = slice(block * width, (block + 1) * width)
-        tiles = [own[:, cols].astype(jnp.float32)]
-        for number, chunks in enumerate(others):
-            chunk_width = chunks[0].shape[1]
-            index, offset = divmod(block * width, chunk_width)
-            tiles.append(chunks[index][:, offset : offset + width].astype(jnp.float32))
+    for block in range(attention.shape[1] // width):
+        tiles = []
+        for chunks in parts:
+            offset = block * width
+            for chunk in chunks:
+                if offset < chunk.shape[1]:
+                    break
+                offset -= chunk.shape[1]
+            tiles.append(chunk[:, offset : offset + width].astype(jnp.float32))
         shares = []
         for head in range(per_block):
             lses = []
@@ -184,6 +167,37 @@
             )
             start = block * width + head * HD
             attention[:, start : start + HD] = mixed.astype(jnp.bfloat16)
+
+
+def merge(partner, parts):
+    flat = [chunk for chunks in parts for chunk in chunks]
+    rows = flat[0].shape[0] - EXTRA
+    features = sum(chunk.shape[1] for chunk in parts[0])
+    vmem = pl.BlockSpec(memory_space=pltpu.VMEM)
+    return pl.pallas_call(
+        functools.partial(merge_kernel, rows, [len(c) for c in parts]),
+        in_specs=[pl.BlockSpec(memory_space=pltpu.SMEM)] + [vmem] * len(flat),
+        out_specs=vmem,
+        out_shape=jax.ShapeDtypeStruct((rows, features), jnp.bfloat16),
+        compiler_params=pltpu.CompilerParams(vmem_limit_bytes=VMEM_BYTES),
+        cost_estimate=pl.CostEstimate(flops=WEIGHTY, bytes_accessed=0, transcendentals=0),
+    )(partner, *flat)
+
+
+def project_kernel(plan, *refs):
+    weights = refs[: len(plan)]
+    attention, out_ref, held, sems = refs[len(plan) :]
+    copies = []
+    for source, moves in zip(weights, plan):
+        for from_row, count, place in moves:
+            into = pl.multiple_of(place(), 16)
+            copy = pltpu.make_async_copy(
+                source.at[pl.ds(from_row, count), :],
+                held.at[pl.ds(into, count), :],
+                sems.at[len(copies)],
+            )
+            copy.start()
+            copies.append(copy)
     for copy in copies:
         copy.wait()
     columns = out_ref.shape[1]
@@ -197,75 +211,64 @@
         ).astype(out_ref.dtype)
 
 
-def project(pieces, partner, own, others):
+def project(pieces, attention):
     arrays = [array for array, _ in pieces]
     plan = [moves for _, moves in pieces]
-    rows, features = own.shape[0] - EXTRA, own.shape[1]
+    rows, features = attention.shape
     columns = arrays[0].shape[1]
-    flat = [chunk for chunks in others for chunk in chunks]
     vmem = pl.BlockSpec(memory_space=pltpu.VMEM)
     return pl.pallas_call(
-        functools.partial(project_kernel, rows, plan, [len(c) for c in others]),
-        in_specs=[pl.BlockSpec(memory_space=pl.ANY)] * len(arrays)
-        + [pl.BlockSpec(memory_space=pltpu.SMEM)]
-        + [vmem] * (1 + len(flat)),
+        functools.partial(project_kernel, plan),
+        in_specs=[pl.BlockSpec(memory_space=pl.ANY)] * len(arrays) + [vmem],
         out_specs=vmem,
         out_shape=jax.ShapeDtypeStruct((rows, columns), jnp.bfloat16),
         scratch_shapes=[
             pltpu.VMEM((features, columns), jnp.bfloat16),
-            pltpu.VMEM((rows, features), jnp.bfloat16),
             pltpu.SemaphoreType.DMA((sum(len(m) for m in plan),)),
         ],
         compiler_params=pltpu.CompilerParams(vmem_limit_bytes=VMEM_BYTES),
-        cost_estimate=pl.CostEstimate(
-            flops=2 * rows * features * columns,
-            bytes_accessed=2 * features * columns,
-            transcendentals=0,
-        ),
-    )(*arrays, partner, own, *flat)
-
-
-def gather_weight(out_weight, groups, devices):
-    shard = out_weight.shape[0]
-    if devices != 16 or groups != 2 or shard % 32:
-        whole = lax.all_gather(out_weight, "seq", axis=0, tiled=True)
-        return [(whole, [(0, whole.shape[0], lambda: 0)])]
-    half = shard // 2
-
-    def full(*bits):
+    )(*arrays, attention)
+
+
+def after(value, *done):
+    return lax.optimization_barrier((value, *done))[0]
+
+
+class Cube:
+    def __init__(self, out_weight):
+        self.near = out_weight
+        self.shard = out_weight.shape[0]
+        self.half = self.shard // 2
+
+    def cross(self):
+        first = lax.axis_index("group") * self.half
+        self.c0 = swap_bit(lax.dynamic_slice_in_dim(self.near, first, self.half, 0), 8)
+
+    def full(self, *bits):
         def at(bit):
-            return lambda: (lax.axis_index("seq") ^ bit) * shard
-
-        return [(i * shard, shard, at(bit)) for i, bit in enumerate(bits)]
-
-    def halves(*bits):
+            return lambda: (lax.axis_index("seq") ^ bit) * self.shard
+
+        return [(i * self.shard, self.shard, at(bit)) for i, bit in enumerate(bits)]
+
+    def halves(self, *bits):
         def at(bit, turn):
-            return lambda: (lax.axis_index("seq") ^ bit) * shard + (
+            return lambda: (lax.axis_index("seq") ^ bit) * self.shard + (
                 lax.axis_index("group") ^ turn
-            ) * half
-
-        return [(i * half, half, at(bit, turn)) for i, (bit, turn) in enumerate(bits)]
-
-    mine = lax.dynamic_slice_in_dim(out_weight, lax.axis_index("group") * half, half, 0)
-    c0 = swap_bit(mine, 8)
-    wz = swap_bit(out_weight, 4)
-    cz = swap_bit(c0, 4)
-    near = jnp.concatenate([out_weight, wz], axis=0)
-    wy = swap_bit(near, 2)
-    far = jnp.concatenate([c0, cz], axis=0)
-    cy = swap_bit(far, 2)
-    quad = jnp.concatenate([near, wy], axis=0)
-    wc = swap_bit(quad, 1)
-    four = jnp.concatenate([far, cy], axis=0)
-    cx = swap_group(four, groups)
-    eight = jnp.concatenate([four, cx], axis=0)
-    cc = swap_bit(eight, 1)
-    return [
-        (quad, full(0, 4, 2, 6)),
-        (wc, full(1, 5, 3, 7)),
-        (eight, halves((8, 0), (12, 0), (10, 0), (14, 0), (8, 1), (12, 1), (10, 1), (14, 1))),
-        (cc, halves((9, 0), (13, 0), (11, 0), (15, 0), (9, 1), (13, 1), (11, 1), (15, 1))),
-    ]
+            ) * self.half
+
+        return [(i * self.half, self.half, at(bit, turn)) for i, (bit, turn) in enumerate(bits)]
+
+    def pieces(self):
+        return [
+            (self.quad, self.full(0, 4, 2, 6)),
+            (self.wc, self.full(1, 5, 3, 7)),
+            (self.eight, self.halves(*[(b, t) for t in (0, 1) for b in (8, 12, 10, 14)])),
+            (self.cc, self.halves(*[(b, t) for t in (0, 1) for b in (9, 13, 11, 15)])),
+        ]
+
+
+def join(*arrays):
+    return jnp.concatenate(arrays, axis=0)
 
 
 def body(groups, query_rows, key_rows, value_rows, block_list, out_weight):
@@ -287,8 +290,15 @@
         member = jnp.any(block_list[:, :, None] == ids[None, None, :], axis=1)
         return jnp.repeat(jnp.where(member, 0.0, -jnp.inf), tile, axis=1)
 
+    cube = None
+    if devices == 16 and groups == 2 and out_weight.shape[0] % 32 == 0:
+        cube = Cube(out_weight)
+        cube.cross()
     kv = jnp.stack([key_rows, value_rows])
-    pieces = gather_weight(out_weight, groups, devices)
+    kv_up = column_shift(kv, 1)
+    kv_down = column_shift(kv, -1)
+    if cube:
+        wz = swap_bit(out_weight, 4)
     phases = [parity for parity in range(2) if parity + 1 < grid_rows]
     sent = []
     for parity in phases:
@@ -296,26 +306,42 @@
         bias = bias_for(there).reshape(-1).astype(jnp.bfloat16)
         bias = jnp.pad(bias, (0, EXTRA * chunk - bias.shape[0])).reshape(EXTRA, chunk)
         pairs = row_pairs(parity)
-        first = jnp.concatenate([query_rows[:, :chunk], bias], axis=0)
-        sent.append(
-            [
-                lax.ppermute(first, "seq", pairs),
-                lax.ppermute(query_rows[:, chunk:], "seq", pairs),
-            ]
-        )
-    kv_up = column_shift(kv, 1)
-    kv_down = column_shift(kv, -1)
+        first = lax.ppermute(join(query_rows[:, :chunk], bias), "seq", pairs)
+        second = query_rows[:, chunk:]
+        if cube:
+            cz = swap_bit(cube.c0, 4)
+            second = after(second, wz)
+        sent.append([first, lax.ppermute(second, "seq", pairs)])
+    if cube:
+        far = join(cube.c0, cz)
+        cy = swap_bit(far, 2)
+        sent[0][0] = after(sent[0][0], far)
     common = (key_rows, value_rows, kv_up, kv_down)
     others = []
     for parity, asked in zip(phases, sent):
         bias = asked[0][rows:, :].reshape(-1)[: FRAMES * 3 * rows].reshape(FRAMES, 3 * rows)
-        pairs = row_pairs(parity)
         back = []
         for number, q in enumerate(asked):
+            if number:
+                q = after(q, part, near, four) if cube else after(q, part)
             part = attend(bias, q, 0, chunk_heads, *common, number * chunk_heads, jnp.bfloat16)
-            back.append(lax.ppermute(part, "seq", pairs))
+            if cube and not number:
+                four = join(far, after(cy, part))
+                cx = swap_group(four, groups)
+                near = join(out_weight, after(wz, part))
+                wy = swap_bit(near, 2)
+            back.append(lax.ppermute(part, "seq", row_pairs(parity)))
+            last = part
         others.append(back)
-    own = attend(bias_for(row), query_rows, 0, heads, *common, 0, jnp.float32)
+    own_bias = bias_for(row)
+    early = heads - rows // HD
+    awaited = [others[0][0]] if phases else []
+    if cube:
+        awaited += [cx, wy]
+    q = after(query_rows, last) if phases else query_rows
+    own = [attend(own_bias, q, 0, early, *common, 0, jnp.float32, 0)]
+    q = after(query_rows, *awaited)
+    own.append(attend(own_bias, q, early, heads - early, *common, early, jnp.float32))
     partner = jnp.stack(
         [
             jnp.where(row % 2 == parity, row + 1 < grid_rows, row > 0).astype(jnp.int32)
@@ -323,7 +349,17 @@
         ]
         or [jnp.int32(0)]
     )
-    return project(pieces, partner, own, others)
+    attention = merge(partner, [own] + others)
+    if cube:
+        cube.quad = join(near, after(wy, own[0]))
+        cube.wc = after(swap_bit(cube.quad, 1), attention)
+        cube.eight = join(four, after(cx, own[0]))
+        cube.cc = after(swap_bit(cube.eight, 1), attention)
+        pieces = cube.pieces()
+    else:
+        whole = lax.all_gather(out_weight, "seq", axis=0, tiled=True)
+        pieces = [(whole, [(0, whole.shape[0], lambda: 0)])]
+    return project(pieces, attention)
 
 
 def solution(mesh):

time: 198 us -> 137 us (0.69)
  the two profiles are of different devices: /device:TPU:0 before, /device:TPU:13 now
where the time goes in v2:
time: 137 us; the launch traced here: 136 us
  starting transfers between devices  42.5 us (31%)
  waiting for transfers between devices  36.7 us (27%)
  Pallas kernels  34.1 us (25%)
  local copies, waits for them, and re-layouts  18.7 us (14%)
  other arithmetic  3.79 us (3%)
    ppermute x7, starting transfers between devices, swap_bit(): return lax.ppermute(value, 'seq', [(s, s ^ bit) for s in range(count)])  28.3 us
    ppermute x7, waiting for transfers between devices, swap_bit(): return lax.ppermute(value, 'seq', [(s, s ^ bit) for s in range(count)])  26.5 us
    pallas_call x4, Pallas kernels, attend(): pl.pallas_call(functools.partial(attend_kernel, rows, per_block), grid=(h...  23.3 us
    ppermute x1, waiting for transfers between devices, body(): sent.append([first, lax.ppermute(second, 'seq', pairs)])  10.2 us
    pallas_call x1, Pallas kernels, project(): pl.pallas_call(functools.partial(project_kernel, plan), in_specs=[pl.Bloc...  8.46 us
    unnamed x20, local copies, waits for them, and re-layouts  7.68 us
    concatenate x3, local copies, waits for them, and re-layouts, join(): return jnp.concatenate(arrays, axis=0)  7.04 us
    ppermute x2, starting transfers between devices, column_shift(): return lax.ppermute(value, 'seq', pairs)  4.59 us
  transfers between devices with their start and end apart: 14, of which 4 were waited for; matrix products, arithmetic and copies ran while one was open for 15% of the time, Pallas kernels for 19%

profile of v2, /device:TPU:13, one launch (start us, length us, event | category | flops | bytes accessed | tf_op | source)
XLA Modules:
  0.0 135.9 jit_solution(12341081714766276027)
XLA Ops:
  0.0 2.7 %pad_maximum_fusion = bf16[2,256,1536]{2,1,0:T(8,128)(2,1)} fusion(bf16[1,256,1536]{2,1,0:T(8,128)(2,1)} %bitcast.9, bf16[1,256,1536]{2,1,0:T(8,128)(2,1)} %bitcast.8), kind=kLoop, calls=%fused_computation | loop fusion | flops 786432 | bytes 3145728 | tf_op jit(solution)/shard_map/stack | solution.py:297
  2.7 1.3 collective-permute-start.4
  4.0 3.3 %collective-permute-start.5 = (bf16[2,256,1536]{2,1,0:T(8,128)(2,1)}, bf16[2,256,1536]{2,1,0:T(8,128)(2,1)S(1)}, u32[]{:S(2)}, u32[]{:S(2)}) collective-permute-start(bf16[2,256,1536]{2,1,0:T(8,128)(2,1)} %pad_maximum_fusion), channel_id=1, source_target_pairs={{1,0},{2,1},{3,2},{4,3},{5,4},{6,5},{7,6},{9,8},{10,9},{11,10},{12... | collective-permute-start | bytes 4718600 | tf_op jit(solution)/shard_map/ppermute | solution.py:33
  7.4 0.1 iota_add_fusion
  7.4 0.1 add.97
  7.5 0.1 add.89
  7.6 0.2 compare_reduce_fusion
  7.8 0.1 broadcast_in_dim.32
  8.0 1.9 %fusion = (bf16[256,768]{1,0:T(8,128)(2,1)}, bf16[256,768]{1,0:T(8,128)(2,1)S(1)}) fusion(bf16[256,1536]{1,0:T(8,128)(2,1)} %q_ref.1), kind=kLoop, calls=%fused_computation.29 | loop fusion | bytes 1572864 | tf_op jit(solution)/shard_map/slice | solution.py:310
  9.9 0.8 pad_maximum_fusion.1
  10.7 2.3 %collective-permute-start.1 = (bf16[272,768]{1,0:T(8,128)(2,1)}, bf16[272,768]{1,0:T(8,128)(2,1)}, u32[]{:S(2)}, u32[]{:S(2)}) collective-permute-start(bf16[272,768]{1,0:T(8,128)(2,1)} %pad_maximum_fusion.1), channel_id=1, source_target_pairs={{0,8},{1,9},{2,10},{3,11},{4,12},{5,13},{6,14},{7,15},{8,0},{9,1},... | collective-permute-start | bytes 1253384 | tf_op jit(solution)/shard_map/ppermute | solution.py:309
  13.0 1.2 collective-permute-start
  14.2 1.0 constant_dynamic-slice_fusion
  15.2 0.1 collective-permute-start.2
  15.4 0.1 broadcast_bitcast_fusion
  15.4 2.2 %constant_dynamic-update-slice_fusion.3 = (bf16[192,3072]{1,0:T(8,128)(2,1)}, bf16[384,3072]{1,0:T(8,128)(2,1)}) fusion(bf16[96,3072]{1,0:T(8,128)(2,1)} %param.11), kind=kLoop, calls=%fused_computation.5 | loop fusion | bytes 1769472
  17.7 22.8 %collective-permute-done.2 = bf16[48,3072]{1,0:T(8,128)(2,1)} collective-permute-done((bf16[48,3072]{1,0:T(8,128)(2,1)S(1)}, bf16[48,3072]{1,0:T(8,128)(2,1)}, u32[]{:S(2)}, u32[]{:S(2)}) %collective-permute-start.2) | collective-permute-done | bytes 294944 | tf_op jit(solution)/shard_map/ppermute | solution.py:23
  40.5 14.7 %collective-permute-start.3 = (bf16[48,3072]{1,0:T(8,128)(2,1)}, bf16[48,3072]{1,0:T(8,128)(2,1)S(1)}, u32[]{:S(2)}, u32[]{:S(2)}) collective-permute-start(bf16[48,3072]{1,0:T(8,128)(2,1)} %collective-permute-done.2), channel_id=1, source_target_pairs={{0,4},{1,5},{2,6},{3,7},{4,0},{5,1},{6,2},{7,3},{8,12},{9,13},{10,... | collective-permute-start | bytes 884744 | tf_op jit(solution)/shard_map/ppermute | solution.py:23
  55.2 2.0 %constant_dynamic-update-slice_fusion.13 = (bf16[384,3072]{1,0:T(8,128)(2,1)}, bf16[192,3072]{1,0:T(8,128)(2,1)}, bf16[96,3072]{1,0:T(8,128)(2,1)}) fusion(bf16[48,3072]{1,0:T(8,128)(2,1)} %collective-permute-done.2), kind=kLoop, calls=%fused_computation.15 | loop fusion | bytes 1179648
  57.3 2.3 %collective-permute-done.3 = bf16[48,3072]{1,0:T(8,128)(2,1)S(1)} collective-permute-done((bf16[48,3072]{1,0:T(8,128)(2,1)}, bf16[48,3072]{1,0:T(8,128)(2,1)S(1)}, u32[]{:S(2)}, u32[]{:S(2)}) %collective-permute-start.3) | collective-permute-done | bytes 294944 | tf_op jit(solution)/shard_map/ppermute | solution.py:23
  59.5 1.0 constant_dynamic-update-slice_fusion.12
  60.6 0.0 collective-permute-start.8
  60.6 0.0 collective-permute-done.1.q_ref
  60.6 0.7 slice.13.bias_ref
  61.3 0.0 collective-permute-done
  61.3 2.9 %collective-permute-start.7 = (bf16[256,768]{1,0:T(8,128)(2,1)}, bf16[256,768]{1,0:T(8,128)(2,1)}, u32[]{:S(2)}, u32[]{:S(2)}) collective-permute-start(bf16[256,768]{1,0:T(8,128)(2,1)} %get-tuple-element.18), channel_id=1, source_target_pairs={{0,8},{1,9},{2,10},{3,11},{4,12},{5,13},{6,14},{7,15},{8,0},{9,1},... | collective-permute-start | bytes 1179656 | tf_op jit(solution)/shard_map/ppermute | solution.py:314
  64.2 0.0 copy-start
  64.2 6.4 %shard_map.73 = bf16[272,768]{1,0:T(8,128)(2,1)} custom-call(bf16[2,768]{1,0:T(2,128)(2,1)S(1)} %slice.13.bias_ref, bf16[272,768]{1,0:T(8,128)(2,1)} %collective-permute-done.1.q_ref, bf16[256,1536]{1,0:T(8,128)(2,1)S(1)} %copy-done.3, bf16[2,256,1536]{2,1,0:T(8,128)(2,1)S(1)} %collective-permute-done.4.ka.va, ...), custom_call_target="tpu_custom_call" | custom-call | flops 999999995904 | tf_op jit(solution)/shard_map/pallas_call | solution.py:103
  70.7 0.0 collective-permute-start.10
  70.7 0.0 collective-permute-done.8
  70.7 2.3 %constant_dynamic-update-slice_fusion.11 = (bf16[384,3072]{1,0:T(8,128)(2,1)}, bf16[192,3072]{1,0:T(8,128)(2,1)}) fusion(bf16[384,3072]{1,0:T(8,128)(2,1)} %get-tuple-element.37, bf16[96,3072]{1,0:T(8,128)(2,1)} %collective-permute-done.8, bf16[192,3072]{1,0:T(8,128)(2,1)} %get-tuple-element.38), kind=kLoop, calls=%fused_computation.13 | loop fusion | bytes 1769472
  73.0 1.2 collective-permute-start.11
  74.2 2.2 %constant_dynamic-update-slice_fusion.2 = (bf16[192,3072]{1,0:T(8,128)(2,1)}, bf16[384,3072]{1,0:T(8,128)(2,1)}) fusion(bf16[192,3072]{1,0:T(8,128)(2,1)} %get-tuple-element.35, bf16[96,3072]{1,0:T(8,128)(2,1)} %collective-permute-done, bf16[384,3072]{1,0:T(8,128)(2,1)} %get-tuple-element.36), kind=kLoop, calls=%fused_computation.4 | loop fusion | bytes 1769472 | tf_op jit(solution)/shard_map/concatenate | solution.py:271
  76.4 1.5 %collective-permute-start.6 = (bf16[192,3072]{1,0:T(8,128)(2,1)}, bf16[192,3072]{1,0:T(8,128)(2,1)}, u32[]{:S(2)}, u32[]{:S(2)}) collective-permute-start(bf16[192,3072]{1,0:T(8,128)(2,1)} %get-tuple-element.33), channel_id=1, source_target_pairs={{0,2},{1,3},{2,0},{3,1},{4,6},{5,7},{6,4},{7,5},{8,10},{9,11},{10,... | collective-permute-start | bytes 3538952 | tf_op jit(solution)/shard_map/ppermute | solution.py:23
  77.9 10.2 %collective-permute-done.7.q_ref = bf16[256,768]{1,0:T(8,128)(2,1)} collective-permute-done((bf16[256,768]{1,0:T(8,128)(2,1)}, bf16[256,768]{1,0:T(8,128)(2,1)}, u32[]{:S(2)}, u32[]{:S(2)}) %collective-permute-start.7) | collective-permute-done | bytes 393248 | tf_op jit(solution)/shard_map/ppermute | solution.py:314
  88.1 6.3 %shard_map.74 = bf16[272,768]{1,0:T(8,128)(2,1)} custom-call(bf16[2,768]{1,0:T(2,128)(2,1)S(1)} %slice.13.bias_ref, bf16[256,768]{1,0:T(8,128)(2,1)} %collective-permute-done.7.q_ref, bf16[256,1536]{1,0:T(8,128)(2,1)S(1)} %copy-done.3, bf16[2,256,1536]{2,1,0:T(8,128)(2,1)S(1)} %collective-permute-done.4.ka.va, ...), custom_call_target="tpu_custom_call" | custom-call | flops 999999995904 | tf_op jit(solution)/shard_map/pallas_call | solution.py:103
  94.4 3.1 %collective-permute-start.12 = (bf16[272,768]{1,0:T(8,128)(2,1)}, bf16[272,768]{1,0:T(8,128)(2,1)}, u32[]{:S(2)}, u32[]{:S(2)}) collective-permute-start(bf16[272,768]{1,0:T(8,128)(2,1)} %shard_map.74), channel_id=1, source_target_pairs={{0,8},{1,9},{2,10},{3,11},{4,12},{5,13},{6,14},{7,15},{8,0},{9,1},... | collective-permute-start | bytes 1253384 | tf_op jit(solution)/shard_map/ppermute | solution.py:333
  97.5 8.9 %shard_map.75.refs_0_ = f32[272,1280]{1,0:T(8,128)S(1)} custom-call(f32[2,768]{1,0:T(2,128)S(1)} %bitcast.10, bf16[256,1536]{1,0:T(8,128)(2,1)S(1)} %copy-done.2, bf16[256,1536]{1,0:T(8,128)(2,1)S(1)} %copy-done.3, bf16[2,256,1536]{2,1,0:T(8,128)(2,1)S(1)} %collective-permute-done.4.ka.va, bf16[2,256,1536]{2,1,0:T(8,128)(2,1)} %copy-done, ...), custom_call_target="tpu_custom_call" | custom-call | tf_op jit(solution)/shard_map/pallas_call | solution.py:103
  106.5 2.4 %constant_dynamic-update-slice_fusion.10.refs_2_ = bf16[384,3072]{1,0:T(8,128)(2,1)} fusion(bf16[384,3072]{1,0:T(8,128)(2,1)} %get-tuple-element.31, bf16[192,3072]{1,0:T(8,128)(2,1)} %collective-permute-done.11), kind=kLoop, calls=%fused_computation.12 | loop fusion | bytes 2359296 | tf_op jit(solution)/shard_map/concatenate | solution.py:271
  108.9 10.7 %collective-permute-start.13 = (bf16[384,3072]{1,0:T(8,128)(2,1)}, bf16[384,3072]{1,0:T(8,128)(2,1)}, u32[]{:S(2)}, u32[]{:S(2)}) collective-permute-start(bf16[384,3072]{1,0:T(8,128)(2,1)} %constant_dynamic-update-slice_fusion.10.refs_2_), channel_id=1, source_target_pairs={{0,1},{1,0},{2,3},{3,2},{4,5},{5,4},{6,7},{7,6},{8,9},{9,8},{10,11... | collective-permute-start | bytes 7077896 | tf_op jit(solution)/shard_map/ppermute | solution.py:23
  119.6 2.4 %constant_dynamic-update-slice_fusion.7.refs_0_ = bf16[384,3072]{1,0:T(8,128)(2,1)} fusion(bf16[384,3072]{1,0:T(8,128)(2,1)} %get-tuple-element.34, bf16[192,3072]{1,0:T(8,128)(2,1)} %collective-permute-done.6), kind=kLoop, calls=%fused_computation.9 | loop fusion | bytes 2359296 | tf_op jit(solution)/shard_map/concatenate | solution.py:271
  122.0 0.1 collective-permute-start.9
  122.1 1.6 %shard_map.76.refs_1_ = f32[272,256]{1,0:T(8,128)S(1)} custom-call(f32[2,768]{1,0:T(2,128)S(1)} %bitcast.11, bf16[256,1536]{1,0:T(8,128)(2,1)S(1)} %copy-done.2, bf16[256,1536]{1,0:T(8,128)(2,1)S(1)} %copy-done.3, bf16[2,256,1536]{2,1,0:T(8,128)(2,1)S(1)} %collective-permute-done.4.ka.va, bf16[2,256,1536]{2,1,0:T(8,128)(2,1)S(1)} %copy-done.1, ...), custom_call_target="tpu_custom_call" | custom-call | flops 999999995904 | tf_op jit(solution)/shard_map/pallas_call | solution.py:103
  123.7 0.0 collective-permute-done.12.refs_3_
  123.7 2.4 %shard_map.77.refs_4_ = bf16[256,1536]{1,0:T(8,128)(2,1)S(1)} custom-call(s32[1]{0:T(128)} %bitcast.2.partner_ref, f32[272,1280]{1,0:T(8,128)S(1)} %shard_map.75.refs_0_, f32[272,256]{1,0:T(8,128)S(1)} %shard_map.76.refs_1_, bf16[272,768]{1,0:T(8,128)(2,1)} %collective-permute-done.10.refs_2_, bf16[272,768]{1,0:T(8,128)(2,1)} %collective-permute-done.12.refs_3_), custom_call_target="tpu_custom_call" | custom-call | flops 999999995904 | tf_op jit(solution)/shard_map/pallas_call | solution.py:177
  126.1 0.0 collective-permute-done.13.refs_3_
  126.1 1.4 %collective-permute-done.9.refs_1_ = bf16[384,3072]{1,0:T(8,128)(2,1)} collective-permute-done((bf16[384,3072]{1,0:T(8,128)(2,1)}, bf16[384,3072]{1,0:T(8,128)(2,1)}, u32[]{:S(2)}, u32[]{:S(2)}) %collective-permute-start.9) | collective-permute-done | bytes 2359328 | tf_op jit(solution)/shard_map/ppermute | solution.py:23
  127.5 8.5 %shard_map.78 = bf16[256,3072]{1,0:T(8,128)(2,1)} custom-call(bf16[384,3072]{1,0:T(8,128)(2,1)} %constant_dynamic-update-slice_fusion.7.refs_0_, bf16[384,3072]{1,0:T(8,128)(2,1)} %collective-permute-done.9.refs_1_, bf16[384,3072]{1,0:T(8,128)(2,1)} %constant_dynamic-update-slice_fusion.10.refs_2_, bf16[384,3072]{1,0:T(8,128)(2,1)} %collective-permute-done.13.refs_3_, ...), custom_call_target="tpu_custom_call" | custom-call | tf_op jit(solution)/shard_map/pallas_call | solution.py:220
  (27 shorter events, 0.1 us)
Async XLA Ops:
  0.0 7.3 %copy-start.6 = (s32[3]{0:T(128)S(1)}, s32[3]{0:T(128)}, u32[]{:S(2)}) copy-start(s32[3]{0:T(128)} %constant.69.clone) | copy-start | bytes 40
  0.0 7.6 %copy-start.5 = (s32[2,27]{1,0:T(2,128)S(1)}, s32[2,27]{1,0:T(2,128)}, u32[]{:S(2)}) copy-start(s32[2,27]{1,0:T(2,128)} %param.10) | copy-start | bytes 652
  2.7 61.5 %collective-permute-start.4 = (bf16[2,256,1536]{2,1,0:T(8,128)(2,1)}, bf16[2,256,1536]{2,1,0:T(8,128)(2,1)S(1)}, u32[]{:S(2)}, u32[]{:S(2)}) collective-permute-start(bf16[2,256,1536]{2,1,0:T(8,128)(2,1)} %pad_maximum_fusion), channel_id=1, source_target_pairs={{0,1},{1,2},{2,3},{3,4},{4,5},{5,6},{6,7},{8,9},{9,10},{10,11},{11... | collective-permute-start | bytes 4718600 | tf_op jit(solution)/shard_map/ppermute | solution.py:33
  4.0 60.2 %collective-permute-start.5 = (bf16[2,256,1536]{2,1,0:T(8,128)(2,1)}, bf16[2,256,1536]{2,1,0:T(8,128)(2,1)S(1)}, u32[]{:S(2)}, u32[]{:S(2)}) collective-permute-start(bf16[2,256,1536]{2,1,0:T(8,128)(2,1)} %pad_maximum_fusion), channel_id=1, source_target_pairs={{1,0},{2,1},{3,2},{4,3},{5,4},{6,5},{7,6},{9,8},{10,9},{11,10},{12... | collective-permute-start | bytes 4718600 | tf_op jit(solution)/shard_map/ppermute | solution.py:33
  10.7 49.9 %collective-permute-start.1 = (bf16[272,768]{1,0:T(8,128)(2,1)}, bf16[272,768]{1,0:T(8,128)(2,1)}, u32[]{:S(2)}, u32[]{:S(2)}) collective-permute-start(bf16[272,768]{1,0:T(8,128)(2,1)} %pad_maximum_fusion.1), channel_id=1, source_target_pairs={{0,8},{1,9},{2,10},{3,11},{4,12},{5,13},{6,14},{7,15},{8,0},{9,1},... | collective-permute-start | bytes 1253384 | tf_op jit(solution)/shard_map/ppermute | solution.py:309
  13.0 48.3 %collective-permute-start = (bf16[96,3072]{1,0:T(8,128)(2,1)}, bf16[96,3072]{1,0:T(8,128)(2,1)}, u32[]{:S(2)}, u32[]{:S(2)}) collective-permute-start(bf16[96,3072]{1,0:T(8,128)(2,1)} %param.11), channel_id=1, source_target_pairs={{0,4},{1,5},{2,6},{3,7},{4,0},{5,1},{6,2},{7,3},{8,12},{9,13},{10,... | collective-permute-start | bytes 1769480 | tf_op jit(solution)/shard_map/ppermute | solution.py:23
  15.2 25.3 %collective-permute-start.2 = (bf16[48,3072]{1,0:T(8,128)(2,1)S(1)}, bf16[48,3072]{1,0:T(8,128)(2,1)}, u32[]{:S(2)}, u32[]{:S(2)}) collective-permute-start(bf16[48,3072]{1,0:T(8,128)(2,1)S(1)} %constant_dynamic-slice_fusion), channel_id=1, source_target_pairs={{0,8},{1,9},{2,10},{3,11},{4,12},{5,13},{6,14},{7,15},{8,0},{9,1},... | collective-permute-start | bytes 884744 | tf_op jit(solution)/shard_map/ppermute | solution.py:23
  17.7 46.5 %copy-start.3 = (bf16[256,1536]{1,0:T(8,128)(2,1)S(1)}, bf16[256,1536]{1,0:T(8,128)(2,1)}, u32[]{:S(2)}) copy-start(bf16[256,1536]{1,0:T(8,128)(2,1)} %k0.7) | copy-start | bytes 2359300
  17.7 46.5 %copy-start.4 = (bf16[256,1536]{1,0:T(8,128)(2,1)S(1)}, bf16[256,1536]{1,0:T(8,128)(2,1)}, u32[]{:S(2)}) copy-start(bf16[256,1536]{1,0:T(8,128)(2,1)} %v0.7) | copy-start | bytes 2359300
  40.5 19.0 %collective-permute-start.3 = (bf16[48,3072]{1,0:T(8,128)(2,1)}, bf16[48,3072]{1,0:T(8,128)(2,1)S(1)}, u32[]{:S(2)}, u32[]{:S(2)}) collective-permute-start(bf16[48,3072]{1,0:T(8,128)(2,1)} %collective-permute-done.2), channel_id=1, source_target_pairs={{0,4},{1,5},{2,6},{3,7},{4,0},{5,1},{6,2},{7,3},{8,12},{9,13},{10,... | collective-permute-start | bytes 884744 | tf_op jit(solution)/shard_map/ppermute | solution.py:23
  60.6 10.1 %collective-permute-start.8 = (bf16[96,3072]{1,0:T(8,128)(2,1)}, bf16[96,3072]{1,0:T(8,128)(2,1)}, u32[]{:S(2)}, u32[]{:S(2)}) collective-permute-start(bf16[96,3072]{1,0:T(8,128)(2,1)} %get-tuple-element.39), channel_id=1, source_target_pairs={{0,2},{1,3},{2,0},{3,1},{4,6},{5,7},{6,4},{7,5},{8,10},{9,11},{10,... | collective-permute-start | bytes 1769480 | tf_op jit(solution)/shard_map/ppermute | solution.py:23
  61.3 26.8 %collective-permute-start.7 = (bf16[256,768]{1,0:T(8,128)(2,1)}, bf16[256,768]{1,0:T(8,128)(2,1)}, u32[]{:S(2)}, u32[]{:S(2)}) collective-permute-start(bf16[256,768]{1,0:T(8,128)(2,1)} %get-tuple-element.18), channel_id=1, source_target_pairs={{0,8},{1,9},{2,10},{3,11},{4,12},{5,13},{6,14},{7,15},{8,0},{9,1},... | collective-permute-start | bytes 1179656 | tf_op jit(solution)/shard_map/ppermute | solution.py:314
  64.2 23.8 %copy-start = (bf16[2,256,1536]{2,1,0:T(8,128)(2,1)}, bf16[2,256,1536]{2,1,0:T(8,128)(2,1)S(1)}, u32[]{:S(2)}) copy-start(bf16[2,256,1536]{2,1,0:T(8,128)(2,1)S(1)} %collective-permute-done.5.kb.vb) | copy-start | bytes 4718596
  70.7 48.9 %collective-permute-start.10 = (bf16[272,768]{1,0:T(8,128)(2,1)}, bf16[272,768]{1,0:T(8,128)(2,1)}, u32[]{:S(2)}, u32[]{:S(2)}) collective-permute-start(bf16[272,768]{1,0:T(8,128)(2,1)} %shard_map.73), channel_id=1, source_target_pairs={{0,8},{1,9},{2,10},{3,11},{4,12},{5,13},{6,14},{7,15},{8,0},{9,1},... | collective-permute-start | bytes 1253384 | tf_op jit(solution)/shard_map/ppermute | solution.py:333
  73.0 33.5 %collective-permute-start.11 = (bf16[192,3072]{1,0:T(8,128)(2,1)}, bf16[192,3072]{1,0:T(8,128)(2,1)}, u32[]{:S(2)}, u32[]{:S(2)}) collective-permute-start(bf16[192,3072]{1,0:T(8,128)(2,1)} %get-tuple-element.32), channel_id=1, source_target_pairs={{0,16},{16,0},{1,17},{17,1},{2,18},{18,2},{3,19},{19,3},{4,20},{20... | collective-permute-start | bytes 3538952 | tf_op jit(solution)/shard_map/ppermute | solution.py:27
  76.4 43.2 %collective-permute-start.6 = (bf16[192,3072]{1,0:T(8,128)(2,1)}, bf16[192,3072]{1,0:T(8,128)(2,1)}, u32[]{:S(2)}, u32[]{:S(2)}) collective-permute-start(bf16[192,3072]{1,0:T(8,128)(2,1)} %get-tuple-element.33), channel_id=1, source_target_pairs={{0,2},{1,3},{2,0},{3,1},{4,6},{5,7},{6,4},{7,5},{8,10},{9,11},{10,... | collective-permute-start | bytes 3538952 | tf_op jit(solution)/shard_map/ppermute | solution.py:23
  88.1 9.4 %copy-start.2 = (bf16[256,1536]{1,0:T(8,128)(2,1)S(1)}, bf16[256,1536]{1,0:T(8,128)(2,1)}, u32[]{:S(2)}) copy-start(bf16[256,1536]{1,0:T(8,128)(2,1)} %q_ref.1) | copy-start | bytes 2359300
  94.4 29.3 %collective-permute-start.12 = (bf16[272,768]{1,0:T(8,128)(2,1)}, bf16[272,768]{1,0:T(8,128)(2,1)}, u32[]{:S(2)}, u32[]{:S(2)}) collective-permute-start(bf16[272,768]{1,0:T(8,128)(2,1)} %shard_map.74), channel_id=1, source_target_pairs={{0,8},{1,9},{2,10},{3,11},{4,12},{5,13},{6,14},{7,15},{8,0},{9,1},... | collective-permute-start | bytes 1253384 | tf_op jit(solution)/shard_map/ppermute | solution.py:333
  108.9 13.2 %copy-start.1 = (bf16[2,256,1536]{2,1,0:T(8,128)(2,1)S(1)}, bf16[2,256,1536]{2,1,0:T(8,128)(2,1)}, u32[]{:S(2)}) copy-start(bf16[2,256,1536]{2,1,0:T(8,128)(2,1)} %copy-done) | copy-start | bytes 4718596
  108.9 17.1 %collective-permute-start.13 = (bf16[384,3072]{1,0:T(8,128)(2,1)}, bf16[384,3072]{1,0:T(8,128)(2,1)}, u32[]{:S(2)}, u32[]{:S(2)}) collective-permute-start(bf16[384,3072]{1,0:T(8,128)(2,1)} %constant_dynamic-update-slice_fusion.10.refs_2_), channel_id=1, source_target_pairs={{0,1},{1,0},{2,3},{3,2},{4,5},{5,4},{6,7},{7,6},{8,9},{9,8},{10,11... | collective-permute-start | bytes 7077896 | tf_op jit(solution)/shard_map/ppermute | solution.py:23
  122.0 5.5 %collective-permute-start.9 = (bf16[384,3072]{1,0:T(8,128)(2,1)}, bf16[384,3072]{1,0:T(8,128)(2,1)}, u32[]{:S(2)}, u32[]{:S(2)}) collective-permute-start(bf16[384,3072]{1,0:T(8,128)(2,1)} %constant_dynamic-update-slice_fusion.7.refs_0_), channel_id=1, source_target_pairs={{0,1},{1,0},{2,3},{3,2},{4,5},{5,4},{6,7},{7,6},{8,9},{9,8},{10,11... | collective-permute-start | bytes 7077896 | tf_op jit(solution)/shard_map/ppermute | solution.py:23

commit v3 on v2

--- a/solution.py
+++ b/solution.py
@@ -45,9 +45,46 @@
     return pairs
 
 
-def attend_kernel(rows, per_block, bias_ref, q_ref, k0, ka, kb, v0, va, vb, out_ref):
+def join_kernel(count, *refs):
+    sources, (out_ref, sems) = refs[:count], refs[count:]
+    copies, first = [], 0
+    for i, source in enumerate(sources):
+        size = source.shape[0]
+        copy = pltpu.make_async_copy(source, out_ref.at[pl.ds(first, size), :], sems.at[i])
+        copy.start()
+        copies.append(copy)
+        first += size
+    for copy in copies:
+        copy.wait()
+
+
+def join(*arrays):
+    rows = sum(array.shape[0] for array in arrays)
+    hbm = pl.BlockSpec(memory_space=pltpu.HBM)
+    return pl.pallas_call(
+        functools.partial(join_kernel, len(arrays)),
+        in_specs=[hbm] * len(arrays),
+        out_specs=hbm,
+        out_shape=jax.ShapeDtypeStruct((rows, arrays[0].shape[1]), arrays[0].dtype),
+        scratch_shapes=[pltpu.SemaphoreType.DMA((len(arrays),))],
+        cost_estimate=pl.CostEstimate(flops=0, bytes_accessed=0, transcendentals=0),
+    )(*arrays)
+
+
+def attend_kernel(rows, per_block, list_ref, q_ref, k0, ka, kb, v0, va, vb, out_ref):
     factor = HD ** (-0.5) * LOG2E
     tile = rows // FRAMES
+    position = lax.axis_index("seq")
+    lists = list_ref[...].astype(jnp.float32)
+    masks = []
+    for step in (0, -1, 1):
+        bits = []
+        for frame in range(FRAMES):
+            tile_id = (position + step) * FRAMES + frame
+            tile_id = jnp.where(tile_id >= 0, tile_id, -2).astype(jnp.float32)
+            hit = jnp.max(jnp.where(lists == tile_id, 0.0, -jnp.inf), axis=1, keepdims=True)
+            bits.append(jnp.broadcast_to(hit, (hit.shape[0], tile)))
+        masks.append(jnp.concatenate(bits, axis=1))
     nt = (((1,), (1,)), ((), ()))
     lse = jnp.zeros((rows, HD), jnp.float32)
     lane = lax.broadcasted_iota(jnp.int32, (rows, HD), 1)
@@ -59,11 +96,10 @@
         for frame in range(FRAMES):
             here = slice(frame * tile, (frame + 1) * tile)
             q = q_ref[here, cols]
-            bias = bias_ref[frame : frame + 1, :].astype(jnp.float32)
             scores = [
                 lax.dot_general(q, key, nt, preferred_element_type=jnp.float32)
-                + bias[:, i * rows : (i + 1) * rows]
-                for i, key in enumerate(keys)
+                + mask[frame : frame + 1, :]
+                for key, mask in zip(keys, masks)
             ]
             peak = functools.reduce(jnp.maximum, scores)
             peak = jnp.max(peak, axis=1, keepdims=True)
@@ -91,7 +127,7 @@
     out_ref[rows:, :] = jnp.concatenate(stats, axis=0).astype(out_ref.dtype)
 
 
-def attend(bias, q, q_first, heads, keys, values, kv_up, kv_down, first, kind, cost=WEIGHTY):
+def attend(lists, q, q_first, heads, keys, values, kv_up, kv_down, first, kind, cost=WEIGHTY):
     rows = keys.shape[0]
     per_block = rows // HD
     width = per_block * HD
@@ -104,7 +140,7 @@
         functools.partial(attend_kernel, rows, per_block),
         grid=(heads // per_block,),
         in_specs=[
-            pl.BlockSpec(bias.shape, lambda i: (0, 0)),
+            pl.BlockSpec((EXTRA, HD), lambda i: (lists.shape[0] // EXTRA - 1, 0)),
             pl.BlockSpec((rows, width), lambda i: (0, q_lo + i)),
             here,
             key_spec,
@@ -119,7 +155,7 @@
         cost_estimate=pl.CostEstimate(
             flops=cost, bytes_accessed=0, transcendentals=0
         ),
-    )(bias, q, keys, kv_up, kv_down, values, kv_up, kv_down)
+    )(lists, q, keys, kv_up, kv_down, values, kv_up, kv_down)
 
 
 def merge_kernel(rows, chunk_counts, partner_ref, *refs):
@@ -258,17 +294,18 @@
 
         return [(i * self.half, self.half, at(bit, turn)) for i, (bit, turn) in enumerate(bits)]
 
-    def pieces(self):
+    def pieces(self, near, wy, four, cx, swapped):
+        far = (8, 12, 10, 14)
         return [
-            (self.quad, self.full(0, 4, 2, 6)),
-            (self.wc, self.full(1, 5, 3, 7)),
-            (self.eight, self.halves(*[(b, t) for t in (0, 1) for b in (8, 12, 10, 14)])),
-            (self.cc, self.halves(*[(b, t) for t in (0, 1) for b in (9, 13, 11, 15)])),
+            (near, self.full(0, 4)),
+            (wy, self.full(2, 6)),
+            (four, self.halves(*[(b, 0) for b in far])),
+            (cx, self.halves(*[(b, 1) for b in far])),
+            (swapped[0], self.full(1, 5)),
+            (swapped[1], self.full(3, 7)),
+            (swapped[2], self.halves(*[(b ^ 1, 0) for b in far])),
+            (swapped[3], self.halves(*[(b ^ 1, 1) for b in far])),
         ]
-
-
-def join(*arrays):
-    return jnp.concatenate(arrays, axis=0)
 
 
 def body(groups, query_rows, key_rows, value_rows, block_list, out_weight):
@@ -276,41 +313,33 @@
     heads = features // HD
     devices = lax.axis_size("seq")
     grid_rows = devices // GRID_COLS
-    position = lax.axis_index("seq")
-    row = position // GRID_COLS
-    tile = rows // FRAMES
+    row = lax.axis_index("seq") // GRID_COLS
     chunk_heads = heads // 2
     chunk = chunk_heads * HD
-
-    def bias_for(there):
-        centre = there * GRID_COLS + position % GRID_COLS
-        places = centre + jnp.array([0, -1, 1], jnp.int32)
-        ids = (places[:, None] * FRAMES + jnp.arange(FRAMES, dtype=jnp.int32)[None, :]).reshape(-1)
-        ids = jnp.where(ids >= 0, ids, -2)
-        member = jnp.any(block_list[:, :, None] == ids[None, None, :], axis=1)
-        return jnp.repeat(jnp.where(member, 0.0, -jnp.inf), tile, axis=1)
-
+    phases = [parity for parity in range(2) if parity + 1 < grid_rows]
     cube = None
     if devices == 16 and groups == 2 and out_weight.shape[0] % 32 == 0:
         cube = Cube(out_weight)
         cube.cross()
-    kv = jnp.stack([key_rows, value_rows])
+    lists = jnp.pad(
+        block_list.astype(jnp.bfloat16),
+        ((0, EXTRA - FRAMES), (0, HD - block_list.shape[1])),
+        constant_values=-1,
+    )
+    asking = jnp.concatenate([query_rows[:, :chunk], jnp.tile(lists, (1, chunk_heads))], axis=0)
+    kv = join(key_rows, value_rows).reshape(2, rows, features)
     kv_up = column_shift(kv, 1)
     kv_down = column_shift(kv, -1)
     if cube:
         wz = swap_bit(out_weight, 4)
-    phases = [parity for parity in range(2) if parity + 1 < grid_rows]
     sent = []
     for parity in phases:
-        there = jnp.where(row % 2 == parity, row + 1, row - 1)
-        bias = bias_for(there).reshape(-1).astype(jnp.bfloat16)
-        bias = jnp.pad(bias, (0, EXTRA * chunk - bias.shape[0])).reshape(EXTRA, chunk)
         pairs = row_pairs(parity)
-        first = lax.ppermute(join(query_rows[:, :chunk], bias), "seq", pairs)
+        first = lax.ppermute(asking, "seq", pairs)
         second = query_rows[:, chunk:]
         if cube:
             cz = swap_bit(cube.c0, 4)
-            second = after(second, wz)
+            second = after(second, wz, cube.c0)
         sent.append([first, lax.ppermute(second, "seq", pairs)])
     if cube:
         far = join(cube.c0, cz)
@@ -319,12 +348,11 @@
     common = (key_rows, value_rows, kv_up, kv_down)
     others = []
     for parity, asked in zip(phases, sent):
-        bias = asked[0][rows:, :].reshape(-1)[: FRAMES * 3 * rows].reshape(FRAMES, 3 * rows)
         back = []
         for number, q in enumerate(asked):
             if number:
                 q = after(q, part, near, four) if cube else after(q, part)
-            part = attend(bias, q, 0, chunk_heads, *common, number * chunk_heads, jnp.bfloat16)
+            part = attend(asked[0], q, 0, chunk_heads, *common, number * chunk_heads, jnp.bfloat16)
             if cube and not number:
                 four = join(far, after(cy, part))
                 cx = swap_group(four, groups)
@@ -333,15 +361,14 @@
             back.append(lax.ppermute(part, "seq", row_pairs(parity)))
             last = part
         others.append(back)
-    own_bias = bias_for(row)
     early = heads - rows // HD
     awaited = [others[0][0]] if phases else []
     if cube:
         awaited += [cx, wy]
     q = after(query_rows, last) if phases else query_rows
-    own = [attend(own_bias, q, 0, early, *common, 0, jnp.float32, 0)]
+    own = [attend(lists, q, 0, early, *common, 0, jnp.float32, 0)]
     q = after(query_rows, *awaited)
-    own.append(attend(own_bias, q, early, heads - early, *common, early, jnp.float32))
+    own.append(attend(lists, q, early, heads - early, *common, early, jnp.float32))
     partner = jnp.stack(
         [
             jnp.where(row % 2 == parity, row + 1 < grid_rows, row > 0).astype(jnp.int32)
@@ -351,11 +378,9 @@
     )
     attention = merge(partner, [own] + others)
     if cube:
-        cube.quad = join(near, after(wy, own[0]))
-        cube.wc = after(swap_bit(cube.quad, 1), attention)
-        cube.eight = join(four, after(cx, own[0]))
-        cube.cc = after(swap_bit(cube.eight, 1), attention)
-        pieces = cube.pieces()
+        swapped = [swap_bit(after(piece, own[0]), 1) for piece in (near, wy, four, cx)]
+        swapped = [after(piece, attention) for piece in swapped]
+        pieces = cube.pieces(near, wy, four, cx, swapped)
     else:
         whole = lax.all_gather(out_weight, "seq", axis=0, tiled=True)
         pieces = [(whole, [(0, whole.shape[0], lambda: 0)])]

time: 137 us -> 260 us (1.90)
  the two profiles are of different devices: /device:TPU:13 before, /device:TPU:0 now
where the time goes in v3:
time: 260 us; the launch traced here: 259 us
  Pallas kernels  176 us (68%)
  starting transfers between devices  44.5 us (17%)
  waiting for transfers between devices  29.5 us (11%)
  local copies, waits for them, and re-layouts  8.67 us (3%)
    pallas_call x4, Pallas kernels, join(): pl.pallas_call(functools.partial(join_kernel, len(arrays)), in_specs=[hbm...  141 us
    ppermute x9, starting transfers between devices, swap_bit(): return lax.ppermute(value, 'seq', [(s, s ^ bit) for s in range(count)])  32.7 us
    ppermute x9, waiting for transfers between devices, swap_bit(): return lax.ppermute(value, 'seq', [(s, s ^ bit) for s in range(count)])  27.8 us
    pallas_call x4, Pallas kernels, attend(): pl.pallas_call(functools.partial(attend_kernel, rows, per_block), grid=(h...  23.2 us
    pallas_call x1, Pallas kernels, project(): pl.pallas_call(functools.partial(project_kernel, plan), in_specs=[pl.Bloc...  8.55 us
    unnamed x27, local copies, waits for them, and re-layouts  5.72 us
  transfers between devices with their start and end apart: 16, of which 6 were waited for; matrix products, arithmetic and copies ran while one was open for 1% of the time, Pallas kernels for 46%

profile of v3, /device:TPU:0, one launch (start us, length us, event | category | flops | bytes accessed | tf_op | source)
XLA Modules:
  0.0 259.3 jit_solution(9872940735900100350)
XLA Ops:
  0.0 48.8 %shard_map.56 = bf16[512,1536]{1,0:T(8,128)(2,1)} custom-call(bf16[256,1536]{1,0:T(8,128)(2,1)} %k0.7, bf16[256,1536]{1,0:T(8,128)(2,1)} %v0.7), custom_call_target="tpu_custom_call" | custom-call | tf_op jit(solution)/shard_map/pallas_call | solution.py:64
  48.8 0.0 copy-start.12
  48.8 1.3 collective-permute-start.5
  50.1 3.1 %collective-permute-start.4 = (bf16[2,256,1536]{2,1,0:T(8,128)(2,1)}, bf16[2,256,1536]{2,1,0:T(8,128)(2,1)S(1)}, u32[]{:S(2)}, u32[]{:S(2)}) collective-permute-start(bf16[2,256,1536]{2,1,0:T(8,128)(2,1)} %bitcast.7), channel_id=1, source_target_pairs={{0,1},{1,2},{2,3},{3,4},{4,5},{5,6},{6,7},{8,9},{9,10},{10,11},{11... | collective-permute-start | bytes 4718600 | tf_op jit(solution)/shard_map/ppermute | solution.py:33
  53.2 3.3 %collective-permute-start = (bf16[96,3072]{1,0:T(8,128)(2,1)}, bf16[96,3072]{1,0:T(8,128)(2,1)}, u32[]{:S(2)}, u32[]{:S(2)}) collective-permute-start(bf16[96,3072]{1,0:T(8,128)(2,1)} %refs_0_.3), channel_id=1, source_target_pairs={{0,4},{1,5},{2,6},{3,7},{4,0},{5,1},{6,2},{7,3},{8,12},{9,13},{10,... | collective-permute-start | bytes 1769480 | tf_op jit(solution)/shard_map/ppermute | solution.py:23
  56.6 1.0 constant_dynamic-slice_fusion
  57.6 2.7 %collective-permute-start.2 = (bf16[48,3072]{1,0:T(8,128)(2,1)S(1)}, bf16[48,3072]{1,0:T(8,128)(2,1)S(1)}, u32[]{:S(2)}, u32[]{:S(2)}) collective-permute-start(bf16[48,3072]{1,0:T(8,128)(2,1)S(1)} %constant_dynamic-slice_fusion), channel_id=1, source_target_pairs={{0,8},{1,9},{2,10},{3,11},{4,12},{5,13},{6,14},{7,15},{8,0},{9,1},... | collective-permute-start | bytes 884744 | tf_op jit(solution)/shard_map/ppermute | solution.py:23
  60.2 1.9 fusion
  62.2 0.6 copy-done.9
  62.8 0.8 pad_maximum_fusion
  63.6 0.3 collective-permute-start.1
  63.9 13.0 %collective-permute-done.2.refs_0_ = bf16[48,3072]{1,0:T(8,128)(2,1)S(1)} collective-permute-done((bf16[48,3072]{1,0:T(8,128)(2,1)S(1)}, bf16[48,3072]{1,0:T(8,128)(2,1)S(1)}, u32[]{:S(2)}, u32[]{:S(2)}) %collective-permute-start.2) | collective-permute-done | bytes 294944 | tf_op jit(solution)/shard_map/ppermute | solution.py:23
  76.9 25.5 %collective-permute-start.3 = (bf16[48,3072]{1,0:T(8,128)(2,1)S(1)}, bf16[48,3072]{1,0:T(8,128)(2,1)}, u32[]{:S(2)}, u32[]{:S(2)}) collective-permute-start(bf16[48,3072]{1,0:T(8,128)(2,1)S(1)} %collective-permute-done.2.refs_0_), channel_id=1, source_target_pairs={{0,4},{1,5},{2,6},{3,7},{4,0},{5,1},{6,2},{7,3},{8,12},{9,13},{10,... | collective-permute-start | bytes 884744 | tf_op jit(solution)/shard_map/ppermute | solution.py:23
  102.3 5.2 %collective-permute-done.3.refs_1_ = bf16[48,3072]{1,0:T(8,128)(2,1)} collective-permute-done((bf16[48,3072]{1,0:T(8,128)(2,1)S(1)}, bf16[48,3072]{1,0:T(8,128)(2,1)}, u32[]{:S(2)}, u32[]{:S(2)}) %collective-permute-start.3) | collective-permute-done | bytes 294944 | tf_op jit(solution)/shard_map/ppermute | solution.py:23
  107.5 19.0 %shard_map.55.refs_0_ = bf16[96,3072]{1,0:T(8,128)(2,1)} custom-call(bf16[48,3072]{1,0:T(8,128)(2,1)} %copy-done.11, bf16[48,3072]{1,0:T(8,128)(2,1)} %collective-permute-done.3.refs_1_), custom_call_target="tpu_custom_call" | custom-call | tf_op jit(solution)/shard_map/pallas_call | solution.py:64
  126.5 0.1 collective-permute-start.7
  126.6 0.0 collective-permute-done.refs_1_
  126.6 2.7 %collective-permute-start.9 = (bf16[256,768]{1,0:T(8,128)(2,1)}, bf16[256,768]{1,0:T(8,128)(2,1)}, u32[]{:S(2)}, u32[]{:S(2)}) collective-permute-start(bf16[256,768]{1,0:T(8,128)(2,1)} %get-tuple-element.23), channel_id=1, source_target_pairs={{0,8},{1,9},{2,10},{3,11},{4,12},{5,13},{6,14},{7,15},{8,0},{9,1},... | collective-permute-start | bytes 1179656 | tf_op jit(solution)/shard_map/ppermute | solution.py:343
  129.2 0.0 collective-permute-done.4.ka.va
  129.2 0.0 copy-start.3
  129.3 1.7 copy-done.3
  131.0 1.1 copy-done.6
  132.1 6.2 %shard_map.57 = bf16[272,768]{1,0:T(8,128)(2,1)} custom-call(bf16[272,768]{1,0:T(8,128)(2,1)} %collective-permute-done.1.list_ref.q_ref, bf16[272,768]{1,0:T(8,128)(2,1)} %collective-permute-done.1.list_ref.q_ref, bf16[256,1536]{1,0:T(8,128)(2,1)S(1)} %copy-done.3, bf16[2,256,1536]{2,1,0:T(8,128)(2,1)S(1)} %collective-permute-done.4.ka.va, ...), custom_call_target="tpu_custom_call" | custom-call | flops 999999995904 | tf_op jit(solution)/shard_map/pallas_call | solution.py:139
  138.3 0.4 collective-permute-start.11
  138.6 4.1 %collective-permute-done.7.refs_1_ = bf16[96,3072]{1,0:T(8,128)(2,1)} collective-permute-done((bf16[96,3072]{1,0:T(8,128)(2,1)}, bf16[96,3072]{1,0:T(8,128)(2,1)}, u32[]{:S(2)}, u32[]{:S(2)}) %collective-permute-start.7) | collective-permute-done | bytes 589856 | tf_op jit(solution)/shard_map/ppermute | solution.py:23
  142.7 36.9 %shard_map.59.refs_2_ = bf16[192,3072]{1,0:T(8,128)(2,1)} custom-call(bf16[96,3072]{1,0:T(8,128)(2,1)} %shard_map.55.refs_0_, bf16[96,3072]{1,0:T(8,128)(2,1)} %collective-permute-done.7.refs_1_), custom_call_target="tpu_custom_call" | custom-call | tf_op jit(solution)/shard_map/pallas_call | solution.py:64
  179.6 36.9 %shard_map.58.refs_0_ = bf16[192,3072]{1,0:T(8,128)(2,1)} custom-call(bf16[96,3072]{1,0:T(8,128)(2,1)} %refs_0_.3, bf16[96,3072]{1,0:T(8,128)(2,1)} %collective-permute-done.refs_1_), custom_call_target="tpu_custom_call" | custom-call | tf_op jit(solution)/shard_map/pallas_call | solution.py:64
  216.4 0.1 collective-permute-start.6
  216.5 1.6 collective-permute-start.8
  218.1 0.0 collective-permute-done.9.q_ref
  218.1 1.1 copy-done.4
  219.2 1.1 copy-done.7
  220.4 6.5 %shard_map.60 = bf16[272,768]{1,0:T(8,128)(2,1)} custom-call(bf16[272,768]{1,0:T(8,128)(2,1)} %collective-permute-done.1.list_ref.q_ref, bf16[256,768]{1,0:T(8,128)(2,1)} %collective-permute-done.9.q_ref, bf16[256,1536]{1,0:T(8,128)(2,1)S(1)} %copy-done.4, bf16[2,256,1536]{2,1,0:T(8,128)(2,1)S(1)} %collective-permute-done.4.ka.va, ...), custom_call_target="tpu_custom_call" | custom-call | flops 999999995904 | tf_op jit(solution)/shard_map/pallas_call | solution.py:139
  226.8 2.5 collective-permute-start.12
  229.4 9.0 %shard_map.61.refs_0_ = f32[272,1280]{1,0:T(8,128)S(1)} custom-call(bf16[16,128]{1,0:T(8,128)(2,1)S(1)} %copy-done.10, bf16[256,1536]{1,0:T(8,128)(2,1)S(1)} %copy-done.2, bf16[256,1536]{1,0:T(8,128)(2,1)S(1)} %copy-done.5, bf16[2,256,1536]{2,1,0:T(8,128)(2,1)S(1)} %collective-permute-done.4.ka.va, bf16[2,256,1536]{2,1,0:T(8,128)(2,1)} %copy-done, ...), custom_call_target="tpu_custom_call" | custom-call | tf_op jit(solution)/shard_map/pallas_call | solution.py:139
  238.4 0.1 collective-permute-start.10
  238.5 0.5 collective-permute-start.14
  239.0 5.6 %collective-permute-done.6.refs_1_ = bf16[192,3072]{1,0:T(8,128)(2,1)} collective-permute-done((bf16[192,3072]{1,0:T(8,128)(2,1)}, bf16[192,3072]{1,0:T(8,128)(2,1)}, u32[]{:S(2)}, u32[]{:S(2)}) %collective-permute-start.6) | collective-permute-done | bytes 1179680 | tf_op jit(solution)/shard_map/ppermute | solution.py:23
  244.5 0.3 collective-permute-done.8.refs_3_
  244.9 0.0 collective-permute-start.13
  244.9 0.5 collective-permute-start.15
  245.4 1.5 shard_map.62.refs_1_
  246.9 1.4 collective-permute-done.12.refs_3_
  248.3 2.4 shard_map.63.refs_8_
  250.7 0.0 collective-permute-done.10.refs_4_
  250.7 0.0 collective-permute-done.13.refs_5_
  250.7 0.0 collective-permute-done.15.refs_7_
  250.7 8.6 %shard_map.64 = bf16[256,3072]{1,0:T(8,128)(2,1)} custom-call(bf16[192,3072]{1,0:T(8,128)(2,1)} %shard_map.58.refs_0_, bf16[192,3072]{1,0:T(8,128)(2,1)} %collective-permute-done.6.refs_1_, bf16[192,3072]{1,0:T(8,128)(2,1)} %shard_map.59.refs_2_, bf16[192,3072]{1,0:T(8,128)(2,1)} %collective-permute-done.8.refs_3_, ...), custom_call_target="tpu_custom_call" | custom-call | tf_op jit(solution)/shard_map/pallas_call | solution.py:256
  (27 shorter events, 0.1 us)
Async XLA Ops:
  48.8 13.4 %copy-start.12 = (s32[2,27]{1,0:T(2,128)S(1)}, s32[2,27]{1,0:T(2,128)}, u32[]{:S(2)}) copy-start(s32[2,27]{1,0:T(2,128)} %param.8) | copy-start | bytes 652
  48.8 80.4 %collective-permute-start.5 = (bf16[2,256,1536]{2,1,0:T(8,128)(2,1)}, bf16[2,256,1536]{2,1,0:T(8,128)(2,1)S(1)}, u32[]{:S(2)}, u32[]{:S(2)}) collective-permute-start(bf16[2,256,1536]{2,1,0:T(8,128)(2,1)} %bitcast.6), channel_id=1, source_target_pairs={{1,0},{2,1},{3,2},{4,3},{5,4},{6,5},{7,6},{9,8},{10,9},{11,10},{12... | collective-permute-start | bytes 4718600 | tf_op jit(solution)/shard_map/ppermute | solution.py:33
  50.1 79.2 %collective-permute-start.4 = (bf16[2,256,1536]{2,1,0:T(8,128)(2,1)}, bf16[2,256,1536]{2,1,0:T(8,128)(2,1)S(1)}, u32[]{:S(2)}, u32[]{:S(2)}) collective-permute-start(bf16[2,256,1536]{2,1,0:T(8,128)(2,1)} %bitcast.7), channel_id=1, source_target_pairs={{0,1},{1,2},{2,3},{3,4},{4,5},{5,6},{6,7},{8,9},{9,10},{10,11},{11... | collective-permute-start | bytes 4718600 | tf_op jit(solution)/shard_map/ppermute | solution.py:33
  53.2 73.3 %collective-permute-start = (bf16[96,3072]{1,0:T(8,128)(2,1)}, bf16[96,3072]{1,0:T(8,128)(2,1)}, u32[]{:S(2)}, u32[]{:S(2)}) collective-permute-start(bf16[96,3072]{1,0:T(8,128)(2,1)} %refs_0_.3), channel_id=1, source_target_pairs={{0,4},{1,5},{2,6},{3,7},{4,0},{5,1},{6,2},{7,3},{8,12},{9,13},{10,... | collective-permute-start | bytes 1769480 | tf_op jit(solution)/shard_map/ppermute | solution.py:23
  57.6 19.3 %collective-permute-start.2 = (bf16[48,3072]{1,0:T(8,128)(2,1)S(1)}, bf16[48,3072]{1,0:T(8,128)(2,1)S(1)}, u32[]{:S(2)}, u32[]{:S(2)}) collective-permute-start(bf16[48,3072]{1,0:T(8,128)(2,1)S(1)} %constant_dynamic-slice_fusion), channel_id=1, source_target_pairs={{0,8},{1,9},{2,10},{3,11},{4,12},{5,13},{6,14},{7,15},{8,0},{9,1},... | collective-permute-start | bytes 884744 | tf_op jit(solution)/shard_map/ppermute | solution.py:23
  62.2 0.6 copy-start.9
  63.6 65.7 %collective-permute-start.1 = (bf16[272,768]{1,0:T(8,128)(2,1)}, bf16[272,768]{1,0:T(8,128)(2,1)}, u32[]{:S(2)}, u32[]{:S(2)}) collective-permute-start(bf16[272,768]{1,0:T(8,128)(2,1)} %pad_maximum_fusion), channel_id=1, source_target_pairs={{0,8},{1,9},{2,10},{3,11},{4,12},{5,13},{6,14},{7,15},{8,0},{9,1},... | collective-permute-start | bytes 1253384 | tf_op jit(solution)/shard_map/ppermute | solution.py:338
  76.9 30.6 %copy-start.11 = (bf16[48,3072]{1,0:T(8,128)(2,1)}, bf16[48,3072]{1,0:T(8,128)(2,1)S(1)}, u32[]{:S(2)}) copy-start(bf16[48,3072]{1,0:T(8,128)(2,1)S(1)} %collective-permute-done.2.refs_0_) | copy-start | bytes 884740
  76.9 30.6 %collective-permute-start.3 = (bf16[48,3072]{1,0:T(8,128)(2,1)S(1)}, bf16[48,3072]{1,0:T(8,128)(2,1)}, u32[]{:S(2)}, u32[]{:S(2)}) collective-permute-start(bf16[48,3072]{1,0:T(8,128)(2,1)S(1)} %collective-permute-done.2.refs_0_), channel_id=1, source_target_pairs={{0,4},{1,5},{2,6},{3,7},{4,0},{5,1},{6,2},{7,3},{8,12},{9,13},{10,... | collective-permute-start | bytes 884744 | tf_op jit(solution)/shard_map/ppermute | solution.py:23
  126.5 16.2 %collective-permute-start.7 = (bf16[96,3072]{1,0:T(8,128)(2,1)}, bf16[96,3072]{1,0:T(8,128)(2,1)}, u32[]{:S(2)}, u32[]{:S(2)}) collective-permute-start(bf16[96,3072]{1,0:T(8,128)(2,1)} %shard_map.55.refs_0_), channel_id=1, source_target_pairs={{0,2},{1,3},{2,0},{3,1},{4,6},{5,7},{6,4},{7,5},{8,10},{9,11},{10,... | collective-permute-start | bytes 1769480 | tf_op jit(solution)/shard_map/ppermute | solution.py:23
  126.6 91.5 %collective-permute-start.9 = (bf16[256,768]{1,0:T(8,128)(2,1)}, bf16[256,768]{1,0:T(8,128)(2,1)}, u32[]{:S(2)}, u32[]{:S(2)}) collective-permute-start(bf16[256,768]{1,0:T(8,128)(2,1)} %get-tuple-element.23), channel_id=1, source_target_pairs={{0,8},{1,9},{2,10},{3,11},{4,12},{5,13},{6,14},{7,15},{8,0},{9,1},... | collective-permute-start | bytes 1179656 | tf_op jit(solution)/shard_map/ppermute | solution.py:343
  129.2 88.8 %copy-start = (bf16[2,256,1536]{2,1,0:T(8,128)(2,1)}, bf16[2,256,1536]{2,1,0:T(8,128)(2,1)S(1)}, u32[]{:S(2)}) copy-start(bf16[2,256,1536]{2,1,0:T(8,128)(2,1)S(1)} %collective-permute-done.5.kb.vb) | copy-start | bytes 4718596
  129.2 1.7 copy-start.3
  131.0 1.1 copy-start.6
  138.3 100.2 %collective-permute-start.11 = (bf16[272,768]{1,0:T(8,128)(2,1)}, bf16[272,768]{1,0:T(8,128)(2,1)}, u32[]{:S(2)}, u32[]{:S(2)}) collective-permute-start(bf16[272,768]{1,0:T(8,128)(2,1)} %shard_map.57), channel_id=1, source_target_pairs={{0,8},{1,9},{2,10},{3,11},{4,12},{5,13},{6,14},{7,15},{8,0},{9,1},... | collective-permute-start | bytes 1253384 | tf_op jit(solution)/shard_map/ppermute | solution.py:361
  216.4 28.1 %collective-permute-start.6 = (bf16[192,3072]{1,0:T(8,128)(2,1)}, bf16[192,3072]{1,0:T(8,128)(2,1)}, u32[]{:S(2)}, u32[]{:S(2)}) collective-permute-start(bf16[192,3072]{1,0:T(8,128)(2,1)} %shard_map.58.refs_0_), channel_id=1, source_target_pairs={{0,2},{1,3},{2,0},{3,1},{4,6},{5,7},{6,4},{7,5},{8,10},{9,11},{10,... | collective-permute-start | bytes 3538952 | tf_op jit(solution)/shard_map/ppermute | solution.py:23
  216.5 28.4 %collective-permute-start.8 = (bf16[192,3072]{1,0:T(8,128)(2,1)}, bf16[192,3072]{1,0:T(8,128)(2,1)}, u32[]{:S(2)}, u32[]{:S(2)}) collective-permute-start(bf16[192,3072]{1,0:T(8,128)(2,1)} %shard_map.59.refs_2_), channel_id=1, source_target_pairs={{0,16},{16,0},{1,17},{17,1},{2,18},{18,2},{3,19},{19,3},{4,20},{20... | collective-permute-start | bytes 3538952 | tf_op jit(solution)/shard_map/ppermute | solution.py:27
  218.1 1.1 copy-start.4
  219.2 1.1 copy-start.7
  220.3 9.0 %copy-start.2 = (bf16[256,1536]{1,0:T(8,128)(2,1)S(1)}, bf16[256,1536]{1,0:T(8,128)(2,1)}, u32[]{:S(2)}) copy-start(bf16[256,1536]{1,0:T(8,128)(2,1)} %q_ref.1) | copy-start | bytes 2359300
  220.4 9.0 %copy-start.5 = (bf16[256,1536]{1,0:T(8,128)(2,1)S(1)}, bf16[256,1536]{1,0:T(8,128)(2,1)}, u32[]{:S(2)}) copy-start(bf16[256,1536]{1,0:T(8,128)(2,1)} %k0.7) | copy-start | bytes 2359300
  220.4 9.0 %copy-start.8 = (bf16[256,1536]{1,0:T(8,128)(2,1)S(1)}, bf16[256,1536]{1,0:T(8,128)(2,1)}, u32[]{:S(2)}) copy-start(bf16[256,1536]{1,0:T(8,128)(2,1)} %v0.7) | copy-start | bytes 2359300
  220.4 9.0 %copy-start.10 = (bf16[16,128]{1,0:T(8,128)(2,1)S(1)}, bf16[16,128]{1,0:T(8,128)(2,1)}, u32[]{:S(2)}) copy-start(bf16[16,128]{1,0:T(8,128)(2,1)} %copy-done.9) | copy-start | bytes 12292
  226.8 18.6 %copy-start.1 = (bf16[2,256,1536]{2,1,0:T(8,128)(2,1)S(1)}, bf16[2,256,1536]{2,1,0:T(8,128)(2,1)}, u32[]{:S(2)}) copy-start(bf16[2,256,1536]{2,1,0:T(8,128)(2,1)} %copy-done) | copy-start | bytes 4718596
  226.8 21.5 %collective-permute-start.12 = (bf16[272,768]{1,0:T(8,128)(2,1)}, bf16[272,768]{1,0:T(8,128)(2,1)}, u32[]{:S(2)}, u32[]{:S(2)}) collective-permute-start(bf16[272,768]{1,0:T(8,128)(2,1)} %shard_map.60), channel_id=1, source_target_pairs={{0,8},{1,9},{2,10},{3,11},{4,12},{5,13},{6,14},{7,15},{8,0},{9,1},... | collective-permute-start | bytes 1253384 | tf_op jit(solution)/shard_map/ppermute | solution.py:361
  238.4 12.3 %collective-permute-start.10 = (bf16[192,3072]{1,0:T(8,128)(2,1)}, bf16[192,3072]{1,0:T(8,128)(2,1)}, u32[]{:S(2)}, u32[]{:S(2)}) collective-permute-start(bf16[192,3072]{1,0:T(8,128)(2,1)} %shard_map.58.refs_0_), channel_id=1, source_target_pairs={{0,1},{1,0},{2,3},{3,2},{4,5},{5,4},{6,7},{7,6},{8,9},{9,8},{10,11... | collective-permute-start | bytes 3538952 | tf_op jit(solution)/shard_map/ppermute | solution.py:23
  238.5 12.2 %collective-permute-start.14 = (bf16[192,3072]{1,0:T(8,128)(2,1)}, bf16[192,3072]{1,0:T(8,128)(2,1)}, u32[]{:S(2)}, u32[]{:S(2)}) collective-permute-start(bf16[192,3072]{1,0:T(8,128)(2,1)} %shard_map.59.refs_2_), channel_id=1, source_target_pairs={{0,1},{1,0},{2,3},{3,2},{4,5},{5,4},{6,7},{7,6},{8,9},{9,8},{10,11... | collective-permute-start | bytes 3538952 | tf_op jit(solution)/shard_map/ppermute | solution.py:23
  244.9 5.8 %collective-permute-start.13 = (bf16[192,3072]{1,0:T(8,128)(2,1)}, bf16[192,3072]{1,0:T(8,128)(2,1)}, u32[]{:S(2)}, u32[]{:S(2)}) collective-permute-start(bf16[192,3072]{1,0:T(8,128)(2,1)} %collective-permute-done.6.refs_1_), channel_id=1, source_target_pairs={{0,1},{1,0},{2,3},{3,2},{4,5},{5,4},{6,7},{7,6},{8,9},{9,8},{10,11... | collective-permute-start | bytes 3538952 | tf_op jit(solution)/shard_map/ppermute | solution.py:23
  244.9 5.8 %collective-permute-start.15 = (bf16[192,3072]{1,0:T(8,128)(2,1)}, bf16[192,3072]{1,0:T(8,128)(2,1)}, u32[]{:S(2)}, u32[]{:S(2)}) collective-permute-start(bf16[192,3072]{1,0:T(8,128)(2,1)} %collective-permute-done.8.refs_3_), channel_id=1, source_target_pairs={{0,1},{1,0},{2,3},{3,2},{4,5},{5,4},{6,7},{7,6},{8,9},{9,8},{10,11... | collective-permute-start | bytes 3538952 | tf_op jit(solution)/shard_map/ppermute | solution.py:23

commit v4 on v3

--- a/solution.py
+++ b/solution.py
@@ -60,13 +60,13 @@
 
 def join(*arrays):
     rows = sum(array.shape[0] for array in arrays)
-    hbm = pl.BlockSpec(memory_space=pltpu.HBM)
     return pl.pallas_call(
         functools.partial(join_kernel, len(arrays)),
-        in_specs=[hbm] * len(arrays),
-        out_specs=hbm,
+        in_specs=[pl.BlockSpec(memory_space=pl.ANY)] * len(arrays),
+        out_specs=pl.BlockSpec(memory_space=pltpu.VMEM),
         out_shape=jax.ShapeDtypeStruct((rows, arrays[0].shape[1]), arrays[0].dtype),
         scratch_shapes=[pltpu.SemaphoreType.DMA((len(arrays),))],
+        compiler_params=pltpu.CompilerParams(vmem_limit_bytes=VMEM_BYTES),
         cost_estimate=pl.CostEstimate(flops=0, bytes_accessed=0, transcendentals=0),
     )(*arrays)
 
@@ -331,7 +331,7 @@
     kv_up = column_shift(kv, 1)
     kv_down = column_shift(kv, -1)
     if cube:
-        wz = swap_bit(out_weight, 4)
+        wz = swap_bit(after(out_weight, cube.c0), 4)
     sent = []
     for parity in phases:
         pairs = row_pairs(parity)
@@ -339,12 +339,10 @@
         second = query_rows[:, chunk:]
         if cube:
             cz = swap_bit(cube.c0, 4)
-            second = after(second, wz, cube.c0)
+            far = join(cube.c0, cz)
+            cy = swap_bit(far, 2)
+            second = after(second, first, far)
         sent.append([first, lax.ppermute(second, "seq", pairs)])
-    if cube:
-        far = join(cube.c0, cz)
-        cy = swap_bit(far, 2)
-        sent[0][0] = after(sent[0][0], far)
     common = (key_rows, value_rows, kv_up, kv_down)
     others = []
     for parity, asked in zip(phases, sent):

time: 260 us -> 125 us (0.48)
  Pallas kernels: 176 us -> 41.8 us
  starting transfers between devices: 44.5 us -> 36 us
  waiting for transfers between devices: 29.5 us -> 37.1 us
    pallas_call x4, Pallas kernels: 141 us -> 7.73 us  [join(): pl.pallas_call(functools.partial(join_kernel, len(arrays)), in_specs=[pl....]
    ppermute x1, waiting for transfers between devices: 0.01 us -> 6.92 us  [body(): sent.append([first, lax.ppermute(second, 'seq', pairs)])]
    ppermute x9, starting transfers between devices: 32.7 us -> 27.5 us  [swap_bit(): return lax.ppermute(value, 'seq', [(s, s ^ bit) for s in range(count)])]
    unnamed x27 -> x25, local copies, waits for them, and re-layouts: 5.72 us -> 4.59 us
  transfers between devices with their start and end apart: 16 -> 16, of which waited for: 6 -> 5; matrix products, arithmetic and copies ran while one was open for 1% -> 3% of each run, Pallas kernels for 46% -> 26%
where the time goes in v4:
time: 125 us; the launch traced here: 123 us
  Pallas kernels  41.8 us (33%)
  waiting for transfers between devices  37.1 us (30%)
  starting transfers between devices  36 us (29%)
  local copies, waits for them, and re-layouts  7.52 us (6%)
    ppermute x9, starting transfers between devices, swap_bit(): return lax.ppermute(value, 'seq', [(s, s ^ bit) for s in range(count)])  27.5 us
    ppermute x9, waiting for transfers between devices, swap_bit(): return lax.ppermute(value, 'seq', [(s, s ^ bit) for s in range(count)])  26.7 us
    pallas_call x4, Pallas kernels, attend(): pl.pallas_call(functools.partial(attend_kernel, rows, per_block), grid=(h...  23.2 us
    pallas_call x1, Pallas kernels, project(): pl.pallas_call(functools.partial(project_kernel, plan), in_specs=[pl.Bloc...  8.55 us
    pallas_call x4, Pallas kernels, join(): pl.pallas_call(functools.partial(join_kernel, len(arrays)), in_specs=[pl....  7.73 us
    ppermute x1, waiting for transfers between devices, body(): sent.append([first, lax.ppermute(second, 'seq', pairs)])  6.92 us
    unnamed x25, local copies, waits for them, and re-layouts  4.59 us
    ppermute x2, starting transfers between devices, column_shift(): return lax.ppermute(value, 'seq', pairs)  4.42 us
  transfers between devices with their start and end apart: 16, of which 5 were waited for; matrix products, arithmetic and copies ran while one was open for 3% of the time, Pallas kernels for 26%

profile of v4, /device:TPU:0, one launch (start us, length us, event | category | flops | bytes accessed | tf_op | source)
XLA Modules:
  0.0 123.5 jit_solution(13965289283956480513)
XLA Ops:
  0.0 1.1 copy-done.3
  1.1 1.1 copy-done.5
  2.3 1.3 %shard_map.55 = bf16[512,1536]{1,0:T(8,128)(2,1)} custom-call(bf16[256,1536]{1,0:T(8,128)(2,1)S(1)} %copy-done.3, bf16[256,1536]{1,0:T(8,128)(2,1)S(1)} %copy-done.5), custom_call_target="tpu_custom_call" | custom-call | tf_op jit(solution)/shard_map/pallas_call | solution.py:63
  3.5 0.0 copy-start.11
  3.6 1.3 %collective-permute-start.4 = (bf16[2,256,1536]{2,1,0:T(8,128)(2,1)}, bf16[2,256,1536]{2,1,0:T(8,128)(2,1)S(1)}, u32[]{:S(2)}, u32[]{:S(2)}) collective-permute-start(bf16[2,256,1536]{2,1,0:T(8,128)(2,1)} %bitcast), channel_id=1, source_target_pairs={{1,0},{2,1},{3,2},{4,3},{5,4},{6,5},{7,6},{9,8},{10,9},{11,10},{12... | collective-permute-start | bytes 4718600 | tf_op jit(solution)/shard_map/ppermute | solution.py:33
  4.9 3.1 %collective-permute-start.3 = (bf16[2,256,1536]{2,1,0:T(8,128)(2,1)}, bf16[2,256,1536]{2,1,0:T(8,128)(2,1)S(1)}, u32[]{:S(2)}, u32[]{:S(2)}) collective-permute-start(bf16[2,256,1536]{2,1,0:T(8,128)(2,1)} %bitcast), channel_id=1, source_target_pairs={{0,1},{1,2},{2,3},{3,4},{4,5},{5,6},{6,7},{8,9},{9,10},{10,11},{11... | collective-permute-start | bytes 4718600 | tf_op jit(solution)/shard_map/ppermute | solution.py:33
  8.0 1.0 constant_dynamic-slice_fusion
  9.0 4.1 %collective-permute-start = (bf16[48,3072]{1,0:T(8,128)(2,1)S(1)}, bf16[48,3072]{1,0:T(8,128)(2,1)S(1)}, u32[]{:S(2)}, u32[]{:S(2)}) collective-permute-start(bf16[48,3072]{1,0:T(8,128)(2,1)S(1)} %constant_dynamic-slice_fusion), channel_id=1, source_target_pairs={{0,8},{1,9},{2,10},{3,11},{4,12},{5,13},{6,14},{7,15},{8,0},{9,1},... | collective-permute-start | bytes 884744 | tf_op jit(solution)/shard_map/ppermute | solution.py:23
  13.1 1.9 %fusion = (bf16[256,768]{1,0:T(8,128)(2,1)}, bf16[256,768]{1,0:T(8,128)(2,1)S(1)}) fusion(bf16[256,1536]{1,0:T(8,128)(2,1)} %q_ref.1), kind=kLoop, calls=%fused_computation.3 | loop fusion | bytes 1572864 | tf_op jit(solution)/shard_map/slice | solution.py:339
  15.1 0.6 copy-done.9
  15.6 0.8 pad_maximum_fusion
  16.4 0.0 collective-permute-start.2
  16.4 8.8 %collective-permute-done.refs_0_ = bf16[48,3072]{1,0:T(8,128)(2,1)S(1)} collective-permute-done((bf16[48,3072]{1,0:T(8,128)(2,1)S(1)}, bf16[48,3072]{1,0:T(8,128)(2,1)S(1)}, u32[]{:S(2)}, u32[]{:S(2)}) %collective-permute-start) | collective-permute-done | bytes 294944 | tf_op jit(solution)/shard_map/ppermute | solution.py:23
  25.2 16.1 %collective-permute-start.6 = (bf16[48,3072]{1,0:T(8,128)(2,1)S(1)}, bf16[48,3072]{1,0:T(8,128)(2,1)}, u32[]{:S(2)}, u32[]{:S(2)}) collective-permute-start(bf16[48,3072]{1,0:T(8,128)(2,1)S(1)} %collective-permute-done.refs_0_), channel_id=1, source_target_pairs={{0,4},{1,5},{2,6},{3,7},{4,0},{5,1},{6,2},{7,3},{8,12},{9,13},{10,... | collective-permute-start | bytes 884744 | tf_op jit(solution)/shard_map/ppermute | solution.py:23
  41.4 0.0 collective-permute-start.1
  41.4 13.3 %collective-permute-done.6.refs_1_ = bf16[48,3072]{1,0:T(8,128)(2,1)} collective-permute-done((bf16[48,3072]{1,0:T(8,128)(2,1)S(1)}, bf16[48,3072]{1,0:T(8,128)(2,1)}, u32[]{:S(2)}, u32[]{:S(2)}) %collective-permute-start.6) | collective-permute-done | bytes 294944 | tf_op jit(solution)/shard_map/ppermute | solution.py:23
  54.6 1.9 %shard_map.58.refs_0_ = bf16[96,3072]{1,0:T(8,128)(2,1)} custom-call(bf16[48,3072]{1,0:T(8,128)(2,1)S(1)} %collective-permute-done.refs_0_, bf16[48,3072]{1,0:T(8,128)(2,1)} %collective-permute-done.6.refs_1_), custom_call_target="tpu_custom_call" | custom-call | tf_op jit(solution)/shard_map/pallas_call | solution.py:63
  56.5 0.1 collective-permute-start.7
  56.6 0.0 collective-permute-done.2.list_ref.q_ref
  56.6 1.9 %collective-permute-start.9 = (bf16[256,768]{1,0:T(8,128)(2,1)}, bf16[256,768]{1,0:T(8,128)(2,1)}, u32[]{:S(2)}, u32[]{:S(2)}) collective-permute-start(bf16[256,768]{1,0:T(8,128)(2,1)} %get-tuple-element.23), channel_id=1, source_target_pairs={{0,8},{1,9},{2,10},{3,11},{4,12},{5,13},{6,14},{7,15},{8,0},{9,1},... | collective-permute-start | bytes 1179656 | tf_op jit(solution)/shard_map/ppermute | solution.py:345
  58.5 0.0 collective-permute-done.4.kb.vb
  58.5 0.0 copy-start.6
  58.5 1.7 %copy-done.6 = bf16[256,1536]{1,0:T(8,128)(2,1)S(1)} copy-done((bf16[256,1536]{1,0:T(8,128)(2,1)S(1)}, bf16[256,1536]{1,0:T(8,128)(2,1)}, u32[]{:S(2)}) %copy-start.6) | copy-done | bytes 786456
  60.2 6.2 %shard_map.56 = bf16[272,768]{1,0:T(8,128)(2,1)} custom-call(bf16[272,768]{1,0:T(8,128)(2,1)} %collective-permute-done.2.list_ref.q_ref, bf16[272,768]{1,0:T(8,128)(2,1)} %collective-permute-done.2.list_ref.q_ref, bf16[256,1536]{1,0:T(8,128)(2,1)S(1)} %copy-done.4, bf16[2,256,1536]{2,1,0:T(8,128)(2,1)S(1)} %collective-permute-done.3.ka.va, ...), custom_call_target="tpu_custom_call" | custom-call | flops 999999995904 | tf_op jit(solution)/shard_map/pallas_call | solution.py:139
  66.4 1.1 collective-permute-start.11
  67.5 4.6 %collective-permute-done.7.refs_1_ = bf16[96,3072]{1,0:T(8,128)(2,1)} collective-permute-done((bf16[96,3072]{1,0:T(8,128)(2,1)}, bf16[96,3072]{1,0:T(8,128)(2,1)}, u32[]{:S(2)}, u32[]{:S(2)}) %collective-permute-start.7) | collective-permute-done | bytes 589856 | tf_op jit(solution)/shard_map/ppermute | solution.py:23
  72.1 2.3 %shard_map.59.refs_2_ = bf16[192,3072]{1,0:T(8,128)(2,1)} custom-call(bf16[96,3072]{1,0:T(8,128)(2,1)} %shard_map.58.refs_0_, bf16[96,3072]{1,0:T(8,128)(2,1)} %collective-permute-done.7.refs_1_), custom_call_target="tpu_custom_call" | custom-call | tf_op jit(solution)/shard_map/pallas_call | solution.py:63
  74.4 0.0 copy-start.7
  74.4 2.3 %shard_map.57.refs_0_ = bf16[192,3072]{1,0:T(8,128)(2,1)} custom-call(bf16[96,3072]{1,0:T(8,128)(2,1)S(1)} %copy-done.8, bf16[96,3072]{1,0:T(8,128)(2,1)} %collective-permute-done.1.refs_1_), custom_call_target="tpu_custom_call" | custom-call | tf_op jit(solution)/shard_map/pallas_call | solution.py:63
  76.8 0.1 collective-permute-start.5
  76.8 1.1 collective-permute-start.8
  78.0 6.9 %collective-permute-done.9.q_ref = bf16[256,768]{1,0:T(8,128)(2,1)} collective-permute-done((bf16[256,768]{1,0:T(8,128)(2,1)}, bf16[256,768]{1,0:T(8,128)(2,1)}, u32[]{:S(2)}, u32[]{:S(2)}) %collective-permute-start.9) | collective-permute-done | bytes 393248 | tf_op jit(solution)/shard_map/ppermute | solution.py:345
  84.9 6.3 %shard_map.60 = bf16[272,768]{1,0:T(8,128)(2,1)} custom-call(bf16[272,768]{1,0:T(8,128)(2,1)} %collective-permute-done.2.list_ref.q_ref, bf16[256,768]{1,0:T(8,128)(2,1)} %collective-permute-done.9.q_ref, bf16[256,1536]{1,0:T(8,128)(2,1)S(1)} %copy-done.4, bf16[2,256,1536]{2,1,0:T(8,128)(2,1)S(1)} %collective-permute-done.3.ka.va, ...), custom_call_target="tpu_custom_call" | custom-call | flops 999999995904 | tf_op jit(solution)/shard_map/pallas_call | solution.py:139
  91.2 0.0 collective-permute-start.12
  91.3 9.1 %shard_map.61.refs_0_ = f32[272,1280]{1,0:T(8,128)S(1)} custom-call(bf16[16,128]{1,0:T(8,128)(2,1)S(1)} %copy-done.10, bf16[256,1536]{1,0:T(8,128)(2,1)S(1)} %copy-done.2, bf16[256,1536]{1,0:T(8,128)(2,1)S(1)} %copy-done.4, bf16[2,256,1536]{2,1,0:T(8,128)(2,1)S(1)} %collective-permute-done.3.ka.va, bf16[2,256,1536]{2,1,0:T(8,128)(2,1)} %copy-done, ...), custom_call_target="tpu_custom_call" | custom-call | tf_op jit(solution)/shard_map/pallas_call | solution.py:139
  100.4 4.9 %collective-permute-start.10 = (bf16[192,3072]{1,0:T(8,128)(2,1)}, bf16[192,3072]{1,0:T(8,128)(2,1)}, u32[]{:S(2)}, u32[]{:S(2)}) collective-permute-start(bf16[192,3072]{1,0:T(8,128)(2,1)} %shard_map.57.refs_0_), channel_id=1, source_target_pairs={{0,1},{1,0},{2,3},{3,2},{4,5},{5,4},{6,7},{7,6},{8,9},{9,8},{10,11... | collective-permute-start | bytes 3538952 | tf_op jit(solution)/shard_map/ppermute | solution.py:23
  105.3 0.0 collective-permute-done.11.refs_2_
  105.3 1.6 %collective-permute-start.14 = (bf16[192,3072]{1,0:T(8,128)(2,1)}, bf16[192,3072]{1,0:T(8,128)(2,1)}, u32[]{:S(2)}, u32[]{:S(2)}) collective-permute-start(bf16[192,3072]{1,0:T(8,128)(2,1)} %shard_map.59.refs_2_), channel_id=1, source_target_pairs={{0,1},{1,0},{2,3},{3,2},{4,5},{5,4},{6,7},{7,6},{8,9},{9,8},{10,11... | collective-permute-start | bytes 3538952 | tf_op jit(solution)/shard_map/ppermute | solution.py:23
  107.0 0.0 collective-permute-done.8.refs_3_
  107.0 0.1 collective-permute-start.13
  107.0 0.4 collective-permute-start.15
  107.5 1.6 %shard_map.62.refs_1_ = f32[272,256]{1,0:T(8,128)S(1)} custom-call(bf16[16,128]{1,0:T(8,128)(2,1)S(1)} %copy-done.10, bf16[256,1536]{1,0:T(8,128)(2,1)S(1)} %copy-done.2, bf16[256,1536]{1,0:T(8,128)(2,1)S(1)} %copy-done.4, bf16[2,256,1536]{2,1,0:T(8,128)(2,1)S(1)} %collective-permute-done.3.ka.va, bf16[2,256,1536]{2,1,0:T(8,128)(2,1)S(1)} %copy-done.1, ...), custom_call_target="tpu_custom_call" | custom-call | flops 999999995904 | tf_op jit(solution)/shard_map/pallas_call | solution.py:139
  109.0 3.5 %collective-permute-done.12.refs_3_ = bf16[272,768]{1,0:T(8,128)(2,1)} collective-permute-done((bf16[272,768]{1,0:T(8,128)(2,1)}, bf16[272,768]{1,0:T(8,128)(2,1)}, u32[]{:S(2)}, u32[]{:S(2)}) %collective-permute-start.12) | collective-permute-done | bytes 417824 | tf_op jit(solution)/shard_map/ppermute | solution.py:359
  112.5 2.3 %shard_map.63.refs_8_ = bf16[256,1536]{1,0:T(8,128)(2,1)S(1)} custom-call(s32[1]{0:T(128)} %bitcast.1.partner_ref, f32[272,1280]{1,0:T(8,128)S(1)} %shard_map.61.refs_0_, f32[272,256]{1,0:T(8,128)S(1)} %shard_map.62.refs_1_, bf16[272,768]{1,0:T(8,128)(2,1)} %collective-permute-done.11.refs_2_, bf16[272,768]{1,0:T(8,128)(2,1)} %collective-permute-done.12.refs_3_), custom_call_target="tpu_custom_call" | custom-call | flops 999999995904 | tf_op jit(solution)/shard_map/pallas_call | solution.py:213
  114.9 0.0 collective-permute-done.10.refs_4_
  114.9 0.0 collective-permute-done.14.refs_6_
  114.9 0.0 collective-permute-done.15.refs_7_
  114.9 8.6 %shard_map.64 = bf16[256,3072]{1,0:T(8,128)(2,1)} custom-call(bf16[192,3072]{1,0:T(8,128)(2,1)} %shard_map.57.refs_0_, bf16[192,3072]{1,0:T(8,128)(2,1)} %collective-permute-done.5.refs_1_, bf16[192,3072]{1,0:T(8,128)(2,1)} %shard_map.59.refs_2_, bf16[192,3072]{1,0:T(8,128)(2,1)} %collective-permute-done.8.refs_3_, ...), custom_call_target="tpu_custom_call" | custom-call | tf_op jit(solution)/shard_map/pallas_call | solution.py:256
  (25 shorter events, 0.1 us)
Async XLA Ops:
  0.0 1.1 copy-start.3
  1.1 1.1 copy-start.5
  3.5 11.5 %copy-start.11 = (s32[2,27]{1,0:T(2,128)S(1)}, s32[2,27]{1,0:T(2,128)}, u32[]{:S(2)}) copy-start(s32[2,27]{1,0:T(2,128)} %param.8) | copy-start | bytes 652
  3.6 54.9 %collective-permute-start.4 = (bf16[2,256,1536]{2,1,0:T(8,128)(2,1)}, bf16[2,256,1536]{2,1,0:T(8,128)(2,1)S(1)}, u32[]{:S(2)}, u32[]{:S(2)}) collective-permute-start(bf16[2,256,1536]{2,1,0:T(8,128)(2,1)} %bitcast), channel_id=1, source_target_pairs={{1,0},{2,1},{3,2},{4,3},{5,4},{6,5},{7,6},{9,8},{10,9},{11,10},{12... | collective-permute-start | bytes 4718600 | tf_op jit(solution)/shard_map/ppermute | solution.py:33
  4.9 53.6 %collective-permute-start.3 = (bf16[2,256,1536]{2,1,0:T(8,128)(2,1)}, bf16[2,256,1536]{2,1,0:T(8,128)(2,1)S(1)}, u32[]{:S(2)}, u32[]{:S(2)}) collective-permute-start(bf16[2,256,1536]{2,1,0:T(8,128)(2,1)} %bitcast), channel_id=1, source_target_pairs={{0,1},{1,2},{2,3},{3,4},{4,5},{5,6},{6,7},{8,9},{9,10},{10,11},{11... | collective-permute-start | bytes 4718600 | tf_op jit(solution)/shard_map/ppermute | solution.py:33
  9.0 16.3 %collective-permute-start = (bf16[48,3072]{1,0:T(8,128)(2,1)S(1)}, bf16[48,3072]{1,0:T(8,128)(2,1)S(1)}, u32[]{:S(2)}, u32[]{:S(2)}) collective-permute-start(bf16[48,3072]{1,0:T(8,128)(2,1)S(1)} %constant_dynamic-slice_fusion), channel_id=1, source_target_pairs={{0,8},{1,9},{2,10},{3,11},{4,12},{5,13},{6,14},{7,15},{8,0},{9,1},... | collective-permute-start | bytes 884744 | tf_op jit(solution)/shard_map/ppermute | solution.py:23
  15.0 0.6 copy-start.9
  16.4 40.2 %collective-permute-start.2 = (bf16[272,768]{1,0:T(8,128)(2,1)}, bf16[272,768]{1,0:T(8,128)(2,1)}, u32[]{:S(2)}, u32[]{:S(2)}) collective-permute-start(bf16[272,768]{1,0:T(8,128)(2,1)} %pad_maximum_fusion), channel_id=1, source_target_pairs={{0,8},{1,9},{2,10},{3,11},{4,12},{5,13},{6,14},{7,15},{8,0},{9,1},... | collective-permute-start | bytes 1253384 | tf_op jit(solution)/shard_map/ppermute | solution.py:338
  25.2 29.4 %collective-permute-start.6 = (bf16[48,3072]{1,0:T(8,128)(2,1)S(1)}, bf16[48,3072]{1,0:T(8,128)(2,1)}, u32[]{:S(2)}, u32[]{:S(2)}) collective-permute-start(bf16[48,3072]{1,0:T(8,128)(2,1)S(1)} %collective-permute-done.refs_0_), channel_id=1, source_target_pairs={{0,4},{1,5},{2,6},{3,7},{4,0},{5,1},{6,2},{7,3},{8,12},{9,13},{10,... | collective-permute-start | bytes 884744 | tf_op jit(solution)/shard_map/ppermute | solution.py:23
  41.3 17.1 %copy-start.4 = (bf16[256,1536]{1,0:T(8,128)(2,1)S(1)}, bf16[256,1536]{1,0:T(8,128)(2,1)}, u32[]{:S(2)}) copy-start(bf16[256,1536]{1,0:T(8,128)(2,1)} %k0.7) | copy-start | bytes 2359300
  41.4 33.1 %collective-permute-start.1 = (bf16[96,3072]{1,0:T(8,128)(2,1)}, bf16[96,3072]{1,0:T(8,128)(2,1)}, u32[]{:S(2)}, u32[]{:S(2)}) collective-permute-start(bf16[96,3072]{1,0:T(8,128)(2,1)} %refs_0_.3), channel_id=1, source_target_pairs={{0,4},{1,5},{2,6},{3,7},{4,0},{5,1},{6,2},{7,3},{8,12},{9,13},{10,... | collective-permute-start | bytes 1769480 | tf_op jit(solution)/shard_map/ppermute | solution.py:23
  56.5 15.6 %collective-permute-start.7 = (bf16[96,3072]{1,0:T(8,128)(2,1)}, bf16[96,3072]{1,0:T(8,128)(2,1)}, u32[]{:S(2)}, u32[]{:S(2)}) collective-permute-start(bf16[96,3072]{1,0:T(8,128)(2,1)} %shard_map.58.refs_0_), channel_id=1, source_target_pairs={{0,2},{1,3},{2,0},{3,1},{4,6},{5,7},{6,4},{7,5},{8,10},{9,11},{10,... | collective-permute-start | bytes 1769480 | tf_op jit(solution)/shard_map/ppermute | solution.py:23
  56.6 28.3 %collective-permute-start.9 = (bf16[256,768]{1,0:T(8,128)(2,1)}, bf16[256,768]{1,0:T(8,128)(2,1)}, u32[]{:S(2)}, u32[]{:S(2)}) collective-permute-start(bf16[256,768]{1,0:T(8,128)(2,1)} %get-tuple-element.23), channel_id=1, source_target_pairs={{0,8},{1,9},{2,10},{3,11},{4,12},{5,13},{6,14},{7,15},{8,0},{9,1},... | collective-permute-start | bytes 1179656 | tf_op jit(solution)/shard_map/ppermute | solution.py:345
  58.5 26.5 %copy-start = (bf16[2,256,1536]{2,1,0:T(8,128)(2,1)}, bf16[2,256,1536]{2,1,0:T(8,128)(2,1)S(1)}, u32[]{:S(2)}) copy-start(bf16[2,256,1536]{2,1,0:T(8,128)(2,1)S(1)} %collective-permute-done.4.kb.vb) | copy-start | bytes 4718596
  58.5 1.7 %copy-start.6 = (bf16[256,1536]{1,0:T(8,128)(2,1)S(1)}, bf16[256,1536]{1,0:T(8,128)(2,1)}, u32[]{:S(2)}) copy-start(bf16[256,1536]{1,0:T(8,128)(2,1)} %v0.7) | copy-start | bytes 2359300
  66.4 8.0 %copy-start.8 = (bf16[96,3072]{1,0:T(8,128)(2,1)S(1)}, bf16[96,3072]{1,0:T(8,128)(2,1)}, u32[]{:S(2)}) copy-start(bf16[96,3072]{1,0:T(8,128)(2,1)} %refs_0_.3) | copy-start | bytes 1769476
  66.4 38.9 %collective-permute-start.11 = (bf16[272,768]{1,0:T(8,128)(2,1)}, bf16[272,768]{1,0:T(8,128)(2,1)}, u32[]{:S(2)}, u32[]{:S(2)}) collective-permute-start(bf16[272,768]{1,0:T(8,128)(2,1)} %shard_map.56), channel_id=1, source_target_pairs={{0,8},{1,9},{2,10},{3,11},{4,12},{5,13},{6,14},{7,15},{8,0},{9,1},... | collective-permute-start | bytes 1253384 | tf_op jit(solution)/shard_map/ppermute | solution.py:359
  74.4 10.5 %copy-start.7 = (bf16[256,1536]{1,0:T(8,128)(2,1)S(1)}, bf16[256,1536]{1,0:T(8,128)(2,1)}, u32[]{:S(2)}) copy-start(bf16[256,1536]{1,0:T(8,128)(2,1)} %v0.7) | copy-start | bytes 2359300
  76.8 30.2 %collective-permute-start.5 = (bf16[192,3072]{1,0:T(8,128)(2,1)}, bf16[192,3072]{1,0:T(8,128)(2,1)}, u32[]{:S(2)}, u32[]{:S(2)}) collective-permute-start(bf16[192,3072]{1,0:T(8,128)(2,1)} %shard_map.57.refs_0_), channel_id=1, source_target_pairs={{0,2},{1,3},{2,0},{3,1},{4,6},{5,7},{6,4},{7,5},{8,10},{9,11},{10,... | collective-permute-start | bytes 3538952 | tf_op jit(solution)/shard_map/ppermute | solution.py:23
  76.8 30.1 %collective-permute-start.8 = (bf16[192,3072]{1,0:T(8,128)(2,1)}, bf16[192,3072]{1,0:T(8,128)(2,1)}, u32[]{:S(2)}, u32[]{:S(2)}) collective-permute-start(bf16[192,3072]{1,0:T(8,128)(2,1)} %shard_map.59.refs_2_), channel_id=1, source_target_pairs={{0,16},{16,0},{1,17},{17,1},{2,18},{18,2},{3,19},{19,3},{4,20},{20... | collective-permute-start | bytes 3538952 | tf_op jit(solution)/shard_map/ppermute | solution.py:27
  84.9 6.3 %copy-start.2 = (bf16[256,1536]{1,0:T(8,128)(2,1)S(1)}, bf16[256,1536]{1,0:T(8,128)(2,1)}, u32[]{:S(2)}) copy-start(bf16[256,1536]{1,0:T(8,128)(2,1)} %q_ref.1) | copy-start | bytes 2359300
  84.9 6.3 %copy-start.10 = (bf16[16,128]{1,0:T(8,128)(2,1)S(1)}, bf16[16,128]{1,0:T(8,128)(2,1)}, u32[]{:S(2)}) copy-start(bf16[16,128]{1,0:T(8,128)(2,1)} %copy-done.9) | copy-start | bytes 12292
  91.2 16.2 %copy-start.1 = (bf16[2,256,1536]{2,1,0:T(8,128)(2,1)S(1)}, bf16[2,256,1536]{2,1,0:T(8,128)(2,1)}, u32[]{:S(2)}) copy-start(bf16[2,256,1536]{2,1,0:T(8,128)(2,1)} %copy-done) | copy-start | bytes 4718596
  91.2 21.3 %collective-permute-start.12 = (bf16[272,768]{1,0:T(8,128)(2,1)}, bf16[272,768]{1,0:T(8,128)(2,1)}, u32[]{:S(2)}, u32[]{:S(2)}) collective-permute-start(bf16[272,768]{1,0:T(8,128)(2,1)} %shard_map.60), channel_id=1, source_target_pairs={{0,8},{1,9},{2,10},{3,11},{4,12},{5,13},{6,14},{7,15},{8,0},{9,1},... | collective-permute-start | bytes 1253384 | tf_op jit(solution)/shard_map/ppermute | solution.py:359
  100.4 14.5 %collective-permute-start.10 = (bf16[192,3072]{1,0:T(8,128)(2,1)}, bf16[192,3072]{1,0:T(8,128)(2,1)}, u32[]{:S(2)}, u32[]{:S(2)}) collective-permute-start(bf16[192,3072]{1,0:T(8,128)(2,1)} %shard_map.57.refs_0_), channel_id=1, source_target_pairs={{0,1},{1,0},{2,3},{3,2},{4,5},{5,4},{6,7},{7,6},{8,9},{9,8},{10,11... | collective-permute-start | bytes 3538952 | tf_op jit(solution)/shard_map/ppermute | solution.py:23
  105.3 9.6 %collective-permute-start.14 = (bf16[192,3072]{1,0:T(8,128)(2,1)}, bf16[192,3072]{1,0:T(8,128)(2,1)}, u32[]{:S(2)}, u32[]{:S(2)}) collective-permute-start(bf16[192,3072]{1,0:T(8,128)(2,1)} %shard_map.59.refs_2_), channel_id=1, source_target_pairs={{0,1},{1,0},{2,3},{3,2},{4,5},{5,4},{6,7},{7,6},{8,9},{9,8},{10,11... | collective-permute-start | bytes 3538952 | tf_op jit(solution)/shard_map/ppermute | solution.py:23
  107.0 7.9 %collective-permute-start.13 = (bf16[192,3072]{1,0:T(8,128)(2,1)}, bf16[192,3072]{1,0:T(8,128)(2,1)}, u32[]{:S(2)}, u32[]{:S(2)}) collective-permute-start(bf16[192,3072]{1,0:T(8,128)(2,1)} %collective-permute-done.5.refs_1_), channel_id=1, source_target_pairs={{0,1},{1,0},{2,3},{3,2},{4,5},{5,4},{6,7},{7,6},{8,9},{9,8},{10,11... | collective-permute-start | bytes 3538952 | tf_op jit(solution)/shard_map/ppermute | solution.py:23
  107.0 7.9 %collective-permute-start.15 = (bf16[192,3072]{1,0:T(8,128)(2,1)}, bf16[192,3072]{1,0:T(8,128)(2,1)}, u32[]{:S(2)}, u32[]{:S(2)}) collective-permute-start(bf16[192,3072]{1,0:T(8,128)(2,1)} %collective-permute-done.8.refs_3_), channel_id=1, source_target_pairs={{0,1},{1,0},{2,3},{3,2},{4,5},{5,4},{6,7},{7,6},{8,9},{9,8},{10,11... | collective-permute-start | bytes 3538952 | tf_op jit(solution)/shard_map/ppermute | solution.py:23

commit v5 on v4

--- a/solution.py
+++ b/solution.py
@@ -58,7 +58,7 @@
         copy.wait()
 
 
-def join(*arrays):
+def join(*arrays, cost=0):
     rows = sum(array.shape[0] for array in arrays)
     return pl.pallas_call(
         functools.partial(join_kernel, len(arrays)),
@@ -67,8 +67,23 @@
         out_shape=jax.ShapeDtypeStruct((rows, arrays[0].shape[1]), arrays[0].dtype),
         scratch_shapes=[pltpu.SemaphoreType.DMA((len(arrays),))],
         compiler_params=pltpu.CompilerParams(vmem_limit_bytes=VMEM_BYTES),
-        cost_estimate=pl.CostEstimate(flops=0, bytes_accessed=0, transcendentals=0),
+        cost_estimate=pl.CostEstimate(flops=cost, bytes_accessed=0, transcendentals=0),
     )(*arrays)
+
+
+def fence_kernel(in_ref, out_ref):
+    out_ref[...] = in_ref[...]
+
+
+def fence(value):
+    vmem = pl.BlockSpec(memory_space=pltpu.VMEM)
+    return pl.pallas_call(
+        fence_kernel,
+        in_specs=[vmem],
+        out_specs=vmem,
+        out_shape=jax.ShapeDtypeStruct(value.shape, value.dtype),
+        cost_estimate=pl.CostEstimate(flops=WEIGHTY, bytes_accessed=0, transcendentals=0),
+    )(value)
 
 
 def attend_kernel(rows, per_block, list_ref, q_ref, k0, ka, kb, v0, va, vb, out_ref):
@@ -278,7 +293,8 @@
 
     def cross(self):
         first = lax.axis_index("group") * self.half
-        self.c0 = swap_bit(lax.dynamic_slice_in_dim(self.near, first, self.half, 0), 8)
+        self.mine = lax.dynamic_slice_in_dim(self.near, first, self.half, 0)
+        self.c0 = swap_bit(self.mine, 8)
 
     def full(self, *bits):
         def at(bit):
@@ -327,21 +343,22 @@
         constant_values=-1,
     )
     asking = jnp.concatenate([query_rows[:, :chunk], jnp.tile(lists, (1, chunk_heads))], axis=0)
-    kv = join(key_rows, value_rows).reshape(2, rows, features)
+    ahead = [asking] + ([cube.mine] if cube else [])
+    kv = join(after(key_rows, *ahead), value_rows, cost=WEIGHTY).reshape(2, rows, features)
     kv_up = column_shift(kv, 1)
     kv_down = column_shift(kv, -1)
-    if cube:
-        wz = swap_bit(after(out_weight, cube.c0), 4)
     sent = []
     for parity in phases:
         pairs = row_pairs(parity)
         first = lax.ppermute(asking, "seq", pairs)
         second = query_rows[:, chunk:]
         if cube:
+            cube.c0 = fence(after(cube.c0, kv))
             cz = swap_bit(cube.c0, 4)
             far = join(cube.c0, cz)
+            wz = swap_bit(after(out_weight, first), 4)
             cy = swap_bit(far, 2)
-            second = after(second, first, far)
+            second = after(second, cube.c0)
         sent.append([first, lax.ppermute(second, "seq", pairs)])
     common = (key_rows, value_rows, kv_up, kv_down)
     others = []

time: 125 us -> 130 us (1.040)
  waiting for transfers between devices: 37.1 us -> 55.5 us
  starting transfers between devices: 36 us -> 21.7 us
  Pallas kernels: 41.8 us -> 44.2 us
    ppermute x9, waiting for transfers between devices: 26.7 us -> 48.9 us  [swap_bit(): return lax.ppermute(value, 'seq', [(s, s ^ bit) for s in range(count)])]
    ppermute x9, starting transfers between devices: 27.5 us -> 9.05 us  [swap_bit(): return lax.ppermute(value, 'seq', [(s, s ^ bit) for s in range(count)])]
    ppermute x1, waiting for transfers between devices: 6.92 us -> 0.01 us  [body(): sent.append([first, lax.ppermute(second, 'seq', pairs)])]
    ppermute x1, waiting for transfers between devices: 0.01 us -> 3.99 us  [body(): first = lax.ppermute(asking, 'seq', pairs)]
    unnamed x25 -> x19, local copies, waits for them, and re-layouts: 4.59 us -> 2.7 us
    pallas_call x0 -> x1, Pallas kernels: none -> 1.69 us  [fence(): pl.pallas_call(fence_kernel, in_specs=[vmem], out_specs=vmem, out_shape=j...]
    pallas_call x4, Pallas kernels: 23.2 us -> 24.8 us  [attend(): pl.pallas_call(functools.partial(attend_kernel, rows, per_block), grid=(h...]
    ppermute x1, starting transfers between devices: 1.86 us -> 3.27 us  [body(): sent.append([first, lax.ppermute(second, 'seq', pairs)])]
  transfers between devices with their start and end apart: 16 -> 16, of which waited for: 5 -> 8; matrix products, arithmetic and copies ran while one was open for 3% -> 3% of each run, Pallas kernels for 26% -> 28%
where the time goes in v5:
time: 130 us
  waiting for transfers between devices  55.5 us (43%)
  Pallas kernels  44.2 us (34%)
  starting transfers between devices  21.7 us (17%)
  local copies, waits for them, and re-layouts  6.47 us (5%)
  other arithmetic  1.46 us (1%)
    ppermute x9, waiting for transfers between devices, swap_bit(): return lax.ppermute(value, 'seq', [(s, s ^ bit) for s in range(count)])  48.9 us
    pallas_call x4, Pallas kernels, attend(): pl.pallas_call(functools.partial(attend_kernel, rows, per_block), grid=(h...  24.8 us
    ppermute x9, starting transfers between devices, swap_bit(): return lax.ppermute(value, 'seq', [(s, s ^ bit) for s in range(count)])  9.05 us
    pallas_call x1, Pallas kernels, project(): pl.pallas_call(functools.partial(project_kernel, plan), in_specs=[pl.Bloc...  8.48 us
    pallas_call x4, Pallas kernels, join(): pl.pallas_call(functools.partial(join_kernel, len(arrays)), in_specs=[pl....  6.89 us
    ppermute x2, starting transfers between devices, column_shift(): return lax.ppermute(value, 'seq', pairs)  5.5 us
    ppermute x1, waiting for transfers between devices, body(): first = lax.ppermute(asking, 'seq', pairs)  3.99 us
    ppermute x1, starting transfers between devices, body(): sent.append([first, lax.ppermute(second, 'seq', pairs)])  3.27 us
  transfers between devices with their start and end apart: 16, of which 8 were waited for; matrix products, arithmetic and copies ran while one was open for 3% of the time, Pallas kernels for 28%

profile of v5, /device:TPU:0, one launch (start us, length us, event | category | flops | bytes accessed | tf_op | source)
XLA Modules:
  0.0 129.5 jit_solution(12953047769052898518)
XLA Ops:
  0.0 1.7 %constant_dynamic-slice_fusion = bf16[48,3072]{1,0:T(8,128)(2,1)} fusion(bf16[96,3072]{1,0:T(8,128)(2,1)} %refs_0_.2, s32[]{:T(128)S(6)} %select_n.18), kind=kLoop, calls=%fused_computation.2 | loop fusion | bytes 589828 | tf_op jit(solution)/shard_map/dynamic_slice | solution.py:296
  1.7 4.0 %collective-permute-start.5 = (bf16[48,3072]{1,0:T(8,128)(2,1)}, bf16[48,3072]{1,0:T(8,128)(2,1)}, u32[]{:S(2)}, u32[]{:S(2)}) collective-permute-start(bf16[48,3072]{1,0:T(8,128)(2,1)} %constant_dynamic-slice_fusion), channel_id=1, source_target_pairs={{0,8},{1,9},{2,10},{3,11},{4,12},{5,13},{6,14},{7,15},{8,0},{9,1},... | collective-permute-start | bytes 884744 | tf_op jit(solution)/shard_map/ppermute | solution.py:23
  5.7 0.7 convert_element_type.6
  6.4 0.6 copy-done.7
  7.0 0.0 copy-start.3
  7.0 2.1 %fusion = (bf16[256,768]{1,0:T(8,128)(2,1)}, bf16[256,768]{1,0:T(8,128)(2,1)S(1)}) fusion(bf16[256,1536]{1,0:T(8,128)(2,1)} %q_ref.1), kind=kLoop, calls=%fused_computation.3 | loop fusion | bytes 1572864 | tf_op jit(solution)/shard_map/slice | solution.py:354
  9.1 0.8 pad_maximum_fusion
  9.9 0.0 collective-permute-start
  9.9 1.3 shard_map.55
  11.2 1.3 collective-permute-start.3
  12.5 4.2 %collective-permute-start.2 = (bf16[2,256,1536]{2,1,0:T(8,128)(2,1)}, bf16[2,256,1536]{2,1,0:T(8,128)(2,1)}, u32[]{:S(2)}, u32[]{:S(2)}) collective-permute-start(bf16[2,256,1536]{2,1,0:T(8,128)(2,1)} %bitcast), channel_id=1, source_target_pairs={{0,1},{1,2},{2,3},{3,4},{4,5},{5,6},{6,7},{8,9},{9,10},{10,11},{11... | collective-permute-start | bytes 4718600 | tf_op jit(solution)/shard_map/ppermute | solution.py:33
  16.7 12.6 %collective-permute-done.5.in_ref = bf16[48,3072]{1,0:T(8,128)(2,1)} collective-permute-done((bf16[48,3072]{1,0:T(8,128)(2,1)}, bf16[48,3072]{1,0:T(8,128)(2,1)}, u32[]{:S(2)}, u32[]{:S(2)}) %collective-permute-start.5) | collective-permute-done | bytes 294944 | tf_op jit(solution)/shard_map/ppermute | solution.py:23
  29.3 1.7 %shard_map.58.refs_0_ = bf16[48,3072]{1,0:T(8,128)(2,1)} custom-call(bf16[48,3072]{1,0:T(8,128)(2,1)} %collective-permute-done.5.in_ref), custom_call_target="tpu_custom_call" | custom-call | flops 999999995904 | tf_op jit(solution)/shard_map/pallas_call | solution.py:80
  31.0 3.3 %collective-permute-start.9 = (bf16[256,768]{1,0:T(8,128)(2,1)}, bf16[256,768]{1,0:T(8,128)(2,1)}, u32[]{:S(2)}, u32[]{:S(2)}) collective-permute-start(bf16[256,768]{1,0:T(8,128)(2,1)} %get-tuple-element.27), channel_id=1, source_target_pairs={{0,8},{1,9},{2,10},{3,11},{4,12},{5,13},{6,14},{7,15},{8,0},{9,1},... | collective-permute-start | bytes 1179656 | tf_op jit(solution)/shard_map/ppermute | solution.py:362
  34.2 4.0 %collective-permute-done.list_ref.q_ref = bf16[272,768]{1,0:T(8,128)(2,1)} collective-permute-done((bf16[272,768]{1,0:T(8,128)(2,1)}, bf16[272,768]{1,0:T(8,128)(2,1)}, u32[]{:S(2)}, u32[]{:S(2)}) %collective-permute-start) | collective-permute-done | bytes 417824 | tf_op jit(solution)/shard_map/ppermute | solution.py:353
  38.2 0.0 collective-permute-start.1
  38.2 30.9 %collective-permute-done.6.refs_1_ = bf16[48,3072]{1,0:T(8,128)(2,1)S(1)} collective-permute-done((bf16[48,3072]{1,0:T(8,128)(2,1)}, bf16[48,3072]{1,0:T(8,128)(2,1)S(1)}, u32[]{:S(2)}, u32[]{:S(2)}) %collective-permute-start.6) | collective-permute-done | bytes 294944 | tf_op jit(solution)/shard_map/ppermute | solution.py:23
  69.1 1.0 copy-done.6
  70.0 1.0 shard_map.59.refs_0_
  71.0 0.1 collective-permute-start.7
  71.1 0.0 collective-permute-done.3.kb.vb
  71.1 0.0 collective-permute-done.2.ka.va
  71.1 0.0 copy-start.4
  71.1 1.1 copy-done.4
  72.3 6.5 %shard_map.56 = bf16[272,768]{1,0:T(8,128)(2,1)} custom-call(bf16[272,768]{1,0:T(8,128)(2,1)} %collective-permute-done.list_ref.q_ref, bf16[272,768]{1,0:T(8,128)(2,1)} %collective-permute-done.list_ref.q_ref, bf16[256,1536]{1,0:T(8,128)(2,1)S(1)} %copy-done.2, bf16[2,256,1536]{2,1,0:T(8,128)(2,1)} %collective-permute-done.2.ka.va, ...), custom_call_target="tpu_custom_call" | custom-call | flops 999999995904 | tf_op jit(solution)/shard_map/pallas_call | solution.py:154
  78.7 0.0 collective-permute-start.11
  78.7 2.5 %collective-permute-done.7.refs_1_ = bf16[96,3072]{1,0:T(8,128)(2,1)} collective-permute-done((bf16[96,3072]{1,0:T(8,128)(2,1)}, bf16[96,3072]{1,0:T(8,128)(2,1)}, u32[]{:S(2)}, u32[]{:S(2)}) %collective-permute-start.7) | collective-permute-done | bytes 589856 | tf_op jit(solution)/shard_map/ppermute | solution.py:23
  81.3 2.3 %shard_map.60.refs_2_ = bf16[192,3072]{1,0:T(8,128)(2,1)} custom-call(bf16[96,3072]{1,0:T(8,128)(2,1)} %shard_map.59.refs_0_, bf16[96,3072]{1,0:T(8,128)(2,1)} %collective-permute-done.7.refs_1_), custom_call_target="tpu_custom_call" | custom-call | tf_op jit(solution)/shard_map/pallas_call | solution.py:63
  83.5 0.0 copy-start.5
  83.6 0.0 collective-permute-done.1.refs_1_
  83.6 2.4 %shard_map.57.refs_0_ = bf16[192,3072]{1,0:T(8,128)(2,1)} custom-call(bf16[96,3072]{1,0:T(8,128)(2,1)} %refs_0_.2, bf16[96,3072]{1,0:T(8,128)(2,1)} %collective-permute-done.1.refs_1_), custom_call_target="tpu_custom_call" | custom-call | tf_op jit(solution)/shard_map/pallas_call | solution.py:63
  86.0 0.1 collective-permute-start.4
  86.0 1.6 %collective-permute-start.8 = (bf16[192,3072]{1,0:T(8,128)(2,1)}, bf16[192,3072]{1,0:T(8,128)(2,1)}, u32[]{:S(2)}, u32[]{:S(2)}) collective-permute-start(bf16[192,3072]{1,0:T(8,128)(2,1)} %shard_map.60.refs_2_), channel_id=1, source_target_pairs={{0,16},{16,0},{1,17},{17,1},{2,18},{18,2},{3,19},{19,3},{4,20},{20... | collective-permute-start | bytes 3538952 | tf_op jit(solution)/shard_map/ppermute | solution.py:27
  87.7 6.6 %shard_map.61 = bf16[272,768]{1,0:T(8,128)(2,1)} custom-call(bf16[272,768]{1,0:T(8,128)(2,1)} %collective-permute-done.list_ref.q_ref, bf16[256,768]{1,0:T(8,128)(2,1)} %collective-permute-done.9.q_ref, bf16[256,1536]{1,0:T(8,128)(2,1)S(1)} %copy-done.2, bf16[2,256,1536]{2,1,0:T(8,128)(2,1)} %collective-permute-done.2.ka.va, ...), custom_call_target="tpu_custom_call" | custom-call | flops 999999995904 | tf_op jit(solution)/shard_map/pallas_call | solution.py:154
  94.2 2.3 %collective-permute-start.12 = (bf16[272,768]{1,0:T(8,128)(2,1)}, bf16[272,768]{1,0:T(8,128)(2,1)}, u32[]{:S(2)}, u32[]{:S(2)}) collective-permute-start(bf16[272,768]{1,0:T(8,128)(2,1)} %shard_map.61), channel_id=1, source_target_pairs={{0,8},{1,9},{2,10},{3,11},{4,12},{5,13},{6,14},{7,15},{8,0},{9,1},... | collective-permute-start | bytes 1253384 | tf_op jit(solution)/shard_map/ppermute | solution.py:376
  96.5 9.1 %shard_map.62.refs_0_ = f32[272,1280]{1,0:T(8,128)S(1)} custom-call(bf16[16,128]{1,0:T(8,128)(2,1)S(1)} %copy-done.8, bf16[256,1536]{1,0:T(8,128)(2,1)S(1)} %copy-done, bf16[256,1536]{1,0:T(8,128)(2,1)S(1)} %copy-done.2, bf16[2,256,1536]{2,1,0:T(8,128)(2,1)} %collective-permute-done.2.ka.va, bf16[2,256,1536]{2,1,0:T(8,128)(2,1)} %collective-permute-done.3.kb.vb, ...), custom_call_target="tpu_custom_call" | custom-call | tf_op jit(solution)/shard_map/pallas_call | solution.py:154
  105.6 2.2 %collective-permute-start.10 = (bf16[192,3072]{1,0:T(8,128)(2,1)}, bf16[192,3072]{1,0:T(8,128)(2,1)}, u32[]{:S(2)}, u32[]{:S(2)}) collective-permute-start(bf16[192,3072]{1,0:T(8,128)(2,1)} %shard_map.57.refs_0_), channel_id=1, source_target_pairs={{0,1},{1,0},{2,3},{3,2},{4,5},{5,4},{6,7},{7,6},{8,9},{9,8},{10,11... | collective-permute-start | bytes 3538952 | tf_op jit(solution)/shard_map/ppermute | solution.py:23
  107.8 1.9 %collective-permute-done.11.refs_2_ = bf16[272,768]{1,0:T(8,128)(2,1)} collective-permute-done((bf16[272,768]{1,0:T(8,128)(2,1)}, bf16[272,768]{1,0:T(8,128)(2,1)}, u32[]{:S(2)}, u32[]{:S(2)}) %collective-permute-start.11) | collective-permute-done | bytes 417824 | tf_op jit(solution)/shard_map/ppermute | solution.py:376
  109.7 0.3 collective-permute-start.14
  110.0 2.9 %collective-permute-done.4.refs_1_ = bf16[192,3072]{1,0:T(8,128)(2,1)} collective-permute-done((bf16[192,3072]{1,0:T(8,128)(2,1)}, bf16[192,3072]{1,0:T(8,128)(2,1)}, u32[]{:S(2)}, u32[]{:S(2)}) %collective-permute-start.4) | collective-permute-done | bytes 1179680 | tf_op jit(solution)/shard_map/ppermute | solution.py:23
  113.0 0.1 collective-permute-done.8.refs_3_
  113.0 2.4 %collective-permute-start.13 = (bf16[192,3072]{1,0:T(8,128)(2,1)}, bf16[192,3072]{1,0:T(8,128)(2,1)}, u32[]{:S(2)}, u32[]{:S(2)}) collective-permute-start(bf16[192,3072]{1,0:T(8,128)(2,1)} %collective-permute-done.4.refs_1_), channel_id=1, source_target_pairs={{0,1},{1,0},{2,3},{3,2},{4,5},{5,4},{6,7},{7,6},{8,9},{9,8},{10,11... | collective-permute-start | bytes 3538952 | tf_op jit(solution)/shard_map/ppermute | solution.py:23
  115.4 0.0 collective-permute-start.15
  115.4 2.6 %shard_map.63.refs_1_ = f32[272,256]{1,0:T(8,128)S(1)} custom-call(bf16[16,128]{1,0:T(8,128)(2,1)S(1)} %copy-done.8, bf16[256,1536]{1,0:T(8,128)(2,1)S(1)} %copy-done, bf16[256,1536]{1,0:T(8,128)(2,1)S(1)} %copy-done.2, bf16[2,256,1536]{2,1,0:T(8,128)(2,1)} %collective-permute-done.2.ka.va, bf16[2,256,1536]{2,1,0:T(8,128)(2,1)} %collective-permute-done.3.kb.vb, ...), custom_call_target="tpu_custom_call" | custom-call | flops 999999995904 | tf_op jit(solution)/shard_map/pallas_call | solution.py:154
  118.0 0.6 collective-permute-done.12.refs_3_
  118.7 2.3 %shard_map.64.refs_8_ = bf16[256,1536]{1,0:T(8,128)(2,1)S(1)} custom-call(s32[1]{0:T(128)} %bitcast.1.partner_ref, f32[272,1280]{1,0:T(8,128)S(1)} %shard_map.62.refs_0_, f32[272,256]{1,0:T(8,128)S(1)} %shard_map.63.refs_1_, bf16[272,768]{1,0:T(8,128)(2,1)} %collective-permute-done.11.refs_2_, bf16[272,768]{1,0:T(8,128)(2,1)} %collective-permute-done.12.refs_3_), custom_call_target="tpu_custom_call" | custom-call | flops 999999995904 | tf_op jit(solution)/shard_map/pallas_call | solution.py:228
  121.0 0.0 collective-permute-done.10.refs_4_
  121.1 8.5 %shard_map.65 = bf16[256,3072]{1,0:T(8,128)(2,1)} custom-call(bf16[192,3072]{1,0:T(8,128)(2,1)} %shard_map.57.refs_0_, bf16[192,3072]{1,0:T(8,128)(2,1)} %collective-permute-done.4.refs_1_, bf16[192,3072]{1,0:T(8,128)(2,1)} %shard_map.60.refs_2_, bf16[192,3072]{1,0:T(8,128)(2,1)} %collective-permute-done.8.refs_3_, ...), custom_call_target="tpu_custom_call" | custom-call | tf_op jit(solution)/shard_map/pallas_call | solution.py:271
  (20 shorter events, 0.1 us)
Async XLA Ops:
  1.7 27.6 %collective-permute-start.5 = (bf16[48,3072]{1,0:T(8,128)(2,1)}, bf16[48,3072]{1,0:T(8,128)(2,1)}, u32[]{:S(2)}, u32[]{:S(2)}) collective-permute-start(bf16[48,3072]{1,0:T(8,128)(2,1)} %constant_dynamic-slice_fusion), channel_id=1, source_target_pairs={{0,8},{1,9},{2,10},{3,11},{4,12},{5,13},{6,14},{7,15},{8,0},{9,1},... | collective-permute-start | bytes 884744 | tf_op jit(solution)/shard_map/ppermute | solution.py:23
  6.4 0.6 copy-start.7
  7.0 2.9 %copy-start.1 = (bf16[256,1536]{1,0:T(8,128)(2,1)S(1)}, bf16[256,1536]{1,0:T(8,128)(2,1)}, u32[]{:S(2)}) copy-start(bf16[256,1536]{1,0:T(8,128)(2,1)} %k0.7) | copy-start | bytes 2359300
  7.0 2.9 %copy-start.3 = (bf16[256,1536]{1,0:T(8,128)(2,1)S(1)}, bf16[256,1536]{1,0:T(8,128)(2,1)}, u32[]{:S(2)}) copy-start(bf16[256,1536]{1,0:T(8,128)(2,1)} %v0.7) | copy-start | bytes 2359300
  9.9 28.3 %collective-permute-start = (bf16[272,768]{1,0:T(8,128)(2,1)}, bf16[272,768]{1,0:T(8,128)(2,1)}, u32[]{:S(2)}, u32[]{:S(2)}) collective-permute-start(bf16[272,768]{1,0:T(8,128)(2,1)} %pad_maximum_fusion), channel_id=1, source_target_pairs={{0,8},{1,9},{2,10},{3,11},{4,12},{5,13},{6,14},{7,15},{8,0},{9,1},... | collective-permute-start | bytes 1253384 | tf_op jit(solution)/shard_map/ppermute | solution.py:353
  11.2 59.9 %collective-permute-start.3 = (bf16[2,256,1536]{2,1,0:T(8,128)(2,1)}, bf16[2,256,1536]{2,1,0:T(8,128)(2,1)}, u32[]{:S(2)}, u32[]{:S(2)}) collective-permute-start(bf16[2,256,1536]{2,1,0:T(8,128)(2,1)} %bitcast), channel_id=1, source_target_pairs={{1,0},{2,1},{3,2},{4,3},{5,4},{6,5},{7,6},{9,8},{10,9},{11,10},{12... | collective-permute-start | bytes 4718600 | tf_op jit(solution)/shard_map/ppermute | solution.py:33
  12.5 58.6 %collective-permute-start.2 = (bf16[2,256,1536]{2,1,0:T(8,128)(2,1)}, bf16[2,256,1536]{2,1,0:T(8,128)(2,1)}, u32[]{:S(2)}, u32[]{:S(2)}) collective-permute-start(bf16[2,256,1536]{2,1,0:T(8,128)(2,1)} %bitcast), channel_id=1, source_target_pairs={{0,1},{1,2},{2,3},{3,4},{4,5},{5,6},{6,7},{8,9},{9,10},{10,11},{11... | collective-permute-start | bytes 4718600 | tf_op jit(solution)/shard_map/ppermute | solution.py:33
  30.9 40.2 %copy-start.2 = (bf16[256,1536]{1,0:T(8,128)(2,1)S(1)}, bf16[256,1536]{1,0:T(8,128)(2,1)}, u32[]{:S(2)}) copy-start(bf16[256,1536]{1,0:T(8,128)(2,1)} %k0.7) | copy-start | bytes 2359300
  30.9 38.1 %collective-permute-start.6 = (bf16[48,3072]{1,0:T(8,128)(2,1)}, bf16[48,3072]{1,0:T(8,128)(2,1)S(1)}, u32[]{:S(2)}, u32[]{:S(2)}) collective-permute-start(bf16[48,3072]{1,0:T(8,128)(2,1)} %shard_map.58.refs_0_), channel_id=1, source_target_pairs={{0,4},{1,5},{2,6},{3,7},{4,0},{5,1},{6,2},{7,3},{8,12},{9,13},{10,... | collective-permute-start | bytes 884744 | tf_op jit(solution)/shard_map/ppermute | solution.py:23
  31.0 56.7 %collective-permute-start.9 = (bf16[256,768]{1,0:T(8,128)(2,1)}, bf16[256,768]{1,0:T(8,128)(2,1)}, u32[]{:S(2)}, u32[]{:S(2)}) collective-permute-start(bf16[256,768]{1,0:T(8,128)(2,1)} %get-tuple-element.27), channel_id=1, source_target_pairs={{0,8},{1,9},{2,10},{3,11},{4,12},{5,13},{6,14},{7,15},{8,0},{9,1},... | collective-permute-start | bytes 1179656 | tf_op jit(solution)/shard_map/ppermute | solution.py:362
  38.2 45.4 %collective-permute-start.1 = (bf16[96,3072]{1,0:T(8,128)(2,1)}, bf16[96,3072]{1,0:T(8,128)(2,1)}, u32[]{:S(2)}, u32[]{:S(2)}) collective-permute-start(bf16[96,3072]{1,0:T(8,128)(2,1)} %refs_0_.2), channel_id=1, source_target_pairs={{0,4},{1,5},{2,6},{3,7},{4,0},{5,1},{6,2},{7,3},{8,12},{9,13},{10,... | collective-permute-start | bytes 1769480 | tf_op jit(solution)/shard_map/ppermute | solution.py:23
  69.1 1.0 copy-start.6
  71.0 10.3 %collective-permute-start.7 = (bf16[96,3072]{1,0:T(8,128)(2,1)}, bf16[96,3072]{1,0:T(8,128)(2,1)}, u32[]{:S(2)}, u32[]{:S(2)}) collective-permute-start(bf16[96,3072]{1,0:T(8,128)(2,1)} %shard_map.59.refs_0_), channel_id=1, source_target_pairs={{0,2},{1,3},{2,0},{3,1},{4,6},{5,7},{6,4},{7,5},{8,10},{9,11},{10,... | collective-permute-start | bytes 1769480 | tf_op jit(solution)/shard_map/ppermute | solution.py:23
  71.1 1.1 copy-start.4
  78.7 31.0 %collective-permute-start.11 = (bf16[272,768]{1,0:T(8,128)(2,1)}, bf16[272,768]{1,0:T(8,128)(2,1)}, u32[]{:S(2)}, u32[]{:S(2)}) collective-permute-start(bf16[272,768]{1,0:T(8,128)(2,1)} %shard_map.56), channel_id=1, source_target_pairs={{0,8},{1,9},{2,10},{3,11},{4,12},{5,13},{6,14},{7,15},{8,0},{9,1},... | collective-permute-start | bytes 1253384 | tf_op jit(solution)/shard_map/ppermute | solution.py:376
  83.5 4.1 %copy-start.5 = (bf16[256,1536]{1,0:T(8,128)(2,1)S(1)}, bf16[256,1536]{1,0:T(8,128)(2,1)}, u32[]{:S(2)}) copy-start(bf16[256,1536]{1,0:T(8,128)(2,1)} %v0.7) | copy-start | bytes 2359300
  86.0 27.0 %collective-permute-start.4 = (bf16[192,3072]{1,0:T(8,128)(2,1)}, bf16[192,3072]{1,0:T(8,128)(2,1)}, u32[]{:S(2)}, u32[]{:S(2)}) collective-permute-start(bf16[192,3072]{1,0:T(8,128)(2,1)} %shard_map.57.refs_0_), channel_id=1, source_target_pairs={{0,2},{1,3},{2,0},{3,1},{4,6},{5,7},{6,4},{7,5},{8,10},{9,11},{10,... | collective-permute-start | bytes 3538952 | tf_op jit(solution)/shard_map/ppermute | solution.py:23
  86.0 27.0 %collective-permute-start.8 = (bf16[192,3072]{1,0:T(8,128)(2,1)}, bf16[192,3072]{1,0:T(8,128)(2,1)}, u32[]{:S(2)}, u32[]{:S(2)}) collective-permute-start(bf16[192,3072]{1,0:T(8,128)(2,1)} %shard_map.60.refs_2_), channel_id=1, source_target_pairs={{0,16},{16,0},{1,17},{17,1},{2,18},{18,2},{3,19},{19,3},{4,20},{20... | collective-permute-start | bytes 3538952 | tf_op jit(solution)/shard_map/ppermute | solution.py:27
  87.7 8.9 %copy-start = (bf16[256,1536]{1,0:T(8,128)(2,1)S(1)}, bf16[256,1536]{1,0:T(8,128)(2,1)}, u32[]{:S(2)}) copy-start(bf16[256,1536]{1,0:T(8,128)(2,1)} %q_ref.1) | copy-start | bytes 2359300
  87.7 8.9 %copy-start.8 = (bf16[16,128]{1,0:T(8,128)(2,1)S(1)}, bf16[16,128]{1,0:T(8,128)(2,1)}, u32[]{:S(2)}) copy-start(bf16[16,128]{1,0:T(8,128)(2,1)} %copy-done.7) | copy-start | bytes 12292
  94.2 24.4 %collective-permute-start.12 = (bf16[272,768]{1,0:T(8,128)(2,1)}, bf16[272,768]{1,0:T(8,128)(2,1)}, u32[]{:S(2)}, u32[]{:S(2)}) collective-permute-start(bf16[272,768]{1,0:T(8,128)(2,1)} %shard_map.61), channel_id=1, source_target_pairs={{0,8},{1,9},{2,10},{3,11},{4,12},{5,13},{6,14},{7,15},{8,0},{9,1},... | collective-permute-start | bytes 1253384 | tf_op jit(solution)/shard_map/ppermute | solution.py:376
  105.6 15.4 %collective-permute-start.10 = (bf16[192,3072]{1,0:T(8,128)(2,1)}, bf16[192,3072]{1,0:T(8,128)(2,1)}, u32[]{:S(2)}, u32[]{:S(2)}) collective-permute-start(bf16[192,3072]{1,0:T(8,128)(2,1)} %shard_map.57.refs_0_), channel_id=1, source_target_pairs={{0,1},{1,0},{2,3},{3,2},{4,5},{5,4},{6,7},{7,6},{8,9},{9,8},{10,11... | collective-permute-start | bytes 3538952 | tf_op jit(solution)/shard_map/ppermute | solution.py:23
  109.7 11.3 %collective-permute-start.14 = (bf16[192,3072]{1,0:T(8,128)(2,1)}, bf16[192,3072]{1,0:T(8,128)(2,1)}, u32[]{:S(2)}, u32[]{:S(2)}) collective-permute-start(bf16[192,3072]{1,0:T(8,128)(2,1)} %shard_map.60.refs_2_), channel_id=1, source_target_pairs={{0,1},{1,0},{2,3},{3,2},{4,5},{5,4},{6,7},{7,6},{8,9},{9,8},{10,11... | collective-permute-start | bytes 3538952 | tf_op jit(solution)/shard_map/ppermute | solution.py:23
  113.0 8.0 %collective-permute-start.13 = (bf16[192,3072]{1,0:T(8,128)(2,1)}, bf16[192,3072]{1,0:T(8,128)(2,1)}, u32[]{:S(2)}, u32[]{:S(2)}) collective-permute-start(bf16[192,3072]{1,0:T(8,128)(2,1)} %collective-permute-done.4.refs_1_), channel_id=1, source_target_pairs={{0,1},{1,0},{2,3},{3,2},{4,5},{5,4},{6,7},{7,6},{8,9},{9,8},{10,11... | collective-permute-start | bytes 3538952 | tf_op jit(solution)/shard_map/ppermute | solution.py:23
  115.4 5.7 %collective-permute-start.15 = (bf16[192,3072]{1,0:T(8,128)(2,1)}, bf16[192,3072]{1,0:T(8,128)(2,1)}, u32[]{:S(2)}, u32[]{:S(2)}) collective-permute-start(bf16[192,3072]{1,0:T(8,128)(2,1)} %collective-permute-done.8.refs_3_), channel_id=1, source_target_pairs={{0,1},{1,0},{2,3},{3,2},{4,5},{5,4},{6,7},{7,6},{8,9},{9,8},{10,11... | collective-permute-start | bytes 3538952 | tf_op jit(solution)/shard_map/ppermute | solution.py:23

commit v6 on v5

--- a/solution.py
+++ b/solution.py
@@ -173,23 +173,19 @@
     )(lists, q, keys, kv_up, kv_down, values, kv_up, kv_down)
 
 
-def merge_kernel(rows, chunk_counts, partner_ref, *refs):
-    parts, cursor = [], 0
-    for count in chunk_counts:
-        parts.append(refs[cursor : cursor + count])
-        cursor += count
-    attention = refs[cursor]
+def merge_kernel(rows, count, partner_ref, *refs):
+    parts, refs = refs[:count], refs[count:]
+    attention = refs[-1]
+    first = 0
+    if len(refs) > 1:
+        first = refs[0].shape[1]
+        attention[:, :first] = refs[0][...]
     per_block = rows // HD
     width = per_block * HD
-    for block in range(attention.shape[1] // width):
+    for block in range((attention.shape[1] - first) // width):
         tiles = []
-        for chunks in parts:
-            offset = block * width
-            for chunk in chunks:
-                if offset < chunk.shape[1]:
-                    break
-                offset -= chunk.shape[1]
-            tiles.append(chunk[:, offset : offset + width].astype(jnp.float32))
+        for part in parts:
+            tiles.append(part[:, block * width : (block + 1) * width].astype(jnp.float32))
         shares = []
         for head in range(per_block):
             lses = []
@@ -216,65 +212,79 @@
                     for n, t in enumerate(tiles)
                 ],
             )
-            start = block * width + head * HD
+            start = first + block * width + head * HD
             attention[:, start : start + HD] = mixed.astype(jnp.bfloat16)
 
 
-def merge(partner, parts):
-    flat = [chunk for chunks in parts for chunk in chunks]
-    rows = flat[0].shape[0] - EXTRA
-    features = sum(chunk.shape[1] for chunk in parts[0])
+def merge(partner, parts, width, merged=None):
+    rows = parts[0].shape[0] - EXTRA
     vmem = pl.BlockSpec(memory_space=pltpu.VMEM)
+    before = [] if merged is None else [merged]
+    total = width + sum(array.shape[1] for array in before)
     return pl.pallas_call(
-        functools.partial(merge_kernel, rows, [len(c) for c in parts]),
-        in_specs=[pl.BlockSpec(memory_space=pltpu.SMEM)] + [vmem] * len(flat),
+        functools.partial(merge_kernel, rows, len(parts)),
+        in_specs=[pl.BlockSpec(memory_space=pltpu.SMEM)] + [vmem] * (len(parts) + len(before)),
         out_specs=vmem,
-        out_shape=jax.ShapeDtypeStruct((rows, features), jnp.bfloat16),
+        out_shape=jax.ShapeDtypeStruct((rows, total), jnp.bfloat16),
         compiler_params=pltpu.CompilerParams(vmem_limit_bytes=VMEM_BYTES),
         cost_estimate=pl.CostEstimate(flops=WEIGHTY, bytes_accessed=0, transcendentals=0),
-    )(partner, *flat)
-
-
-def project_kernel(plan, *refs):
+    )(partner, *parts, *before)
+
+
+def project_kernel(plan, steps, *refs):
     weights = refs[: len(plan)]
-    attention, out_ref, held, sems = refs[len(plan) :]
+    attention, out_ref, held, total, sems = refs[len(plan) :]
+    moves = [(source, move) for source, moves in zip(weights, plan) for move in moves]
     copies = []
-    for source, moves in zip(weights, plan):
-        for from_row, count, place in moves:
-            into = pl.multiple_of(place(), 16)
-            copy = pltpu.make_async_copy(
-                source.at[pl.ds(from_row, count), :],
-                held.at[pl.ds(into, count), :],
-                sems.at[len(copies)],
+    for step in range(len(steps)):
+        for source, (from_row, count, place, wanted) in moves:
+            if wanted == step:
+                into = pl.multiple_of(place(), 16)
+                copy = pltpu.make_async_copy(
+                    source.at[pl.ds(from_row, count), :],
+                    held.at[pl.ds(into, count), :],
+                    sems.at[len(copies)],
+                )
+                copy.start()
+                copies.append((step, copy))
+    columns = out_ref.shape[1]
+    width = math.gcd(columns, 512)
+    depth = attention.shape[1] // len(steps)
+    for step, place in enumerate(steps):
+        for wanted, copy in copies:
+            if wanted == step:
+                copy.wait()
+        base = pl.multiple_of(place(), HD)
+        features = attention[:, pl.ds(base, depth)]
+
+        @pl.loop(0, columns // width)
+        def _(i):
+            there = pl.ds(pl.multiple_of(i * width, width), width)
+            sums = jnp.dot(
+                features, held[pl.ds(base, depth), there], preferred_element_type=jnp.float32
             )
-            copy.start()
-            copies.append(copy)
-    for copy in copies:
-        copy.wait()
-    columns = out_ref.shape[1]
-    step = math.gcd(columns, 512)
-
-    @pl.loop(0, columns // step)
-    def _(i):
-        there = pl.ds(pl.multiple_of(i * step, step), step)
-        out_ref[:, there] = jnp.dot(
-            attention[...], held[:, there], preferred_element_type=jnp.float32
-        ).astype(out_ref.dtype)
-
-
-def project(pieces, attention):
+            if step:
+                sums += total[:, there]
+            if step + 1 < len(steps):
+                total[:, there] = sums
+            else:
+                out_ref[:, there] = sums.astype(out_ref.dtype)
+
+
+def project(pieces, steps, attention):
     arrays = [array for array, _ in pieces]
     plan = [moves for _, moves in pieces]
     rows, features = attention.shape
     columns = arrays[0].shape[1]
     vmem = pl.BlockSpec(memory_space=pltpu.VMEM)
     return pl.pallas_call(
-        functools.partial(project_kernel, plan),
+        functools.partial(project_kernel, plan, steps),
         in_specs=[pl.BlockSpec(memory_space=pl.ANY)] * len(arrays) + [vmem],
         out_specs=vmem,
         out_shape=jax.ShapeDtypeStruct((rows, columns), jnp.bfloat16),
         scratch_shapes=[
             pltpu.VMEM((features, columns), jnp.bfloat16),
+            pltpu.VMEM((rows, columns), jnp.float32),
             pltpu.SemaphoreType.DMA((sum(len(m) for m in plan),)),
         ],
         compiler_params=pltpu.CompilerParams(vmem_limit_bytes=VMEM_BYTES),
@@ -287,41 +297,28 @@
 
 class Cube:
     def __init__(self, out_weight):
-        self.near = out_weight
         self.shard = out_weight.shape[0]
         self.half = self.shard // 2
-
-    def cross(self):
-        first = lax.axis_index("group") * self.half
-        self.mine = lax.dynamic_slice_in_dim(self.near, first, self.half, 0)
-        self.c0 = swap_bit(self.mine, 8)
-
-    def full(self, *bits):
-        def at(bit):
-            return lambda: (lax.axis_index("seq") ^ bit) * self.shard
-
-        return [(i * self.shard, self.shard, at(bit)) for i, bit in enumerate(bits)]
-
-    def halves(self, *bits):
-        def at(bit, turn):
-            return lambda: (lax.axis_index("seq") ^ bit) * self.shard + (
-                lax.axis_index("group") ^ turn
-            ) * self.half
-
-        return [(i * self.half, self.half, at(bit, turn)) for i, (bit, turn) in enumerate(bits)]
-
-    def pieces(self, near, wy, four, cx, swapped):
-        far = (8, 12, 10, 14)
-        return [
-            (near, self.full(0, 4)),
-            (wy, self.full(2, 6)),
-            (four, self.halves(*[(b, 0) for b in far])),
-            (cx, self.halves(*[(b, 1) for b in far])),
-            (swapped[0], self.full(1, 5)),
-            (swapped[1], self.full(3, 7)),
-            (swapped[2], self.halves(*[(b ^ 1, 0) for b in far])),
-            (swapped[3], self.halves(*[(b ^ 1, 1) for b in far])),
-        ]
+        self.list = []
+
+    def add(self, array, *places):
+        moves, row = [], 0
+        for bit, turn in places:
+            count = self.shard if turn is None else self.half
+
+            def place(bit=bit, turn=turn):
+                base = (lax.axis_index("seq") ^ bit) * self.shard
+                if turn is None:
+                    return base
+                return base + (lax.axis_index("group") ^ turn) * self.half
+
+            moves.append((row, count, place, bit // 8))
+            row += count
+        self.list.append((array, moves))
+
+    def steps(self):
+        depth = 8 * self.shard
+        return [lambda r=r: (lax.axis_index("seq") // 8 ^ r) * depth for r in range(2)]
 
 
 def body(groups, query_rows, key_rows, value_rows, block_list, out_weight):
@@ -336,29 +333,33 @@
     cube = None
     if devices == 16 and groups == 2 and out_weight.shape[0] % 32 == 0:
         cube = Cube(out_weight)
-        cube.cross()
+        first = lax.axis_index("group") * cube.half
+        mine = lax.dynamic_slice_in_dim(out_weight, first, cube.half, 0)
+        mz = swap_bit(mine, 4)
+        c0 = swap_bit(mine, 8)
     lists = jnp.pad(
         block_list.astype(jnp.bfloat16),
         ((0, EXTRA - FRAMES), (0, HD - block_list.shape[1])),
         constant_values=-1,
     )
     asking = jnp.concatenate([query_rows[:, :chunk], jnp.tile(lists, (1, chunk_heads))], axis=0)
-    ahead = [asking] + ([cube.mine] if cube else [])
+    ahead = [asking] + ([mine] if cube else [])
     kv = join(after(key_rows, *ahead), value_rows, cost=WEIGHTY).reshape(2, rows, features)
     kv_up = column_shift(kv, 1)
     kv_down = column_shift(kv, -1)
+    if cube:
+        mz = fence(after(mz, kv))
     sent = []
     for parity in phases:
         pairs = row_pairs(parity)
         first = lax.ppermute(asking, "seq", pairs)
         second = query_rows[:, chunk:]
         if cube:
-            cube.c0 = fence(after(cube.c0, kv))
-            cz = swap_bit(cube.c0, 4)
-            far = join(cube.c0, cz)
-            wz = swap_bit(after(out_weight, first), 4)
-            cy = swap_bit(far, 2)
-            second = after(second, cube.c0)
+            second = after(second, mz)
+            c0 = after(c0, mz)
+            cz = swap_bit(c0, 4)
+            first = after(first, c0)
+            x0 = swap_group(after(mz, first), groups)
         sent.append([first, lax.ppermute(second, "seq", pairs)])
     common = (key_rows, value_rows, kv_up, kv_down)
     others = []
@@ -366,24 +367,26 @@
         back = []
         for number, q in enumerate(asked):
             if number:
-                q = after(q, part, near, four) if cube else after(q, part)
+                q = after(q, part, far) if cube else after(q, part)
             part = attend(asked[0], q, 0, chunk_heads, *common, number * chunk_heads, jnp.bfloat16)
             if cube and not number:
-                four = join(far, after(cy, part))
-                cx = swap_group(four, groups)
-                near = join(out_weight, after(wz, part))
+                far = join(c0, after(cz, part))
+                cy = swap_bit(far, 2)
+                x1 = swap_group(far, groups)
+                near = join(out_weight, mz, after(x0, part))
                 wy = swap_bit(near, 2)
             back.append(lax.ppermute(part, "seq", row_pairs(parity)))
             last = part
         others.append(back)
-    early = heads - rows // HD
-    awaited = [others[0][0]] if phases else []
     if cube:
-        awaited += [cx, wy]
-    q = after(query_rows, last) if phases else query_rows
-    own = [attend(lists, q, 0, early, *common, 0, jnp.float32, 0)]
-    q = after(query_rows, *awaited)
-    own.append(attend(lists, q, early, heads - early, *common, early, jnp.float32))
+        cy = after(cy, last)
+        x2 = swap_group(cy, groups)
+    own = []
+    for number in range(2):
+        q, begin = query_rows, number * chunk_heads
+        if phases:
+            q = after(q, last, *own, *([cy] if cube and number else []))
+        own.append(attend(lists, q, begin, chunk_heads, *common, begin, jnp.float32, 0))
     partner = jnp.stack(
         [
             jnp.where(row % 2 == parity, row + 1 < grid_rows, row > 0).astype(jnp.int32)
@@ -391,15 +394,30 @@
         ]
         or [jnp.int32(0)]
     )
-    attention = merge(partner, [own] + others)
+    attention = merge(partner, [own[0]] + [b[0] for b in others], chunk)
+    attention = merge(partner, [own[1]] + [b[1] for b in others], features - chunk, attention)
     if cube:
-        swapped = [swap_bit(after(piece, own[0]), 1) for piece in (near, wy, four, cx)]
-        swapped = [after(piece, attention) for piece in swapped]
-        pieces = cube.pieces(near, wy, four, cx, swapped)
+        spread = [
+            (near, [(0, None), (4, 0), (4, 1)]),
+            (far, [(8, 0), (12, 0)]),
+            (wy, [(2, None), (6, 0), (6, 1)]),
+            (x1, [(8, 1), (12, 1)]),
+            (cy, [(10, 0), (14, 0)]),
+            (x2, [(10, 1), (14, 1)]),
+        ]
+        landed = []
+        for number, (array, _) in enumerate(spread):
+            ready = after(array, own[1], *(landed[:2] if number in (2, 5) else []))
+            landed.append(swap_bit(ready, 1))
+        landed = [after(array, attention) for array in landed]
+        for (array, places), turned in zip(spread, landed):
+            cube.add(array, *places)
+            cube.add(turned, *[(bit ^ 1, turn) for bit, turn in places])
+        pieces, steps = cube.list, cube.steps()
     else:
-        whole = lax.all_gather(out_weight, "seq", axis=0, tiled=True)
-        pieces = [(whole, [(0, whole.shape[0], lambda: 0)])]
-    return project(pieces, attention)
+        gathered = lax.all_gather(out_weight, "seq", axis=0, tiled=True)
+        pieces, steps = [(gathered, [(0, gathered.shape[0], lambda: 0, 0)])], [lambda: 0]
+    return project(pieces, steps, attention)
 
 
 def solution(mesh):

time: 130 us -> 126 us (0.969)
  the two profiles are of different devices: /device:TPU:0 before, /device:TPU:9 now
where the time goes in v6:
time: 126 us
  starting transfers between devices  47.1 us (37%)
  Pallas kernels  43.5 us (35%)
  waiting for transfers between devices  29.4 us (23%)
  local copies, waits for them, and re-layouts  4.35 us (3%)
  other arithmetic  1.45 us (1%)
    pallas_call x4, Pallas kernels, attend(): pl.pallas_call(functools.partial(attend_kernel, rows, per_block), grid=(h...  24.8 us
    ppermute x1, waiting for transfers between devices, body(): first = lax.ppermute(asking, 'seq', pairs)  22.3 us
    ppermute x2, starting transfers between devices, body(): back.append(lax.ppermute(part, 'seq', row_pairs(parity)))  18.9 us
    ppermute x11, starting transfers between devices, swap_bit(): return lax.ppermute(value, 'seq', [(s, s ^ bit) for s in range(count)])  17.5 us
    pallas_call x1, Pallas kernels, project(): pl.pallas_call(functools.partial(project_kernel, plan, steps), in_specs=[...  8.26 us
    ppermute x11, waiting for transfers between devices, swap_bit(): return lax.ppermute(value, 'seq', [(s, s ^ bit) for s in range(count)])  7.06 us
    ppermute x2, starting transfers between devices, column_shift(): return lax.ppermute(value, 'seq', pairs)  6.52 us
    pallas_call x3, Pallas kernels, join(): pl.pallas_call(functools.partial(join_kernel, len(arrays)), in_specs=[pl....  5.35 us
  transfers between devices with their start and end apart: 20, of which 4 were waited for; matrix products, arithmetic and copies ran while one was open for 3% of the time, Pallas kernels for 28%

profile of v6, /device:TPU:9, one launch (start us, length us, event | category | flops | bytes accessed | tf_op | source)
XLA Modules:
  0.0 126.0 jit_solution(12984903620511613901)
XLA Ops:
  0.0 1.8 %constant_dynamic-slice_fusion = bf16[48,3072]{1,0:T(8,128)(2,1)} fusion(bf16[96,3072]{1,0:T(8,128)(2,1)} %refs_0_.2, s32[]{:T(128)S(6)} %select_n.18), kind=kLoop, calls=%fused_computation.2 | loop fusion | bytes 589828 | tf_op jit(solution)/shard_map/dynamic_slice | solution.py:337
  1.8 2.3 %collective-permute-start.2 = (bf16[48,3072]{1,0:T(8,128)(2,1)}, bf16[48,3072]{1,0:T(8,128)(2,1)}, u32[]{:S(2)}, u32[]{:S(2)}) collective-permute-start(bf16[48,3072]{1,0:T(8,128)(2,1)} %constant_dynamic-slice_fusion), channel_id=1, source_target_pairs={{0,8},{1,9},{2,10},{3,11},{4,12},{5,13},{6,14},{7,15},{8,0},{9,1},... | collective-permute-start | bytes 884744 | tf_op jit(solution)/shard_map/ppermute | solution.py:23
  4.1 0.2 collective-permute-start
  4.3 0.7 convert_element_type.6
  5.0 0.6 copy-done.5
  5.6 1.9 %fusion = (bf16[256,768]{1,0:T(8,128)(2,1)}, bf16[256,768]{1,0:T(8,128)(2,1)S(1)}) fusion(bf16[256,1536]{1,0:T(8,128)(2,1)} %q_ref.1), kind=kLoop, calls=%fused_computation.3 | loop fusion | bytes 1572864 | tf_op jit(solution)/shard_map/slice | solution.py:356
  7.5 0.8 pad_maximum_fusion
  8.3 0.0 collective-permute-start.1
  8.3 1.3 %shard_map.55 = bf16[512,1536]{1,0:T(8,128)(2,1)} custom-call(bf16[256,1536]{1,0:T(8,128)(2,1)S(1)} %copy-done.1, bf16[256,1536]{1,0:T(8,128)(2,1)S(1)} %copy-done.2), custom_call_target="tpu_custom_call" | custom-call | flops 999999995904 | tf_op jit(solution)/shard_map/pallas_call | solution.py:63
  9.6 3.1 %collective-permute-start.5 = (bf16[2,256,1536]{2,1,0:T(8,128)(2,1)}, bf16[2,256,1536]{2,1,0:T(8,128)(2,1)}, u32[]{:S(2)}, u32[]{:S(2)}) collective-permute-start(bf16[2,256,1536]{2,1,0:T(8,128)(2,1)} %bitcast), channel_id=1, source_target_pairs={{1,0},{2,1},{3,2},{4,3},{5,4},{6,5},{7,6},{9,8},{10,9},{11,10},{12... | collective-permute-start | bytes 4718600 | tf_op jit(solution)/shard_map/ppermute | solution.py:33
  12.7 3.4 %collective-permute-start.4 = (bf16[2,256,1536]{2,1,0:T(8,128)(2,1)}, bf16[2,256,1536]{2,1,0:T(8,128)(2,1)}, u32[]{:S(2)}, u32[]{:S(2)}) collective-permute-start(bf16[2,256,1536]{2,1,0:T(8,128)(2,1)} %bitcast), channel_id=1, source_target_pairs={{0,1},{1,2},{2,3},{3,4},{4,5},{5,6},{6,7},{8,9},{9,10},{10,11},{11... | collective-permute-start | bytes 4718600 | tf_op jit(solution)/shard_map/ppermute | solution.py:33
  16.1 1.2 collective-permute-done.in_ref
  17.4 1.7 %shard_map.56.refs_1_ = bf16[48,3072]{1,0:T(8,128)(2,1)} custom-call(bf16[48,3072]{1,0:T(8,128)(2,1)} %collective-permute-done.in_ref), custom_call_target="tpu_custom_call" | custom-call | flops 999999995904 | tf_op jit(solution)/shard_map/pallas_call | solution.py:80
  19.1 0.0 collective-permute-done.2.refs_0_
  19.1 0.1 collective-permute-start.7
  19.1 2.4 %collective-permute-start.6 = (bf16[256,768]{1,0:T(8,128)(2,1)}, bf16[256,768]{1,0:T(8,128)(2,1)}, u32[]{:S(2)}, u32[]{:S(2)}) collective-permute-start(bf16[256,768]{1,0:T(8,128)(2,1)} %get-tuple-element.35), channel_id=1, source_target_pairs={{0,8},{1,9},{2,10},{3,11},{4,12},{5,13},{6,14},{7,15},{8,0},{9,1},... | collective-permute-start | bytes 1179656 | tf_op jit(solution)/shard_map/ppermute | solution.py:363
  21.5 22.3 %collective-permute-done.1.list_ref.q_ref = bf16[272,768]{1,0:T(8,128)(2,1)} collective-permute-done((bf16[272,768]{1,0:T(8,128)(2,1)}, bf16[272,768]{1,0:T(8,128)(2,1)}, u32[]{:S(2)}, u32[]{:S(2)}) %collective-permute-start.1) | collective-permute-done | bytes 417824 | tf_op jit(solution)/shard_map/ppermute | solution.py:355
  43.8 1.2 collective-permute-start.3
  45.0 0.0 collective-permute-done.5.kb.vb
  45.0 0.0 collective-permute-done.4.ka.va
  45.0 6.5 %shard_map.57 = bf16[272,768]{1,0:T(8,128)(2,1)} custom-call(bf16[272,768]{1,0:T(8,128)(2,1)} %collective-permute-done.1.list_ref.q_ref, bf16[272,768]{1,0:T(8,128)(2,1)} %collective-permute-done.1.list_ref.q_ref, bf16[256,1536]{1,0:T(8,128)(2,1)S(1)} %copy-done.1, bf16[2,256,1536]{2,1,0:T(8,128)(2,1)} %collective-permute-done.4.ka.va, ...), custom_call_target="tpu_custom_call" | custom-call | flops 999999995904 | tf_op jit(solution)/shard_map/pallas_call | solution.py:154
  51.5 3.1 %collective-permute-start.11 = (bf16[272,768]{1,0:T(8,128)(2,1)}, bf16[272,768]{1,0:T(8,128)(2,1)}, u32[]{:S(2)}, u32[]{:S(2)}) collective-permute-start(bf16[272,768]{1,0:T(8,128)(2,1)} %shard_map.57), channel_id=1, source_target_pairs={{0,8},{1,9},{2,10},{3,11},{4,12},{5,13},{6,14},{7,15},{8,0},{9,1},... | collective-permute-start | bytes 1253384 | tf_op jit(solution)/shard_map/ppermute | solution.py:378
  54.6 0.0 collective-permute-done.7.refs_1_
  54.6 1.9 %shard_map.59.refs_2_ = bf16[96,3072]{1,0:T(8,128)(2,1)} custom-call(bf16[48,3072]{1,0:T(8,128)(2,1)} %collective-permute-done.2.refs_0_, bf16[48,3072]{1,0:T(8,128)(2,1)} %collective-permute-done.7.refs_1_), custom_call_target="tpu_custom_call" | custom-call | tf_op jit(solution)/shard_map/pallas_call | solution.py:63
  56.5 0.3 collective-permute-start.15
  56.8 2.6 %collective-permute-start.8 = (bf16[96,3072]{1,0:T(8,128)(2,1)}, bf16[96,3072]{1,0:T(8,128)(2,1)}, u32[]{:S(2)}, u32[]{:S(2)}) collective-permute-start(bf16[96,3072]{1,0:T(8,128)(2,1)} %shard_map.59.refs_2_), channel_id=1, source_target_pairs={{0,2},{1,3},{2,0},{3,1},{4,6},{5,7},{6,4},{7,5},{8,10},{9,11},{10,... | collective-permute-start | bytes 1769480 | tf_op jit(solution)/shard_map/ppermute | solution.py:23
  59.4 0.0 collective-permute-done.6.q_ref
  59.4 6.5 %shard_map.60 = bf16[272,768]{1,0:T(8,128)(2,1)} custom-call(bf16[272,768]{1,0:T(8,128)(2,1)} %collective-permute-done.1.list_ref.q_ref, bf16[256,768]{1,0:T(8,128)(2,1)} %collective-permute-done.6.q_ref, bf16[256,1536]{1,0:T(8,128)(2,1)S(1)} %copy-done.1, bf16[2,256,1536]{2,1,0:T(8,128)(2,1)} %collective-permute-done.4.ka.va, ...), custom_call_target="tpu_custom_call" | custom-call | flops 999999995904 | tf_op jit(solution)/shard_map/pallas_call | solution.py:154
  66.0 15.8 %collective-permute-start.10 = (bf16[272,768]{1,0:T(8,128)(2,1)}, bf16[272,768]{1,0:T(8,128)(2,1)}, u32[]{:S(2)}, u32[]{:S(2)}) collective-permute-start(bf16[272,768]{1,0:T(8,128)(2,1)} %shard_map.60), channel_id=1, source_target_pairs={{0,8},{1,9},{2,10},{3,11},{4,12},{5,13},{6,14},{7,15},{8,0},{9,1},... | collective-permute-start | bytes 1253384 | tf_op jit(solution)/shard_map/ppermute | solution.py:378
  81.7 0.0 collective-permute-done.3.refs_2_
  81.7 2.2 %shard_map.58.refs_0_ = bf16[192,3072]{1,0:T(8,128)(2,1)} custom-call(bf16[96,3072]{1,0:T(8,128)(2,1)S(1)} %copy-done.3, bf16[48,3072]{1,0:T(8,128)(2,1)S(1)} %copy-done.4, bf16[48,3072]{1,0:T(8,128)(2,1)} %collective-permute-done.3.refs_2_), custom_call_target="tpu_custom_call" | custom-call | tf_op jit(solution)/shard_map/pallas_call | solution.py:63
  83.9 0.1 collective-permute-start.13
  84.0 5.9 %shard_map.61.refs_0_ = f32[272,768]{1,0:T(8,128)S(1)} custom-call(bf16[16,128]{1,0:T(8,128)(2,1)S(1)} %copy-done.6, bf16[256,1536]{1,0:T(8,128)(2,1)S(1)} %copy-done, bf16[256,1536]{1,0:T(8,128)(2,1)S(1)} %copy-done.1, bf16[2,256,1536]{2,1,0:T(8,128)(2,1)} %collective-permute-done.4.ka.va, bf16[2,256,1536]{2,1,0:T(8,128)(2,1)} %collective-permute-done.5.kb.vb, ...), custom_call_target="tpu_custom_call" | custom-call | tf_op jit(solution)/shard_map/pallas_call | solution.py:154
  89.9 0.3 collective-permute-start.18
  90.2 5.8 %shard_map.62.refs_0_ = f32[272,768]{1,0:T(8,128)S(1)} custom-call(bf16[16,128]{1,0:T(8,128)(2,1)S(1)} %copy-done.6, bf16[256,1536]{1,0:T(8,128)(2,1)S(1)} %copy-done, bf16[256,1536]{1,0:T(8,128)(2,1)S(1)} %copy-done.1, bf16[2,256,1536]{2,1,0:T(8,128)(2,1)} %collective-permute-done.4.ka.va, bf16[2,256,1536]{2,1,0:T(8,128)(2,1)} %collective-permute-done.5.kb.vb, ...), custom_call_target="tpu_custom_call" | custom-call | tf_op jit(solution)/shard_map/pallas_call | solution.py:154
  96.1 6.7 %collective-permute-start.12 = (bf16[96,3072]{1,0:T(8,128)(2,1)}, bf16[96,3072]{1,0:T(8,128)(2,1)}, u32[]{:S(2)}, u32[]{:S(2)}) collective-permute-start(bf16[96,3072]{1,0:T(8,128)(2,1)} %shard_map.59.refs_2_), channel_id=1, source_target_pairs={{0,1},{1,0},{2,3},{3,2},{4,5},{5,4},{6,7},{7,6},{8,9},{9,8},{10,11... | collective-permute-start | bytes 1769480 | tf_op jit(solution)/shard_map/ppermute | solution.py:23
  102.8 0.1 collective-permute-start.9
  102.8 1.7 %shard_map.63.refs_2_ = bf16[256,768]{1,0:T(8,128)(2,1)S(1)} custom-call(s32[1]{0:T(128)} %bitcast.1.partner_ref, f32[272,768]{1,0:T(8,128)S(1)} %shard_map.61.refs_0_, bf16[272,768]{1,0:T(8,128)(2,1)} %collective-permute-done.11.refs_1_), custom_call_target="tpu_custom_call" | custom-call | flops 999999995904 | tf_op jit(solution)/shard_map/pallas_call | solution.py:224
  104.6 1.9 %collective-permute-start.16 = (bf16[96,3072]{1,0:T(8,128)(2,1)}, bf16[96,3072]{1,0:T(8,128)(2,1)}, u32[]{:S(2)}, u32[]{:S(2)}) collective-permute-start(bf16[96,3072]{1,0:T(8,128)(2,1)} %collective-permute-done.15.refs_6_), channel_id=1, source_target_pairs={{0,1},{1,0},{2,3},{3,2},{4,5},{5,4},{6,7},{7,6},{8,9},{9,8},{10,11... | collective-permute-start | bytes 1769480 | tf_op jit(solution)/shard_map/ppermute | solution.py:23
  106.5 0.0 collective-permute-start.17
  106.5 0.5 collective-permute-start.19
  107.0 4.8 %collective-permute-done.13.refs_4_ = bf16[192,3072]{1,0:T(8,128)(2,1)} collective-permute-done((bf16[192,3072]{1,0:T(8,128)(2,1)}, bf16[192,3072]{1,0:T(8,128)(2,1)}, u32[]{:S(2)}, u32[]{:S(2)}) %collective-permute-start.13) | collective-permute-done | bytes 1179680 | tf_op jit(solution)/shard_map/ppermute | solution.py:23
  111.8 3.1 %collective-permute-start.14 = (bf16[192,3072]{1,0:T(8,128)(2,1)}, bf16[192,3072]{1,0:T(8,128)(2,1)}, u32[]{:S(2)}, u32[]{:S(2)}) collective-permute-start(bf16[192,3072]{1,0:T(8,128)(2,1)} %collective-permute-done.13.refs_4_), channel_id=1, source_target_pairs={{0,1},{1,0},{2,3},{3,2},{4,5},{5,4},{6,7},{7,6},{8,9},{9,8},{10,11... | collective-permute-start | bytes 3538952 | tf_op jit(solution)/shard_map/ppermute | solution.py:23
  114.9 1.7 %shard_map.64.refs_12_ = bf16[256,1536]{1,0:T(8,128)(2,1)S(1)} custom-call(s32[1]{0:T(128)} %bitcast.1.partner_ref, f32[272,768]{1,0:T(8,128)S(1)} %shard_map.62.refs_0_, bf16[272,768]{1,0:T(8,128)(2,1)} %collective-permute-done.10.refs_1_, bf16[256,768]{1,0:T(8,128)(2,1)S(1)} %shard_map.63.refs_2_), custom_call_target="tpu_custom_call" | custom-call | flops 999999995904 | tf_op jit(solution)/shard_map/pallas_call | solution.py:224
  116.6 0.0 collective-permute-done.16.refs_7_
  116.6 0.0 collective-permute-done.17.refs_9_
  116.7 1.0 collective-permute-done.14.refs_5_
  117.7 8.3 %shard_map.65 = bf16[256,3072]{1,0:T(8,128)(2,1)} custom-call(bf16[192,3072]{1,0:T(8,128)(2,1)} %shard_map.58.refs_0_, bf16[192,3072]{1,0:T(8,128)(2,1)} %collective-permute-done.9.refs_1_, bf16[96,3072]{1,0:T(8,128)(2,1)} %shard_map.59.refs_2_, bf16[96,3072]{1,0:T(8,128)(2,1)} %collective-permute-done.12.refs_3_, ...), custom_call_target="tpu_custom_call" | custom-call | tf_op jit(solution)/shard_map/pallas_call | solution.py:280
  (24 shorter events, 0.1 us)
Async XLA Ops:
  0.0 8.3 %copy-start.1 = (bf16[256,1536]{1,0:T(8,128)(2,1)S(1)}, bf16[256,1536]{1,0:T(8,128)(2,1)}, u32[]{:S(2)}) copy-start(bf16[256,1536]{1,0:T(8,128)(2,1)} %k0.7) | copy-start | bytes 2359300
  0.0 8.3 %copy-start.2 = (bf16[256,1536]{1,0:T(8,128)(2,1)S(1)}, bf16[256,1536]{1,0:T(8,128)(2,1)}, u32[]{:S(2)}) copy-start(bf16[256,1536]{1,0:T(8,128)(2,1)} %v0.7) | copy-start | bytes 2359300
  1.8 17.3 %collective-permute-start.2 = (bf16[48,3072]{1,0:T(8,128)(2,1)}, bf16[48,3072]{1,0:T(8,128)(2,1)}, u32[]{:S(2)}, u32[]{:S(2)}) collective-permute-start(bf16[48,3072]{1,0:T(8,128)(2,1)} %constant_dynamic-slice_fusion), channel_id=1, source_target_pairs={{0,8},{1,9},{2,10},{3,11},{4,12},{5,13},{6,14},{7,15},{8,0},{9,1},... | collective-permute-start | bytes 884744 | tf_op jit(solution)/shard_map/ppermute | solution.py:23
  4.1 13.3 %collective-permute-start = (bf16[48,3072]{1,0:T(8,128)(2,1)}, bf16[48,3072]{1,0:T(8,128)(2,1)}, u32[]{:S(2)}, u32[]{:S(2)}) collective-permute-start(bf16[48,3072]{1,0:T(8,128)(2,1)} %constant_dynamic-slice_fusion), channel_id=1, source_target_pairs={{0,4},{1,5},{2,6},{3,7},{4,0},{5,1},{6,2},{7,3},{8,12},{9,13},{10,... | collective-permute-start | bytes 884744 | tf_op jit(solution)/shard_map/ppermute | solution.py:23
  5.0 0.6 copy-start.5
  8.3 35.5 %collective-permute-start.1 = (bf16[272,768]{1,0:T(8,128)(2,1)}, bf16[272,768]{1,0:T(8,128)(2,1)}, u32[]{:S(2)}, u32[]{:S(2)}) collective-permute-start(bf16[272,768]{1,0:T(8,128)(2,1)} %pad_maximum_fusion), channel_id=1, source_target_pairs={{0,8},{1,9},{2,10},{3,11},{4,12},{5,13},{6,14},{7,15},{8,0},{9,1},... | collective-permute-start | bytes 1253384 | tf_op jit(solution)/shard_map/ppermute | solution.py:355
  9.6 35.4 %collective-permute-start.5 = (bf16[2,256,1536]{2,1,0:T(8,128)(2,1)}, bf16[2,256,1536]{2,1,0:T(8,128)(2,1)}, u32[]{:S(2)}, u32[]{:S(2)}) collective-permute-start(bf16[2,256,1536]{2,1,0:T(8,128)(2,1)} %bitcast), channel_id=1, source_target_pairs={{1,0},{2,1},{3,2},{4,3},{5,4},{6,5},{7,6},{9,8},{10,9},{11,10},{12... | collective-permute-start | bytes 4718600 | tf_op jit(solution)/shard_map/ppermute | solution.py:33
  12.7 32.3 %collective-permute-start.4 = (bf16[2,256,1536]{2,1,0:T(8,128)(2,1)}, bf16[2,256,1536]{2,1,0:T(8,128)(2,1)}, u32[]{:S(2)}, u32[]{:S(2)}) collective-permute-start(bf16[2,256,1536]{2,1,0:T(8,128)(2,1)} %bitcast), channel_id=1, source_target_pairs={{0,1},{1,2},{2,3},{3,4},{4,5},{5,6},{6,7},{8,9},{9,10},{10,11},{11... | collective-permute-start | bytes 4718600 | tf_op jit(solution)/shard_map/ppermute | solution.py:33
  19.1 35.5 %collective-permute-start.7 = (bf16[48,3072]{1,0:T(8,128)(2,1)}, bf16[48,3072]{1,0:T(8,128)(2,1)}, u32[]{:S(2)}, u32[]{:S(2)}) collective-permute-start(bf16[48,3072]{1,0:T(8,128)(2,1)} %collective-permute-done.2.refs_0_), channel_id=1, source_target_pairs={{0,4},{1,5},{2,6},{3,7},{4,0},{5,1},{6,2},{7,3},{8,12},{9,13},{10,... | collective-permute-start | bytes 884744 | tf_op jit(solution)/shard_map/ppermute | solution.py:23
  19.1 40.3 %collective-permute-start.6 = (bf16[256,768]{1,0:T(8,128)(2,1)}, bf16[256,768]{1,0:T(8,128)(2,1)}, u32[]{:S(2)}, u32[]{:S(2)}) collective-permute-start(bf16[256,768]{1,0:T(8,128)(2,1)} %get-tuple-element.35), channel_id=1, source_target_pairs={{0,8},{1,9},{2,10},{3,11},{4,12},{5,13},{6,14},{7,15},{8,0},{9,1},... | collective-permute-start | bytes 1179656 | tf_op jit(solution)/shard_map/ppermute | solution.py:363
  43.8 38.0 %collective-permute-start.3 = (bf16[48,3072]{1,0:T(8,128)(2,1)}, bf16[48,3072]{1,0:T(8,128)(2,1)}, u32[]{:S(2)}, u32[]{:S(2)}) collective-permute-start(bf16[48,3072]{1,0:T(8,128)(2,1)} %shard_map.56.refs_1_), channel_id=1, source_target_pairs={{0,16},{16,0},{1,17},{17,1},{2,18},{18,2},{3,19},{19,3},{4,20},{20... | collective-permute-start | bytes 884744 | tf_op jit(solution)/shard_map/ppermute | solution.py:27
  51.5 44.6 %collective-permute-start.11 = (bf16[272,768]{1,0:T(8,128)(2,1)}, bf16[272,768]{1,0:T(8,128)(2,1)}, u32[]{:S(2)}, u32[]{:S(2)}) collective-permute-start(bf16[272,768]{1,0:T(8,128)(2,1)} %shard_map.57), channel_id=1, source_target_pairs={{0,8},{1,9},{2,10},{3,11},{4,12},{5,13},{6,14},{7,15},{8,0},{9,1},... | collective-permute-start | bytes 1253384 | tf_op jit(solution)/shard_map/ppermute | solution.py:378
  56.5 46.3 %collective-permute-start.15 = (bf16[96,3072]{1,0:T(8,128)(2,1)}, bf16[96,3072]{1,0:T(8,128)(2,1)}, u32[]{:S(2)}, u32[]{:S(2)}) collective-permute-start(bf16[96,3072]{1,0:T(8,128)(2,1)} %shard_map.59.refs_2_), channel_id=1, source_target_pairs={{0,16},{16,0},{1,17},{17,1},{2,18},{18,2},{3,19},{19,3},{4,20},{20... | collective-permute-start | bytes 1769480 | tf_op jit(solution)/shard_map/ppermute | solution.py:27
  56.8 33.1 %collective-permute-start.8 = (bf16[96,3072]{1,0:T(8,128)(2,1)}, bf16[96,3072]{1,0:T(8,128)(2,1)}, u32[]{:S(2)}, u32[]{:S(2)}) collective-permute-start(bf16[96,3072]{1,0:T(8,128)(2,1)} %shard_map.59.refs_2_), channel_id=1, source_target_pairs={{0,2},{1,3},{2,0},{3,1},{4,6},{5,7},{6,4},{7,5},{8,10},{9,11},{10,... | collective-permute-start | bytes 1769480 | tf_op jit(solution)/shard_map/ppermute | solution.py:23
  59.4 22.3 %copy-start.3 = (bf16[96,3072]{1,0:T(8,128)(2,1)S(1)}, bf16[96,3072]{1,0:T(8,128)(2,1)}, u32[]{:S(2)}) copy-start(bf16[96,3072]{1,0:T(8,128)(2,1)} %refs_0_.2) | copy-start | bytes 1769476
  59.4 22.3 %copy-start.4 = (bf16[48,3072]{1,0:T(8,128)(2,1)S(1)}, bf16[48,3072]{1,0:T(8,128)(2,1)}, u32[]{:S(2)}) copy-start(bf16[48,3072]{1,0:T(8,128)(2,1)} %shard_map.56.refs_1_) | copy-start | bytes 884740
  65.9 18.1 %copy-start = (bf16[256,1536]{1,0:T(8,128)(2,1)S(1)}, bf16[256,1536]{1,0:T(8,128)(2,1)}, u32[]{:S(2)}) copy-start(bf16[256,1536]{1,0:T(8,128)(2,1)} %q_ref.1) | copy-start | bytes 2359300
  65.9 18.1 %copy-start.6 = (bf16[16,128]{1,0:T(8,128)(2,1)S(1)}, bf16[16,128]{1,0:T(8,128)(2,1)}, u32[]{:S(2)}) copy-start(bf16[16,128]{1,0:T(8,128)(2,1)} %copy-done.5) | copy-start | bytes 12292
  66.0 48.9 %collective-permute-start.10 = (bf16[272,768]{1,0:T(8,128)(2,1)}, bf16[272,768]{1,0:T(8,128)(2,1)}, u32[]{:S(2)}, u32[]{:S(2)}) collective-permute-start(bf16[272,768]{1,0:T(8,128)(2,1)} %shard_map.60), channel_id=1, source_target_pairs={{0,8},{1,9},{2,10},{3,11},{4,12},{5,13},{6,14},{7,15},{8,0},{9,1},... | collective-permute-start | bytes 1253384 | tf_op jit(solution)/shard_map/ppermute | solution.py:378
  83.9 27.9 %collective-permute-start.13 = (bf16[192,3072]{1,0:T(8,128)(2,1)}, bf16[192,3072]{1,0:T(8,128)(2,1)}, u32[]{:S(2)}, u32[]{:S(2)}) collective-permute-start(bf16[192,3072]{1,0:T(8,128)(2,1)} %shard_map.58.refs_0_), channel_id=1, source_target_pairs={{0,2},{1,3},{2,0},{3,1},{4,6},{5,7},{6,4},{7,5},{8,10},{9,11},{10,... | collective-permute-start | bytes 3538952 | tf_op jit(solution)/shard_map/ppermute | solution.py:23
  89.9 14.6 %collective-permute-start.18 = (bf16[96,3072]{1,0:T(8,128)(2,1)}, bf16[96,3072]{1,0:T(8,128)(2,1)}, u32[]{:S(2)}, u32[]{:S(2)}) collective-permute-start(bf16[96,3072]{1,0:T(8,128)(2,1)} %collective-permute-done.8.refs_8_), channel_id=1, source_target_pairs={{0,16},{16,0},{1,17},{17,1},{2,18},{18,2},{3,19},{19,3},{4,20},{20... | collective-permute-start | bytes 1769480 | tf_op jit(solution)/shard_map/ppermute | solution.py:27
  96.1 10.4 %collective-permute-start.12 = (bf16[96,3072]{1,0:T(8,128)(2,1)}, bf16[96,3072]{1,0:T(8,128)(2,1)}, u32[]{:S(2)}, u32[]{:S(2)}) collective-permute-start(bf16[96,3072]{1,0:T(8,128)(2,1)} %shard_map.59.refs_2_), channel_id=1, source_target_pairs={{0,1},{1,0},{2,3},{3,2},{4,5},{5,4},{6,7},{7,6},{8,9},{9,8},{10,11... | collective-permute-start | bytes 1769480 | tf_op jit(solution)/shard_map/ppermute | solution.py:23
  102.8 3.8 %collective-permute-start.9 = (bf16[192,3072]{1,0:T(8,128)(2,1)}, bf16[192,3072]{1,0:T(8,128)(2,1)}, u32[]{:S(2)}, u32[]{:S(2)}) collective-permute-start(bf16[192,3072]{1,0:T(8,128)(2,1)} %shard_map.58.refs_0_), channel_id=1, source_target_pairs={{0,1},{1,0},{2,3},{3,2},{4,5},{5,4},{6,7},{7,6},{8,9},{9,8},{10,11... | collective-permute-start | bytes 3538952 | tf_op jit(solution)/shard_map/ppermute | solution.py:23
  104.6 12.1 %collective-permute-start.16 = (bf16[96,3072]{1,0:T(8,128)(2,1)}, bf16[96,3072]{1,0:T(8,128)(2,1)}, u32[]{:S(2)}, u32[]{:S(2)}) collective-permute-start(bf16[96,3072]{1,0:T(8,128)(2,1)} %collective-permute-done.15.refs_6_), channel_id=1, source_target_pairs={{0,1},{1,0},{2,3},{3,2},{4,5},{5,4},{6,7},{7,6},{8,9},{9,8},{10,11... | collective-permute-start | bytes 1769480 | tf_op jit(solution)/shard_map/ppermute | solution.py:23
  106.5 10.1 %collective-permute-start.17 = (bf16[96,3072]{1,0:T(8,128)(2,1)}, bf16[96,3072]{1,0:T(8,128)(2,1)}, u32[]{:S(2)}, u32[]{:S(2)}) collective-permute-start(bf16[96,3072]{1,0:T(8,128)(2,1)} %collective-permute-done.8.refs_8_), channel_id=1, source_target_pairs={{0,1},{1,0},{2,3},{3,2},{4,5},{5,4},{6,7},{7,6},{8,9},{9,8},{10,11... | collective-permute-start | bytes 1769480 | tf_op jit(solution)/shard_map/ppermute | solution.py:23
  106.5 10.1 %collective-permute-start.19 = (bf16[96,3072]{1,0:T(8,128)(2,1)}, bf16[96,3072]{1,0:T(8,128)(2,1)}, u32[]{:S(2)}, u32[]{:S(2)}) collective-permute-start(bf16[96,3072]{1,0:T(8,128)(2,1)} %collective-permute-done.18.refs_10_), channel_id=1, source_target_pairs={{0,1},{1,0},{2,3},{3,2},{4,5},{5,4},{6,7},{7,6},{8,9},{9,8},{10,11... | collective-permute-start | bytes 1769480 | tf_op jit(solution)/shard_map/ppermute | solution.py:23
  111.8 5.9 %collective-permute-start.14 = (bf16[192,3072]{1,0:T(8,128)(2,1)}, bf16[192,3072]{1,0:T(8,128)(2,1)}, u32[]{:S(2)}, u32[]{:S(2)}) collective-permute-start(bf16[192,3072]{1,0:T(8,128)(2,1)} %collective-permute-done.13.refs_4_), channel_id=1, source_target_pairs={{0,1},{1,0},{2,3},{3,2},{4,5},{5,4},{6,7},{7,6},{8,9},{9,8},{10,11... | collective-permute-start | bytes 3538952 | tf_op jit(solution)/shard_map/ppermute | solution.py:23

commit v7 on v6

--- a/solution.py
+++ b/solution.py
@@ -355,11 +355,13 @@
         first = lax.ppermute(asking, "seq", pairs)
         second = query_rows[:, chunk:]
         if cube:
-            second = after(second, mz)
+            second = after(second, first)
             c0 = after(c0, mz)
             cz = swap_bit(c0, 4)
             first = after(first, c0)
-            x0 = swap_group(after(mz, first), groups)
+            x0 = swap_group(mz, groups)
+            near = join(out_weight, mz, x0)
+            wy = swap_bit(near, 2)
         sent.append([first, lax.ppermute(second, "seq", pairs)])
     common = (key_rows, value_rows, kv_up, kv_down)
     others = []
@@ -373,8 +375,6 @@
                 far = join(c0, after(cz, part))
                 cy = swap_bit(far, 2)
                 x1 = swap_group(far, groups)
-                near = join(out_weight, mz, after(x0, part))
-                wy = swap_bit(near, 2)
             back.append(lax.ppermute(part, "seq", row_pairs(parity)))
             last = part
         others.append(back)

time: 126 us -> 119 us (0.944)
  the two profiles are of different devices: /device:TPU:9 before, /device:TPU:0 now
where the time goes in v7:
time: 119 us; the launch traced here: 118 us
  Pallas kernels  42.6 us (36%)
  waiting for transfers between devices  36 us (30%)
  starting transfers between devices  32.6 us (27%)
  local copies, waits for them, and re-layouts  5.34 us (4%)
  other arithmetic  1.45 us (1%)
    pallas_call x4, Pallas kernels, attend(): pl.pallas_call(functools.partial(attend_kernel, rows, per_block), grid=(h...  24.7 us
    ppermute x11, waiting for transfers between devices, swap_bit(): return lax.ppermute(value, 'seq', [(s, s ^ bit) for s in range(count)])  21.4 us
    ppermute x11, starting transfers between devices, swap_bit(): return lax.ppermute(value, 'seq', [(s, s ^ bit) for s in range(count)])  18.6 us
    ppermute x1, waiting for transfers between devices, body(): first = lax.ppermute(asking, 'seq', pairs)  11.9 us
    pallas_call x1, Pallas kernels, project(): pl.pallas_call(functools.partial(project_kernel, plan, steps), in_specs=[...  8.26 us
    ppermute x2, starting transfers between devices, column_shift(): return lax.ppermute(value, 'seq', pairs)  5.51 us
    ppermute x3, starting transfers between devices, swap_group(): return lax.ppermute(value, 'group', [(s, s ^ 1) for s in range(groups)])  5.14 us
    pallas_call x3, Pallas kernels, join(): pl.pallas_call(functools.partial(join_kernel, len(arrays)), in_specs=[pl....  4.44 us
  transfers between devices with their start and end apart: 20, of which 8 were waited for; matrix products, arithmetic and copies ran while one was open for 3% of the time, Pallas kernels for 29%

profile of v7, /device:TPU:0, one launch (start us, length us, event | category | flops | bytes accessed | tf_op | source)
XLA Modules:
  0.0 118.1 jit_solution(15473912513718086314)
XLA Ops:
  0.0 1.8 %constant_dynamic-slice_fusion = bf16[48,3072]{1,0:T(8,128)(2,1)} fusion(bf16[96,3072]{1,0:T(8,128)(2,1)} %refs_0_.2, s32[]{:T(128)S(6)} %select_n.18), kind=kLoop, calls=%fused_computation.2 | loop fusion | bytes 589828 | tf_op jit(solution)/shard_map/dynamic_slice | solution.py:337
  1.8 4.0 %collective-permute-start.3 = (bf16[48,3072]{1,0:T(8,128)(2,1)}, bf16[48,3072]{1,0:T(8,128)(2,1)}, u32[]{:S(2)}, u32[]{:S(2)}) collective-permute-start(bf16[48,3072]{1,0:T(8,128)(2,1)} %constant_dynamic-slice_fusion), channel_id=1, source_target_pairs={{0,8},{1,9},{2,10},{3,11},{4,12},{5,13},{6,14},{7,15},{8,0},{9,1},... | collective-permute-start | bytes 884744 | tf_op jit(solution)/shard_map/ppermute | solution.py:23
  5.9 1.6 %collective-permute-start = (bf16[48,3072]{1,0:T(8,128)(2,1)}, bf16[48,3072]{1,0:T(8,128)(2,1)}, u32[]{:S(2)}, u32[]{:S(2)}) collective-permute-start(bf16[48,3072]{1,0:T(8,128)(2,1)} %constant_dynamic-slice_fusion), channel_id=1, source_target_pairs={{0,4},{1,5},{2,6},{3,7},{4,0},{5,1},{6,2},{7,3},{8,12},{9,13},{10,... | collective-permute-start | bytes 884744 | tf_op jit(solution)/shard_map/ppermute | solution.py:23
  7.4 0.7 convert_element_type.6
  8.1 0.6 copy-done.5
  8.7 1.9 %fusion = (bf16[256,768]{1,0:T(8,128)(2,1)}, bf16[256,768]{1,0:T(8,128)(2,1)S(1)}) fusion(bf16[256,1536]{1,0:T(8,128)(2,1)} %q_ref.1), kind=kLoop, calls=%fused_computation.3 | loop fusion | bytes 1572864 | tf_op jit(solution)/shard_map/slice | solution.py:356
  10.7 0.8 pad_maximum_fusion
  11.4 0.3 collective-permute-start.2
  11.8 1.3 %shard_map.55 = bf16[512,1536]{1,0:T(8,128)(2,1)} custom-call(bf16[256,1536]{1,0:T(8,128)(2,1)S(1)} %copy-done.1, bf16[256,1536]{1,0:T(8,128)(2,1)S(1)} %copy-done.2), custom_call_target="tpu_custom_call" | custom-call | flops 999999995904 | tf_op jit(solution)/shard_map/pallas_call | solution.py:63
  13.1 1.3 %collective-permute-start.6 = (bf16[2,256,1536]{2,1,0:T(8,128)(2,1)}, bf16[2,256,1536]{2,1,0:T(8,128)(2,1)}, u32[]{:S(2)}, u32[]{:S(2)}) collective-permute-start(bf16[2,256,1536]{2,1,0:T(8,128)(2,1)} %bitcast), channel_id=1, source_target_pairs={{1,0},{2,1},{3,2},{4,3},{5,4},{6,5},{7,6},{9,8},{10,9},{11,10},{12... | collective-permute-start | bytes 4718600 | tf_op jit(solution)/shard_map/ppermute | solution.py:33
  14.4 4.2 %collective-permute-start.5 = (bf16[2,256,1536]{2,1,0:T(8,128)(2,1)}, bf16[2,256,1536]{2,1,0:T(8,128)(2,1)}, u32[]{:S(2)}, u32[]{:S(2)}) collective-permute-start(bf16[2,256,1536]{2,1,0:T(8,128)(2,1)} %bitcast), channel_id=1, source_target_pairs={{0,1},{1,2},{2,3},{3,4},{4,5},{5,6},{6,7},{8,9},{9,10},{10,11},{11... | collective-permute-start | bytes 4718600 | tf_op jit(solution)/shard_map/ppermute | solution.py:33
  18.6 1.4 %collective-permute-done.in_ref = bf16[48,3072]{1,0:T(8,128)(2,1)} collective-permute-done((bf16[48,3072]{1,0:T(8,128)(2,1)}, bf16[48,3072]{1,0:T(8,128)(2,1)}, u32[]{:S(2)}, u32[]{:S(2)}) %collective-permute-start) | collective-permute-done | bytes 294944 | tf_op jit(solution)/shard_map/ppermute | solution.py:23
  20.0 1.7 %shard_map.56.refs_1_ = bf16[48,3072]{1,0:T(8,128)(2,1)} custom-call(bf16[48,3072]{1,0:T(8,128)(2,1)} %collective-permute-done.in_ref), custom_call_target="tpu_custom_call" | custom-call | flops 999999995904 | tf_op jit(solution)/shard_map/pallas_call | solution.py:80
  21.8 1.5 %collective-permute-start.1 = (bf16[48,3072]{1,0:T(8,128)(2,1)}, bf16[48,3072]{1,0:T(8,128)(2,1)S(1)}, u32[]{:S(2)}, u32[]{:S(2)}) collective-permute-start(bf16[48,3072]{1,0:T(8,128)(2,1)} %shard_map.56.refs_1_), channel_id=1, source_target_pairs={{0,16},{16,0},{1,17},{17,1},{2,18},{18,2},{3,19},{19,3},{4,20},{20... | collective-permute-start | bytes 884744 | tf_op jit(solution)/shard_map/ppermute | solution.py:27
  23.2 0.0 collective-permute-done.3.refs_0_
  23.2 2.4 %collective-permute-start.7 = (bf16[48,3072]{1,0:T(8,128)(2,1)}, bf16[48,3072]{1,0:T(8,128)(2,1)}, u32[]{:S(2)}, u32[]{:S(2)}) collective-permute-start(bf16[48,3072]{1,0:T(8,128)(2,1)} %collective-permute-done.3.refs_0_), channel_id=1, source_target_pairs={{0,4},{1,5},{2,6},{3,7},{4,0},{5,1},{6,2},{7,3},{8,12},{9,13},{10,... | collective-permute-start | bytes 884744 | tf_op jit(solution)/shard_map/ppermute | solution.py:23
  25.7 11.9 %collective-permute-done.2.list_ref.q_ref = bf16[272,768]{1,0:T(8,128)(2,1)} collective-permute-done((bf16[272,768]{1,0:T(8,128)(2,1)}, bf16[272,768]{1,0:T(8,128)(2,1)}, u32[]{:S(2)}, u32[]{:S(2)}) %collective-permute-start.2) | collective-permute-done | bytes 417824 | tf_op jit(solution)/shard_map/ppermute | solution.py:355
  37.6 0.0 collective-permute-start.4
  37.6 0.0 collective-permute-done.1.refs_2_
  37.6 1.0 copy-done.4
  38.5 1.3 %shard_map.57.refs_0_ = bf16[192,3072]{1,0:T(8,128)(2,1)} custom-call(bf16[96,3072]{1,0:T(8,128)(2,1)S(1)} %copy-done.3, bf16[48,3072]{1,0:T(8,128)(2,1)S(1)} %copy-done.4, bf16[48,3072]{1,0:T(8,128)(2,1)S(1)} %collective-permute-done.1.refs_2_), custom_call_target="tpu_custom_call" | custom-call | tf_op jit(solution)/shard_map/pallas_call | solution.py:63
  39.8 1.6 %collective-permute-start.13 = (bf16[192,3072]{1,0:T(8,128)(2,1)}, bf16[192,3072]{1,0:T(8,128)(2,1)}, u32[]{:S(2)}, u32[]{:S(2)}) collective-permute-start(bf16[192,3072]{1,0:T(8,128)(2,1)} %shard_map.57.refs_0_), channel_id=1, source_target_pairs={{0,2},{1,3},{2,0},{3,1},{4,6},{5,7},{6,4},{7,5},{8,10},{9,11},{10,... | collective-permute-start | bytes 3538952 | tf_op jit(solution)/shard_map/ppermute | solution.py:23
  41.5 0.0 collective-permute-done.6.kb.vb
  41.5 6.5 %shard_map.58 = bf16[272,768]{1,0:T(8,128)(2,1)} custom-call(bf16[272,768]{1,0:T(8,128)(2,1)} %collective-permute-done.2.list_ref.q_ref, bf16[272,768]{1,0:T(8,128)(2,1)} %collective-permute-done.2.list_ref.q_ref, bf16[256,1536]{1,0:T(8,128)(2,1)S(1)} %copy-done.1, bf16[2,256,1536]{2,1,0:T(8,128)(2,1)} %collective-permute-done.5.ka.va, ...), custom_call_target="tpu_custom_call" | custom-call | flops 999999995904 | tf_op jit(solution)/shard_map/pallas_call | solution.py:154
  48.0 2.9 %collective-permute-start.11 = (bf16[272,768]{1,0:T(8,128)(2,1)}, bf16[272,768]{1,0:T(8,128)(2,1)}, u32[]{:S(2)}, u32[]{:S(2)}) collective-permute-start(bf16[272,768]{1,0:T(8,128)(2,1)} %shard_map.58), channel_id=1, source_target_pairs={{0,8},{1,9},{2,10},{3,11},{4,12},{5,13},{6,14},{7,15},{8,0},{9,1},... | collective-permute-start | bytes 1253384 | tf_op jit(solution)/shard_map/ppermute | solution.py:378
  50.9 13.4 %collective-permute-done.7.refs_1_ = bf16[48,3072]{1,0:T(8,128)(2,1)} collective-permute-done((bf16[48,3072]{1,0:T(8,128)(2,1)}, bf16[48,3072]{1,0:T(8,128)(2,1)}, u32[]{:S(2)}, u32[]{:S(2)}) %collective-permute-start.7) | collective-permute-done | bytes 294944 | tf_op jit(solution)/shard_map/ppermute | solution.py:23
  64.3 1.9 %shard_map.59.refs_2_ = bf16[96,3072]{1,0:T(8,128)(2,1)} custom-call(bf16[48,3072]{1,0:T(8,128)(2,1)} %collective-permute-done.3.refs_0_, bf16[48,3072]{1,0:T(8,128)(2,1)} %collective-permute-done.7.refs_1_), custom_call_target="tpu_custom_call" | custom-call | tf_op jit(solution)/shard_map/pallas_call | solution.py:63
  66.2 1.9 %collective-permute-start.15 = (bf16[96,3072]{1,0:T(8,128)(2,1)}, bf16[96,3072]{1,0:T(8,128)(2,1)}, u32[]{:S(2)}, u32[]{:S(2)}) collective-permute-start(bf16[96,3072]{1,0:T(8,128)(2,1)} %shard_map.59.refs_2_), channel_id=1, source_target_pairs={{0,16},{16,0},{1,17},{17,1},{2,18},{18,2},{3,19},{19,3},{4,20},{20... | collective-permute-start | bytes 1769480 | tf_op jit(solution)/shard_map/ppermute | solution.py:27
  68.0 4.2 %collective-permute-start.8 = (bf16[96,3072]{1,0:T(8,128)(2,1)}, bf16[96,3072]{1,0:T(8,128)(2,1)}, u32[]{:S(2)}, u32[]{:S(2)}) collective-permute-start(bf16[96,3072]{1,0:T(8,128)(2,1)} %shard_map.59.refs_2_), channel_id=1, source_target_pairs={{0,2},{1,3},{2,0},{3,1},{4,6},{5,7},{6,4},{7,5},{8,10},{9,11},{10,... | collective-permute-start | bytes 1769480 | tf_op jit(solution)/shard_map/ppermute | solution.py:23
  72.2 6.5 %shard_map.60 = bf16[272,768]{1,0:T(8,128)(2,1)} custom-call(bf16[272,768]{1,0:T(8,128)(2,1)} %collective-permute-done.2.list_ref.q_ref, bf16[256,768]{1,0:T(8,128)(2,1)} %collective-permute-done.4.q_ref, bf16[256,1536]{1,0:T(8,128)(2,1)S(1)} %copy-done.1, bf16[2,256,1536]{2,1,0:T(8,128)(2,1)} %collective-permute-done.5.ka.va, ...), custom_call_target="tpu_custom_call" | custom-call | flops 999999995904 | tf_op jit(solution)/shard_map/pallas_call | solution.py:154
  78.8 0.0 collective-permute-start.10
  78.8 5.9 %shard_map.61.refs_0_ = f32[272,768]{1,0:T(8,128)S(1)} custom-call(bf16[16,128]{1,0:T(8,128)(2,1)S(1)} %copy-done.6, bf16[256,1536]{1,0:T(8,128)(2,1)S(1)} %copy-done, bf16[256,1536]{1,0:T(8,128)(2,1)S(1)} %copy-done.1, bf16[2,256,1536]{2,1,0:T(8,128)(2,1)} %collective-permute-done.5.ka.va, bf16[2,256,1536]{2,1,0:T(8,128)(2,1)} %collective-permute-done.6.kb.vb, ...), custom_call_target="tpu_custom_call" | custom-call | tf_op jit(solution)/shard_map/pallas_call | solution.py:154
  84.7 3.5 %collective-permute-done.8.refs_8_ = bf16[96,3072]{1,0:T(8,128)(2,1)} collective-permute-done((bf16[96,3072]{1,0:T(8,128)(2,1)}, bf16[96,3072]{1,0:T(8,128)(2,1)}, u32[]{:S(2)}, u32[]{:S(2)}) %collective-permute-start.8) | collective-permute-done | bytes 589856 | tf_op jit(solution)/shard_map/ppermute | solution.py:23
  88.2 1.8 %collective-permute-start.18 = (bf16[96,3072]{1,0:T(8,128)(2,1)}, bf16[96,3072]{1,0:T(8,128)(2,1)}, u32[]{:S(2)}, u32[]{:S(2)}) collective-permute-start(bf16[96,3072]{1,0:T(8,128)(2,1)} %collective-permute-done.8.refs_8_), channel_id=1, source_target_pairs={{0,16},{16,0},{1,17},{17,1},{2,18},{18,2},{3,19},{19,3},{4,20},{20... | collective-permute-start | bytes 1769480 | tf_op jit(solution)/shard_map/ppermute | solution.py:27
  90.0 5.8 %shard_map.62.refs_0_ = f32[272,768]{1,0:T(8,128)S(1)} custom-call(bf16[16,128]{1,0:T(8,128)(2,1)S(1)} %copy-done.6, bf16[256,1536]{1,0:T(8,128)(2,1)S(1)} %copy-done, bf16[256,1536]{1,0:T(8,128)(2,1)S(1)} %copy-done.1, bf16[2,256,1536]{2,1,0:T(8,128)(2,1)} %collective-permute-done.5.ka.va, bf16[2,256,1536]{2,1,0:T(8,128)(2,1)} %collective-permute-done.6.kb.vb, ...), custom_call_target="tpu_custom_call" | custom-call | tf_op jit(solution)/shard_map/pallas_call | solution.py:154
  95.8 2.1 %collective-permute-start.12 = (bf16[96,3072]{1,0:T(8,128)(2,1)}, bf16[96,3072]{1,0:T(8,128)(2,1)}, u32[]{:S(2)}, u32[]{:S(2)}) collective-permute-start(bf16[96,3072]{1,0:T(8,128)(2,1)} %shard_map.59.refs_2_), channel_id=1, source_target_pairs={{0,1},{1,0},{2,3},{3,2},{4,5},{5,4},{6,7},{7,6},{8,9},{9,8},{10,11... | collective-permute-start | bytes 1769480 | tf_op jit(solution)/shard_map/ppermute | solution.py:23
  98.0 0.1 collective-permute-start.9
  98.1 1.7 %shard_map.63.refs_2_ = bf16[256,768]{1,0:T(8,128)(2,1)S(1)} custom-call(s32[1]{0:T(128)} %bitcast.1.partner_ref, f32[272,768]{1,0:T(8,128)S(1)} %shard_map.61.refs_0_, bf16[272,768]{1,0:T(8,128)(2,1)} %collective-permute-done.11.refs_1_), custom_call_target="tpu_custom_call" | custom-call | flops 999999995904 | tf_op jit(solution)/shard_map/pallas_call | solution.py:224
  99.8 2.8 %collective-permute-done.18.refs_10_ = bf16[96,3072]{1,0:T(8,128)(2,1)} collective-permute-done((bf16[96,3072]{1,0:T(8,128)(2,1)}, bf16[96,3072]{1,0:T(8,128)(2,1)}, u32[]{:S(2)}, u32[]{:S(2)}) %collective-permute-start.18) | collective-permute-done | bytes 589856 | tf_op jit(solution)/shard_map/ppermute | solution.py:27
  102.6 2.0 %collective-permute-start.16 = (bf16[96,3072]{1,0:T(8,128)(2,1)}, bf16[96,3072]{1,0:T(8,128)(2,1)}, u32[]{:S(2)}, u32[]{:S(2)}) collective-permute-start(bf16[96,3072]{1,0:T(8,128)(2,1)} %collective-permute-done.15.refs_6_), channel_id=1, source_target_pairs={{0,1},{1,0},{2,3},{3,2},{4,5},{5,4},{6,7},{7,6},{8,9},{9,8},{10,11... | collective-permute-start | bytes 1769480 | tf_op jit(solution)/shard_map/ppermute | solution.py:23
  104.5 0.0 collective-permute-start.17
  104.6 0.5 collective-permute-start.19
  105.1 0.1 collective-permute-start.14
  105.1 1.7 %shard_map.64.refs_12_ = bf16[256,1536]{1,0:T(8,128)(2,1)S(1)} custom-call(s32[1]{0:T(128)} %bitcast.1.partner_ref, f32[272,768]{1,0:T(8,128)S(1)} %shard_map.62.refs_0_, bf16[272,768]{1,0:T(8,128)(2,1)} %collective-permute-done.10.refs_1_, bf16[256,768]{1,0:T(8,128)(2,1)S(1)} %shard_map.63.refs_2_), custom_call_target="tpu_custom_call" | custom-call | flops 999999995904 | tf_op jit(solution)/shard_map/pallas_call | solution.py:224
  106.9 0.5 collective-permute-done.17.refs_9_
  107.3 0.8 collective-permute-done.19.refs_11_
  108.2 1.7 %collective-permute-done.14.refs_5_ = bf16[192,3072]{1,0:T(8,128)(2,1)} collective-permute-done((bf16[192,3072]{1,0:T(8,128)(2,1)}, bf16[192,3072]{1,0:T(8,128)(2,1)}, u32[]{:S(2)}, u32[]{:S(2)}) %collective-permute-start.14) | collective-permute-done | bytes 1179680 | tf_op jit(solution)/shard_map/ppermute | solution.py:23
  109.9 8.3 %shard_map.65 = bf16[256,3072]{1,0:T(8,128)(2,1)} custom-call(bf16[192,3072]{1,0:T(8,128)(2,1)} %shard_map.57.refs_0_, bf16[192,3072]{1,0:T(8,128)(2,1)} %collective-permute-done.9.refs_1_, bf16[96,3072]{1,0:T(8,128)(2,1)} %shard_map.59.refs_2_, bf16[96,3072]{1,0:T(8,128)(2,1)} %collective-permute-done.12.refs_3_, ...), custom_call_target="tpu_custom_call" | custom-call | tf_op jit(solution)/shard_map/pallas_call | solution.py:280
  (24 shorter events, 0.1 us)
Async XLA Ops:
  0.0 11.8 %copy-start.1 = (bf16[256,1536]{1,0:T(8,128)(2,1)S(1)}, bf16[256,1536]{1,0:T(8,128)(2,1)}, u32[]{:S(2)}) copy-start(bf16[256,1536]{1,0:T(8,128)(2,1)} %k0.7) | copy-start | bytes 2359300
  0.0 11.8 %copy-start.2 = (bf16[256,1536]{1,0:T(8,128)(2,1)S(1)}, bf16[256,1536]{1,0:T(8,128)(2,1)}, u32[]{:S(2)}) copy-start(bf16[256,1536]{1,0:T(8,128)(2,1)} %v0.7) | copy-start | bytes 2359300
  1.8 21.4 %collective-permute-start.3 = (bf16[48,3072]{1,0:T(8,128)(2,1)}, bf16[48,3072]{1,0:T(8,128)(2,1)}, u32[]{:S(2)}, u32[]{:S(2)}) collective-permute-start(bf16[48,3072]{1,0:T(8,128)(2,1)} %constant_dynamic-slice_fusion), channel_id=1, source_target_pairs={{0,8},{1,9},{2,10},{3,11},{4,12},{5,13},{6,14},{7,15},{8,0},{9,1},... | collective-permute-start | bytes 884744 | tf_op jit(solution)/shard_map/ppermute | solution.py:23
  5.9 14.1 %collective-permute-start = (bf16[48,3072]{1,0:T(8,128)(2,1)}, bf16[48,3072]{1,0:T(8,128)(2,1)}, u32[]{:S(2)}, u32[]{:S(2)}) collective-permute-start(bf16[48,3072]{1,0:T(8,128)(2,1)} %constant_dynamic-slice_fusion), channel_id=1, source_target_pairs={{0,4},{1,5},{2,6},{3,7},{4,0},{5,1},{6,2},{7,3},{8,12},{9,13},{10,... | collective-permute-start | bytes 884744 | tf_op jit(solution)/shard_map/ppermute | solution.py:23
  8.1 0.6 copy-start.5
  11.4 26.1 %collective-permute-start.2 = (bf16[272,768]{1,0:T(8,128)(2,1)}, bf16[272,768]{1,0:T(8,128)(2,1)}, u32[]{:S(2)}, u32[]{:S(2)}) collective-permute-start(bf16[272,768]{1,0:T(8,128)(2,1)} %pad_maximum_fusion), channel_id=1, source_target_pairs={{0,8},{1,9},{2,10},{3,11},{4,12},{5,13},{6,14},{7,15},{8,0},{9,1},... | collective-permute-start | bytes 1253384 | tf_op jit(solution)/shard_map/ppermute | solution.py:355
  13.1 28.4 %collective-permute-start.6 = (bf16[2,256,1536]{2,1,0:T(8,128)(2,1)}, bf16[2,256,1536]{2,1,0:T(8,128)(2,1)}, u32[]{:S(2)}, u32[]{:S(2)}) collective-permute-start(bf16[2,256,1536]{2,1,0:T(8,128)(2,1)} %bitcast), channel_id=1, source_target_pairs={{1,0},{2,1},{3,2},{4,3},{5,4},{6,5},{7,6},{9,8},{10,9},{11,10},{12... | collective-permute-start | bytes 4718600 | tf_op jit(solution)/shard_map/ppermute | solution.py:33
  14.4 27.1 %collective-permute-start.5 = (bf16[2,256,1536]{2,1,0:T(8,128)(2,1)}, bf16[2,256,1536]{2,1,0:T(8,128)(2,1)}, u32[]{:S(2)}, u32[]{:S(2)}) collective-permute-start(bf16[2,256,1536]{2,1,0:T(8,128)(2,1)} %bitcast), channel_id=1, source_target_pairs={{0,1},{1,2},{2,3},{3,4},{4,5},{5,6},{6,7},{8,9},{9,10},{10,11},{11... | collective-permute-start | bytes 4718600 | tf_op jit(solution)/shard_map/ppermute | solution.py:33
  20.0 17.6 %copy-start.3 = (bf16[96,3072]{1,0:T(8,128)(2,1)S(1)}, bf16[96,3072]{1,0:T(8,128)(2,1)}, u32[]{:S(2)}) copy-start(bf16[96,3072]{1,0:T(8,128)(2,1)} %refs_0_.2) | copy-start | bytes 1769476
  21.8 15.8 %collective-permute-start.1 = (bf16[48,3072]{1,0:T(8,128)(2,1)}, bf16[48,3072]{1,0:T(8,128)(2,1)S(1)}, u32[]{:S(2)}, u32[]{:S(2)}) collective-permute-start(bf16[48,3072]{1,0:T(8,128)(2,1)} %shard_map.56.refs_1_), channel_id=1, source_target_pairs={{0,16},{16,0},{1,17},{17,1},{2,18},{18,2},{3,19},{19,3},{4,20},{20... | collective-permute-start | bytes 884744 | tf_op jit(solution)/shard_map/ppermute | solution.py:27
  23.2 41.0 %collective-permute-start.7 = (bf16[48,3072]{1,0:T(8,128)(2,1)}, bf16[48,3072]{1,0:T(8,128)(2,1)}, u32[]{:S(2)}, u32[]{:S(2)}) collective-permute-start(bf16[48,3072]{1,0:T(8,128)(2,1)} %collective-permute-done.3.refs_0_), channel_id=1, source_target_pairs={{0,4},{1,5},{2,6},{3,7},{4,0},{5,1},{6,2},{7,3},{8,12},{9,13},{10,... | collective-permute-start | bytes 884744 | tf_op jit(solution)/shard_map/ppermute | solution.py:23
  37.6 34.7 %collective-permute-start.4 = (bf16[256,768]{1,0:T(8,128)(2,1)}, bf16[256,768]{1,0:T(8,128)(2,1)}, u32[]{:S(2)}, u32[]{:S(2)}) collective-permute-start(bf16[256,768]{1,0:T(8,128)(2,1)} %get-tuple-element.31), channel_id=1, source_target_pairs={{0,8},{1,9},{2,10},{3,11},{4,12},{5,13},{6,14},{7,15},{8,0},{9,1},... | collective-permute-start | bytes 1179656 | tf_op jit(solution)/shard_map/ppermute | solution.py:365
  37.6 1.0 copy-start.4
  39.8 64.7 %collective-permute-start.13 = (bf16[192,3072]{1,0:T(8,128)(2,1)}, bf16[192,3072]{1,0:T(8,128)(2,1)}, u32[]{:S(2)}, u32[]{:S(2)}) collective-permute-start(bf16[192,3072]{1,0:T(8,128)(2,1)} %shard_map.57.refs_0_), channel_id=1, source_target_pairs={{0,2},{1,3},{2,0},{3,1},{4,6},{5,7},{6,4},{7,5},{8,10},{9,11},{10,... | collective-permute-start | bytes 3538952 | tf_op jit(solution)/shard_map/ppermute | solution.py:23
  48.0 47.9 %collective-permute-start.11 = (bf16[272,768]{1,0:T(8,128)(2,1)}, bf16[272,768]{1,0:T(8,128)(2,1)}, u32[]{:S(2)}, u32[]{:S(2)}) collective-permute-start(bf16[272,768]{1,0:T(8,128)(2,1)} %shard_map.58), channel_id=1, source_target_pairs={{0,8},{1,9},{2,10},{3,11},{4,12},{5,13},{6,14},{7,15},{8,0},{9,1},... | collective-permute-start | bytes 1253384 | tf_op jit(solution)/shard_map/ppermute | solution.py:378
  66.2 31.8 %collective-permute-start.15 = (bf16[96,3072]{1,0:T(8,128)(2,1)}, bf16[96,3072]{1,0:T(8,128)(2,1)}, u32[]{:S(2)}, u32[]{:S(2)}) collective-permute-start(bf16[96,3072]{1,0:T(8,128)(2,1)} %shard_map.59.refs_2_), channel_id=1, source_target_pairs={{0,16},{16,0},{1,17},{17,1},{2,18},{18,2},{3,19},{19,3},{4,20},{20... | collective-permute-start | bytes 1769480 | tf_op jit(solution)/shard_map/ppermute | solution.py:27
  68.0 20.2 %collective-permute-start.8 = (bf16[96,3072]{1,0:T(8,128)(2,1)}, bf16[96,3072]{1,0:T(8,128)(2,1)}, u32[]{:S(2)}, u32[]{:S(2)}) collective-permute-start(bf16[96,3072]{1,0:T(8,128)(2,1)} %shard_map.59.refs_2_), channel_id=1, source_target_pairs={{0,2},{1,3},{2,0},{3,1},{4,6},{5,7},{6,4},{7,5},{8,10},{9,11},{10,... | collective-permute-start | bytes 1769480 | tf_op jit(solution)/shard_map/ppermute | solution.py:23
  72.2 6.6 %copy-start = (bf16[256,1536]{1,0:T(8,128)(2,1)S(1)}, bf16[256,1536]{1,0:T(8,128)(2,1)}, u32[]{:S(2)}) copy-start(bf16[256,1536]{1,0:T(8,128)(2,1)} %q_ref.1) | copy-start | bytes 2359300
  72.2 6.6 %copy-start.6 = (bf16[16,128]{1,0:T(8,128)(2,1)S(1)}, bf16[16,128]{1,0:T(8,128)(2,1)}, u32[]{:S(2)}) copy-start(bf16[16,128]{1,0:T(8,128)(2,1)} %copy-done.5) | copy-start | bytes 12292
  78.8 26.4 %collective-permute-start.10 = (bf16[272,768]{1,0:T(8,128)(2,1)}, bf16[272,768]{1,0:T(8,128)(2,1)}, u32[]{:S(2)}, u32[]{:S(2)}) collective-permute-start(bf16[272,768]{1,0:T(8,128)(2,1)} %shard_map.60), channel_id=1, source_target_pairs={{0,8},{1,9},{2,10},{3,11},{4,12},{5,13},{6,14},{7,15},{8,0},{9,1},... | collective-permute-start | bytes 1253384 | tf_op jit(solution)/shard_map/ppermute | solution.py:378
  88.2 14.4 %collective-permute-start.18 = (bf16[96,3072]{1,0:T(8,128)(2,1)}, bf16[96,3072]{1,0:T(8,128)(2,1)}, u32[]{:S(2)}, u32[]{:S(2)}) collective-permute-start(bf16[96,3072]{1,0:T(8,128)(2,1)} %collective-permute-done.8.refs_8_), channel_id=1, source_target_pairs={{0,16},{16,0},{1,17},{17,1},{2,18},{18,2},{3,19},{19,3},{4,20},{20... | collective-permute-start | bytes 1769480 | tf_op jit(solution)/shard_map/ppermute | solution.py:27
  95.8 8.7 %collective-permute-start.12 = (bf16[96,3072]{1,0:T(8,128)(2,1)}, bf16[96,3072]{1,0:T(8,128)(2,1)}, u32[]{:S(2)}, u32[]{:S(2)}) collective-permute-start(bf16[96,3072]{1,0:T(8,128)(2,1)} %shard_map.59.refs_2_), channel_id=1, source_target_pairs={{0,1},{1,0},{2,3},{3,2},{4,5},{5,4},{6,7},{7,6},{8,9},{9,8},{10,11... | collective-permute-start | bytes 1769480 | tf_op jit(solution)/shard_map/ppermute | solution.py:23
  98.0 6.5 %collective-permute-start.9 = (bf16[192,3072]{1,0:T(8,128)(2,1)}, bf16[192,3072]{1,0:T(8,128)(2,1)}, u32[]{:S(2)}, u32[]{:S(2)}) collective-permute-start(bf16[192,3072]{1,0:T(8,128)(2,1)} %shard_map.57.refs_0_), channel_id=1, source_target_pairs={{0,1},{1,0},{2,3},{3,2},{4,5},{5,4},{6,7},{7,6},{8,9},{9,8},{10,11... | collective-permute-start | bytes 3538952 | tf_op jit(solution)/shard_map/ppermute | solution.py:23
  102.6 4.3 %collective-permute-start.16 = (bf16[96,3072]{1,0:T(8,128)(2,1)}, bf16[96,3072]{1,0:T(8,128)(2,1)}, u32[]{:S(2)}, u32[]{:S(2)}) collective-permute-start(bf16[96,3072]{1,0:T(8,128)(2,1)} %collective-permute-done.15.refs_6_), channel_id=1, source_target_pairs={{0,1},{1,0},{2,3},{3,2},{4,5},{5,4},{6,7},{7,6},{8,9},{9,8},{10,11... | collective-permute-start | bytes 1769480 | tf_op jit(solution)/shard_map/ppermute | solution.py:23
  104.5 2.8 %collective-permute-start.17 = (bf16[96,3072]{1,0:T(8,128)(2,1)}, bf16[96,3072]{1,0:T(8,128)(2,1)}, u32[]{:S(2)}, u32[]{:S(2)}) collective-permute-start(bf16[96,3072]{1,0:T(8,128)(2,1)} %collective-permute-done.8.refs_8_), channel_id=1, source_target_pairs={{0,1},{1,0},{2,3},{3,2},{4,5},{5,4},{6,7},{7,6},{8,9},{9,8},{10,11... | collective-permute-start | bytes 1769480 | tf_op jit(solution)/shard_map/ppermute | solution.py:23
  104.6 3.6 %collective-permute-start.19 = (bf16[96,3072]{1,0:T(8,128)(2,1)}, bf16[96,3072]{1,0:T(8,128)(2,1)}, u32[]{:S(2)}, u32[]{:S(2)}) collective-permute-start(bf16[96,3072]{1,0:T(8,128)(2,1)} %collective-permute-done.18.refs_10_), channel_id=1, source_target_pairs={{0,1},{1,0},{2,3},{3,2},{4,5},{5,4},{6,7},{7,6},{8,9},{9,8},{10,11... | collective-permute-start | bytes 1769480 | tf_op jit(solution)/shard_map/ppermute | solution.py:23
  105.1 4.8 %collective-permute-start.14 = (bf16[192,3072]{1,0:T(8,128)(2,1)}, bf16[192,3072]{1,0:T(8,128)(2,1)}, u32[]{:S(2)}, u32[]{:S(2)}) collective-permute-start(bf16[192,3072]{1,0:T(8,128)(2,1)} %collective-permute-done.13.refs_4_), channel_id=1, source_target_pairs={{0,1},{1,0},{2,3},{3,2},{4,5},{5,4},{6,7},{7,6},{8,9},{9,8},{10,11... | collective-permute-start | bytes 3538952 | tf_op jit(solution)/shard_map/ppermute | solution.py:23

commit v8 on v7

--- a/solution.py
+++ b/solution.py
@@ -14,7 +14,8 @@
 EXTRA = 16
 PIECES = 3
 LOG2E = math.log2(math.e)
-VMEM_BYTES = 48 * 1024 * 1024
+MIB = 1024 * 1024
+VMEM_BYTES = 48 * MIB
 WEIGHTY = 10**12
 
 
@@ -66,7 +67,7 @@
         out_specs=pl.BlockSpec(memory_space=pltpu.VMEM),
         out_shape=jax.ShapeDtypeStruct((rows, arrays[0].shape[1]), arrays[0].dtype),
         scratch_shapes=[pltpu.SemaphoreType.DMA((len(arrays),))],
-        compiler_params=pltpu.CompilerParams(vmem_limit_bytes=VMEM_BYTES),
+        compiler_params=pltpu.CompilerParams(vmem_limit_bytes=8 * MIB),
         cost_estimate=pl.CostEstimate(flops=cost, bytes_accessed=0, transcendentals=0),
     )(*arrays)
 
@@ -166,23 +167,17 @@
         ],
         out_specs=pl.BlockSpec((rows + EXTRA, width), lambda i: (0, i)),
         out_shape=jax.ShapeDtypeStruct((rows + EXTRA, heads * HD), kind),
-        compiler_params=pltpu.CompilerParams(vmem_limit_bytes=VMEM_BYTES),
+        compiler_params=pltpu.CompilerParams(vmem_limit_bytes=12 * MIB),
         cost_estimate=pl.CostEstimate(
             flops=cost, bytes_accessed=0, transcendentals=0
         ),
     )(lists, q, keys, kv_up, kv_down, values, kv_up, kv_down)
 
 
-def merge_kernel(rows, count, partner_ref, *refs):
-    parts, refs = refs[:count], refs[count:]
-    attention = refs[-1]
-    first = 0
-    if len(refs) > 1:
-        first = refs[0].shape[1]
-        attention[:, :first] = refs[0][...]
+def merge_parts(rows, parts, partner_ref, attention):
     per_block = rows // HD
     width = per_block * HD
-    for block in range((attention.shape[1] - first) // width):
+    for block in range(attention.shape[1] // width):
         tiles = []
         for part in parts:
             tiles.append(part[:, block * width : (block + 1) * width].astype(jnp.float32))
@@ -212,83 +207,104 @@
                     for n, t in enumerate(tiles)
                 ],
             )
-            start = first + block * width + head * HD
+            start = block * width + head * HD
             attention[:, start : start + HD] = mixed.astype(jnp.bfloat16)
 
 
-def merge(partner, parts, width, merged=None):
-    rows = parts[0].shape[0] - EXTRA
+def merge_kernel(rows, partner_ref, *refs):
+    merge_parts(rows, refs[:-1], partner_ref, refs[-1])
+
+
+def merge(partner, parts):
+    rows, columns = parts[0].shape[0] - EXTRA, parts[0].shape[1]
     vmem = pl.BlockSpec(memory_space=pltpu.VMEM)
-    before = [] if merged is None else [merged]
-    total = width + sum(array.shape[1] for array in before)
-    return pl.pallas_call(
-        functools.partial(merge_kernel, rows, len(parts)),
-        in_specs=[pl.BlockSpec(memory_space=pltpu.SMEM)] + [vmem] * (len(parts) + len(before)),
-        out_specs=vmem,
-        out_shape=jax.ShapeDtypeStruct((rows, total), jnp.bfloat16),
-        compiler_params=pltpu.CompilerParams(vmem_limit_bytes=VMEM_BYTES),
-        cost_estimate=pl.CostEstimate(flops=WEIGHTY, bytes_accessed=0, transcendentals=0),
-    )(partner, *parts, *before)
-
-
-def project_kernel(plan, steps, *refs):
-    weights = refs[: len(plan)]
-    attention, out_ref, held, total, sems = refs[len(plan) :]
-    moves = [(source, move) for source, moves in zip(weights, plan) for move in moves]
-    copies = []
-    for step in range(len(steps)):
-        for source, (from_row, count, place, wanted) in moves:
-            if wanted == step:
-                into = pl.multiple_of(place(), 16)
-                copy = pltpu.make_async_copy(
-                    source.at[pl.ds(from_row, count), :],
-                    held.at[pl.ds(into, count), :],
-                    sems.at[len(copies)],
-                )
-                copy.start()
-                copies.append((step, copy))
-    columns = out_ref.shape[1]
-    width = math.gcd(columns, 512)
-    depth = attention.shape[1] // len(steps)
-    for step, place in enumerate(steps):
-        for wanted, copy in copies:
-            if wanted == step:
-                copy.wait()
-        base = pl.multiple_of(place(), HD)
-        features = attention[:, pl.ds(base, depth)]
-
-        @pl.loop(0, columns // width)
-        def _(i):
-            there = pl.ds(pl.multiple_of(i * width, width), width)
-            sums = jnp.dot(
-                features, held[pl.ds(base, depth), there], preferred_element_type=jnp.float32
-            )
-            if step:
-                sums += total[:, there]
-            if step + 1 < len(steps):
-                total[:, there] = sums
-            else:
-                out_ref[:, there] = sums.astype(out_ref.dtype)
-
-
-def project(pieces, steps, attention):
-    arrays = [array for array, _ in pieces]
-    plan = [moves for _, moves in pieces]
-    rows, features = attention.shape
-    columns = arrays[0].shape[1]
-    vmem = pl.BlockSpec(memory_space=pltpu.VMEM)
-    return pl.pallas_call(
-        functools.partial(project_kernel, plan, steps),
-        in_specs=[pl.BlockSpec(memory_space=pl.ANY)] * len(arrays) + [vmem],
+    return pl.pallas_call(
+        functools.partial(merge_kernel, rows),
+        in_specs=[pl.BlockSpec(memory_space=pltpu.SMEM)] + [vmem] * len(parts),
         out_specs=vmem,
         out_shape=jax.ShapeDtypeStruct((rows, columns), jnp.bfloat16),
+        compiler_params=pltpu.CompilerParams(vmem_limit_bytes=8 * MIB),
+        cost_estimate=pl.CostEstimate(flops=WEIGHTY, bytes_accessed=0, transcendentals=0),
+    )(partner, *parts)
+
+
+def bring(plan, sources, held, sems):
+    copies = []
+    for source, moves in zip(sources, plan):
+        for from_row, size, place, _ in moves:
+            copy = pltpu.make_async_copy(
+                source.at[pl.ds(from_row, size), :],
+                held.at[pl.ds(pl.multiple_of(place(), 16), size), :],
+                sems.at[len(copies)],
+            )
+            copy.start()
+            copies.append(copy)
+    return copies
+
+
+def load_kernel(plan, *refs):
+    sources, (_, held, sems) = refs[: len(plan)], refs[len(plan) :]
+    copies = bring(plan, sources, held, sems)
+    for copy in copies:
+        copy.wait()
+
+
+def load(pieces, features, merged):
+    arrays, plan = zip(*pieces)
+    vmem = pl.BlockSpec(memory_space=pltpu.VMEM)
+    return pl.pallas_call(
+        functools.partial(load_kernel, plan),
+        in_specs=[pl.BlockSpec(memory_space=pl.ANY)] * (len(arrays) + 1),
+        out_specs=vmem,
+        out_shape=jax.ShapeDtypeStruct((features, arrays[0].shape[1]), arrays[0].dtype),
+        scratch_shapes=[pltpu.SemaphoreType.DMA((sum(len(m) for m in plan),))],
+        compiler_params=pltpu.CompilerParams(vmem_limit_bytes=16 * MIB),
+        cost_estimate=pl.CostEstimate(flops=WEIGHTY, bytes_accessed=0, transcendentals=0),
+    )(*arrays, merged)
+
+
+def project_kernel(plan, count, partner_ref, *refs):
+    sources, refs = refs[: len(plan)], refs[len(plan) :]
+    parts, (merged, _, out_ref, held, attention, sems) = refs[:count], refs[count:]
+    copies = bring(plan, sources, held, sems)
+    first = merged.shape[1]
+    attention[:, :first] = merged[...]
+    merge_parts(attention.shape[0], parts, partner_ref, attention.at[:, first:])
+    for copy in copies:
+        copy.wait()
+    columns = out_ref.shape[1]
+    width = math.gcd(columns, 1024)
+
+    @pl.loop(0, columns // width)
+    def _(i):
+        there = pl.ds(pl.multiple_of(i * width, width), width)
+        out_ref[:, there] = jnp.dot(
+            attention[...], held[:, there], preferred_element_type=jnp.float32
+        ).astype(out_ref.dtype)
+
+
+def project(pieces, held, partner, parts, merged):
+    arrays, plan = zip(*pieces) if pieces else ((), ())
+    rows, (features, columns) = merged.shape[0], held.shape
+    vmem = pl.BlockSpec(memory_space=pltpu.VMEM)
+    given = len(arrays) + len(parts)
+    return pl.pallas_call(
+        functools.partial(project_kernel, plan, len(parts)),
+        in_specs=[pl.BlockSpec(memory_space=pltpu.SMEM)]
+        + [pl.BlockSpec(memory_space=pl.ANY)] * len(arrays)
+        + [vmem] * (len(parts) + 2),
+        out_specs=(vmem, vmem),
+        out_shape=(
+            jax.ShapeDtypeStruct((rows, columns), jnp.bfloat16),
+            jax.ShapeDtypeStruct(held.shape, held.dtype),
+        ),
+        input_output_aliases={given + 2: 1},
         scratch_shapes=[
-            pltpu.VMEM((features, columns), jnp.bfloat16),
-            pltpu.VMEM((rows, columns), jnp.float32),
-            pltpu.SemaphoreType.DMA((sum(len(m) for m in plan),)),
+            pltpu.VMEM((rows, features), jnp.bfloat16),
+            pltpu.SemaphoreType.DMA((max(1, sum(len(m) for m in plan)),)),
         ],
-        compiler_params=pltpu.CompilerParams(vmem_limit_bytes=VMEM_BYTES),
-    )(*arrays, attention)
+        compiler_params=pltpu.CompilerParams(vmem_limit_bytes=28 * MIB),
+    )(partner, *arrays, *parts, merged, held)[0]
 
 
 def after(value, *done):
@@ -336,19 +352,21 @@
         first = lax.axis_index("group") * cube.half
         mine = lax.dynamic_slice_in_dim(out_weight, first, cube.half, 0)
         mz = swap_bit(mine, 4)
+        my = swap_bit(mine, 2)
         c0 = swap_bit(mine, 8)
     lists = jnp.pad(
         block_list.astype(jnp.bfloat16),
         ((0, EXTRA - FRAMES), (0, HD - block_list.shape[1])),
         constant_values=-1,
     )
-    asking = jnp.concatenate([query_rows[:, :chunk], jnp.tile(lists, (1, chunk_heads))], axis=0)
-    ahead = [asking] + ([mine] if cube else [])
+    ahead = [mine] if cube else []
     kv = join(after(key_rows, *ahead), value_rows, cost=WEIGHTY).reshape(2, rows, features)
     kv_up = column_shift(kv, 1)
     kv_down = column_shift(kv, -1)
     if cube:
-        mz = fence(after(mz, kv))
+        mz = fence(after(mz, kv, my))
+    asking = after(query_rows, kv, *([mz, my] if cube else []))[:, :chunk]
+    asking = jnp.concatenate([asking, jnp.tile(lists, (1, chunk_heads))], axis=0)
     sent = []
     for parity in phases:
         pairs = row_pairs(parity)
@@ -359,9 +377,11 @@
             c0 = after(c0, mz)
             cz = swap_bit(c0, 4)
             first = after(first, c0)
-            x0 = swap_group(mz, groups)
-            near = join(out_weight, mz, x0)
-            wy = swap_bit(near, 2)
+            near = join(mz, my, c0, cost=WEIGHTY)
+            x0 = swap_group(near, groups)
+            second = after(second, near)
+            pair = join(mz, after(c0, first))
+            y1 = swap_bit(pair, 2)
         sent.append([first, lax.ppermute(second, "seq", pairs)])
     common = (key_rows, value_rows, kv_up, kv_down)
     others = []
@@ -369,18 +389,20 @@
         back = []
         for number, q in enumerate(asked):
             if number:
-                q = after(q, part, far) if cube else after(q, part)
+                q = after(q, part, cz) if cube else after(q, part)
             part = attend(asked[0], q, 0, chunk_heads, *common, number * chunk_heads, jnp.bfloat16)
             if cube and not number:
-                far = join(c0, after(cz, part))
-                cy = swap_bit(far, 2)
-                x1 = swap_group(far, groups)
+                cz = after(cz, part)
+                cy = swap_bit(cz, 2)
+                x1 = swap_group(cz, groups)
             back.append(lax.ppermute(part, "seq", row_pairs(parity)))
             last = part
         others.append(back)
     if cube:
-        cy = after(cy, last)
-        x2 = swap_group(cy, groups)
+        y1, cy = after(y1, last), after(cy, last)
+        x2 = swap_group(y1, groups)
+        x3 = swap_group(cy, groups)
+        base = join(out_weight, near, after(x0, last), cz, after(x1, last))
     own = []
     for number in range(2):
         q, begin = query_rows, number * chunk_heads
@@ -394,30 +416,21 @@
         ]
         or [jnp.int32(0)]
     )
-    attention = merge(partner, [own[0]] + [b[0] for b in others], chunk)
-    attention = merge(partner, [own[1]] + [b[1] for b in others], features - chunk, attention)
+    runs = [[own[n]] + [back[n] for back in others] for n in range(2)]
+    merged = merge(partner, runs[0])
     if cube:
-        spread = [
-            (near, [(0, None), (4, 0), (4, 1)]),
-            (far, [(8, 0), (12, 0)]),
-            (wy, [(2, None), (6, 0), (6, 1)]),
-            (x1, [(8, 1), (12, 1)]),
-            (cy, [(10, 0), (14, 0)]),
-            (x2, [(10, 1), (14, 1)]),
-        ]
-        landed = []
-        for number, (array, _) in enumerate(spread):
-            ready = after(array, own[1], *(landed[:2] if number in (2, 5) else []))
-            landed.append(swap_bit(ready, 1))
-        landed = [after(array, attention) for array in landed]
-        for (array, places), turned in zip(spread, landed):
+        tail = join(y1, after(x2, own[1]), cy, x3)
+        at_base = [(0, None), (4, 0), (2, 0), (8, 0), (4, 1), (2, 1), (8, 1), (12, 0), (12, 1)]
+        at_tail = [(6, 0), (10, 0), (6, 1), (10, 1), (14, 0), (14, 1)]
+        for array, places in ((base, at_base), (tail, at_tail)):
             cube.add(array, *places)
-            cube.add(turned, *[(bit ^ 1, turn) for bit, turn in places])
-        pieces, steps = cube.list, cube.steps()
+            cube.add(swap_bit(array, 1), *[(bit ^ 1, turn) for bit, turn in places])
+        pieces = cube.list
     else:
         gathered = lax.all_gather(out_weight, "seq", axis=0, tiled=True)
-        pieces, steps = [(gathered, [(0, gathered.shape[0], lambda: 0, 0)])], [lambda: 0]
-    return project(pieces, steps, attention)
+        pieces = [(gathered, [(0, gathered.shape[0], lambda: 0, 0)])]
+    held = load(pieces[:2], features, merged)
+    return project(pieces[2:], held, partner, runs[1], merged)
 
 
 def solution(mesh):

time: 119 us -> 113 us (0.950)
  the two profiles are of different devices: /device:TPU:0 before, /device:TPU:7 now
where the time goes in v8:
time: 113 us
  Pallas kernels  49.6 us (44%)
  starting transfers between devices  29.6 us (26%)
  waiting for transfers between devices  25.5 us (23%)
  local copies, waits for them, and re-layouts  6.93 us (6%)
    pallas_call x4, Pallas kernels, attend(): pl.pallas_call(functools.partial(attend_kernel, rows, per_block), grid=(h...  24.7 us
    ppermute x1, waiting for transfers between devices, body(): first = lax.ppermute(asking, 'seq', pairs)  23.8 us
    ppermute x8, starting transfers between devices, swap_bit(): return lax.ppermute(value, 'seq', [(s, s ^ bit) for s in range(count)])  13.8 us
    pallas_call x5, Pallas kernels, join(): pl.pallas_call(functools.partial(join_kernel, len(arrays)), in_specs=[pl....  11.3 us
    pallas_call x1, Pallas kernels, project(): pl.pallas_call(functools.partial(project_kernel, plan, len(parts)), in_sp...  7.33 us
    ppermute x2, starting transfers between devices, column_shift(): return lax.ppermute(value, 'seq', pairs)  6.46 us
    unnamed x25, local copies, waits for them, and re-layouts  4.44 us
    ppermute x2, starting transfers between devices, body(): back.append(lax.ppermute(part, 'seq', row_pairs(parity)))  2.98 us
  transfers between devices with their start and end apart: 18, of which 4 were waited for; matrix products, arithmetic and copies ran while one was open for 2% of the time, Pallas kernels for 38%

profile of v8, /device:TPU:7, one launch (start us, length us, event | category | flops | bytes accessed | tf_op | source)
XLA Modules:
  0.0 112.7 jit_solution(7541251460351465313)
XLA Ops:
  0.0 1.7 %constant_dynamic-slice_fusion = bf16[48,3072]{1,0:T(8,128)(2,1)} fusion(bf16[96,3072]{1,0:T(8,128)(2,1)} %refs_0_.2, s32[]{:T(128)S(6)} %select_n.21), kind=kLoop, calls=%fused_computation.2 | loop fusion | bytes 589828 | tf_op jit(solution)/shard_map/dynamic_slice | solution.py:353
  1.7 2.3 %collective-permute-start.2 = (bf16[48,3072]{1,0:T(8,128)(2,1)}, bf16[48,3072]{1,0:T(8,128)(2,1)}, u32[]{:S(2)}, u32[]{:S(2)}) collective-permute-start(bf16[48,3072]{1,0:T(8,128)(2,1)} %constant_dynamic-slice_fusion), channel_id=1, source_target_pairs={{0,8},{1,9},{2,10},{3,11},{4,12},{5,13},{6,14},{7,15},{8,0},{9,1},... | collective-permute-start | bytes 884744 | tf_op jit(solution)/shard_map/ppermute | solution.py:24
  4.0 0.2 collective-permute-start.1
  4.2 1.3 %collective-permute-start = (bf16[48,3072]{1,0:T(8,128)(2,1)}, bf16[48,3072]{1,0:T(8,128)(2,1)}, u32[]{:S(2)}, u32[]{:S(2)}) collective-permute-start(bf16[48,3072]{1,0:T(8,128)(2,1)} %constant_dynamic-slice_fusion), channel_id=1, source_target_pairs={{0,4},{1,5},{2,6},{3,7},{4,0},{5,1},{6,2},{7,3},{8,12},{9,13},{10,... | collective-permute-start | bytes 884744 | tf_op jit(solution)/shard_map/ppermute | solution.py:24
  5.5 1.1 %copy-done.2 = bf16[256,1536]{1,0:T(8,128)(2,1)S(1)} copy-done((bf16[256,1536]{1,0:T(8,128)(2,1)S(1)}, bf16[256,1536]{1,0:T(8,128)(2,1)}, u32[]{:S(2)}) %copy-start.2) | copy-done | bytes 786456
  6.7 1.1 %copy-done.4 = bf16[256,1536]{1,0:T(8,128)(2,1)S(1)} copy-done((bf16[256,1536]{1,0:T(8,128)(2,1)S(1)}, bf16[256,1536]{1,0:T(8,128)(2,1)}, u32[]{:S(2)}) %copy-start.4) | copy-done | bytes 786456
  7.8 1.3 %shard_map.55 = bf16[512,1536]{1,0:T(8,128)(2,1)} custom-call(bf16[256,1536]{1,0:T(8,128)(2,1)S(1)} %copy-done.2, bf16[256,1536]{1,0:T(8,128)(2,1)S(1)} %copy-done.4), custom_call_target="tpu_custom_call" | custom-call | flops 999999995904 | tf_op jit(solution)/shard_map/pallas_call | solution.py:64
  9.1 3.4 %collective-permute-start.7 = (bf16[2,256,1536]{2,1,0:T(8,128)(2,1)}, bf16[2,256,1536]{2,1,0:T(8,128)(2,1)}, u32[]{:S(2)}, u32[]{:S(2)}) collective-permute-start(bf16[2,256,1536]{2,1,0:T(8,128)(2,1)} %bitcast.1), channel_id=1, source_target_pairs={{1,0},{2,1},{3,2},{4,3},{5,4},{6,5},{7,6},{9,8},{10,9},{11,10},{12... | collective-permute-start | bytes 4718600 | tf_op jit(solution)/shard_map/ppermute | solution.py:34
  12.5 3.0 %collective-permute-start.6 = (bf16[2,256,1536]{2,1,0:T(8,128)(2,1)}, bf16[2,256,1536]{2,1,0:T(8,128)(2,1)}, u32[]{:S(2)}, u32[]{:S(2)}) collective-permute-start(bf16[2,256,1536]{2,1,0:T(8,128)(2,1)} %bitcast.1), channel_id=1, source_target_pairs={{0,1},{1,2},{2,3},{3,4},{4,5},{5,6},{6,7},{8,9},{9,10},{10,11},{11... | collective-permute-start | bytes 4718600 | tf_op jit(solution)/shard_map/ppermute | solution.py:34
  15.7 0.6 copy-done.8
  16.2 0.6 copy.9
  16.9 0.8 slice.7
  17.6 0.0 collective-permute-done.in_ref
  17.6 1.7 %shard_map.56.refs_0_ = bf16[48,3072]{1,0:T(8,128)(2,1)} custom-call(bf16[48,3072]{1,0:T(8,128)(2,1)} %collective-permute-done.in_ref), custom_call_target="tpu_custom_call" | custom-call | flops 999999995904 | tf_op jit(solution)/shard_map/pallas_call | solution.py:81
  19.4 0.0 collective-permute-done.2.refs_1_.refs_2_
  19.4 0.9 collective-permute-start.8
  20.3 0.8 pad_maximum_fusion
  21.1 1.4 %collective-permute-start.3 = (bf16[272,768]{1,0:T(8,128)(2,1)}, bf16[272,768]{1,0:T(8,128)(2,1)}, u32[]{:S(2)}, u32[]{:S(2)}) collective-permute-start(bf16[272,768]{1,0:T(8,128)(2,1)} %pad_maximum_fusion), channel_id=1, source_target_pairs={{0,8},{1,9},{2,10},{3,11},{4,12},{5,13},{6,14},{7,15},{8,0},{9,1},... | collective-permute-start | bytes 1253384 | tf_op jit(solution)/shard_map/ppermute | solution.py:373
  22.5 1.0 copy-done.7
  23.5 2.2 %shard_map.58.refs_1_ = bf16[144,3072]{1,0:T(8,128)(2,1)} custom-call(bf16[48,3072]{1,0:T(8,128)(2,1)S(1)} %copy-done.7, bf16[48,3072]{1,0:T(8,128)(2,1)} %collective-permute-done.1.refs_1_, bf16[48,3072]{1,0:T(8,128)(2,1)} %collective-permute-done.2.refs_1_.refs_2_), custom_call_target="tpu_custom_call" | custom-call | flops 999999995904 | tf_op jit(solution)/shard_map/pallas_call | solution.py:64
  25.7 0.3 collective-permute-start.15
  26.0 23.8 %collective-permute-done.3.list_ref.q_ref = bf16[272,768]{1,0:T(8,128)(2,1)} collective-permute-done((bf16[272,768]{1,0:T(8,128)(2,1)}, bf16[272,768]{1,0:T(8,128)(2,1)}, u32[]{:S(2)}, u32[]{:S(2)}) %collective-permute-start.3) | collective-permute-done | bytes 417824 | tf_op jit(solution)/shard_map/ppermute | solution.py:373
  49.7 1.9 %shard_map.57 = bf16[96,3072]{1,0:T(8,128)(2,1)} custom-call(bf16[48,3072]{1,0:T(8,128)(2,1)S(1)} %copy-done.7, bf16[48,3072]{1,0:T(8,128)(2,1)} %collective-permute-done.2.refs_1_.refs_2_), custom_call_target="tpu_custom_call" | custom-call | tf_op jit(solution)/shard_map/pallas_call | solution.py:64
  51.6 2.9 %collective-permute-start.5 = (bf16[256,768]{1,0:T(8,128)(2,1)}, bf16[256,768]{1,0:T(8,128)(2,1)}, u32[]{:S(2)}, u32[]{:S(2)}) collective-permute-start(bf16[256,768]{1,0:T(8,128)(2,1)} %slice.7), channel_id=1, source_target_pairs={{0,8},{1,9},{2,10},{3,11},{4,12},{5,13},{6,14},{7,15},{8,0},{9,1},... | collective-permute-start | bytes 1179656 | tf_op jit(solution)/shard_map/ppermute | solution.py:385
  54.5 0.1 collective-permute-done.7.kb.vb
  54.6 0.0 collective-permute-start.4
  54.6 0.0 collective-permute-done.6.ka.va
  54.6 6.5 %shard_map.59 = bf16[272,768]{1,0:T(8,128)(2,1)} custom-call(bf16[272,768]{1,0:T(8,128)(2,1)} %collective-permute-done.3.list_ref.q_ref, bf16[272,768]{1,0:T(8,128)(2,1)} %collective-permute-done.3.list_ref.q_ref, bf16[256,1536]{1,0:T(8,128)(2,1)S(1)} %copy-done.3, bf16[2,256,1536]{2,1,0:T(8,128)(2,1)} %collective-permute-done.6.ka.va, ...), custom_call_target="tpu_custom_call" | custom-call | flops 999999995904 | tf_op jit(solution)/shard_map/pallas_call | solution.py:155
  61.1 0.0 collective-permute-done.8.refs_3_
  61.1 0.2 collective-permute-start.16
  61.3 1.4 %collective-permute-start.10 = (bf16[48,3072]{1,0:T(8,128)(2,1)}, bf16[48,3072]{1,0:T(8,128)(2,1)}, u32[]{:S(2)}, u32[]{:S(2)}) collective-permute-start(bf16[48,3072]{1,0:T(8,128)(2,1)} %collective-permute-done.8.refs_3_), channel_id=1, source_target_pairs={{0,2},{1,3},{2,0},{3,1},{4,6},{5,7},{6,4},{7,5},{8,10},{9,11},{10,... | collective-permute-start | bytes 884744 | tf_op jit(solution)/shard_map/ppermute | solution.py:24
  62.8 0.4 collective-permute-done.5.q_ref
  63.2 2.9 %collective-permute-start.14 = (bf16[272,768]{1,0:T(8,128)(2,1)}, bf16[272,768]{1,0:T(8,128)(2,1)}, u32[]{:S(2)}, u32[]{:S(2)}) collective-permute-start(bf16[272,768]{1,0:T(8,128)(2,1)} %shard_map.59), channel_id=1, source_target_pairs={{0,8},{1,9},{2,10},{3,11},{4,12},{5,13},{6,14},{7,15},{8,0},{9,1},... | collective-permute-start | bytes 1253384 | tf_op jit(solution)/shard_map/ppermute | solution.py:398
  66.1 6.5 %shard_map.60 = bf16[272,768]{1,0:T(8,128)(2,1)} custom-call(bf16[272,768]{1,0:T(8,128)(2,1)} %collective-permute-done.3.list_ref.q_ref, bf16[256,768]{1,0:T(8,128)(2,1)} %collective-permute-done.5.q_ref, bf16[256,1536]{1,0:T(8,128)(2,1)S(1)} %copy-done.3, bf16[2,256,1536]{2,1,0:T(8,128)(2,1)} %collective-permute-done.6.ka.va, ...), custom_call_target="tpu_custom_call" | custom-call | flops 999999995904 | tf_op jit(solution)/shard_map/pallas_call | solution.py:155
  72.7 0.0 collective-permute-done.15.refs_2_
  72.7 0.1 collective-permute-start.13
  72.8 0.3 collective-permute-start.9
  73.0 5.9 %shard_map.61.refs_0_ = f32[272,768]{1,0:T(8,128)S(1)} custom-call(bf16[16,128]{1,0:T(8,128)(2,1)S(1)} %copy-done.9, bf16[256,1536]{1,0:T(8,128)(2,1)S(1)} %copy-done.1, bf16[256,1536]{1,0:T(8,128)(2,1)S(1)} %copy-done.3, bf16[2,256,1536]{2,1,0:T(8,128)(2,1)} %collective-permute-done.6.ka.va, bf16[2,256,1536]{2,1,0:T(8,128)(2,1)} %collective-permute-done.7.kb.vb, ...), custom_call_target="tpu_custom_call" | custom-call | tf_op jit(solution)/shard_map/pallas_call | solution.py:155
  78.9 1.3 %collective-permute-start.11 = (bf16[48,3072]{1,0:T(8,128)(2,1)}, bf16[48,3072]{1,0:T(8,128)(2,1)}, u32[]{:S(2)}, u32[]{:S(2)}) collective-permute-start(bf16[48,3072]{1,0:T(8,128)(2,1)} %collective-permute-done.10.refs_2_), channel_id=1, source_target_pairs={{0,16},{16,0},{1,17},{17,1},{2,18},{18,2},{3,19},{19,3},{4,20},{20... | collective-permute-start | bytes 884744 | tf_op jit(solution)/shard_map/ppermute | solution.py:28
  80.2 3.3 %shard_map.65.refs_0_ = bf16[480,3072]{1,0:T(8,128)(2,1)} custom-call(bf16[96,3072]{1,0:T(8,128)(2,1)S(1)} %copy-done.6, bf16[144,3072]{1,0:T(8,128)(2,1)} %shard_map.58.refs_1_, bf16[144,3072]{1,0:T(8,128)(2,1)} %collective-permute-done.15.refs_2_, bf16[48,3072]{1,0:T(8,128)(2,1)} %collective-permute-done.8.refs_3_, ...), custom_call_target="tpu_custom_call" | custom-call | tf_op jit(solution)/shard_map/pallas_call | solution.py:64
  83.6 7.5 %collective-permute-start.17 = (bf16[480,3072]{1,0:T(8,128)(2,1)}, bf16[480,3072]{1,0:T(8,128)(2,1)}, u32[]{:S(2)}, u32[]{:S(2)}) collective-permute-start(bf16[480,3072]{1,0:T(8,128)(2,1)} %shard_map.65.refs_0_), channel_id=1, source_target_pairs={{0,1},{1,0},{2,3},{3,2},{4,5},{5,4},{6,7},{7,6},{8,9},{9,8},{10,11... | collective-permute-start | bytes 8847368 | tf_op jit(solution)/shard_map/ppermute | solution.py:24
  91.1 5.8 %shard_map.62.refs_2_ = f32[272,768]{1,0:T(8,128)S(1)} custom-call(bf16[16,128]{1,0:T(8,128)(2,1)S(1)} %copy-done.9, bf16[256,1536]{1,0:T(8,128)(2,1)S(1)} %copy-done.1, bf16[256,1536]{1,0:T(8,128)(2,1)S(1)} %copy-done.3, bf16[2,256,1536]{2,1,0:T(8,128)(2,1)} %collective-permute-done.6.ka.va, bf16[2,256,1536]{2,1,0:T(8,128)(2,1)} %collective-permute-done.7.kb.vb, ...), custom_call_target="tpu_custom_call" | custom-call | tf_op jit(solution)/shard_map/pallas_call | solution.py:155
  96.9 1.7 %shard_map.64.refs_2_.refs_4_ = bf16[256,768]{1,0:T(8,128)(2,1)S(1)} custom-call(s32[1]{0:T(128)} %bitcast.partner_ref, f32[272,768]{1,0:T(8,128)S(1)} %shard_map.61.refs_0_, bf16[272,768]{1,0:T(8,128)(2,1)} %collective-permute-done.14.refs_1_), custom_call_target="tpu_custom_call" | custom-call | flops 999999995904 | tf_op jit(solution)/shard_map/pallas_call | solution.py:221
  98.7 2.6 %shard_map.63.refs_0_ = bf16[288,3072]{1,0:T(8,128)(2,1)} custom-call(bf16[96,3072]{1,0:T(8,128)(2,1)} %collective-permute-done.4.refs_0_, bf16[96,3072]{1,0:T(8,128)(2,1)} %collective-permute-done.9.refs_1_, bf16[48,3072]{1,0:T(8,128)(2,1)} %collective-permute-done.10.refs_2_, bf16[48,3072]{1,0:T(8,128)(2,1)} %collective-permute-done.11.refs_3_), custom_call_target="tpu_custom_call" | custom-call | tf_op jit(solution)/shard_map/pallas_call | solution.py:64
  101.3 0.1 collective-permute-start.12
  101.4 2.8 %shard_map.66.refs_5_ = bf16[1536,3072]{1,0:T(8,128)(2,1)S(1)} custom-call(bf16[480,3072]{1,0:T(8,128)(2,1)} %shard_map.65.refs_0_, bf16[480,3072]{1,0:T(8,128)(2,1)} %collective-permute-done.17.refs_1_, bf16[256,768]{1,0:T(8,128)(2,1)S(1)} %shard_map.64.refs_2_.refs_4_), custom_call_target="tpu_custom_call" | custom-call | flops 999999995904 | tf_op jit(solution)/shard_map/pallas_call | solution.py:255
  104.2 1.2 %collective-permute-done.12.refs_1_ = bf16[288,3072]{1,0:T(8,128)(2,1)} collective-permute-done((bf16[288,3072]{1,0:T(8,128)(2,1)}, bf16[288,3072]{1,0:T(8,128)(2,1)}, u32[]{:S(2)}, u32[]{:S(2)}) %collective-permute-start.12) | collective-permute-done | bytes 1769504 | tf_op jit(solution)/shard_map/ppermute | solution.py:24
  105.4 7.3 %shard_map.67 = (bf16[256,3072]{1,0:T(8,128)(2,1)}, bf16[1536,3072]{1,0:T(8,128)(2,1)S(1)}) custom-call(s32[1]{0:T(128)} %bitcast.partner_ref, bf16[288,3072]{1,0:T(8,128)(2,1)} %shard_map.63.refs_0_, bf16[288,3072]{1,0:T(8,128)(2,1)} %collective-permute-done.12.refs_1_, f32[272,768]{1,0:T(8,128)S(1)} %shard_map.62.refs_2_, ...), custom_call_target="tpu_custom_call", output_to_operand_aliasing={{1}: (6, {})} | custom-call | tf_op jit(solution)/shard_map/pallas_call | solution.py:291
  (34 shorter events, 0.1 us)
Async XLA Ops:
  1.7 17.7 %collective-permute-start.2 = (bf16[48,3072]{1,0:T(8,128)(2,1)}, bf16[48,3072]{1,0:T(8,128)(2,1)}, u32[]{:S(2)}, u32[]{:S(2)}) collective-permute-start(bf16[48,3072]{1,0:T(8,128)(2,1)} %constant_dynamic-slice_fusion), channel_id=1, source_target_pairs={{0,8},{1,9},{2,10},{3,11},{4,12},{5,13},{6,14},{7,15},{8,0},{9,1},... | collective-permute-start | bytes 884744 | tf_op jit(solution)/shard_map/ppermute | solution.py:24
  4.0 13.6 %collective-permute-start.1 = (bf16[48,3072]{1,0:T(8,128)(2,1)}, bf16[48,3072]{1,0:T(8,128)(2,1)}, u32[]{:S(2)}, u32[]{:S(2)}) collective-permute-start(bf16[48,3072]{1,0:T(8,128)(2,1)} %constant_dynamic-slice_fusion), channel_id=1, source_target_pairs={{0,2},{1,3},{2,0},{3,1},{4,6},{5,7},{6,4},{7,5},{8,10},{9,11},{10,... | collective-permute-start | bytes 884744 | tf_op jit(solution)/shard_map/ppermute | solution.py:24
  4.2 13.4 %collective-permute-start = (bf16[48,3072]{1,0:T(8,128)(2,1)}, bf16[48,3072]{1,0:T(8,128)(2,1)}, u32[]{:S(2)}, u32[]{:S(2)}) collective-permute-start(bf16[48,3072]{1,0:T(8,128)(2,1)} %constant_dynamic-slice_fusion), channel_id=1, source_target_pairs={{0,4},{1,5},{2,6},{3,7},{4,0},{5,1},{6,2},{7,3},{8,12},{9,13},{10,... | collective-permute-start | bytes 884744 | tf_op jit(solution)/shard_map/ppermute | solution.py:24
  5.5 1.1 %copy-start.2 = (bf16[256,1536]{1,0:T(8,128)(2,1)S(1)}, bf16[256,1536]{1,0:T(8,128)(2,1)}, u32[]{:S(2)}) copy-start(bf16[256,1536]{1,0:T(8,128)(2,1)} %k0.7) | copy-start | bytes 2359300
  6.7 1.1 %copy-start.4 = (bf16[256,1536]{1,0:T(8,128)(2,1)S(1)}, bf16[256,1536]{1,0:T(8,128)(2,1)}, u32[]{:S(2)}) copy-start(bf16[256,1536]{1,0:T(8,128)(2,1)} %v0.7) | copy-start | bytes 2359300
  7.8 7.8 %copy-start.11 = (s32[2,27]{1,0:T(2,128)S(1)}, s32[2,27]{1,0:T(2,128)}, u32[]{:S(2)}) copy-start(s32[2,27]{1,0:T(2,128)} %param.8) | copy-start | bytes 652
  7.8 9.0 %copy-start = (bf16[256,1536]{1,0:T(8,128)(2,1)S(1)}, bf16[256,1536]{1,0:T(8,128)(2,1)}, u32[]{:S(2)}) copy-start(bf16[256,1536]{1,0:T(8,128)(2,1)} %q_ref.1) | copy-start | bytes 2359300
  9.1 45.5 %collective-permute-start.7 = (bf16[2,256,1536]{2,1,0:T(8,128)(2,1)}, bf16[2,256,1536]{2,1,0:T(8,128)(2,1)}, u32[]{:S(2)}, u32[]{:S(2)}) collective-permute-start(bf16[2,256,1536]{2,1,0:T(8,128)(2,1)} %bitcast.1), channel_id=1, source_target_pairs={{1,0},{2,1},{3,2},{4,3},{5,4},{6,5},{7,6},{9,8},{10,9},{11,10},{12... | collective-permute-start | bytes 4718600 | tf_op jit(solution)/shard_map/ppermute | solution.py:34
  12.5 42.1 %collective-permute-start.6 = (bf16[2,256,1536]{2,1,0:T(8,128)(2,1)}, bf16[2,256,1536]{2,1,0:T(8,128)(2,1)}, u32[]{:S(2)}, u32[]{:S(2)}) collective-permute-start(bf16[2,256,1536]{2,1,0:T(8,128)(2,1)} %bitcast.1), channel_id=1, source_target_pairs={{0,1},{1,2},{2,3},{3,4},{4,5},{5,6},{6,7},{8,9},{9,10},{10,11},{11... | collective-permute-start | bytes 4718600 | tf_op jit(solution)/shard_map/ppermute | solution.py:34
  15.7 0.6 copy-start.8
  17.6 2.7 %slice-start = ((bf16[256,1536]{1,0:T(8,128)(2,1)}), bf16[256,768]{1,0:T(8,128)(2,1)S(1)}, s32[]{:S(2)}) async-start(bf16[256,1536]{1,0:T(8,128)(2,1)} %q_ref.1), calls=%async_computation | async-start | bytes 786432 | tf_op jit(solution)/shard_map/slice | solution.py:368
  17.6 2.7 %copy-start.10 = (bf16[2,8,6,128]{3,1,2,0:T(8,128)(2,1)S(1)}, bf16[2,8,6,128]{3,1,2,0:T(8,128)(2,1)}, u32[]{:S(2)}) copy-start(bf16[2,8,6,128]{3,1,2,0:T(8,128)(2,1)} %copy.9) | copy-start | bytes 73732
  19.4 41.7 %collective-permute-start.8 = (bf16[48,3072]{1,0:T(8,128)(2,1)}, bf16[48,3072]{1,0:T(8,128)(2,1)}, u32[]{:S(2)}, u32[]{:S(2)}) collective-permute-start(bf16[48,3072]{1,0:T(8,128)(2,1)} %collective-permute-done.2.refs_1_.refs_2_), channel_id=1, source_target_pairs={{0,4},{1,5},{2,6},{3,7},{4,0},{5,1},{6,2},{7,3},{8,12},{9,13},{10,... | collective-permute-start | bytes 884744 | tf_op jit(solution)/shard_map/ppermute | solution.py:24
  21.1 28.6 %collective-permute-start.3 = (bf16[272,768]{1,0:T(8,128)(2,1)}, bf16[272,768]{1,0:T(8,128)(2,1)}, u32[]{:S(2)}, u32[]{:S(2)}) collective-permute-start(bf16[272,768]{1,0:T(8,128)(2,1)} %pad_maximum_fusion), channel_id=1, source_target_pairs={{0,8},{1,9},{2,10},{3,11},{4,12},{5,13},{6,14},{7,15},{8,0},{9,1},... | collective-permute-start | bytes 1253384 | tf_op jit(solution)/shard_map/ppermute | solution.py:373
  22.5 1.0 copy-start.7
  23.5 31.1 %copy-start.3 = (bf16[256,1536]{1,0:T(8,128)(2,1)S(1)}, bf16[256,1536]{1,0:T(8,128)(2,1)}, u32[]{:S(2)}) copy-start(bf16[256,1536]{1,0:T(8,128)(2,1)} %k0.7) | copy-start | bytes 2359300
  23.5 31.1 %copy-start.5 = (bf16[256,1536]{1,0:T(8,128)(2,1)S(1)}, bf16[256,1536]{1,0:T(8,128)(2,1)}, u32[]{:S(2)}) copy-start(bf16[256,1536]{1,0:T(8,128)(2,1)} %v0.7) | copy-start | bytes 2359300
  25.7 47.0 %collective-permute-start.15 = (bf16[144,3072]{1,0:T(8,128)(2,1)}, bf16[144,3072]{1,0:T(8,128)(2,1)}, u32[]{:S(2)}, u32[]{:S(2)}) collective-permute-start(bf16[144,3072]{1,0:T(8,128)(2,1)} %shard_map.58.refs_1_), channel_id=1, source_target_pairs={{0,16},{16,0},{1,17},{17,1},{2,18},{18,2},{3,19},{19,3},{4,20},{20... | collective-permute-start | bytes 2654216 | tf_op jit(solution)/shard_map/ppermute | solution.py:28
  51.6 11.6 %collective-permute-start.5 = (bf16[256,768]{1,0:T(8,128)(2,1)}, bf16[256,768]{1,0:T(8,128)(2,1)}, u32[]{:S(2)}, u32[]{:S(2)}) collective-permute-start(bf16[256,768]{1,0:T(8,128)(2,1)} %slice.7), channel_id=1, source_target_pairs={{0,8},{1,9},{2,10},{3,11},{4,12},{5,13},{6,14},{7,15},{8,0},{9,1},... | collective-permute-start | bytes 1179656 | tf_op jit(solution)/shard_map/ppermute | solution.py:385
  54.6 18.2 %collective-permute-start.4 = (bf16[96,3072]{1,0:T(8,128)(2,1)}, bf16[96,3072]{1,0:T(8,128)(2,1)}, u32[]{:S(2)}, u32[]{:S(2)}) collective-permute-start(bf16[96,3072]{1,0:T(8,128)(2,1)} %shard_map.57), channel_id=1, source_target_pairs={{0,2},{1,3},{2,0},{3,1},{4,6},{5,7},{6,4},{7,5},{8,10},{9,11},{10,... | collective-permute-start | bytes 1769480 | tf_op jit(solution)/shard_map/ppermute | solution.py:24
  61.1 17.8 %collective-permute-start.16 = (bf16[48,3072]{1,0:T(8,128)(2,1)}, bf16[48,3072]{1,0:T(8,128)(2,1)}, u32[]{:S(2)}, u32[]{:S(2)}) collective-permute-start(bf16[48,3072]{1,0:T(8,128)(2,1)} %collective-permute-done.8.refs_3_), channel_id=1, source_target_pairs={{0,16},{16,0},{1,17},{17,1},{2,18},{18,2},{3,19},{19,3},{4,20},{20... | collective-permute-start | bytes 884744 | tf_op jit(solution)/shard_map/ppermute | solution.py:28
  61.3 17.6 %collective-permute-start.10 = (bf16[48,3072]{1,0:T(8,128)(2,1)}, bf16[48,3072]{1,0:T(8,128)(2,1)}, u32[]{:S(2)}, u32[]{:S(2)}) collective-permute-start(bf16[48,3072]{1,0:T(8,128)(2,1)} %collective-permute-done.8.refs_3_), channel_id=1, source_target_pairs={{0,2},{1,3},{2,0},{3,1},{4,6},{5,7},{6,4},{7,5},{8,10},{9,11},{10,... | collective-permute-start | bytes 884744 | tf_op jit(solution)/shard_map/ppermute | solution.py:24
  63.2 33.7 %collective-permute-start.14 = (bf16[272,768]{1,0:T(8,128)(2,1)}, bf16[272,768]{1,0:T(8,128)(2,1)}, u32[]{:S(2)}, u32[]{:S(2)}) collective-permute-start(bf16[272,768]{1,0:T(8,128)(2,1)} %shard_map.59), channel_id=1, source_target_pairs={{0,8},{1,9},{2,10},{3,11},{4,12},{5,13},{6,14},{7,15},{8,0},{9,1},... | collective-permute-start | bytes 1253384 | tf_op jit(solution)/shard_map/ppermute | solution.py:398
  66.1 6.9 %copy-start.1 = (bf16[256,1536]{1,0:T(8,128)(2,1)S(1)}, bf16[256,1536]{1,0:T(8,128)(2,1)}, u32[]{:S(2)}) copy-start(bf16[256,1536]{1,0:T(8,128)(2,1)} %q_ref.1) | copy-start | bytes 2359300
  66.1 6.9 %copy-start.9 = (bf16[16,128]{1,0:T(8,128)(2,1)S(1)}, bf16[16,128]{1,0:T(8,128)(2,1)}, u32[]{:S(2)}) copy-start(bf16[16,128]{1,0:T(8,128)(2,1)} %copy-done.8) | copy-start | bytes 12292
  72.7 7.6 %copy-start.6 = (bf16[96,3072]{1,0:T(8,128)(2,1)S(1)}, bf16[96,3072]{1,0:T(8,128)(2,1)}, u32[]{:S(2)}) copy-start(bf16[96,3072]{1,0:T(8,128)(2,1)} %refs_0_.2) | copy-start | bytes 1769476
  72.7 31.6 %collective-permute-start.13 = (bf16[272,768]{1,0:T(8,128)(2,1)}, bf16[272,768]{1,0:T(8,128)(2,1)}, u32[]{:S(2)}, u32[]{:S(2)}) collective-permute-start(bf16[272,768]{1,0:T(8,128)(2,1)} %shard_map.60), channel_id=1, source_target_pairs={{0,8},{1,9},{2,10},{3,11},{4,12},{5,13},{6,14},{7,15},{8,0},{9,1},... | collective-permute-start | bytes 1253384 | tf_op jit(solution)/shard_map/ppermute | solution.py:398
  72.8 25.9 %collective-permute-start.9 = (bf16[96,3072]{1,0:T(8,128)(2,1)}, bf16[96,3072]{1,0:T(8,128)(2,1)}, u32[]{:S(2)}, u32[]{:S(2)}) collective-permute-start(bf16[96,3072]{1,0:T(8,128)(2,1)} %collective-permute-done.4.refs_0_), channel_id=1, source_target_pairs={{0,16},{16,0},{1,17},{17,1},{2,18},{18,2},{3,19},{19,3},{4,20},{20... | collective-permute-start | bytes 1769480 | tf_op jit(solution)/shard_map/ppermute | solution.py:28
  78.9 19.7 %collective-permute-start.11 = (bf16[48,3072]{1,0:T(8,128)(2,1)}, bf16[48,3072]{1,0:T(8,128)(2,1)}, u32[]{:S(2)}, u32[]{:S(2)}) collective-permute-start(bf16[48,3072]{1,0:T(8,128)(2,1)} %collective-permute-done.10.refs_2_), channel_id=1, source_target_pairs={{0,16},{16,0},{1,17},{17,1},{2,18},{18,2},{3,19},{19,3},{4,20},{20... | collective-permute-start | bytes 884744 | tf_op jit(solution)/shard_map/ppermute | solution.py:28
  83.6 17.8 %collective-permute-start.17 = (bf16[480,3072]{1,0:T(8,128)(2,1)}, bf16[480,3072]{1,0:T(8,128)(2,1)}, u32[]{:S(2)}, u32[]{:S(2)}) collective-permute-start(bf16[480,3072]{1,0:T(8,128)(2,1)} %shard_map.65.refs_0_), channel_id=1, source_target_pairs={{0,1},{1,0},{2,3},{3,2},{4,5},{5,4},{6,7},{7,6},{8,9},{9,8},{10,11... | collective-permute-start | bytes 8847368 | tf_op jit(solution)/shard_map/ppermute | solution.py:24
  101.3 4.1 %collective-permute-start.12 = (bf16[288,3072]{1,0:T(8,128)(2,1)}, bf16[288,3072]{1,0:T(8,128)(2,1)}, u32[]{:S(2)}, u32[]{:S(2)}) collective-permute-start(bf16[288,3072]{1,0:T(8,128)(2,1)} %shard_map.63.refs_0_), channel_id=1, source_target_pairs={{0,1},{1,0},{2,3},{3,2},{4,5},{5,4},{6,7},{7,6},{8,9},{9,8},{10,11... | collective-permute-start | bytes 5308424 | tf_op jit(solution)/shard_map/ppermute | solution.py:24

commit v9 on v8

--- a/solution.py
+++ b/solution.py
@@ -76,14 +76,14 @@
     out_ref[...] = in_ref[...]
 
 
-def fence(value):
+def fence(value, cost=WEIGHTY):
     vmem = pl.BlockSpec(memory_space=pltpu.VMEM)
     return pl.pallas_call(
         fence_kernel,
         in_specs=[vmem],
         out_specs=vmem,
         out_shape=jax.ShapeDtypeStruct(value.shape, value.dtype),
-        cost_estimate=pl.CostEstimate(flops=WEIGHTY, bytes_accessed=0, transcendentals=0),
+        cost_estimate=pl.CostEstimate(flops=cost, bytes_accessed=0, transcendentals=0),
     )(value)
 
 
@@ -104,33 +104,35 @@
     nt = (((1,), (1,)), ((), ()))
     lse = jnp.zeros((rows, HD), jnp.float32)
     lane = lax.broadcasted_iota(jnp.int32, (rows, HD), 1)
-    for head in range(per_block):
-        cols = slice(head * HD, (head + 1) * HD)
+    frames = [slice(frame * tile, (frame + 1) * tile) for frame in range(FRAMES)]
+    heads = [slice(head * HD, (head + 1) * HD) for head in range(per_block)]
+    for head, cols in enumerate(heads):
         keys = [k0[:, cols], ka[0, :, cols], kb[0, :, cols]]
+        product = [
+            lax.dot_general(q_ref[:rows, cols], key, nt, preferred_element_type=jnp.float32)
+            for key in keys
+        ]
         values = [v0[:, cols], va[0, :, cols], vb[0, :, cols]]
-        parts = []
-        for frame in range(FRAMES):
-            here = slice(frame * tile, (frame + 1) * tile)
-            q = q_ref[here, cols]
-            scores = [
-                lax.dot_general(q, key, nt, preferred_element_type=jnp.float32)
-                + mask[frame : frame + 1, :]
-                for key, mask in zip(keys, masks)
-            ]
+        peaks, totals, probs = [], [], []
+        for frame, here in enumerate(frames):
+            scores = [s[here] + mask[frame : frame + 1, :] for s, mask in zip(product, masks)]
             peak = functools.reduce(jnp.maximum, scores)
             peak = jnp.max(peak, axis=1, keepdims=True)
             weights = [jnp.exp2((s - peak) * factor) for s in scores]
-            total = jnp.sum(functools.reduce(jnp.add, weights), axis=1, keepdims=True)
-            mixed = functools.reduce(
-                jnp.add,
-                [
-                    jnp.dot(w.astype(jnp.bfloat16), v, preferred_element_type=jnp.float32)
-                    for w, v in zip(weights, values)
-                ],
-            )
-            out_ref[here, cols] = (mixed / total).astype(out_ref.dtype)
-            parts.append(peak * factor + jnp.log2(total))
-        lse = jnp.where(lane == head, jnp.concatenate(parts, axis=0), lse)
+            totals.append(jnp.sum(functools.reduce(jnp.add, weights), axis=1, keepdims=True))
+            peaks.append(peak)
+            probs.append([w.astype(jnp.bfloat16) for w in weights])
+        mixed = functools.reduce(
+            jnp.add,
+            [
+                jnp.dot(jnp.concatenate(p, axis=0), v, preferred_element_type=jnp.float32)
+                for p, v in zip(zip(*probs), values)
+            ],
+        )
+        total = jnp.concatenate(totals, axis=0)
+        out_ref[:rows, cols] = (mixed * (1.0 / total)).astype(out_ref.dtype)
+        peak = jnp.concatenate(peaks, axis=0)
+        lse = jnp.where(lane == head, peak * factor + jnp.log2(total), lse)
     turned = jnp.transpose(lse)
     stats = []
     for head in range(per_block):
@@ -273,7 +275,7 @@
     for copy in copies:
         copy.wait()
     columns = out_ref.shape[1]
-    width = math.gcd(columns, 1024)
+    width = math.gcd(columns, 1536)
 
     @pl.loop(0, columns // width)
     def _(i):
@@ -363,10 +365,11 @@
     kv = join(after(key_rows, *ahead), value_rows, cost=WEIGHTY).reshape(2, rows, features)
     kv_up = column_shift(kv, 1)
     kv_down = column_shift(kv, -1)
+    asking = jnp.concatenate(
+        [after(query_rows, kv)[:, :chunk], jnp.tile(lists, (1, chunk_heads))], axis=0
+    )
     if cube:
-        mz = fence(after(mz, kv, my))
-    asking = after(query_rows, kv, *([mz, my] if cube else []))[:, :chunk]
-    asking = jnp.concatenate([asking, jnp.tile(lists, (1, chunk_heads))], axis=0)
+        lists = fence(after(lists, asking, mz, my))
     sent = []
     for parity in phases:
         pairs = row_pairs(parity)
@@ -374,8 +377,8 @@
         second = query_rows[:, chunk:]
         if cube:
             second = after(second, first)
-            c0 = after(c0, mz)
-            cz = swap_bit(c0, 4)
+            c0 = after(c0, lists)
+            cz = swap_bit(after(c0, first), 4)
             first = after(first, c0)
             near = join(mz, my, c0, cost=WEIGHTY)
             x0 = swap_group(near, groups)
@@ -395,7 +398,8 @@
                 cz = after(cz, part)
                 cy = swap_bit(cz, 2)
                 x1 = swap_group(cz, groups)
-            back.append(lax.ppermute(part, "seq", row_pairs(parity)))
+            sending = part if number else fence(after(part, asked[1]), 0)
+            back.append(lax.ppermute(sending, "seq", row_pairs(parity)))
             last = part
         others.append(back)
     if cube:

time: 113 us -> 112 us (level)
  the two profiles are of different devices: /device:TPU:7 before, /device:TPU:0 now
where the time goes in v9:
time: 112 us; the launch traced here: 111 us
  Pallas kernels  44.9 us (40%)
  starting transfers between devices  39.8 us (36%)
  waiting for transfers between devices  19.8 us (18%)
  local copies, waits for them, and re-layouts  5.55 us (5%)
    ppermute x8, starting transfers between devices, swap_bit(): return lax.ppermute(value, 'seq', [(s, s ^ bit) for s in range(count)])  25.7 us
    pallas_call x4, Pallas kernels, attend(): pl.pallas_call(functools.partial(attend_kernel, rows, per_block), grid=(h...  18.8 us
    pallas_call x5, Pallas kernels, join(): pl.pallas_call(functools.partial(join_kernel, len(arrays)), in_specs=[pl....  11.4 us
    ppermute x1, waiting for transfers between devices, body(): first = lax.ppermute(asking, 'seq', pairs)  10.1 us
    pallas_call x1, Pallas kernels, project(): pl.pallas_call(functools.partial(project_kernel, plan, len(parts)), in_sp...  7.16 us
    ppermute x2, waiting for transfers between devices, body(): back.append(lax.ppermute(sending, 'seq', row_pairs(parity)))  6.43 us
    ppermute x2, starting transfers between devices, column_shift(): return lax.ppermute(value, 'seq', pairs)  5.61 us
    ppermute x4, starting transfers between devices, swap_group(): return lax.ppermute(value, 'group', [(s, s ^ 1) for s in range(groups)])  5.15 us
  transfers between devices with their start and end apart: 18, of which 5 were waited for; matrix products, arithmetic and copies ran while one was open for 1% of the time, Pallas kernels for 34%

profile of v9, /device:TPU:0, one launch (start us, length us, event | category | flops | bytes accessed | tf_op | source)
XLA Modules:
  0.0 111.1 jit_solution(1805856728709470122)
XLA Ops:
  0.0 1.7 %constant_dynamic-slice_fusion = bf16[48,3072]{1,0:T(8,128)(2,1)} fusion(bf16[96,3072]{1,0:T(8,128)(2,1)} %refs_0_.2, s32[]{:T(128)S(6)} %select_n.21), kind=kLoop, calls=%fused_computation.2 | loop fusion | bytes 589828 | tf_op jit(solution)/shard_map/dynamic_slice | solution.py:355
  1.7 3.0 %collective-permute-start.2 = (bf16[48,3072]{1,0:T(8,128)(2,1)}, bf16[48,3072]{1,0:T(8,128)(2,1)}, u32[]{:S(2)}, u32[]{:S(2)}) collective-permute-start(bf16[48,3072]{1,0:T(8,128)(2,1)} %constant_dynamic-slice_fusion), channel_id=1, source_target_pairs={{0,2},{1,3},{2,0},{3,1},{4,6},{5,7},{6,4},{7,5},{8,10},{9,11},{10,... | collective-permute-start | bytes 884744 | tf_op jit(solution)/shard_map/ppermute | solution.py:24
  4.7 2.6 %collective-permute-start.1 = (bf16[48,3072]{1,0:T(8,128)(2,1)}, bf16[48,3072]{1,0:T(8,128)(2,1)}, u32[]{:S(2)}, u32[]{:S(2)}) collective-permute-start(bf16[48,3072]{1,0:T(8,128)(2,1)} %constant_dynamic-slice_fusion), channel_id=1, source_target_pairs={{0,8},{1,9},{2,10},{3,11},{4,12},{5,13},{6,14},{7,15},{8,0},{9,1},... | collective-permute-start | bytes 884744 | tf_op jit(solution)/shard_map/ppermute | solution.py:24
  7.3 1.6 %collective-permute-start = (bf16[48,3072]{1,0:T(8,128)(2,1)}, bf16[48,3072]{1,0:T(8,128)(2,1)}, u32[]{:S(2)}, u32[]{:S(2)}) collective-permute-start(bf16[48,3072]{1,0:T(8,128)(2,1)} %constant_dynamic-slice_fusion), channel_id=1, source_target_pairs={{0,4},{1,5},{2,6},{3,7},{4,0},{5,1},{6,2},{7,3},{8,12},{9,13},{10,... | collective-permute-start | bytes 884744 | tf_op jit(solution)/shard_map/ppermute | solution.py:24
  8.8 1.1 %copy-done.1 = bf16[256,1536]{1,0:T(8,128)(2,1)S(1)} copy-done((bf16[256,1536]{1,0:T(8,128)(2,1)S(1)}, bf16[256,1536]{1,0:T(8,128)(2,1)}, u32[]{:S(2)}) %copy-start.1) | copy-done | bytes 786456
  10.0 1.1 %copy-done.3 = bf16[256,1536]{1,0:T(8,128)(2,1)S(1)} copy-done((bf16[256,1536]{1,0:T(8,128)(2,1)S(1)}, bf16[256,1536]{1,0:T(8,128)(2,1)}, u32[]{:S(2)}) %copy-start.3) | copy-done | bytes 786456
  11.1 1.3 %shard_map.55 = bf16[512,1536]{1,0:T(8,128)(2,1)} custom-call(bf16[256,1536]{1,0:T(8,128)(2,1)S(1)} %copy-done.1, bf16[256,1536]{1,0:T(8,128)(2,1)S(1)} %copy-done.3), custom_call_target="tpu_custom_call" | custom-call | flops 999999995904 | tf_op jit(solution)/shard_map/pallas_call | solution.py:64
  12.4 0.0 slice-start
  12.4 1.4 %collective-permute-start.7 = (bf16[2,256,1536]{2,1,0:T(8,128)(2,1)}, bf16[2,256,1536]{2,1,0:T(8,128)(2,1)}, u32[]{:S(2)}, u32[]{:S(2)}) collective-permute-start(bf16[2,256,1536]{2,1,0:T(8,128)(2,1)} %bitcast.1), channel_id=1, source_target_pairs={{1,0},{2,1},{3,2},{4,3},{5,4},{6,5},{7,6},{9,8},{10,9},{11,10},{12... | collective-permute-start | bytes 4718600 | tf_op jit(solution)/shard_map/ppermute | solution.py:34
  13.8 4.2 %collective-permute-start.6 = (bf16[2,256,1536]{2,1,0:T(8,128)(2,1)}, bf16[2,256,1536]{2,1,0:T(8,128)(2,1)}, u32[]{:S(2)}, u32[]{:S(2)}) collective-permute-start(bf16[2,256,1536]{2,1,0:T(8,128)(2,1)} %bitcast.1), channel_id=1, source_target_pairs={{0,1},{1,2},{2,3},{3,4},{4,5},{5,6},{6,7},{8,9},{9,10},{10,11},{11... | collective-permute-start | bytes 4718600 | tf_op jit(solution)/shard_map/ppermute | solution.py:34
  18.0 0.8 slice.7
  18.9 0.8 pad_maximum_fusion
  19.7 0.0 collective-permute-done.2.refs_1_
  19.7 0.3 collective-permute-start.3
  20.0 1.0 collective-permute-done.refs_0_
  21.0 1.3 %shard_map.56.list_ref = bf16[16,128]{1,0:T(8,128)(2,1)} custom-call(bf16[16,128]{1,0:T(8,128)(2,1)} %copy-done.8), custom_call_target="tpu_custom_call" | custom-call | flops 999999995904 | tf_op jit(solution)/shard_map/pallas_call | solution.py:81
  22.2 0.0 collective-permute-done.1.refs_1_.refs_2_
  22.2 2.2 %shard_map.58.refs_1_ = bf16[144,3072]{1,0:T(8,128)(2,1)} custom-call(bf16[48,3072]{1,0:T(8,128)(2,1)} %collective-permute-done.refs_0_, bf16[48,3072]{1,0:T(8,128)(2,1)} %collective-permute-done.2.refs_1_, bf16[48,3072]{1,0:T(8,128)(2,1)} %collective-permute-done.1.refs_1_.refs_2_), custom_call_target="tpu_custom_call" | custom-call | flops 999999995904 | tf_op jit(solution)/shard_map/pallas_call | solution.py:64
  24.5 1.6 %collective-permute-start.15 = (bf16[144,3072]{1,0:T(8,128)(2,1)}, bf16[144,3072]{1,0:T(8,128)(2,1)}, u32[]{:S(2)}, u32[]{:S(2)}) collective-permute-start(bf16[144,3072]{1,0:T(8,128)(2,1)} %shard_map.58.refs_1_), channel_id=1, source_target_pairs={{0,16},{16,0},{1,17},{17,1},{2,18},{18,2},{3,19},{19,3},{4,20},{20... | collective-permute-start | bytes 2654216 | tf_op jit(solution)/shard_map/ppermute | solution.py:28
  26.0 10.1 %collective-permute-done.3.list_ref.q_ref = bf16[272,768]{1,0:T(8,128)(2,1)} collective-permute-done((bf16[272,768]{1,0:T(8,128)(2,1)}, bf16[272,768]{1,0:T(8,128)(2,1)}, u32[]{:S(2)}, u32[]{:S(2)}) %collective-permute-start.3) | collective-permute-done | bytes 417824 | tf_op jit(solution)/shard_map/ppermute | solution.py:376
  36.1 16.3 %collective-permute-start.8 = (bf16[48,3072]{1,0:T(8,128)(2,1)}, bf16[48,3072]{1,0:T(8,128)(2,1)}, u32[]{:S(2)}, u32[]{:S(2)}) collective-permute-start(bf16[48,3072]{1,0:T(8,128)(2,1)} %collective-permute-done.1.refs_1_.refs_2_), channel_id=1, source_target_pairs={{0,4},{1,5},{2,6},{3,7},{4,0},{5,1},{6,2},{7,3},{8,12},{9,13},{10,... | collective-permute-start | bytes 884744 | tf_op jit(solution)/shard_map/ppermute | solution.py:24
  52.4 1.9 %shard_map.57 = bf16[96,3072]{1,0:T(8,128)(2,1)} custom-call(bf16[48,3072]{1,0:T(8,128)(2,1)} %collective-permute-done.refs_0_, bf16[48,3072]{1,0:T(8,128)(2,1)} %collective-permute-done.1.refs_1_.refs_2_), custom_call_target="tpu_custom_call" | custom-call | tf_op jit(solution)/shard_map/pallas_call | solution.py:64
  54.4 0.1 collective-permute-start.4
  54.5 4.6 %shard_map.59.in_ref = bf16[272,768]{1,0:T(8,128)(2,1)S(1)} custom-call(bf16[272,768]{1,0:T(8,128)(2,1)} %collective-permute-done.3.list_ref.q_ref, bf16[272,768]{1,0:T(8,128)(2,1)} %collective-permute-done.3.list_ref.q_ref, bf16[256,1536]{1,0:T(8,128)(2,1)S(1)} %copy-done.2, bf16[2,256,1536]{2,1,0:T(8,128)(2,1)} %collective-permute-done.6.ka.va, ...), custom_call_target="tpu_custom_call" | custom-call | flops 999999995904 | tf_op jit(solution)/shard_map/pallas_call | solution.py:157
  59.1 0.0 copy-start.6
  59.1 0.7 copy-done.6
  59.9 0.0 collective-permute-done.8.refs_3_
  59.9 1.5 %collective-permute-start.16 = (bf16[48,3072]{1,0:T(8,128)(2,1)}, bf16[48,3072]{1,0:T(8,128)(2,1)}, u32[]{:S(2)}, u32[]{:S(2)}) collective-permute-start(bf16[48,3072]{1,0:T(8,128)(2,1)} %collective-permute-done.8.refs_3_), channel_id=1, source_target_pairs={{0,16},{16,0},{1,17},{17,1},{2,18},{18,2},{3,19},{19,3},{4,20},{20... | collective-permute-start | bytes 884744 | tf_op jit(solution)/shard_map/ppermute | solution.py:28
  61.4 2.0 %collective-permute-start.10 = (bf16[48,3072]{1,0:T(8,128)(2,1)}, bf16[48,3072]{1,0:T(8,128)(2,1)}, u32[]{:S(2)}, u32[]{:S(2)}) collective-permute-start(bf16[48,3072]{1,0:T(8,128)(2,1)} %collective-permute-done.8.refs_3_), channel_id=1, source_target_pairs={{0,2},{1,3},{2,0},{3,1},{4,6},{5,7},{6,4},{7,5},{8,10},{9,11},{10,... | collective-permute-start | bytes 884744 | tf_op jit(solution)/shard_map/ppermute | solution.py:24
  63.3 2.3 %collective-permute-done.5.q_ref = bf16[256,768]{1,0:T(8,128)(2,1)} collective-permute-done((bf16[256,768]{1,0:T(8,128)(2,1)}, bf16[256,768]{1,0:T(8,128)(2,1)}, u32[]{:S(2)}, u32[]{:S(2)}) %collective-permute-start.5) | collective-permute-done | bytes 393248 | tf_op jit(solution)/shard_map/ppermute | solution.py:388
  65.7 1.8 %shard_map.64 = bf16[272,768]{1,0:T(8,128)(2,1)} custom-call(bf16[272,768]{1,0:T(8,128)(2,1)} %copy-done.6), custom_call_target="tpu_custom_call" | custom-call | tf_op jit(solution)/shard_map/pallas_call | solution.py:81
  67.4 0.6 collective-permute-start.14
  68.1 5.3 %shard_map.60 = bf16[272,768]{1,0:T(8,128)(2,1)} custom-call(bf16[272,768]{1,0:T(8,128)(2,1)} %collective-permute-done.3.list_ref.q_ref, bf16[256,768]{1,0:T(8,128)(2,1)} %collective-permute-done.5.q_ref, bf16[256,1536]{1,0:T(8,128)(2,1)S(1)} %copy-done.2, bf16[2,256,1536]{2,1,0:T(8,128)(2,1)} %collective-permute-done.6.ka.va, ...), custom_call_target="tpu_custom_call" | custom-call | flops 999999995904 | tf_op jit(solution)/shard_map/pallas_call | solution.py:157
  73.3 0.0 collective-permute-done.15.refs_2_
  73.3 2.4 %collective-permute-start.13 = (bf16[272,768]{1,0:T(8,128)(2,1)}, bf16[272,768]{1,0:T(8,128)(2,1)}, u32[]{:S(2)}, u32[]{:S(2)}) collective-permute-start(bf16[272,768]{1,0:T(8,128)(2,1)} %shard_map.60), channel_id=1, source_target_pairs={{0,8},{1,9},{2,10},{3,11},{4,12},{5,13},{6,14},{7,15},{8,0},{9,1},... | collective-permute-start | bytes 1253384 | tf_op jit(solution)/shard_map/ppermute | solution.py:402
  75.7 1.5 %collective-permute-start.9 = (bf16[96,3072]{1,0:T(8,128)(2,1)}, bf16[96,3072]{1,0:T(8,128)(2,1)}, u32[]{:S(2)}, u32[]{:S(2)}) collective-permute-start(bf16[96,3072]{1,0:T(8,128)(2,1)} %collective-permute-done.4.refs_0_), channel_id=1, source_target_pairs={{0,16},{16,0},{1,17},{17,1},{2,18},{18,2},{3,19},{19,3},{4,20},{20... | collective-permute-start | bytes 1769480 | tf_op jit(solution)/shard_map/ppermute | solution.py:28
  77.2 4.5 %shard_map.61.refs_0_ = f32[272,768]{1,0:T(8,128)S(1)} custom-call(bf16[16,128]{1,0:T(8,128)(2,1)S(1)} %copy-done.7, bf16[256,1536]{1,0:T(8,128)(2,1)S(1)} %copy-done, bf16[256,1536]{1,0:T(8,128)(2,1)S(1)} %copy-done.2, bf16[2,256,1536]{2,1,0:T(8,128)(2,1)} %collective-permute-done.6.ka.va, bf16[2,256,1536]{2,1,0:T(8,128)(2,1)} %collective-permute-done.7.kb.vb, ...), custom_call_target="tpu_custom_call" | custom-call | tf_op jit(solution)/shard_map/pallas_call | solution.py:157
  81.7 0.6 collective-permute-start.11
  82.3 3.3 %shard_map.66.refs_0_ = bf16[480,3072]{1,0:T(8,128)(2,1)} custom-call(bf16[96,3072]{1,0:T(8,128)(2,1)S(1)} %copy-done.5, bf16[144,3072]{1,0:T(8,128)(2,1)} %shard_map.58.refs_1_, bf16[144,3072]{1,0:T(8,128)(2,1)} %collective-permute-done.15.refs_2_, bf16[48,3072]{1,0:T(8,128)(2,1)} %collective-permute-done.8.refs_3_, ...), custom_call_target="tpu_custom_call" | custom-call | tf_op jit(solution)/shard_map/pallas_call | solution.py:64
  85.6 0.1 collective-permute-start.17
  85.7 4.5 %shard_map.62.refs_2_ = f32[272,768]{1,0:T(8,128)S(1)} custom-call(bf16[16,128]{1,0:T(8,128)(2,1)S(1)} %copy-done.7, bf16[256,1536]{1,0:T(8,128)(2,1)S(1)} %copy-done, bf16[256,1536]{1,0:T(8,128)(2,1)S(1)} %copy-done.2, bf16[2,256,1536]{2,1,0:T(8,128)(2,1)} %collective-permute-done.6.ka.va, bf16[2,256,1536]{2,1,0:T(8,128)(2,1)} %collective-permute-done.7.kb.vb, ...), custom_call_target="tpu_custom_call" | custom-call | tf_op jit(solution)/shard_map/pallas_call | solution.py:157
  90.2 4.9 %collective-permute-done.14.refs_1_ = bf16[272,768]{1,0:T(8,128)(2,1)} collective-permute-done((bf16[272,768]{1,0:T(8,128)(2,1)}, bf16[272,768]{1,0:T(8,128)(2,1)}, u32[]{:S(2)}, u32[]{:S(2)}) %collective-permute-start.14) | collective-permute-done | bytes 417824 | tf_op jit(solution)/shard_map/ppermute | solution.py:402
  95.1 1.7 %shard_map.65.refs_2_.refs_4_ = bf16[256,768]{1,0:T(8,128)(2,1)S(1)} custom-call(s32[1]{0:T(128)} %bitcast.partner_ref, f32[272,768]{1,0:T(8,128)S(1)} %shard_map.61.refs_0_, bf16[272,768]{1,0:T(8,128)(2,1)} %collective-permute-done.14.refs_1_), custom_call_target="tpu_custom_call" | custom-call | flops 999999995904 | tf_op jit(solution)/shard_map/pallas_call | solution.py:223
  96.8 2.7 %shard_map.63.refs_0_ = bf16[288,3072]{1,0:T(8,128)(2,1)} custom-call(bf16[96,3072]{1,0:T(8,128)(2,1)} %collective-permute-done.4.refs_0_, bf16[96,3072]{1,0:T(8,128)(2,1)} %collective-permute-done.9.refs_1_, bf16[48,3072]{1,0:T(8,128)(2,1)} %collective-permute-done.10.refs_2_, bf16[48,3072]{1,0:T(8,128)(2,1)} %collective-permute-done.11.refs_3_), custom_call_target="tpu_custom_call" | custom-call | tf_op jit(solution)/shard_map/pallas_call | solution.py:64
  99.5 0.1 collective-permute-start.12
  99.6 2.8 %shard_map.67.refs_5_ = bf16[1536,3072]{1,0:T(8,128)(2,1)S(1)} custom-call(bf16[480,3072]{1,0:T(8,128)(2,1)} %shard_map.66.refs_0_, bf16[480,3072]{1,0:T(8,128)(2,1)} %collective-permute-done.17.refs_1_, bf16[256,768]{1,0:T(8,128)(2,1)S(1)} %shard_map.65.refs_2_.refs_4_), custom_call_target="tpu_custom_call" | custom-call | flops 999999995904 | tf_op jit(solution)/shard_map/pallas_call | solution.py:257
  102.4 1.5 %collective-permute-done.13.refs_3_ = bf16[272,768]{1,0:T(8,128)(2,1)} collective-permute-done((bf16[272,768]{1,0:T(8,128)(2,1)}, bf16[272,768]{1,0:T(8,128)(2,1)}, u32[]{:S(2)}, u32[]{:S(2)}) %collective-permute-start.13) | collective-permute-done | bytes 417824 | tf_op jit(solution)/shard_map/ppermute | solution.py:402
  104.0 7.2 %shard_map.68 = (bf16[256,3072]{1,0:T(8,128)(2,1)}, bf16[1536,3072]{1,0:T(8,128)(2,1)S(1)}) custom-call(s32[1]{0:T(128)} %bitcast.partner_ref, bf16[288,3072]{1,0:T(8,128)(2,1)} %shard_map.63.refs_0_, bf16[288,3072]{1,0:T(8,128)(2,1)} %collective-permute-done.12.refs_1_, f32[272,768]{1,0:T(8,128)S(1)} %shard_map.62.refs_2_, ...), custom_call_target="tpu_custom_call", output_to_operand_aliasing={{1}: (6, {})} | custom-call | tf_op jit(solution)/shard_map/pallas_call | solution.py:293
  (31 shorter events, 0.1 us)
Async XLA Ops:
  1.7 18.0 %collective-permute-start.2 = (bf16[48,3072]{1,0:T(8,128)(2,1)}, bf16[48,3072]{1,0:T(8,128)(2,1)}, u32[]{:S(2)}, u32[]{:S(2)}) collective-permute-start(bf16[48,3072]{1,0:T(8,128)(2,1)} %constant_dynamic-slice_fusion), channel_id=1, source_target_pairs={{0,2},{1,3},{2,0},{3,1},{4,6},{5,7},{6,4},{7,5},{8,10},{9,11},{10,... | collective-permute-start | bytes 884744 | tf_op jit(solution)/shard_map/ppermute | solution.py:24
  4.7 17.6 %collective-permute-start.1 = (bf16[48,3072]{1,0:T(8,128)(2,1)}, bf16[48,3072]{1,0:T(8,128)(2,1)}, u32[]{:S(2)}, u32[]{:S(2)}) collective-permute-start(bf16[48,3072]{1,0:T(8,128)(2,1)} %constant_dynamic-slice_fusion), channel_id=1, source_target_pairs={{0,8},{1,9},{2,10},{3,11},{4,12},{5,13},{6,14},{7,15},{8,0},{9,1},... | collective-permute-start | bytes 884744 | tf_op jit(solution)/shard_map/ppermute | solution.py:24
  7.3 13.7 %collective-permute-start = (bf16[48,3072]{1,0:T(8,128)(2,1)}, bf16[48,3072]{1,0:T(8,128)(2,1)}, u32[]{:S(2)}, u32[]{:S(2)}) collective-permute-start(bf16[48,3072]{1,0:T(8,128)(2,1)} %constant_dynamic-slice_fusion), channel_id=1, source_target_pairs={{0,4},{1,5},{2,6},{3,7},{4,0},{5,1},{6,2},{7,3},{8,12},{9,13},{10,... | collective-permute-start | bytes 884744 | tf_op jit(solution)/shard_map/ppermute | solution.py:24
  8.8 1.1 %copy-start.1 = (bf16[256,1536]{1,0:T(8,128)(2,1)S(1)}, bf16[256,1536]{1,0:T(8,128)(2,1)}, u32[]{:S(2)}) copy-start(bf16[256,1536]{1,0:T(8,128)(2,1)} %k0.7) | copy-start | bytes 2359300
  10.0 1.1 %copy-start.3 = (bf16[256,1536]{1,0:T(8,128)(2,1)S(1)}, bf16[256,1536]{1,0:T(8,128)(2,1)}, u32[]{:S(2)}) copy-start(bf16[256,1536]{1,0:T(8,128)(2,1)} %v0.7) | copy-start | bytes 2359300
  11.1 6.9 %copy-start = (bf16[256,1536]{1,0:T(8,128)(2,1)S(1)}, bf16[256,1536]{1,0:T(8,128)(2,1)}, u32[]{:S(2)}) copy-start(bf16[256,1536]{1,0:T(8,128)(2,1)} %q_ref.1) | copy-start | bytes 2359300
  11.1 7.7 %copy-start.9 = (s32[2,27]{1,0:T(2,128)S(1)}, s32[2,27]{1,0:T(2,128)}, u32[]{:S(2)}) copy-start(s32[2,27]{1,0:T(2,128)} %param.8) | copy-start | bytes 652
  12.4 6.5 %slice-start = ((bf16[256,1536]{1,0:T(8,128)(2,1)}), bf16[256,768]{1,0:T(8,128)(2,1)S(1)}, s32[]{:S(2)}) async-start(bf16[256,1536]{1,0:T(8,128)(2,1)} %q_ref.1), calls=%async_computation | async-start | bytes 786432 | tf_op jit(solution)/shard_map/slice | solution.py:369
  12.4 42.0 %collective-permute-start.7 = (bf16[2,256,1536]{2,1,0:T(8,128)(2,1)}, bf16[2,256,1536]{2,1,0:T(8,128)(2,1)}, u32[]{:S(2)}, u32[]{:S(2)}) collective-permute-start(bf16[2,256,1536]{2,1,0:T(8,128)(2,1)} %bitcast.1), channel_id=1, source_target_pairs={{1,0},{2,1},{3,2},{4,3},{5,4},{6,5},{7,6},{9,8},{10,9},{11,10},{12... | collective-permute-start | bytes 4718600 | tf_op jit(solution)/shard_map/ppermute | solution.py:34
  13.8 40.6 %collective-permute-start.6 = (bf16[2,256,1536]{2,1,0:T(8,128)(2,1)}, bf16[2,256,1536]{2,1,0:T(8,128)(2,1)}, u32[]{:S(2)}, u32[]{:S(2)}) collective-permute-start(bf16[2,256,1536]{2,1,0:T(8,128)(2,1)} %bitcast.1), channel_id=1, source_target_pairs={{0,1},{1,2},{2,3},{3,4},{4,5},{5,6},{6,7},{8,9},{9,10},{10,11},{11... | collective-permute-start | bytes 4718600 | tf_op jit(solution)/shard_map/ppermute | solution.py:34
  18.8 2.1 %copy-start.8 = (bf16[16,128]{1,0:T(8,128)(2,1)}, bf16[16,128]{1,0:T(8,128)(2,1)S(1)}, u32[]{:S(2)}) copy-start(bf16[16,128]{1,0:T(8,128)(2,1)S(1)} %pad.4.in_ref) | copy-start | bytes 12292
  19.7 16.4 %collective-permute-start.3 = (bf16[272,768]{1,0:T(8,128)(2,1)}, bf16[272,768]{1,0:T(8,128)(2,1)}, u32[]{:S(2)}, u32[]{:S(2)}) collective-permute-start(bf16[272,768]{1,0:T(8,128)(2,1)} %pad_maximum_fusion), channel_id=1, source_target_pairs={{0,8},{1,9},{2,10},{3,11},{4,12},{5,13},{6,14},{7,15},{8,0},{9,1},... | collective-permute-start | bytes 1253384 | tf_op jit(solution)/shard_map/ppermute | solution.py:376
  22.2 32.2 %copy-start.2 = (bf16[256,1536]{1,0:T(8,128)(2,1)S(1)}, bf16[256,1536]{1,0:T(8,128)(2,1)}, u32[]{:S(2)}) copy-start(bf16[256,1536]{1,0:T(8,128)(2,1)} %k0.7) | copy-start | bytes 2359300
  22.2 32.2 %copy-start.4 = (bf16[256,1536]{1,0:T(8,128)(2,1)S(1)}, bf16[256,1536]{1,0:T(8,128)(2,1)}, u32[]{:S(2)}) copy-start(bf16[256,1536]{1,0:T(8,128)(2,1)} %v0.7) | copy-start | bytes 2359300
  24.5 48.9 %collective-permute-start.15 = (bf16[144,3072]{1,0:T(8,128)(2,1)}, bf16[144,3072]{1,0:T(8,128)(2,1)}, u32[]{:S(2)}, u32[]{:S(2)}) collective-permute-start(bf16[144,3072]{1,0:T(8,128)(2,1)} %shard_map.58.refs_1_), channel_id=1, source_target_pairs={{0,16},{16,0},{1,17},{17,1},{2,18},{18,2},{3,19},{19,3},{4,20},{20... | collective-permute-start | bytes 2654216 | tf_op jit(solution)/shard_map/ppermute | solution.py:28
  36.1 23.7 %collective-permute-start.8 = (bf16[48,3072]{1,0:T(8,128)(2,1)}, bf16[48,3072]{1,0:T(8,128)(2,1)}, u32[]{:S(2)}, u32[]{:S(2)}) collective-permute-start(bf16[48,3072]{1,0:T(8,128)(2,1)} %collective-permute-done.1.refs_1_.refs_2_), channel_id=1, source_target_pairs={{0,4},{1,5},{2,6},{3,7},{4,0},{5,1},{6,2},{7,3},{8,12},{9,13},{10,... | collective-permute-start | bytes 884744 | tf_op jit(solution)/shard_map/ppermute | solution.py:24
  52.4 13.2 %collective-permute-start.5 = (bf16[256,768]{1,0:T(8,128)(2,1)}, bf16[256,768]{1,0:T(8,128)(2,1)}, u32[]{:S(2)}, u32[]{:S(2)}) collective-permute-start(bf16[256,768]{1,0:T(8,128)(2,1)} %slice.7), channel_id=1, source_target_pairs={{0,8},{1,9},{2,10},{3,11},{4,12},{5,13},{6,14},{7,15},{8,0},{9,1},... | collective-permute-start | bytes 1179656 | tf_op jit(solution)/shard_map/ppermute | solution.py:388
  54.4 21.3 %collective-permute-start.4 = (bf16[96,3072]{1,0:T(8,128)(2,1)}, bf16[96,3072]{1,0:T(8,128)(2,1)}, u32[]{:S(2)}, u32[]{:S(2)}) collective-permute-start(bf16[96,3072]{1,0:T(8,128)(2,1)} %shard_map.57), channel_id=1, source_target_pairs={{0,2},{1,3},{2,0},{3,1},{4,6},{5,7},{6,4},{7,5},{8,10},{9,11},{10,... | collective-permute-start | bytes 1769480 | tf_op jit(solution)/shard_map/ppermute | solution.py:24
  59.1 0.8 copy-start.6
  59.9 21.8 %collective-permute-start.16 = (bf16[48,3072]{1,0:T(8,128)(2,1)}, bf16[48,3072]{1,0:T(8,128)(2,1)}, u32[]{:S(2)}, u32[]{:S(2)}) collective-permute-start(bf16[48,3072]{1,0:T(8,128)(2,1)} %collective-permute-done.8.refs_3_), channel_id=1, source_target_pairs={{0,16},{16,0},{1,17},{17,1},{2,18},{18,2},{3,19},{19,3},{4,20},{20... | collective-permute-start | bytes 884744 | tf_op jit(solution)/shard_map/ppermute | solution.py:28
  61.4 20.3 %collective-permute-start.10 = (bf16[48,3072]{1,0:T(8,128)(2,1)}, bf16[48,3072]{1,0:T(8,128)(2,1)}, u32[]{:S(2)}, u32[]{:S(2)}) collective-permute-start(bf16[48,3072]{1,0:T(8,128)(2,1)} %collective-permute-done.8.refs_3_), channel_id=1, source_target_pairs={{0,2},{1,3},{2,0},{3,1},{4,6},{5,7},{6,4},{7,5},{8,10},{9,11},{10,... | collective-permute-start | bytes 884744 | tf_op jit(solution)/shard_map/ppermute | solution.py:24
  67.4 27.7 %collective-permute-start.14 = (bf16[272,768]{1,0:T(8,128)(2,1)}, bf16[272,768]{1,0:T(8,128)(2,1)}, u32[]{:S(2)}, u32[]{:S(2)}) collective-permute-start(bf16[272,768]{1,0:T(8,128)(2,1)} %shard_map.64), channel_id=1, source_target_pairs={{0,8},{1,9},{2,10},{3,11},{4,12},{5,13},{6,14},{7,15},{8,0},{9,1},... | collective-permute-start | bytes 1253384 | tf_op jit(solution)/shard_map/ppermute | solution.py:402
  68.1 9.2 %copy-start.7 = (bf16[16,128]{1,0:T(8,128)(2,1)S(1)}, bf16[16,128]{1,0:T(8,128)(2,1)}, u32[]{:S(2)}) copy-start(bf16[16,128]{1,0:T(8,128)(2,1)} %shard_map.56.list_ref) | copy-start | bytes 12292
  73.3 9.0 %copy-start.5 = (bf16[96,3072]{1,0:T(8,128)(2,1)S(1)}, bf16[96,3072]{1,0:T(8,128)(2,1)}, u32[]{:S(2)}) copy-start(bf16[96,3072]{1,0:T(8,128)(2,1)} %refs_0_.2) | copy-start | bytes 1769476
  73.3 30.6 %collective-permute-start.13 = (bf16[272,768]{1,0:T(8,128)(2,1)}, bf16[272,768]{1,0:T(8,128)(2,1)}, u32[]{:S(2)}, u32[]{:S(2)}) collective-permute-start(bf16[272,768]{1,0:T(8,128)(2,1)} %shard_map.60), channel_id=1, source_target_pairs={{0,8},{1,9},{2,10},{3,11},{4,12},{5,13},{6,14},{7,15},{8,0},{9,1},... | collective-permute-start | bytes 1253384 | tf_op jit(solution)/shard_map/ppermute | solution.py:402
  75.7 21.1 %collective-permute-start.9 = (bf16[96,3072]{1,0:T(8,128)(2,1)}, bf16[96,3072]{1,0:T(8,128)(2,1)}, u32[]{:S(2)}, u32[]{:S(2)}) collective-permute-start(bf16[96,3072]{1,0:T(8,128)(2,1)} %collective-permute-done.4.refs_0_), channel_id=1, source_target_pairs={{0,16},{16,0},{1,17},{17,1},{2,18},{18,2},{3,19},{19,3},{4,20},{20... | collective-permute-start | bytes 1769480 | tf_op jit(solution)/shard_map/ppermute | solution.py:28
  81.7 15.1 %collective-permute-start.11 = (bf16[48,3072]{1,0:T(8,128)(2,1)}, bf16[48,3072]{1,0:T(8,128)(2,1)}, u32[]{:S(2)}, u32[]{:S(2)}) collective-permute-start(bf16[48,3072]{1,0:T(8,128)(2,1)} %collective-permute-done.10.refs_2_), channel_id=1, source_target_pairs={{0,16},{16,0},{1,17},{17,1},{2,18},{18,2},{3,19},{19,3},{4,20},{20... | collective-permute-start | bytes 884744 | tf_op jit(solution)/shard_map/ppermute | solution.py:28
  85.6 14.0 %collective-permute-start.17 = (bf16[480,3072]{1,0:T(8,128)(2,1)}, bf16[480,3072]{1,0:T(8,128)(2,1)}, u32[]{:S(2)}, u32[]{:S(2)}) collective-permute-start(bf16[480,3072]{1,0:T(8,128)(2,1)} %shard_map.66.refs_0_), channel_id=1, source_target_pairs={{0,1},{1,0},{2,3},{3,2},{4,5},{5,4},{6,7},{7,6},{8,9},{9,8},{10,11... | collective-permute-start | bytes 8847368 | tf_op jit(solution)/shard_map/ppermute | solution.py:24
  99.5 4.5 %collective-permute-start.12 = (bf16[288,3072]{1,0:T(8,128)(2,1)}, bf16[288,3072]{1,0:T(8,128)(2,1)}, u32[]{:S(2)}, u32[]{:S(2)}) collective-permute-start(bf16[288,3072]{1,0:T(8,128)(2,1)} %shard_map.63.refs_0_), channel_id=1, source_target_pairs={{0,1},{1,0},{2,3},{3,2},{4,5},{5,4},{6,7},{7,6},{8,9},{9,8},{10,11... | collective-permute-start | bytes 5308424 | tf_op jit(solution)/shard_map/ppermute | solution.py:24

commit v10 on v9

--- a/solution.py
+++ b/solution.py
@@ -12,6 +12,7 @@
 FRAMES = 2
 GRID_COLS = 8
 EXTRA = 16
+STATS = 8
 PIECES = 3
 LOG2E = math.log2(math.e)
 MIB = 1024 * 1024
@@ -141,7 +142,7 @@
             piece = rest.astype(out_ref.dtype)
             stats.append(piece.astype(jnp.float32))
             rest = rest - stats[-1]
-    stats.append(jnp.zeros((EXTRA - len(stats), rows), jnp.float32))
+    stats.append(jnp.zeros((STATS - len(stats), rows), jnp.float32))
     out_ref[rows:, :] = jnp.concatenate(stats, axis=0).astype(out_ref.dtype)
 
 
@@ -167,8 +168,8 @@
             value_spec,
             value_spec,
         ],
-        out_specs=pl.BlockSpec((rows + EXTRA, width), lambda i: (0, i)),
-        out_shape=jax.ShapeDtypeStruct((rows + EXTRA, heads * HD), kind),
+        out_specs=pl.BlockSpec((rows + STATS, width), lambda i: (0, i)),
+        out_shape=jax.ShapeDtypeStruct((rows + STATS, heads * HD), kind),
         compiler_params=pltpu.CompilerParams(vmem_limit_bytes=12 * MIB),
         cost_estimate=pl.CostEstimate(
             flops=cost, bytes_accessed=0, transcendentals=0
@@ -218,7 +219,7 @@
 
 
 def merge(partner, parts):
-    rows, columns = parts[0].shape[0] - EXTRA, parts[0].shape[1]
+    rows, columns = parts[0].shape[0] - STATS, parts[0].shape[1]
     vmem = pl.BlockSpec(memory_space=pltpu.VMEM)
     return pl.pallas_call(
         functools.partial(merge_kernel, rows),
@@ -267,7 +268,8 @@
 
 def project_kernel(plan, count, partner_ref, *refs):
     sources, refs = refs[: len(plan)], refs[len(plan) :]
-    parts, (merged, _, out_ref, held, attention, sems) = refs[:count], refs[count:]
+    parts, refs = refs[:count], refs[count:]
+    merged, _, out_ref, held, attention, staged, sems, out_sems = refs
     copies = bring(plan, sources, held, sems)
     first = merged.shape[1]
     attention[:, :first] = merged[...]
@@ -275,14 +277,19 @@
     for copy in copies:
         copy.wait()
     columns = out_ref.shape[1]
-    width = math.gcd(columns, 1536)
-
-    @pl.loop(0, columns // width)
-    def _(i):
-        there = pl.ds(pl.multiple_of(i * width, width), width)
-        out_ref[:, there] = jnp.dot(
+    width = staged.shape[2]
+
+    written = []
+    for i in range(columns // width):
+        there = pl.ds(i * width, width)
+        staged[i] = jnp.dot(
             attention[...], held[:, there], preferred_element_type=jnp.float32
         ).astype(out_ref.dtype)
+        copy = pltpu.make_async_copy(staged.at[i], out_ref.at[:, there], out_sems.at[i])
+        copy.start()
+        written.append(copy)
+    for copy in written:
+        copy.wait()
 
 
 def project(pieces, held, partner, parts, merged):
@@ -290,12 +297,13 @@
     rows, (features, columns) = merged.shape[0], held.shape
     vmem = pl.BlockSpec(memory_space=pltpu.VMEM)
     given = len(arrays) + len(parts)
+    width = math.gcd(columns, 768)
     return pl.pallas_call(
         functools.partial(project_kernel, plan, len(parts)),
         in_specs=[pl.BlockSpec(memory_space=pltpu.SMEM)]
         + [pl.BlockSpec(memory_space=pl.ANY)] * len(arrays)
         + [vmem] * (len(parts) + 2),
-        out_specs=(vmem, vmem),
+        out_specs=(pl.BlockSpec(memory_space=pl.ANY), vmem),
         out_shape=(
             jax.ShapeDtypeStruct((rows, columns), jnp.bfloat16),
             jax.ShapeDtypeStruct(held.shape, held.dtype),
@@ -303,7 +311,9 @@
         input_output_aliases={given + 2: 1},
         scratch_shapes=[
             pltpu.VMEM((rows, features), jnp.bfloat16),
+            pltpu.VMEM((columns // width, rows, width), jnp.bfloat16),
             pltpu.SemaphoreType.DMA((max(1, sum(len(m) for m in plan)),)),
+            pltpu.SemaphoreType.DMA((columns // width,)),
         ],
         compiler_params=pltpu.CompilerParams(vmem_limit_bytes=28 * MIB),
     )(partner, *arrays, *parts, merged, held)[0]

time: 112 us -> 110 us (0.982)
  transfers between devices with their start and end apart: 18 -> 18, of which waited for: 5 -> 5; matrix products, arithmetic and copies ran while one was open for 1% -> 1% of each run, Pallas kernels for 34% -> 35%
where the time goes in v10:
time: 110 us
  Pallas kernels  44.4 us (40%)
  starting transfers between devices  39.8 us (36%)
  waiting for transfers between devices  18.8 us (17%)
  local copies, waits for them, and re-layouts  5.54 us (5%)
    ppermute x8, starting transfers between devices, swap_bit(): return lax.ppermute(value, 'seq', [(s, s ^ bit) for s in range(count)])  25.7 us
    pallas_call x4, Pallas kernels, attend(): pl.pallas_call(functools.partial(attend_kernel, rows, per_block), grid=(h...  18.8 us
    pallas_call x5, Pallas kernels, join(): pl.pallas_call(functools.partial(join_kernel, len(arrays)), in_specs=[pl....  11.4 us
    ppermute x1, waiting for transfers between devices, body(): first = lax.ppermute(asking, 'seq', pairs)  10.1 us
    pallas_call x1, Pallas kernels, project(): pl.pallas_call(functools.partial(project_kernel, plan, len(parts)), in_sp...  6.61 us
    ppermute x2, starting transfers between devices, column_shift(): return lax.ppermute(value, 'seq', pairs)  5.61 us
    ppermute x2, waiting for transfers between devices, body(): back.append(lax.ppermute(sending, 'seq', row_pairs(parity)))  5.37 us
    ppermute x4, starting transfers between devices, swap_group(): return lax.ppermute(value, 'group', [(s, s ^ 1) for s in range(groups)])  5.14 us
  transfers between devices with their start and end apart: 18, of which 5 were waited for; matrix products, arithmetic and copies ran while one was open for 1% of the time, Pallas kernels for 35%

profile of v10, /device:TPU:0, one launch (start us, length us, event | category | flops | bytes accessed | tf_op | source)
XLA Modules:
  0.0 109.5 jit_solution(2969720332425032942)
XLA Ops:
  0.0 1.7 %constant_dynamic-slice_fusion = bf16[48,3072]{1,0:T(8,128)(2,1)} fusion(bf16[96,3072]{1,0:T(8,128)(2,1)} %refs_0_.2, s32[]{:T(128)S(6)} %select_n.21), kind=kLoop, calls=%fused_computation.2 | loop fusion | bytes 589828 | tf_op jit(solution)/shard_map/dynamic_slice | solution.py:365
  1.7 3.0 %collective-permute-start.2 = (bf16[48,3072]{1,0:T(8,128)(2,1)}, bf16[48,3072]{1,0:T(8,128)(2,1)}, u32[]{:S(2)}, u32[]{:S(2)}) collective-permute-start(bf16[48,3072]{1,0:T(8,128)(2,1)} %constant_dynamic-slice_fusion), channel_id=1, source_target_pairs={{0,2},{1,3},{2,0},{3,1},{4,6},{5,7},{6,4},{7,5},{8,10},{9,11},{10,... | collective-permute-start | bytes 884744 | tf_op jit(solution)/shard_map/ppermute | solution.py:25
  4.7 2.6 %collective-permute-start.1 = (bf16[48,3072]{1,0:T(8,128)(2,1)}, bf16[48,3072]{1,0:T(8,128)(2,1)}, u32[]{:S(2)}, u32[]{:S(2)}) collective-permute-start(bf16[48,3072]{1,0:T(8,128)(2,1)} %constant_dynamic-slice_fusion), channel_id=1, source_target_pairs={{0,8},{1,9},{2,10},{3,11},{4,12},{5,13},{6,14},{7,15},{8,0},{9,1},... | collective-permute-start | bytes 884744 | tf_op jit(solution)/shard_map/ppermute | solution.py:25
  7.3 1.6 %collective-permute-start = (bf16[48,3072]{1,0:T(8,128)(2,1)}, bf16[48,3072]{1,0:T(8,128)(2,1)}, u32[]{:S(2)}, u32[]{:S(2)}) collective-permute-start(bf16[48,3072]{1,0:T(8,128)(2,1)} %constant_dynamic-slice_fusion), channel_id=1, source_target_pairs={{0,4},{1,5},{2,6},{3,7},{4,0},{5,1},{6,2},{7,3},{8,12},{9,13},{10,... | collective-permute-start | bytes 884744 | tf_op jit(solution)/shard_map/ppermute | solution.py:25
  8.8 1.1 %copy-done.1 = bf16[256,1536]{1,0:T(8,128)(2,1)S(1)} copy-done((bf16[256,1536]{1,0:T(8,128)(2,1)S(1)}, bf16[256,1536]{1,0:T(8,128)(2,1)}, u32[]{:S(2)}) %copy-start.1) | copy-done | bytes 786456
  10.0 1.1 %copy-done.3 = bf16[256,1536]{1,0:T(8,128)(2,1)S(1)} copy-done((bf16[256,1536]{1,0:T(8,128)(2,1)S(1)}, bf16[256,1536]{1,0:T(8,128)(2,1)}, u32[]{:S(2)}) %copy-start.3) | copy-done | bytes 786456
  11.1 1.3 %shard_map.55 = bf16[512,1536]{1,0:T(8,128)(2,1)} custom-call(bf16[256,1536]{1,0:T(8,128)(2,1)S(1)} %copy-done.1, bf16[256,1536]{1,0:T(8,128)(2,1)S(1)} %copy-done.3), custom_call_target="tpu_custom_call" | custom-call | flops 999999995904 | tf_op jit(solution)/shard_map/pallas_call | solution.py:65
  12.4 0.0 slice-start
  12.4 1.4 %collective-permute-start.7 = (bf16[2,256,1536]{2,1,0:T(8,128)(2,1)}, bf16[2,256,1536]{2,1,0:T(8,128)(2,1)}, u32[]{:S(2)}, u32[]{:S(2)}) collective-permute-start(bf16[2,256,1536]{2,1,0:T(8,128)(2,1)} %bitcast.1), channel_id=1, source_target_pairs={{1,0},{2,1},{3,2},{4,3},{5,4},{6,5},{7,6},{9,8},{10,9},{11,10},{12... | collective-permute-start | bytes 4718600 | tf_op jit(solution)/shard_map/ppermute | solution.py:35
  13.8 4.2 %collective-permute-start.6 = (bf16[2,256,1536]{2,1,0:T(8,128)(2,1)}, bf16[2,256,1536]{2,1,0:T(8,128)(2,1)}, u32[]{:S(2)}, u32[]{:S(2)}) collective-permute-start(bf16[2,256,1536]{2,1,0:T(8,128)(2,1)} %bitcast.1), channel_id=1, source_target_pairs={{0,1},{1,2},{2,3},{3,4},{4,5},{5,6},{6,7},{8,9},{9,10},{10,11},{11... | collective-permute-start | bytes 4718600 | tf_op jit(solution)/shard_map/ppermute | solution.py:35
  18.0 0.8 slice.7
  18.9 0.8 pad_maximum_fusion
  19.7 0.0 collective-permute-done.2.refs_1_
  19.7 0.3 collective-permute-start.3
  20.0 1.0 collective-permute-done.refs_0_
  21.0 1.3 %shard_map.56.list_ref = bf16[16,128]{1,0:T(8,128)(2,1)} custom-call(bf16[16,128]{1,0:T(8,128)(2,1)} %copy-done.8), custom_call_target="tpu_custom_call" | custom-call | flops 999999995904 | tf_op jit(solution)/shard_map/pallas_call | solution.py:82
  22.2 0.0 collective-permute-done.1.refs_1_.refs_2_
  22.2 2.2 %shard_map.58.refs_1_ = bf16[144,3072]{1,0:T(8,128)(2,1)} custom-call(bf16[48,3072]{1,0:T(8,128)(2,1)} %collective-permute-done.refs_0_, bf16[48,3072]{1,0:T(8,128)(2,1)} %collective-permute-done.2.refs_1_, bf16[48,3072]{1,0:T(8,128)(2,1)} %collective-permute-done.1.refs_1_.refs_2_), custom_call_target="tpu_custom_call" | custom-call | flops 999999995904 | tf_op jit(solution)/shard_map/pallas_call | solution.py:65
  24.5 1.6 %collective-permute-start.15 = (bf16[144,3072]{1,0:T(8,128)(2,1)}, bf16[144,3072]{1,0:T(8,128)(2,1)}, u32[]{:S(2)}, u32[]{:S(2)}) collective-permute-start(bf16[144,3072]{1,0:T(8,128)(2,1)} %shard_map.58.refs_1_), channel_id=1, source_target_pairs={{0,16},{16,0},{1,17},{17,1},{2,18},{18,2},{3,19},{19,3},{4,20},{20... | collective-permute-start | bytes 2654216 | tf_op jit(solution)/shard_map/ppermute | solution.py:29
  26.0 10.1 %collective-permute-done.3.list_ref.q_ref = bf16[272,768]{1,0:T(8,128)(2,1)} collective-permute-done((bf16[272,768]{1,0:T(8,128)(2,1)}, bf16[272,768]{1,0:T(8,128)(2,1)}, u32[]{:S(2)}, u32[]{:S(2)}) %collective-permute-start.3) | collective-permute-done | bytes 417824 | tf_op jit(solution)/shard_map/ppermute | solution.py:386
  36.1 16.3 %collective-permute-start.8 = (bf16[48,3072]{1,0:T(8,128)(2,1)}, bf16[48,3072]{1,0:T(8,128)(2,1)}, u32[]{:S(2)}, u32[]{:S(2)}) collective-permute-start(bf16[48,3072]{1,0:T(8,128)(2,1)} %collective-permute-done.1.refs_1_.refs_2_), channel_id=1, source_target_pairs={{0,4},{1,5},{2,6},{3,7},{4,0},{5,1},{6,2},{7,3},{8,12},{9,13},{10,... | collective-permute-start | bytes 884744 | tf_op jit(solution)/shard_map/ppermute | solution.py:25
  52.4 1.9 %shard_map.57 = bf16[96,3072]{1,0:T(8,128)(2,1)} custom-call(bf16[48,3072]{1,0:T(8,128)(2,1)} %collective-permute-done.refs_0_, bf16[48,3072]{1,0:T(8,128)(2,1)} %collective-permute-done.1.refs_1_.refs_2_), custom_call_target="tpu_custom_call" | custom-call | tf_op jit(solution)/shard_map/pallas_call | solution.py:65
  54.4 0.1 collective-permute-start.4
  54.5 4.6 %shard_map.59.in_ref = bf16[264,768]{1,0:T(8,128)(2,1)S(1)} custom-call(bf16[272,768]{1,0:T(8,128)(2,1)} %collective-permute-done.3.list_ref.q_ref, bf16[272,768]{1,0:T(8,128)(2,1)} %collective-permute-done.3.list_ref.q_ref, bf16[256,1536]{1,0:T(8,128)(2,1)S(1)} %copy-done.2, bf16[2,256,1536]{2,1,0:T(8,128)(2,1)} %collective-permute-done.6.ka.va, ...), custom_call_target="tpu_custom_call" | custom-call | flops 999999995904 | tf_op jit(solution)/shard_map/pallas_call | solution.py:158
  59.1 0.0 copy-start.6
  59.1 0.7 copy-done.6
  59.8 0.0 collective-permute-done.8.refs_3_
  59.9 1.5 %collective-permute-start.16 = (bf16[48,3072]{1,0:T(8,128)(2,1)}, bf16[48,3072]{1,0:T(8,128)(2,1)}, u32[]{:S(2)}, u32[]{:S(2)}) collective-permute-start(bf16[48,3072]{1,0:T(8,128)(2,1)} %collective-permute-done.8.refs_3_), channel_id=1, source_target_pairs={{0,16},{16,0},{1,17},{17,1},{2,18},{18,2},{3,19},{19,3},{4,20},{20... | collective-permute-start | bytes 884744 | tf_op jit(solution)/shard_map/ppermute | solution.py:29
  61.3 2.0 %collective-permute-start.10 = (bf16[48,3072]{1,0:T(8,128)(2,1)}, bf16[48,3072]{1,0:T(8,128)(2,1)}, u32[]{:S(2)}, u32[]{:S(2)}) collective-permute-start(bf16[48,3072]{1,0:T(8,128)(2,1)} %collective-permute-done.8.refs_3_), channel_id=1, source_target_pairs={{0,2},{1,3},{2,0},{3,1},{4,6},{5,7},{6,4},{7,5},{8,10},{9,11},{10,... | collective-permute-start | bytes 884744 | tf_op jit(solution)/shard_map/ppermute | solution.py:25
  63.3 2.3 %collective-permute-done.5.q_ref = bf16[256,768]{1,0:T(8,128)(2,1)} collective-permute-done((bf16[256,768]{1,0:T(8,128)(2,1)}, bf16[256,768]{1,0:T(8,128)(2,1)}, u32[]{:S(2)}, u32[]{:S(2)}) %collective-permute-start.5) | collective-permute-done | bytes 393248 | tf_op jit(solution)/shard_map/ppermute | solution.py:398
  65.7 1.8 %shard_map.64 = bf16[264,768]{1,0:T(8,128)(2,1)} custom-call(bf16[264,768]{1,0:T(8,128)(2,1)} %copy-done.6), custom_call_target="tpu_custom_call" | custom-call | tf_op jit(solution)/shard_map/pallas_call | solution.py:82
  67.4 0.6 collective-permute-start.14
  68.1 5.3 %shard_map.60 = bf16[264,768]{1,0:T(8,128)(2,1)} custom-call(bf16[272,768]{1,0:T(8,128)(2,1)} %collective-permute-done.3.list_ref.q_ref, bf16[256,768]{1,0:T(8,128)(2,1)} %collective-permute-done.5.q_ref, bf16[256,1536]{1,0:T(8,128)(2,1)S(1)} %copy-done.2, bf16[2,256,1536]{2,1,0:T(8,128)(2,1)} %collective-permute-done.6.ka.va, ...), custom_call_target="tpu_custom_call" | custom-call | flops 999999995904 | tf_op jit(solution)/shard_map/pallas_call | solution.py:158
  73.3 0.0 collective-permute-done.15.refs_2_
  73.3 2.4 %collective-permute-start.13 = (bf16[264,768]{1,0:T(8,128)(2,1)}, bf16[264,768]{1,0:T(8,128)(2,1)}, u32[]{:S(2)}, u32[]{:S(2)}) collective-permute-start(bf16[264,768]{1,0:T(8,128)(2,1)} %shard_map.60), channel_id=1, source_target_pairs={{0,8},{1,9},{2,10},{3,11},{4,12},{5,13},{6,14},{7,15},{8,0},{9,1},... | collective-permute-start | bytes 1216520 | tf_op jit(solution)/shard_map/ppermute | solution.py:412
  75.7 1.5 %collective-permute-start.9 = (bf16[96,3072]{1,0:T(8,128)(2,1)}, bf16[96,3072]{1,0:T(8,128)(2,1)}, u32[]{:S(2)}, u32[]{:S(2)}) collective-permute-start(bf16[96,3072]{1,0:T(8,128)(2,1)} %collective-permute-done.4.refs_0_), channel_id=1, source_target_pairs={{0,16},{16,0},{1,17},{17,1},{2,18},{18,2},{3,19},{19,3},{4,20},{20... | collective-permute-start | bytes 1769480 | tf_op jit(solution)/shard_map/ppermute | solution.py:29
  77.2 4.5 %shard_map.61.refs_0_ = f32[264,768]{1,0:T(8,128)S(1)} custom-call(bf16[16,128]{1,0:T(8,128)(2,1)S(1)} %copy-done.7, bf16[256,1536]{1,0:T(8,128)(2,1)S(1)} %copy-done, bf16[256,1536]{1,0:T(8,128)(2,1)S(1)} %copy-done.2, bf16[2,256,1536]{2,1,0:T(8,128)(2,1)} %collective-permute-done.6.ka.va, bf16[2,256,1536]{2,1,0:T(8,128)(2,1)} %collective-permute-done.7.kb.vb, ...), custom_call_target="tpu_custom_call" | custom-call | tf_op jit(solution)/shard_map/pallas_call | solution.py:158
  81.7 0.6 collective-permute-start.11
  82.3 3.3 %shard_map.66.refs_0_ = bf16[480,3072]{1,0:T(8,128)(2,1)} custom-call(bf16[96,3072]{1,0:T(8,128)(2,1)S(1)} %copy-done.5, bf16[144,3072]{1,0:T(8,128)(2,1)} %shard_map.58.refs_1_, bf16[144,3072]{1,0:T(8,128)(2,1)} %collective-permute-done.15.refs_2_, bf16[48,3072]{1,0:T(8,128)(2,1)} %collective-permute-done.8.refs_3_, ...), custom_call_target="tpu_custom_call" | custom-call | tf_op jit(solution)/shard_map/pallas_call | solution.py:65
  85.6 0.1 collective-permute-start.17
  85.7 4.5 %shard_map.62.refs_2_ = f32[264,768]{1,0:T(8,128)S(1)} custom-call(bf16[16,128]{1,0:T(8,128)(2,1)S(1)} %copy-done.7, bf16[256,1536]{1,0:T(8,128)(2,1)S(1)} %copy-done, bf16[256,1536]{1,0:T(8,128)(2,1)S(1)} %copy-done.2, bf16[2,256,1536]{2,1,0:T(8,128)(2,1)} %collective-permute-done.6.ka.va, bf16[2,256,1536]{2,1,0:T(8,128)(2,1)} %collective-permute-done.7.kb.vb, ...), custom_call_target="tpu_custom_call" | custom-call | tf_op jit(solution)/shard_map/pallas_call | solution.py:158
  90.2 4.1 %collective-permute-done.14.refs_1_ = bf16[264,768]{1,0:T(8,128)(2,1)} collective-permute-done((bf16[264,768]{1,0:T(8,128)(2,1)}, bf16[264,768]{1,0:T(8,128)(2,1)}, u32[]{:S(2)}, u32[]{:S(2)}) %collective-permute-start.14) | collective-permute-done | bytes 405536 | tf_op jit(solution)/shard_map/ppermute | solution.py:412
  94.3 1.7 %shard_map.65.refs_2_.refs_4_ = bf16[256,768]{1,0:T(8,128)(2,1)S(1)} custom-call(s32[1]{0:T(128)} %bitcast.partner_ref, f32[264,768]{1,0:T(8,128)S(1)} %shard_map.61.refs_0_, bf16[264,768]{1,0:T(8,128)(2,1)} %collective-permute-done.14.refs_1_), custom_call_target="tpu_custom_call" | custom-call | flops 999999995904 | tf_op jit(solution)/shard_map/pallas_call | solution.py:224
  96.0 2.7 %shard_map.63.refs_0_ = bf16[288,3072]{1,0:T(8,128)(2,1)} custom-call(bf16[96,3072]{1,0:T(8,128)(2,1)} %collective-permute-done.4.refs_0_, bf16[96,3072]{1,0:T(8,128)(2,1)} %collective-permute-done.9.refs_1_, bf16[48,3072]{1,0:T(8,128)(2,1)} %collective-permute-done.10.refs_2_, bf16[48,3072]{1,0:T(8,128)(2,1)} %collective-permute-done.11.refs_3_), custom_call_target="tpu_custom_call" | custom-call | tf_op jit(solution)/shard_map/pallas_call | solution.py:65
  98.7 0.1 collective-permute-start.12
  98.8 2.8 %shard_map.67.refs_5_ = bf16[1536,3072]{1,0:T(8,128)(2,1)S(1)} custom-call(bf16[480,3072]{1,0:T(8,128)(2,1)} %shard_map.66.refs_0_, bf16[480,3072]{1,0:T(8,128)(2,1)} %collective-permute-done.17.refs_1_, bf16[256,768]{1,0:T(8,128)(2,1)S(1)} %shard_map.65.refs_2_.refs_4_), custom_call_target="tpu_custom_call" | custom-call | flops 999999995904 | tf_op jit(solution)/shard_map/pallas_call | solution.py:258
  101.6 1.3 %collective-permute-done.13.refs_3_ = bf16[264,768]{1,0:T(8,128)(2,1)} collective-permute-done((bf16[264,768]{1,0:T(8,128)(2,1)}, bf16[264,768]{1,0:T(8,128)(2,1)}, u32[]{:S(2)}, u32[]{:S(2)}) %collective-permute-start.13) | collective-permute-done | bytes 405536 | tf_op jit(solution)/shard_map/ppermute | solution.py:412
  102.9 6.6 %shard_map.68 = (bf16[256,3072]{1,0:T(8,128)(2,1)}, bf16[1536,3072]{1,0:T(8,128)(2,1)S(1)}) custom-call(s32[1]{0:T(128)} %bitcast.partner_ref, bf16[288,3072]{1,0:T(8,128)(2,1)} %shard_map.63.refs_0_, bf16[288,3072]{1,0:T(8,128)(2,1)} %collective-permute-done.12.refs_1_, f32[264,768]{1,0:T(8,128)S(1)} %shard_map.62.refs_2_, ...), custom_call_target="tpu_custom_call", output_to_operand_aliasing={{1}: (6, {})} | custom-call | tf_op jit(solution)/shard_map/pallas_call | solution.py:301
  (31 shorter events, 0.1 us)
Async XLA Ops:
  1.7 18.0 %collective-permute-start.2 = (bf16[48,3072]{1,0:T(8,128)(2,1)}, bf16[48,3072]{1,0:T(8,128)(2,1)}, u32[]{:S(2)}, u32[]{:S(2)}) collective-permute-start(bf16[48,3072]{1,0:T(8,128)(2,1)} %constant_dynamic-slice_fusion), channel_id=1, source_target_pairs={{0,2},{1,3},{2,0},{3,1},{4,6},{5,7},{6,4},{7,5},{8,10},{9,11},{10,... | collective-permute-start | bytes 884744 | tf_op jit(solution)/shard_map/ppermute | solution.py:25
  4.7 17.6 %collective-permute-start.1 = (bf16[48,3072]{1,0:T(8,128)(2,1)}, bf16[48,3072]{1,0:T(8,128)(2,1)}, u32[]{:S(2)}, u32[]{:S(2)}) collective-permute-start(bf16[48,3072]{1,0:T(8,128)(2,1)} %constant_dynamic-slice_fusion), channel_id=1, source_target_pairs={{0,8},{1,9},{2,10},{3,11},{4,12},{5,13},{6,14},{7,15},{8,0},{9,1},... | collective-permute-start | bytes 884744 | tf_op jit(solution)/shard_map/ppermute | solution.py:25
  7.3 13.7 %collective-permute-start = (bf16[48,3072]{1,0:T(8,128)(2,1)}, bf16[48,3072]{1,0:T(8,128)(2,1)}, u32[]{:S(2)}, u32[]{:S(2)}) collective-permute-start(bf16[48,3072]{1,0:T(8,128)(2,1)} %constant_dynamic-slice_fusion), channel_id=1, source_target_pairs={{0,4},{1,5},{2,6},{3,7},{4,0},{5,1},{6,2},{7,3},{8,12},{9,13},{10,... | collective-permute-start | bytes 884744 | tf_op jit(solution)/shard_map/ppermute | solution.py:25
  8.8 1.1 %copy-start.1 = (bf16[256,1536]{1,0:T(8,128)(2,1)S(1)}, bf16[256,1536]{1,0:T(8,128)(2,1)}, u32[]{:S(2)}) copy-start(bf16[256,1536]{1,0:T(8,128)(2,1)} %k0.7) | copy-start | bytes 2359300
  10.0 1.1 %copy-start.3 = (bf16[256,1536]{1,0:T(8,128)(2,1)S(1)}, bf16[256,1536]{1,0:T(8,128)(2,1)}, u32[]{:S(2)}) copy-start(bf16[256,1536]{1,0:T(8,128)(2,1)} %v0.7) | copy-start | bytes 2359300
  11.1 6.9 %copy-start = (bf16[256,1536]{1,0:T(8,128)(2,1)S(1)}, bf16[256,1536]{1,0:T(8,128)(2,1)}, u32[]{:S(2)}) copy-start(bf16[256,1536]{1,0:T(8,128)(2,1)} %q_ref.1) | copy-start | bytes 2359300
  11.1 7.7 %copy-start.9 = (s32[2,27]{1,0:T(2,128)S(1)}, s32[2,27]{1,0:T(2,128)}, u32[]{:S(2)}) copy-start(s32[2,27]{1,0:T(2,128)} %param.8) | copy-start | bytes 652
  12.4 6.5 %slice-start = ((bf16[256,1536]{1,0:T(8,128)(2,1)}), bf16[256,768]{1,0:T(8,128)(2,1)S(1)}, s32[]{:S(2)}) async-start(bf16[256,1536]{1,0:T(8,128)(2,1)} %q_ref.1), calls=%async_computation | async-start | bytes 786432 | tf_op jit(solution)/shard_map/slice | solution.py:379
  12.4 42.0 %collective-permute-start.7 = (bf16[2,256,1536]{2,1,0:T(8,128)(2,1)}, bf16[2,256,1536]{2,1,0:T(8,128)(2,1)}, u32[]{:S(2)}, u32[]{:S(2)}) collective-permute-start(bf16[2,256,1536]{2,1,0:T(8,128)(2,1)} %bitcast.1), channel_id=1, source_target_pairs={{1,0},{2,1},{3,2},{4,3},{5,4},{6,5},{7,6},{9,8},{10,9},{11,10},{12... | collective-permute-start | bytes 4718600 | tf_op jit(solution)/shard_map/ppermute | solution.py:35
  13.8 40.6 %collective-permute-start.6 = (bf16[2,256,1536]{2,1,0:T(8,128)(2,1)}, bf16[2,256,1536]{2,1,0:T(8,128)(2,1)}, u32[]{:S(2)}, u32[]{:S(2)}) collective-permute-start(bf16[2,256,1536]{2,1,0:T(8,128)(2,1)} %bitcast.1), channel_id=1, source_target_pairs={{0,1},{1,2},{2,3},{3,4},{4,5},{5,6},{6,7},{8,9},{9,10},{10,11},{11... | collective-permute-start | bytes 4718600 | tf_op jit(solution)/shard_map/ppermute | solution.py:35
  18.8 2.1 %copy-start.8 = (bf16[16,128]{1,0:T(8,128)(2,1)}, bf16[16,128]{1,0:T(8,128)(2,1)S(1)}, u32[]{:S(2)}) copy-start(bf16[16,128]{1,0:T(8,128)(2,1)S(1)} %pad.4.in_ref) | copy-start | bytes 12292
  19.7 16.4 %collective-permute-start.3 = (bf16[272,768]{1,0:T(8,128)(2,1)}, bf16[272,768]{1,0:T(8,128)(2,1)}, u32[]{:S(2)}, u32[]{:S(2)}) collective-permute-start(bf16[272,768]{1,0:T(8,128)(2,1)} %pad_maximum_fusion), channel_id=1, source_target_pairs={{0,8},{1,9},{2,10},{3,11},{4,12},{5,13},{6,14},{7,15},{8,0},{9,1},... | collective-permute-start | bytes 1253384 | tf_op jit(solution)/shard_map/ppermute | solution.py:386
  22.2 32.2 %copy-start.2 = (bf16[256,1536]{1,0:T(8,128)(2,1)S(1)}, bf16[256,1536]{1,0:T(8,128)(2,1)}, u32[]{:S(2)}) copy-start(bf16[256,1536]{1,0:T(8,128)(2,1)} %k0.7) | copy-start | bytes 2359300
  22.2 32.2 %copy-start.4 = (bf16[256,1536]{1,0:T(8,128)(2,1)S(1)}, bf16[256,1536]{1,0:T(8,128)(2,1)}, u32[]{:S(2)}) copy-start(bf16[256,1536]{1,0:T(8,128)(2,1)} %v0.7) | copy-start | bytes 2359300
  24.5 48.9 %collective-permute-start.15 = (bf16[144,3072]{1,0:T(8,128)(2,1)}, bf16[144,3072]{1,0:T(8,128)(2,1)}, u32[]{:S(2)}, u32[]{:S(2)}) collective-permute-start(bf16[144,3072]{1,0:T(8,128)(2,1)} %shard_map.58.refs_1_), channel_id=1, source_target_pairs={{0,16},{16,0},{1,17},{17,1},{2,18},{18,2},{3,19},{19,3},{4,20},{20... | collective-permute-start | bytes 2654216 | tf_op jit(solution)/shard_map/ppermute | solution.py:29
  36.1 23.7 %collective-permute-start.8 = (bf16[48,3072]{1,0:T(8,128)(2,1)}, bf16[48,3072]{1,0:T(8,128)(2,1)}, u32[]{:S(2)}, u32[]{:S(2)}) collective-permute-start(bf16[48,3072]{1,0:T(8,128)(2,1)} %collective-permute-done.1.refs_1_.refs_2_), channel_id=1, source_target_pairs={{0,4},{1,5},{2,6},{3,7},{4,0},{5,1},{6,2},{7,3},{8,12},{9,13},{10,... | collective-permute-start | bytes 884744 | tf_op jit(solution)/shard_map/ppermute | solution.py:25
  52.4 13.2 %collective-permute-start.5 = (bf16[256,768]{1,0:T(8,128)(2,1)}, bf16[256,768]{1,0:T(8,128)(2,1)}, u32[]{:S(2)}, u32[]{:S(2)}) collective-permute-start(bf16[256,768]{1,0:T(8,128)(2,1)} %slice.7), channel_id=1, source_target_pairs={{0,8},{1,9},{2,10},{3,11},{4,12},{5,13},{6,14},{7,15},{8,0},{9,1},... | collective-permute-start | bytes 1179656 | tf_op jit(solution)/shard_map/ppermute | solution.py:398
  54.4 21.3 %collective-permute-start.4 = (bf16[96,3072]{1,0:T(8,128)(2,1)}, bf16[96,3072]{1,0:T(8,128)(2,1)}, u32[]{:S(2)}, u32[]{:S(2)}) collective-permute-start(bf16[96,3072]{1,0:T(8,128)(2,1)} %shard_map.57), channel_id=1, source_target_pairs={{0,2},{1,3},{2,0},{3,1},{4,6},{5,7},{6,4},{7,5},{8,10},{9,11},{10,... | collective-permute-start | bytes 1769480 | tf_op jit(solution)/shard_map/ppermute | solution.py:25
  59.1 0.8 copy-start.6
  59.9 21.8 %collective-permute-start.16 = (bf16[48,3072]{1,0:T(8,128)(2,1)}, bf16[48,3072]{1,0:T(8,128)(2,1)}, u32[]{:S(2)}, u32[]{:S(2)}) collective-permute-start(bf16[48,3072]{1,0:T(8,128)(2,1)} %collective-permute-done.8.refs_3_), channel_id=1, source_target_pairs={{0,16},{16,0},{1,17},{17,1},{2,18},{18,2},{3,19},{19,3},{4,20},{20... | collective-permute-start | bytes 884744 | tf_op jit(solution)/shard_map/ppermute | solution.py:29
  61.3 20.3 %collective-permute-start.10 = (bf16[48,3072]{1,0:T(8,128)(2,1)}, bf16[48,3072]{1,0:T(8,128)(2,1)}, u32[]{:S(2)}, u32[]{:S(2)}) collective-permute-start(bf16[48,3072]{1,0:T(8,128)(2,1)} %collective-permute-done.8.refs_3_), channel_id=1, source_target_pairs={{0,2},{1,3},{2,0},{3,1},{4,6},{5,7},{6,4},{7,5},{8,10},{9,11},{10,... | collective-permute-start | bytes 884744 | tf_op jit(solution)/shard_map/ppermute | solution.py:25
  67.4 26.9 %collective-permute-start.14 = (bf16[264,768]{1,0:T(8,128)(2,1)}, bf16[264,768]{1,0:T(8,128)(2,1)}, u32[]{:S(2)}, u32[]{:S(2)}) collective-permute-start(bf16[264,768]{1,0:T(8,128)(2,1)} %shard_map.64), channel_id=1, source_target_pairs={{0,8},{1,9},{2,10},{3,11},{4,12},{5,13},{6,14},{7,15},{8,0},{9,1},... | collective-permute-start | bytes 1216520 | tf_op jit(solution)/shard_map/ppermute | solution.py:412
  68.1 9.1 %copy-start.7 = (bf16[16,128]{1,0:T(8,128)(2,1)S(1)}, bf16[16,128]{1,0:T(8,128)(2,1)}, u32[]{:S(2)}) copy-start(bf16[16,128]{1,0:T(8,128)(2,1)} %shard_map.56.list_ref) | copy-start | bytes 12292
  73.3 9.0 %copy-start.5 = (bf16[96,3072]{1,0:T(8,128)(2,1)S(1)}, bf16[96,3072]{1,0:T(8,128)(2,1)}, u32[]{:S(2)}) copy-start(bf16[96,3072]{1,0:T(8,128)(2,1)} %refs_0_.2) | copy-start | bytes 1769476
  73.3 29.6 %collective-permute-start.13 = (bf16[264,768]{1,0:T(8,128)(2,1)}, bf16[264,768]{1,0:T(8,128)(2,1)}, u32[]{:S(2)}, u32[]{:S(2)}) collective-permute-start(bf16[264,768]{1,0:T(8,128)(2,1)} %shard_map.60), channel_id=1, source_target_pairs={{0,8},{1,9},{2,10},{3,11},{4,12},{5,13},{6,14},{7,15},{8,0},{9,1},... | collective-permute-start | bytes 1216520 | tf_op jit(solution)/shard_map/ppermute | solution.py:412
  75.7 20.3 %collective-permute-start.9 = (bf16[96,3072]{1,0:T(8,128)(2,1)}, bf16[96,3072]{1,0:T(8,128)(2,1)}, u32[]{:S(2)}, u32[]{:S(2)}) collective-permute-start(bf16[96,3072]{1,0:T(8,128)(2,1)} %collective-permute-done.4.refs_0_), channel_id=1, source_target_pairs={{0,16},{16,0},{1,17},{17,1},{2,18},{18,2},{3,19},{19,3},{4,20},{20... | collective-permute-start | bytes 1769480 | tf_op jit(solution)/shard_map/ppermute | solution.py:29
  81.7 14.4 %collective-permute-start.11 = (bf16[48,3072]{1,0:T(8,128)(2,1)}, bf16[48,3072]{1,0:T(8,128)(2,1)}, u32[]{:S(2)}, u32[]{:S(2)}) collective-permute-start(bf16[48,3072]{1,0:T(8,128)(2,1)} %collective-permute-done.10.refs_2_), channel_id=1, source_target_pairs={{0,16},{16,0},{1,17},{17,1},{2,18},{18,2},{3,19},{19,3},{4,20},{20... | collective-permute-start | bytes 884744 | tf_op jit(solution)/shard_map/ppermute | solution.py:29
  85.6 13.2 %collective-permute-start.17 = (bf16[480,3072]{1,0:T(8,128)(2,1)}, bf16[480,3072]{1,0:T(8,128)(2,1)}, u32[]{:S(2)}, u32[]{:S(2)}) collective-permute-start(bf16[480,3072]{1,0:T(8,128)(2,1)} %shard_map.66.refs_0_), channel_id=1, source_target_pairs={{0,1},{1,0},{2,3},{3,2},{4,5},{5,4},{6,7},{7,6},{8,9},{9,8},{10,11... | collective-permute-start | bytes 8847368 | tf_op jit(solution)/shard_map/ppermute | solution.py:25
  98.7 4.2 %collective-permute-start.12 = (bf16[288,3072]{1,0:T(8,128)(2,1)}, bf16[288,3072]{1,0:T(8,128)(2,1)}, u32[]{:S(2)}, u32[]{:S(2)}) collective-permute-start(bf16[288,3072]{1,0:T(8,128)(2,1)} %shard_map.63.refs_0_), channel_id=1, source_target_pairs={{0,1},{1,0},{2,3},{3,2},{4,5},{5,4},{6,7},{7,6},{8,9},{9,8},{10,11... | collective-permute-start | bytes 5308424 | tf_op jit(solution)/shard_map/ppermute | solution.py:25

commit v11 on v10

--- a/solution.py
+++ b/solution.py
@@ -269,7 +269,7 @@
 def project_kernel(plan, count, partner_ref, *refs):
     sources, refs = refs[: len(plan)], refs[len(plan) :]
     parts, refs = refs[:count], refs[count:]
-    merged, _, out_ref, held, attention, staged, sems, out_sems = refs
+    merged, held, out_ref, _, attention, staged, sems, out_sems = refs
     copies = bring(plan, sources, held, sems)
     first = merged.shape[1]
     attention[:, :first] = merged[...]

time: 110 us -> 110 us (level)
  no operation moved by 1% of the time
where the time goes in v11:
time: 110 us
  Pallas kernels  44.4 us (40%)
  starting transfers between devices  39.8 us (36%)
  waiting for transfers between devices  18.8 us (17%)
  local copies, waits for them, and re-layouts  5.54 us (5%)
    ppermute x8, starting transfers between devices, swap_bit(): return lax.ppermute(value, 'seq', [(s, s ^ bit) for s in range(count)])  25.7 us
    pallas_call x4, Pallas kernels, attend(): pl.pallas_call(functools.partial(attend_kernel, rows, per_block), grid=(h...  18.8 us
    pallas_call x5, Pallas kernels, join(): pl.pallas_call(functools.partial(join_kernel, len(arrays)), in_specs=[pl....  11.4 us
    ppermute x1, waiting for transfers between devices, body(): first = lax.ppermute(asking, 'seq', pairs)  10.1 us
    pallas_call x1, Pallas kernels, project(): pl.pallas_call(functools.partial(project_kernel, plan, len(parts)), in_sp...  6.61 us
    ppermute x2, starting transfers between devices, column_shift(): return lax.ppermute(value, 'seq', pairs)  5.61 us
    ppermute x2, waiting for transfers between devices, body(): back.append(lax.ppermute(sending, 'seq', row_pairs(parity)))  5.37 us
    ppermute x4, starting transfers between devices, swap_group(): return lax.ppermute(value, 'group', [(s, s ^ 1) for s in range(groups)])  5.14 us
  transfers between devices with their start and end apart: 18, of which 5 were waited for; matrix products, arithmetic and copies ran while one was open for 1% of the time, Pallas kernels for 35%

profile of v11, /device:TPU:0, one launch (start us, length us, event | category | flops | bytes accessed | tf_op | source)
XLA Modules:
  0.0 109.5 jit_solution(5833317721779163304)
XLA Ops:
  0.0 1.7 %constant_dynamic-slice_fusion = bf16[48,3072]{1,0:T(8,128)(2,1)} fusion(bf16[96,3072]{1,0:T(8,128)(2,1)} %refs_0_.2, s32[]{:T(128)S(6)} %select_n.21), kind=kLoop, calls=%fused_computation.2 | loop fusion | bytes 589828 | tf_op jit(solution)/shard_map/dynamic_slice | solution.py:365
  1.7 3.0 %collective-permute-start.2 = (bf16[48,3072]{1,0:T(8,128)(2,1)}, bf16[48,3072]{1,0:T(8,128)(2,1)}, u32[]{:S(2)}, u32[]{:S(2)}) collective-permute-start(bf16[48,3072]{1,0:T(8,128)(2,1)} %constant_dynamic-slice_fusion), channel_id=1, source_target_pairs={{0,2},{1,3},{2,0},{3,1},{4,6},{5,7},{6,4},{7,5},{8,10},{9,11},{10,... | collective-permute-start | bytes 884744 | tf_op jit(solution)/shard_map/ppermute | solution.py:25
  4.7 2.6 %collective-permute-start.1 = (bf16[48,3072]{1,0:T(8,128)(2,1)}, bf16[48,3072]{1,0:T(8,128)(2,1)}, u32[]{:S(2)}, u32[]{:S(2)}) collective-permute-start(bf16[48,3072]{1,0:T(8,128)(2,1)} %constant_dynamic-slice_fusion), channel_id=1, source_target_pairs={{0,8},{1,9},{2,10},{3,11},{4,12},{5,13},{6,14},{7,15},{8,0},{9,1},... | collective-permute-start | bytes 884744 | tf_op jit(solution)/shard_map/ppermute | solution.py:25
  7.3 1.6 %collective-permute-start = (bf16[48,3072]{1,0:T(8,128)(2,1)}, bf16[48,3072]{1,0:T(8,128)(2,1)}, u32[]{:S(2)}, u32[]{:S(2)}) collective-permute-start(bf16[48,3072]{1,0:T(8,128)(2,1)} %constant_dynamic-slice_fusion), channel_id=1, source_target_pairs={{0,4},{1,5},{2,6},{3,7},{4,0},{5,1},{6,2},{7,3},{8,12},{9,13},{10,... | collective-permute-start | bytes 884744 | tf_op jit(solution)/shard_map/ppermute | solution.py:25
  8.8 1.1 %copy-done.1 = bf16[256,1536]{1,0:T(8,128)(2,1)S(1)} copy-done((bf16[256,1536]{1,0:T(8,128)(2,1)S(1)}, bf16[256,1536]{1,0:T(8,128)(2,1)}, u32[]{:S(2)}) %copy-start.1) | copy-done | bytes 786456
  10.0 1.1 %copy-done.3 = bf16[256,1536]{1,0:T(8,128)(2,1)S(1)} copy-done((bf16[256,1536]{1,0:T(8,128)(2,1)S(1)}, bf16[256,1536]{1,0:T(8,128)(2,1)}, u32[]{:S(2)}) %copy-start.3) | copy-done | bytes 786456
  11.1 1.3 %shard_map.55 = bf16[512,1536]{1,0:T(8,128)(2,1)} custom-call(bf16[256,1536]{1,0:T(8,128)(2,1)S(1)} %copy-done.1, bf16[256,1536]{1,0:T(8,128)(2,1)S(1)} %copy-done.3), custom_call_target="tpu_custom_call" | custom-call | flops 999999995904 | tf_op jit(solution)/shard_map/pallas_call | solution.py:65
  12.4 0.0 slice-start
  12.4 1.4 %collective-permute-start.7 = (bf16[2,256,1536]{2,1,0:T(8,128)(2,1)}, bf16[2,256,1536]{2,1,0:T(8,128)(2,1)}, u32[]{:S(2)}, u32[]{:S(2)}) collective-permute-start(bf16[2,256,1536]{2,1,0:T(8,128)(2,1)} %bitcast.1), channel_id=1, source_target_pairs={{1,0},{2,1},{3,2},{4,3},{5,4},{6,5},{7,6},{9,8},{10,9},{11,10},{12... | collective-permute-start | bytes 4718600 | tf_op jit(solution)/shard_map/ppermute | solution.py:35
  13.8 4.2 %collective-permute-start.6 = (bf16[2,256,1536]{2,1,0:T(8,128)(2,1)}, bf16[2,256,1536]{2,1,0:T(8,128)(2,1)}, u32[]{:S(2)}, u32[]{:S(2)}) collective-permute-start(bf16[2,256,1536]{2,1,0:T(8,128)(2,1)} %bitcast.1), channel_id=1, source_target_pairs={{0,1},{1,2},{2,3},{3,4},{4,5},{5,6},{6,7},{8,9},{9,10},{10,11},{11... | collective-permute-start | bytes 4718600 | tf_op jit(solution)/shard_map/ppermute | solution.py:35
  18.0 0.8 slice.7
  18.9 0.8 pad_maximum_fusion
  19.7 0.0 collective-permute-done.2.refs_1_
  19.7 0.3 collective-permute-start.3
  20.0 1.0 collective-permute-done.refs_0_
  21.0 1.3 %shard_map.56.list_ref = bf16[16,128]{1,0:T(8,128)(2,1)} custom-call(bf16[16,128]{1,0:T(8,128)(2,1)} %copy-done.8), custom_call_target="tpu_custom_call" | custom-call | flops 999999995904 | tf_op jit(solution)/shard_map/pallas_call | solution.py:82
  22.2 0.0 collective-permute-done.1.refs_1_.refs_2_
  22.2 2.2 %shard_map.58.refs_1_ = bf16[144,3072]{1,0:T(8,128)(2,1)} custom-call(bf16[48,3072]{1,0:T(8,128)(2,1)} %collective-permute-done.refs_0_, bf16[48,3072]{1,0:T(8,128)(2,1)} %collective-permute-done.2.refs_1_, bf16[48,3072]{1,0:T(8,128)(2,1)} %collective-permute-done.1.refs_1_.refs_2_), custom_call_target="tpu_custom_call" | custom-call | flops 999999995904 | tf_op jit(solution)/shard_map/pallas_call | solution.py:65
  24.5 1.6 %collective-permute-start.15 = (bf16[144,3072]{1,0:T(8,128)(2,1)}, bf16[144,3072]{1,0:T(8,128)(2,1)}, u32[]{:S(2)}, u32[]{:S(2)}) collective-permute-start(bf16[144,3072]{1,0:T(8,128)(2,1)} %shard_map.58.refs_1_), channel_id=1, source_target_pairs={{0,16},{16,0},{1,17},{17,1},{2,18},{18,2},{3,19},{19,3},{4,20},{20... | collective-permute-start | bytes 2654216 | tf_op jit(solution)/shard_map/ppermute | solution.py:29
  26.0 10.1 %collective-permute-done.3.list_ref.q_ref = bf16[272,768]{1,0:T(8,128)(2,1)} collective-permute-done((bf16[272,768]{1,0:T(8,128)(2,1)}, bf16[272,768]{1,0:T(8,128)(2,1)}, u32[]{:S(2)}, u32[]{:S(2)}) %collective-permute-start.3) | collective-permute-done | bytes 417824 | tf_op jit(solution)/shard_map/ppermute | solution.py:386
  36.1 16.3 %collective-permute-start.8 = (bf16[48,3072]{1,0:T(8,128)(2,1)}, bf16[48,3072]{1,0:T(8,128)(2,1)}, u32[]{:S(2)}, u32[]{:S(2)}) collective-permute-start(bf16[48,3072]{1,0:T(8,128)(2,1)} %collective-permute-done.1.refs_1_.refs_2_), channel_id=1, source_target_pairs={{0,4},{1,5},{2,6},{3,7},{4,0},{5,1},{6,2},{7,3},{8,12},{9,13},{10,... | collective-permute-start | bytes 884744 | tf_op jit(solution)/shard_map/ppermute | solution.py:25
  52.4 1.9 %shard_map.57 = bf16[96,3072]{1,0:T(8,128)(2,1)} custom-call(bf16[48,3072]{1,0:T(8,128)(2,1)} %collective-permute-done.refs_0_, bf16[48,3072]{1,0:T(8,128)(2,1)} %collective-permute-done.1.refs_1_.refs_2_), custom_call_target="tpu_custom_call" | custom-call | tf_op jit(solution)/shard_map/pallas_call | solution.py:65
  54.4 0.1 collective-permute-start.4
  54.5 4.6 %shard_map.59.in_ref = bf16[264,768]{1,0:T(8,128)(2,1)S(1)} custom-call(bf16[272,768]{1,0:T(8,128)(2,1)} %collective-permute-done.3.list_ref.q_ref, bf16[272,768]{1,0:T(8,128)(2,1)} %collective-permute-done.3.list_ref.q_ref, bf16[256,1536]{1,0:T(8,128)(2,1)S(1)} %copy-done.2, bf16[2,256,1536]{2,1,0:T(8,128)(2,1)} %collective-permute-done.6.ka.va, ...), custom_call_target="tpu_custom_call" | custom-call | flops 999999995904 | tf_op jit(solution)/shard_map/pallas_call | solution.py:158
  59.1 0.0 copy-start.6
  59.1 0.7 copy-done.6
  59.8 0.0 collective-permute-done.8.refs_3_
  59.9 1.5 %collective-permute-start.16 = (bf16[48,3072]{1,0:T(8,128)(2,1)}, bf16[48,3072]{1,0:T(8,128)(2,1)}, u32[]{:S(2)}, u32[]{:S(2)}) collective-permute-start(bf16[48,3072]{1,0:T(8,128)(2,1)} %collective-permute-done.8.refs_3_), channel_id=1, source_target_pairs={{0,16},{16,0},{1,17},{17,1},{2,18},{18,2},{3,19},{19,3},{4,20},{20... | collective-permute-start | bytes 884744 | tf_op jit(solution)/shard_map/ppermute | solution.py:29
  61.3 2.0 %collective-permute-start.10 = (bf16[48,3072]{1,0:T(8,128)(2,1)}, bf16[48,3072]{1,0:T(8,128)(2,1)}, u32[]{:S(2)}, u32[]{:S(2)}) collective-permute-start(bf16[48,3072]{1,0:T(8,128)(2,1)} %collective-permute-done.8.refs_3_), channel_id=1, source_target_pairs={{0,2},{1,3},{2,0},{3,1},{4,6},{5,7},{6,4},{7,5},{8,10},{9,11},{10,... | collective-permute-start | bytes 884744 | tf_op jit(solution)/shard_map/ppermute | solution.py:25
  63.3 2.3 %collective-permute-done.5.q_ref = bf16[256,768]{1,0:T(8,128)(2,1)} collective-permute-done((bf16[256,768]{1,0:T(8,128)(2,1)}, bf16[256,768]{1,0:T(8,128)(2,1)}, u32[]{:S(2)}, u32[]{:S(2)}) %collective-permute-start.5) | collective-permute-done | bytes 393248 | tf_op jit(solution)/shard_map/ppermute | solution.py:398
  65.7 1.8 %shard_map.64 = bf16[264,768]{1,0:T(8,128)(2,1)} custom-call(bf16[264,768]{1,0:T(8,128)(2,1)} %copy-done.6), custom_call_target="tpu_custom_call" | custom-call | tf_op jit(solution)/shard_map/pallas_call | solution.py:82
  67.4 0.6 collective-permute-start.14
  68.1 5.3 %shard_map.60 = bf16[264,768]{1,0:T(8,128)(2,1)} custom-call(bf16[272,768]{1,0:T(8,128)(2,1)} %collective-permute-done.3.list_ref.q_ref, bf16[256,768]{1,0:T(8,128)(2,1)} %collective-permute-done.5.q_ref, bf16[256,1536]{1,0:T(8,128)(2,1)S(1)} %copy-done.2, bf16[2,256,1536]{2,1,0:T(8,128)(2,1)} %collective-permute-done.6.ka.va, ...), custom_call_target="tpu_custom_call" | custom-call | flops 999999995904 | tf_op jit(solution)/shard_map/pallas_call | solution.py:158
  73.3 0.0 collective-permute-done.15.refs_2_
  73.3 2.4 %collective-permute-start.13 = (bf16[264,768]{1,0:T(8,128)(2,1)}, bf16[264,768]{1,0:T(8,128)(2,1)}, u32[]{:S(2)}, u32[]{:S(2)}) collective-permute-start(bf16[264,768]{1,0:T(8,128)(2,1)} %shard_map.60), channel_id=1, source_target_pairs={{0,8},{1,9},{2,10},{3,11},{4,12},{5,13},{6,14},{7,15},{8,0},{9,1},... | collective-permute-start | bytes 1216520 | tf_op jit(solution)/shard_map/ppermute | solution.py:412
  75.7 1.5 %collective-permute-start.9 = (bf16[96,3072]{1,0:T(8,128)(2,1)}, bf16[96,3072]{1,0:T(8,128)(2,1)}, u32[]{:S(2)}, u32[]{:S(2)}) collective-permute-start(bf16[96,3072]{1,0:T(8,128)(2,1)} %collective-permute-done.4.refs_0_), channel_id=1, source_target_pairs={{0,16},{16,0},{1,17},{17,1},{2,18},{18,2},{3,19},{19,3},{4,20},{20... | collective-permute-start | bytes 1769480 | tf_op jit(solution)/shard_map/ppermute | solution.py:29
  77.2 4.5 %shard_map.61.refs_0_ = f32[264,768]{1,0:T(8,128)S(1)} custom-call(bf16[16,128]{1,0:T(8,128)(2,1)S(1)} %copy-done.7, bf16[256,1536]{1,0:T(8,128)(2,1)S(1)} %copy-done, bf16[256,1536]{1,0:T(8,128)(2,1)S(1)} %copy-done.2, bf16[2,256,1536]{2,1,0:T(8,128)(2,1)} %collective-permute-done.6.ka.va, bf16[2,256,1536]{2,1,0:T(8,128)(2,1)} %collective-permute-done.7.kb.vb, ...), custom_call_target="tpu_custom_call" | custom-call | tf_op jit(solution)/shard_map/pallas_call | solution.py:158
  81.7 0.6 collective-permute-start.11
  82.3 3.3 %shard_map.66.refs_0_ = bf16[480,3072]{1,0:T(8,128)(2,1)} custom-call(bf16[96,3072]{1,0:T(8,128)(2,1)S(1)} %copy-done.5, bf16[144,3072]{1,0:T(8,128)(2,1)} %shard_map.58.refs_1_, bf16[144,3072]{1,0:T(8,128)(2,1)} %collective-permute-done.15.refs_2_, bf16[48,3072]{1,0:T(8,128)(2,1)} %collective-permute-done.8.refs_3_, ...), custom_call_target="tpu_custom_call" | custom-call | tf_op jit(solution)/shard_map/pallas_call | solution.py:65
  85.6 0.1 collective-permute-start.17
  85.7 4.5 %shard_map.62.refs_2_ = f32[264,768]{1,0:T(8,128)S(1)} custom-call(bf16[16,128]{1,0:T(8,128)(2,1)S(1)} %copy-done.7, bf16[256,1536]{1,0:T(8,128)(2,1)S(1)} %copy-done, bf16[256,1536]{1,0:T(8,128)(2,1)S(1)} %copy-done.2, bf16[2,256,1536]{2,1,0:T(8,128)(2,1)} %collective-permute-done.6.ka.va, bf16[2,256,1536]{2,1,0:T(8,128)(2,1)} %collective-permute-done.7.kb.vb, ...), custom_call_target="tpu_custom_call" | custom-call | tf_op jit(solution)/shard_map/pallas_call | solution.py:158
  90.2 4.1 %collective-permute-done.14.refs_1_ = bf16[264,768]{1,0:T(8,128)(2,1)} collective-permute-done((bf16[264,768]{1,0:T(8,128)(2,1)}, bf16[264,768]{1,0:T(8,128)(2,1)}, u32[]{:S(2)}, u32[]{:S(2)}) %collective-permute-start.14) | collective-permute-done | bytes 405536 | tf_op jit(solution)/shard_map/ppermute | solution.py:412
  94.3 1.7 %shard_map.65.refs_2_.refs_4_ = bf16[256,768]{1,0:T(8,128)(2,1)S(1)} custom-call(s32[1]{0:T(128)} %bitcast.partner_ref, f32[264,768]{1,0:T(8,128)S(1)} %shard_map.61.refs_0_, bf16[264,768]{1,0:T(8,128)(2,1)} %collective-permute-done.14.refs_1_), custom_call_target="tpu_custom_call" | custom-call | flops 999999995904 | tf_op jit(solution)/shard_map/pallas_call | solution.py:224
  96.0 2.7 %shard_map.63.refs_0_ = bf16[288,3072]{1,0:T(8,128)(2,1)} custom-call(bf16[96,3072]{1,0:T(8,128)(2,1)} %collective-permute-done.4.refs_0_, bf16[96,3072]{1,0:T(8,128)(2,1)} %collective-permute-done.9.refs_1_, bf16[48,3072]{1,0:T(8,128)(2,1)} %collective-permute-done.10.refs_2_, bf16[48,3072]{1,0:T(8,128)(2,1)} %collective-permute-done.11.refs_3_), custom_call_target="tpu_custom_call" | custom-call | tf_op jit(solution)/shard_map/pallas_call | solution.py:65
  98.7 0.1 collective-permute-start.12
  98.8 2.8 %shard_map.67.refs_5_ = bf16[1536,3072]{1,0:T(8,128)(2,1)S(1)} custom-call(bf16[480,3072]{1,0:T(8,128)(2,1)} %shard_map.66.refs_0_, bf16[480,3072]{1,0:T(8,128)(2,1)} %collective-permute-done.17.refs_1_, bf16[256,768]{1,0:T(8,128)(2,1)S(1)} %shard_map.65.refs_2_.refs_4_), custom_call_target="tpu_custom_call" | custom-call | flops 999999995904 | tf_op jit(solution)/shard_map/pallas_call | solution.py:258
  101.6 1.3 %collective-permute-done.13.refs_3_ = bf16[264,768]{1,0:T(8,128)(2,1)} collective-permute-done((bf16[264,768]{1,0:T(8,128)(2,1)}, bf16[264,768]{1,0:T(8,128)(2,1)}, u32[]{:S(2)}, u32[]{:S(2)}) %collective-permute-start.13) | collective-permute-done | bytes 405536 | tf_op jit(solution)/shard_map/ppermute | solution.py:412
  102.9 6.6 %shard_map.68 = (bf16[256,3072]{1,0:T(8,128)(2,1)}, bf16[1536,3072]{1,0:T(8,128)(2,1)S(1)}) custom-call(s32[1]{0:T(128)} %bitcast.partner_ref, bf16[288,3072]{1,0:T(8,128)(2,1)} %shard_map.63.refs_0_, bf16[288,3072]{1,0:T(8,128)(2,1)} %collective-permute-done.12.refs_1_, f32[264,768]{1,0:T(8,128)S(1)} %shard_map.62.refs_2_, ...), custom_call_target="tpu_custom_call", output_to_operand_aliasing={{1}: (6, {})} | custom-call | tf_op jit(solution)/shard_map/pallas_call | solution.py:301
  (31 shorter events, 0.1 us)
Async XLA Ops:
  1.7 18.0 %collective-permute-start.2 = (bf16[48,3072]{1,0:T(8,128)(2,1)}, bf16[48,3072]{1,0:T(8,128)(2,1)}, u32[]{:S(2)}, u32[]{:S(2)}) collective-permute-start(bf16[48,3072]{1,0:T(8,128)(2,1)} %constant_dynamic-slice_fusion), channel_id=1, source_target_pairs={{0,2},{1,3},{2,0},{3,1},{4,6},{5,7},{6,4},{7,5},{8,10},{9,11},{10,... | collective-permute-start | bytes 884744 | tf_op jit(solution)/shard_map/ppermute | solution.py:25
  4.7 17.6 %collective-permute-start.1 = (bf16[48,3072]{1,0:T(8,128)(2,1)}, bf16[48,3072]{1,0:T(8,128)(2,1)}, u32[]{:S(2)}, u32[]{:S(2)}) collective-permute-start(bf16[48,3072]{1,0:T(8,128)(2,1)} %constant_dynamic-slice_fusion), channel_id=1, source_target_pairs={{0,8},{1,9},{2,10},{3,11},{4,12},{5,13},{6,14},{7,15},{8,0},{9,1},... | collective-permute-start | bytes 884744 | tf_op jit(solution)/shard_map/ppermute | solution.py:25
  7.3 13.7 %collective-permute-start = (bf16[48,3072]{1,0:T(8,128)(2,1)}, bf16[48,3072]{1,0:T(8,128)(2,1)}, u32[]{:S(2)}, u32[]{:S(2)}) collective-permute-start(bf16[48,3072]{1,0:T(8,128)(2,1)} %constant_dynamic-slice_fusion), channel_id=1, source_target_pairs={{0,4},{1,5},{2,6},{3,7},{4,0},{5,1},{6,2},{7,3},{8,12},{9,13},{10,... | collective-permute-start | bytes 884744 | tf_op jit(solution)/shard_map/ppermute | solution.py:25
  8.8 1.1 %copy-start.1 = (bf16[256,1536]{1,0:T(8,128)(2,1)S(1)}, bf16[256,1536]{1,0:T(8,128)(2,1)}, u32[]{:S(2)}) copy-start(bf16[256,1536]{1,0:T(8,128)(2,1)} %k0.7) | copy-start | bytes 2359300
  10.0 1.1 %copy-start.3 = (bf16[256,1536]{1,0:T(8,128)(2,1)S(1)}, bf16[256,1536]{1,0:T(8,128)(2,1)}, u32[]{:S(2)}) copy-start(bf16[256,1536]{1,0:T(8,128)(2,1)} %v0.7) | copy-start | bytes 2359300
  11.1 6.9 %copy-start = (bf16[256,1536]{1,0:T(8,128)(2,1)S(1)}, bf16[256,1536]{1,0:T(8,128)(2,1)}, u32[]{:S(2)}) copy-start(bf16[256,1536]{1,0:T(8,128)(2,1)} %q_ref.1) | copy-start | bytes 2359300
  11.1 7.7 %copy-start.9 = (s32[2,27]{1,0:T(2,128)S(1)}, s32[2,27]{1,0:T(2,128)}, u32[]{:S(2)}) copy-start(s32[2,27]{1,0:T(2,128)} %param.8) | copy-start | bytes 652
  12.4 6.5 %slice-start = ((bf16[256,1536]{1,0:T(8,128)(2,1)}), bf16[256,768]{1,0:T(8,128)(2,1)S(1)}, s32[]{:S(2)}) async-start(bf16[256,1536]{1,0:T(8,128)(2,1)} %q_ref.1), calls=%async_computation | async-start | bytes 786432 | tf_op jit(solution)/shard_map/slice | solution.py:379
  12.4 42.0 %collective-permute-start.7 = (bf16[2,256,1536]{2,1,0:T(8,128)(2,1)}, bf16[2,256,1536]{2,1,0:T(8,128)(2,1)}, u32[]{:S(2)}, u32[]{:S(2)}) collective-permute-start(bf16[2,256,1536]{2,1,0:T(8,128)(2,1)} %bitcast.1), channel_id=1, source_target_pairs={{1,0},{2,1},{3,2},{4,3},{5,4},{6,5},{7,6},{9,8},{10,9},{11,10},{12... | collective-permute-start | bytes 4718600 | tf_op jit(solution)/shard_map/ppermute | solution.py:35
  13.8 40.6 %collective-permute-start.6 = (bf16[2,256,1536]{2,1,0:T(8,128)(2,1)}, bf16[2,256,1536]{2,1,0:T(8,128)(2,1)}, u32[]{:S(2)}, u32[]{:S(2)}) collective-permute-start(bf16[2,256,1536]{2,1,0:T(8,128)(2,1)} %bitcast.1), channel_id=1, source_target_pairs={{0,1},{1,2},{2,3},{3,4},{4,5},{5,6},{6,7},{8,9},{9,10},{10,11},{11... | collective-permute-start | bytes 4718600 | tf_op jit(solution)/shard_map/ppermute | solution.py:35
  18.8 2.1 %copy-start.8 = (bf16[16,128]{1,0:T(8,128)(2,1)}, bf16[16,128]{1,0:T(8,128)(2,1)S(1)}, u32[]{:S(2)}) copy-start(bf16[16,128]{1,0:T(8,128)(2,1)S(1)} %pad.4.in_ref) | copy-start | bytes 12292
  19.7 16.4 %collective-permute-start.3 = (bf16[272,768]{1,0:T(8,128)(2,1)}, bf16[272,768]{1,0:T(8,128)(2,1)}, u32[]{:S(2)}, u32[]{:S(2)}) collective-permute-start(bf16[272,768]{1,0:T(8,128)(2,1)} %pad_maximum_fusion), channel_id=1, source_target_pairs={{0,8},{1,9},{2,10},{3,11},{4,12},{5,13},{6,14},{7,15},{8,0},{9,1},... | collective-permute-start | bytes 1253384 | tf_op jit(solution)/shard_map/ppermute | solution.py:386
  22.2 32.2 %copy-start.2 = (bf16[256,1536]{1,0:T(8,128)(2,1)S(1)}, bf16[256,1536]{1,0:T(8,128)(2,1)}, u32[]{:S(2)}) copy-start(bf16[256,1536]{1,0:T(8,128)(2,1)} %k0.7) | copy-start | bytes 2359300
  22.2 32.2 %copy-start.4 = (bf16[256,1536]{1,0:T(8,128)(2,1)S(1)}, bf16[256,1536]{1,0:T(8,128)(2,1)}, u32[]{:S(2)}) copy-start(bf16[256,1536]{1,0:T(8,128)(2,1)} %v0.7) | copy-start | bytes 2359300
  24.5 48.9 %collective-permute-start.15 = (bf16[144,3072]{1,0:T(8,128)(2,1)}, bf16[144,3072]{1,0:T(8,128)(2,1)}, u32[]{:S(2)}, u32[]{:S(2)}) collective-permute-start(bf16[144,3072]{1,0:T(8,128)(2,1)} %shard_map.58.refs_1_), channel_id=1, source_target_pairs={{0,16},{16,0},{1,17},{17,1},{2,18},{18,2},{3,19},{19,3},{4,20},{20... | collective-permute-start | bytes 2654216 | tf_op jit(solution)/shard_map/ppermute | solution.py:29
  36.1 23.7 %collective-permute-start.8 = (bf16[48,3072]{1,0:T(8,128)(2,1)}, bf16[48,3072]{1,0:T(8,128)(2,1)}, u32[]{:S(2)}, u32[]{:S(2)}) collective-permute-start(bf16[48,3072]{1,0:T(8,128)(2,1)} %collective-permute-done.1.refs_1_.refs_2_), channel_id=1, source_target_pairs={{0,4},{1,5},{2,6},{3,7},{4,0},{5,1},{6,2},{7,3},{8,12},{9,13},{10,... | collective-permute-start | bytes 884744 | tf_op jit(solution)/shard_map/ppermute | solution.py:25
  52.4 13.2 %collective-permute-start.5 = (bf16[256,768]{1,0:T(8,128)(2,1)}, bf16[256,768]{1,0:T(8,128)(2,1)}, u32[]{:S(2)}, u32[]{:S(2)}) collective-permute-start(bf16[256,768]{1,0:T(8,128)(2,1)} %slice.7), channel_id=1, source_target_pairs={{0,8},{1,9},{2,10},{3,11},{4,12},{5,13},{6,14},{7,15},{8,0},{9,1},... | collective-permute-start | bytes 1179656 | tf_op jit(solution)/shard_map/ppermute | solution.py:398
  54.4 21.3 %collective-permute-start.4 = (bf16[96,3072]{1,0:T(8,128)(2,1)}, bf16[96,3072]{1,0:T(8,128)(2,1)}, u32[]{:S(2)}, u32[]{:S(2)}) collective-permute-start(bf16[96,3072]{1,0:T(8,128)(2,1)} %shard_map.57), channel_id=1, source_target_pairs={{0,2},{1,3},{2,0},{3,1},{4,6},{5,7},{6,4},{7,5},{8,10},{9,11},{10,... | collective-permute-start | bytes 1769480 | tf_op jit(solution)/shard_map/ppermute | solution.py:25
  59.1 0.8 copy-start.6
  59.9 21.8 %collective-permute-start.16 = (bf16[48,3072]{1,0:T(8,128)(2,1)}, bf16[48,3072]{1,0:T(8,128)(2,1)}, u32[]{:S(2)}, u32[]{:S(2)}) collective-permute-start(bf16[48,3072]{1,0:T(8,128)(2,1)} %collective-permute-done.8.refs_3_), channel_id=1, source_target_pairs={{0,16},{16,0},{1,17},{17,1},{2,18},{18,2},{3,19},{19,3},{4,20},{20... | collective-permute-start | bytes 884744 | tf_op jit(solution)/shard_map/ppermute | solution.py:29
  61.3 20.3 %collective-permute-start.10 = (bf16[48,3072]{1,0:T(8,128)(2,1)}, bf16[48,3072]{1,0:T(8,128)(2,1)}, u32[]{:S(2)}, u32[]{:S(2)}) collective-permute-start(bf16[48,3072]{1,0:T(8,128)(2,1)} %collective-permute-done.8.refs_3_), channel_id=1, source_target_pairs={{0,2},{1,3},{2,0},{3,1},{4,6},{5,7},{6,4},{7,5},{8,10},{9,11},{10,... | collective-permute-start | bytes 884744 | tf_op jit(solution)/shard_map/ppermute | solution.py:25
  67.4 26.9 %collective-permute-start.14 = (bf16[264,768]{1,0:T(8,128)(2,1)}, bf16[264,768]{1,0:T(8,128)(2,1)}, u32[]{:S(2)}, u32[]{:S(2)}) collective-permute-start(bf16[264,768]{1,0:T(8,128)(2,1)} %shard_map.64), channel_id=1, source_target_pairs={{0,8},{1,9},{2,10},{3,11},{4,12},{5,13},{6,14},{7,15},{8,0},{9,1},... | collective-permute-start | bytes 1216520 | tf_op jit(solution)/shard_map/ppermute | solution.py:412
  68.1 9.1 %copy-start.7 = (bf16[16,128]{1,0:T(8,128)(2,1)S(1)}, bf16[16,128]{1,0:T(8,128)(2,1)}, u32[]{:S(2)}) copy-start(bf16[16,128]{1,0:T(8,128)(2,1)} %shard_map.56.list_ref) | copy-start | bytes 12292
  73.3 9.0 %copy-start.5 = (bf16[96,3072]{1,0:T(8,128)(2,1)S(1)}, bf16[96,3072]{1,0:T(8,128)(2,1)}, u32[]{:S(2)}) copy-start(bf16[96,3072]{1,0:T(8,128)(2,1)} %refs_0_.2) | copy-start | bytes 1769476
  73.3 29.6 %collective-permute-start.13 = (bf16[264,768]{1,0:T(8,128)(2,1)}, bf16[264,768]{1,0:T(8,128)(2,1)}, u32[]{:S(2)}, u32[]{:S(2)}) collective-permute-start(bf16[264,768]{1,0:T(8,128)(2,1)} %shard_map.60), channel_id=1, source_target_pairs={{0,8},{1,9},{2,10},{3,11},{4,12},{5,13},{6,14},{7,15},{8,0},{9,1},... | collective-permute-start | bytes 1216520 | tf_op jit(solution)/shard_map/ppermute | solution.py:412
  75.7 20.3 %collective-permute-start.9 = (bf16[96,3072]{1,0:T(8,128)(2,1)}, bf16[96,3072]{1,0:T(8,128)(2,1)}, u32[]{:S(2)}, u32[]{:S(2)}) collective-permute-start(bf16[96,3072]{1,0:T(8,128)(2,1)} %collective-permute-done.4.refs_0_), channel_id=1, source_target_pairs={{0,16},{16,0},{1,17},{17,1},{2,18},{18,2},{3,19},{19,3},{4,20},{20... | collective-permute-start | bytes 1769480 | tf_op jit(solution)/shard_map/ppermute | solution.py:29
  81.7 14.4 %collective-permute-start.11 = (bf16[48,3072]{1,0:T(8,128)(2,1)}, bf16[48,3072]{1,0:T(8,128)(2,1)}, u32[]{:S(2)}, u32[]{:S(2)}) collective-permute-start(bf16[48,3072]{1,0:T(8,128)(2,1)} %collective-permute-done.10.refs_2_), channel_id=1, source_target_pairs={{0,16},{16,0},{1,17},{17,1},{2,18},{18,2},{3,19},{19,3},{4,20},{20... | collective-permute-start | bytes 884744 | tf_op jit(solution)/shard_map/ppermute | solution.py:29
  85.6 13.2 %collective-permute-start.17 = (bf16[480,3072]{1,0:T(8,128)(2,1)}, bf16[480,3072]{1,0:T(8,128)(2,1)}, u32[]{:S(2)}, u32[]{:S(2)}) collective-permute-start(bf16[480,3072]{1,0:T(8,128)(2,1)} %shard_map.66.refs_0_), channel_id=1, source_target_pairs={{0,1},{1,0},{2,3},{3,2},{4,5},{5,4},{6,7},{7,6},{8,9},{9,8},{10,11... | collective-permute-start | bytes 8847368 | tf_op jit(solution)/shard_map/ppermute | solution.py:25
  98.7 4.2 %collective-permute-start.12 = (bf16[288,3072]{1,0:T(8,128)(2,1)}, bf16[288,3072]{1,0:T(8,128)(2,1)}, u32[]{:S(2)}, u32[]{:S(2)}) collective-permute-start(bf16[288,3072]{1,0:T(8,128)(2,1)} %shard_map.63.refs_0_), channel_id=1, source_target_pairs={{0,1},{1,0},{2,3},{3,2},{4,5},{5,4},{6,7},{7,6},{8,9},{9,8},{10,11... | collective-permute-start | bytes 5308424 | tf_op jit(solution)/shard_map/ppermute | solution.py:25

commit v12 on v11

--- a/solution.py
+++ b/solution.py
@@ -11,7 +11,7 @@
 HD = 128
 FRAMES = 2
 GRID_COLS = 8
-EXTRA = 16
+EXTRA = 8
 STATS = 8
 PIECES = 3
 LOG2E = math.log2(math.e)
@@ -159,7 +159,7 @@
         functools.partial(attend_kernel, rows, per_block),
         grid=(heads // per_block,),
         in_specs=[
-            pl.BlockSpec((EXTRA, HD), lambda i: (lists.shape[0] // EXTRA - 1, 0)),
+            pl.BlockSpec((EXTRA, HD), lambda i: (0, 0)),
             pl.BlockSpec((rows, width), lambda i: (0, q_lo + i)),
             here,
             key_spec,
@@ -403,7 +403,7 @@
         for number, q in enumerate(asked):
             if number:
                 q = after(q, part, cz) if cube else after(q, part)
-            part = attend(asked[0], q, 0, chunk_heads, *common, number * chunk_heads, jnp.bfloat16)
+            part = attend(asked[0][rows:, :HD], q, 0, chunk_heads, *common, number * chunk_heads, jnp.bfloat16)
             if cube and not number:
                 cz = after(cz, part)
                 cy = swap_bit(cz, 2)

time: 110 us -> 110 us (level)
    unnamed x21 -> x20, local copies, waits for them, and re-layouts: 3.04 us -> 3.04 us
  transfers between devices with their start and end apart: 18 -> 18, of which waited for: 5 -> 5; matrix products, arithmetic and copies ran while one was open for 1% -> 2% of each run, Pallas kernels for 35% -> 34%
where the time goes in v12:
time: 110 us
  Pallas kernels  44.4 us (40%)
  starting transfers between devices  39.5 us (36%)
  waiting for transfers between devices  18.5 us (17%)
  local copies, waits for them, and re-layouts  6.21 us (6%)
    ppermute x8, starting transfers between devices, swap_bit(): return lax.ppermute(value, 'seq', [(s, s ^ bit) for s in range(count)])  25.4 us
    pallas_call x4, Pallas kernels, attend(): pl.pallas_call(functools.partial(attend_kernel, rows, per_block), grid=(h...  18.8 us
    pallas_call x5, Pallas kernels, join(): pl.pallas_call(functools.partial(join_kernel, len(arrays)), in_specs=[pl....  11.4 us
    ppermute x1, waiting for transfers between devices, body(): first = lax.ppermute(asking, 'seq', pairs)  9.68 us
    pallas_call x1, Pallas kernels, project(): pl.pallas_call(functools.partial(project_kernel, plan, len(parts)), in_sp...  6.62 us
    ppermute x2, starting transfers between devices, column_shift(): return lax.ppermute(value, 'seq', pairs)  5.61 us
    ppermute x2, waiting for transfers between devices, body(): back.append(lax.ppermute(sending, 'seq', row_pairs(parity)))  5.41 us
    ppermute x4, starting transfers between devices, swap_group(): return lax.ppermute(value, 'group', [(s, s ^ 1) for s in range(groups)])  5.14 us
  transfers between devices with their start and end apart: 18, of which 5 were waited for; matrix products, arithmetic and copies ran while one was open for 2% of the time, Pallas kernels for 34%

profile of v12, /device:TPU:0, one launch (start us, length us, event | category | flops | bytes accessed | tf_op | source)
XLA Modules:
  0.0 109.6 jit_solution(11202112491181612566)
XLA Ops:
  0.0 1.7 %constant_dynamic-slice_fusion = bf16[48,3072]{1,0:T(8,128)(2,1)} fusion(bf16[96,3072]{1,0:T(8,128)(2,1)} %refs_0_.2, s32[]{:T(128)S(6)} %select_n.21), kind=kLoop, calls=%fused_computation.2 | loop fusion | bytes 589828 | tf_op jit(solution)/shard_map/dynamic_slice | solution.py:365
  1.7 3.0 %collective-permute-start.2 = (bf16[48,3072]{1,0:T(8,128)(2,1)}, bf16[48,3072]{1,0:T(8,128)(2,1)}, u32[]{:S(2)}, u32[]{:S(2)}) collective-permute-start(bf16[48,3072]{1,0:T(8,128)(2,1)} %constant_dynamic-slice_fusion), channel_id=1, source_target_pairs={{0,2},{1,3},{2,0},{3,1},{4,6},{5,7},{6,4},{7,5},{8,10},{9,11},{10,... | collective-permute-start | bytes 884744 | tf_op jit(solution)/shard_map/ppermute | solution.py:25
  4.7 2.6 %collective-permute-start.1 = (bf16[48,3072]{1,0:T(8,128)(2,1)}, bf16[48,3072]{1,0:T(8,128)(2,1)}, u32[]{:S(2)}, u32[]{:S(2)}) collective-permute-start(bf16[48,3072]{1,0:T(8,128)(2,1)} %constant_dynamic-slice_fusion), channel_id=1, source_target_pairs={{0,8},{1,9},{2,10},{3,11},{4,12},{5,13},{6,14},{7,15},{8,0},{9,1},... | collective-permute-start | bytes 884744 | tf_op jit(solution)/shard_map/ppermute | solution.py:25
  7.3 1.6 %collective-permute-start = (bf16[48,3072]{1,0:T(8,128)(2,1)}, bf16[48,3072]{1,0:T(8,128)(2,1)}, u32[]{:S(2)}, u32[]{:S(2)}) collective-permute-start(bf16[48,3072]{1,0:T(8,128)(2,1)} %constant_dynamic-slice_fusion), channel_id=1, source_target_pairs={{0,4},{1,5},{2,6},{3,7},{4,0},{5,1},{6,2},{7,3},{8,12},{9,13},{10,... | collective-permute-start | bytes 884744 | tf_op jit(solution)/shard_map/ppermute | solution.py:25
  8.8 1.1 %copy-done.1 = bf16[256,1536]{1,0:T(8,128)(2,1)S(1)} copy-done((bf16[256,1536]{1,0:T(8,128)(2,1)S(1)}, bf16[256,1536]{1,0:T(8,128)(2,1)}, u32[]{:S(2)}) %copy-start.1) | copy-done | bytes 786456
  10.0 1.1 %copy-done.3 = bf16[256,1536]{1,0:T(8,128)(2,1)S(1)} copy-done((bf16[256,1536]{1,0:T(8,128)(2,1)S(1)}, bf16[256,1536]{1,0:T(8,128)(2,1)}, u32[]{:S(2)}) %copy-start.3) | copy-done | bytes 786456
  11.1 1.3 %shard_map.55 = bf16[512,1536]{1,0:T(8,128)(2,1)} custom-call(bf16[256,1536]{1,0:T(8,128)(2,1)S(1)} %copy-done.1, bf16[256,1536]{1,0:T(8,128)(2,1)S(1)} %copy-done.3), custom_call_target="tpu_custom_call" | custom-call | flops 999999995904 | tf_op jit(solution)/shard_map/pallas_call | solution.py:65
  12.4 0.0 slice-start
  12.4 1.4 %collective-permute-start.7 = (bf16[2,256,1536]{2,1,0:T(8,128)(2,1)}, bf16[2,256,1536]{2,1,0:T(8,128)(2,1)}, u32[]{:S(2)}, u32[]{:S(2)}) collective-permute-start(bf16[2,256,1536]{2,1,0:T(8,128)(2,1)} %bitcast.1), channel_id=1, source_target_pairs={{1,0},{2,1},{3,2},{4,3},{5,4},{6,5},{7,6},{9,8},{10,9},{11,10},{12... | collective-permute-start | bytes 4718600 | tf_op jit(solution)/shard_map/ppermute | solution.py:35
  13.8 4.2 %collective-permute-start.6 = (bf16[2,256,1536]{2,1,0:T(8,128)(2,1)}, bf16[2,256,1536]{2,1,0:T(8,128)(2,1)}, u32[]{:S(2)}, u32[]{:S(2)}) collective-permute-start(bf16[2,256,1536]{2,1,0:T(8,128)(2,1)} %bitcast.1), channel_id=1, source_target_pairs={{0,1},{1,2},{2,3},{3,4},{4,5},{5,6},{6,7},{8,9},{9,10},{10,11},{11... | collective-permute-start | bytes 4718600 | tf_op jit(solution)/shard_map/ppermute | solution.py:35
  18.0 0.8 slice.12
  18.8 0.8 pad_maximum_fusion
  19.6 0.3 collective-permute-start.3
  20.0 1.0 collective-permute-done.refs_0_
  21.0 1.2 %shard_map.56.list_ref = bf16[8,128]{1,0:T(8,128)(2,1)} custom-call(bf16[8,128]{1,0:T(8,128)(2,1)} %copy-done.8), custom_call_target="tpu_custom_call" | custom-call | flops 999999995904 | tf_op jit(solution)/shard_map/pallas_call | solution.py:82
  22.2 2.2 %shard_map.58.refs_1_ = bf16[144,3072]{1,0:T(8,128)(2,1)} custom-call(bf16[48,3072]{1,0:T(8,128)(2,1)} %collective-permute-done.refs_0_, bf16[48,3072]{1,0:T(8,128)(2,1)} %collective-permute-done.2.refs_1_, bf16[48,3072]{1,0:T(8,128)(2,1)} %collective-permute-done.1.refs_1_.refs_2_), custom_call_target="tpu_custom_call" | custom-call | flops 999999995904 | tf_op jit(solution)/shard_map/pallas_call | solution.py:65
  24.4 1.6 %collective-permute-start.15 = (bf16[144,3072]{1,0:T(8,128)(2,1)}, bf16[144,3072]{1,0:T(8,128)(2,1)}, u32[]{:S(2)}, u32[]{:S(2)}) collective-permute-start(bf16[144,3072]{1,0:T(8,128)(2,1)} %shard_map.58.refs_1_), channel_id=1, source_target_pairs={{0,16},{16,0},{1,17},{17,1},{2,18},{18,2},{3,19},{19,3},{4,20},{20... | collective-permute-start | bytes 2654216 | tf_op jit(solution)/shard_map/ppermute | solution.py:29
  26.0 9.7 %collective-permute-done.3.q_ref = bf16[264,768]{1,0:T(8,128)(2,1)} collective-permute-done((bf16[264,768]{1,0:T(8,128)(2,1)}, bf16[264,768]{1,0:T(8,128)(2,1)}, u32[]{:S(2)}, u32[]{:S(2)}) %collective-permute-start.3) | collective-permute-done | bytes 405536 | tf_op jit(solution)/shard_map/ppermute | solution.py:386
  35.7 0.7 slice.11.list_ref
  36.3 16.1 %collective-permute-start.8 = (bf16[48,3072]{1,0:T(8,128)(2,1)}, bf16[48,3072]{1,0:T(8,128)(2,1)}, u32[]{:S(2)}, u32[]{:S(2)}) collective-permute-start(bf16[48,3072]{1,0:T(8,128)(2,1)} %collective-permute-done.1.refs_1_.refs_2_), channel_id=1, source_target_pairs={{0,4},{1,5},{2,6},{3,7},{4,0},{5,1},{6,2},{7,3},{8,12},{9,13},{10,... | collective-permute-start | bytes 884744 | tf_op jit(solution)/shard_map/ppermute | solution.py:25
  52.4 1.9 %shard_map.57 = bf16[96,3072]{1,0:T(8,128)(2,1)} custom-call(bf16[48,3072]{1,0:T(8,128)(2,1)} %collective-permute-done.refs_0_, bf16[48,3072]{1,0:T(8,128)(2,1)} %collective-permute-done.1.refs_1_.refs_2_), custom_call_target="tpu_custom_call" | custom-call | tf_op jit(solution)/shard_map/pallas_call | solution.py:65
  54.4 0.1 collective-permute-start.4
  54.5 4.6 %shard_map.59.in_ref = bf16[264,768]{1,0:T(8,128)(2,1)S(1)} custom-call(bf16[8,128]{1,0:T(8,128)(2,1)S(1)} %slice.11.list_ref, bf16[264,768]{1,0:T(8,128)(2,1)} %collective-permute-done.3.q_ref, bf16[256,1536]{1,0:T(8,128)(2,1)S(1)} %copy-done.2, bf16[2,256,1536]{2,1,0:T(8,128)(2,1)} %collective-permute-done.6.ka.va, ...), custom_call_target="tpu_custom_call" | custom-call | flops 999999995904 | tf_op jit(solution)/shard_map/pallas_call | solution.py:158
  59.1 0.0 copy-start.6
  59.1 0.7 copy-done.6
  59.8 0.0 collective-permute-done.8.refs_3_
  59.8 1.5 %collective-permute-start.16 = (bf16[48,3072]{1,0:T(8,128)(2,1)}, bf16[48,3072]{1,0:T(8,128)(2,1)}, u32[]{:S(2)}, u32[]{:S(2)}) collective-permute-start(bf16[48,3072]{1,0:T(8,128)(2,1)} %collective-permute-done.8.refs_3_), channel_id=1, source_target_pairs={{0,16},{16,0},{1,17},{17,1},{2,18},{18,2},{3,19},{19,3},{4,20},{20... | collective-permute-start | bytes 884744 | tf_op jit(solution)/shard_map/ppermute | solution.py:29
  61.3 2.0 %collective-permute-start.10 = (bf16[48,3072]{1,0:T(8,128)(2,1)}, bf16[48,3072]{1,0:T(8,128)(2,1)}, u32[]{:S(2)}, u32[]{:S(2)}) collective-permute-start(bf16[48,3072]{1,0:T(8,128)(2,1)} %collective-permute-done.8.refs_3_), channel_id=1, source_target_pairs={{0,2},{1,3},{2,0},{3,1},{4,6},{5,7},{6,4},{7,5},{8,10},{9,11},{10,... | collective-permute-start | bytes 884744 | tf_op jit(solution)/shard_map/ppermute | solution.py:25
  63.3 2.3 %collective-permute-done.5.q_ref = bf16[256,768]{1,0:T(8,128)(2,1)} collective-permute-done((bf16[256,768]{1,0:T(8,128)(2,1)}, bf16[256,768]{1,0:T(8,128)(2,1)}, u32[]{:S(2)}, u32[]{:S(2)}) %collective-permute-start.5) | collective-permute-done | bytes 393248 | tf_op jit(solution)/shard_map/ppermute | solution.py:398
  65.7 1.8 %shard_map.64 = bf16[264,768]{1,0:T(8,128)(2,1)} custom-call(bf16[264,768]{1,0:T(8,128)(2,1)} %copy-done.6), custom_call_target="tpu_custom_call" | custom-call | tf_op jit(solution)/shard_map/pallas_call | solution.py:82
  67.4 0.6 collective-permute-start.14
  68.0 5.3 %shard_map.60 = bf16[264,768]{1,0:T(8,128)(2,1)} custom-call(bf16[8,128]{1,0:T(8,128)(2,1)S(1)} %slice.11.list_ref, bf16[256,768]{1,0:T(8,128)(2,1)} %collective-permute-done.5.q_ref, bf16[256,1536]{1,0:T(8,128)(2,1)S(1)} %copy-done.2, bf16[2,256,1536]{2,1,0:T(8,128)(2,1)} %collective-permute-done.6.ka.va, ...), custom_call_target="tpu_custom_call" | custom-call | flops 999999995904 | tf_op jit(solution)/shard_map/pallas_call | solution.py:158
  73.3 2.4 %collective-permute-start.13 = (bf16[264,768]{1,0:T(8,128)(2,1)}, bf16[264,768]{1,0:T(8,128)(2,1)}, u32[]{:S(2)}, u32[]{:S(2)}) collective-permute-start(bf16[264,768]{1,0:T(8,128)(2,1)} %shard_map.60), channel_id=1, source_target_pairs={{0,8},{1,9},{2,10},{3,11},{4,12},{5,13},{6,14},{7,15},{8,0},{9,1},... | collective-permute-start | bytes 1216520 | tf_op jit(solution)/shard_map/ppermute | solution.py:412
  75.7 0.0 collective-permute-done.4.refs_0_
  75.7 1.5 %collective-permute-start.9 = (bf16[96,3072]{1,0:T(8,128)(2,1)}, bf16[96,3072]{1,0:T(8,128)(2,1)}, u32[]{:S(2)}, u32[]{:S(2)}) collective-permute-start(bf16[96,3072]{1,0:T(8,128)(2,1)} %collective-permute-done.4.refs_0_), channel_id=1, source_target_pairs={{0,16},{16,0},{1,17},{17,1},{2,18},{18,2},{3,19},{19,3},{4,20},{20... | collective-permute-start | bytes 1769480 | tf_op jit(solution)/shard_map/ppermute | solution.py:29
  77.2 4.5 %shard_map.61.refs_0_ = f32[264,768]{1,0:T(8,128)S(1)} custom-call(bf16[8,128]{1,0:T(8,128)(2,1)S(1)} %copy-done.7, bf16[256,1536]{1,0:T(8,128)(2,1)S(1)} %copy-done, bf16[256,1536]{1,0:T(8,128)(2,1)S(1)} %copy-done.2, bf16[2,256,1536]{2,1,0:T(8,128)(2,1)} %collective-permute-done.6.ka.va, bf16[2,256,1536]{2,1,0:T(8,128)(2,1)} %collective-permute-done.7.kb.vb, ...), custom_call_target="tpu_custom_call" | custom-call | tf_op jit(solution)/shard_map/pallas_call | solution.py:158
  81.7 0.0 collective-permute-done.16.refs_4_
  81.7 0.6 collective-permute-start.11
  82.3 3.3 %shard_map.66.refs_0_ = bf16[480,3072]{1,0:T(8,128)(2,1)} custom-call(bf16[96,3072]{1,0:T(8,128)(2,1)S(1)} %copy-done.5, bf16[144,3072]{1,0:T(8,128)(2,1)} %shard_map.58.refs_1_, bf16[144,3072]{1,0:T(8,128)(2,1)} %collective-permute-done.15.refs_2_, bf16[48,3072]{1,0:T(8,128)(2,1)} %collective-permute-done.8.refs_3_, ...), custom_call_target="tpu_custom_call" | custom-call | tf_op jit(solution)/shard_map/pallas_call | solution.py:65
  85.6 0.1 collective-permute-start.17
  85.7 4.5 %shard_map.62.refs_2_ = f32[264,768]{1,0:T(8,128)S(1)} custom-call(bf16[8,128]{1,0:T(8,128)(2,1)S(1)} %copy-done.7, bf16[256,1536]{1,0:T(8,128)(2,1)S(1)} %copy-done, bf16[256,1536]{1,0:T(8,128)(2,1)S(1)} %copy-done.2, bf16[2,256,1536]{2,1,0:T(8,128)(2,1)} %collective-permute-done.6.ka.va, bf16[2,256,1536]{2,1,0:T(8,128)(2,1)} %collective-permute-done.7.kb.vb, ...), custom_call_target="tpu_custom_call" | custom-call | tf_op jit(solution)/shard_map/pallas_call | solution.py:158
  90.2 4.1 %collective-permute-done.14.refs_1_ = bf16[264,768]{1,0:T(8,128)(2,1)} collective-permute-done((bf16[264,768]{1,0:T(8,128)(2,1)}, bf16[264,768]{1,0:T(8,128)(2,1)}, u32[]{:S(2)}, u32[]{:S(2)}) %collective-permute-start.14) | collective-permute-done | bytes 405536 | tf_op jit(solution)/shard_map/ppermute | solution.py:412
  94.3 1.7 %shard_map.65.refs_2_.refs_4_ = bf16[256,768]{1,0:T(8,128)(2,1)S(1)} custom-call(s32[1]{0:T(128)} %bitcast.partner_ref, f32[264,768]{1,0:T(8,128)S(1)} %shard_map.61.refs_0_, bf16[264,768]{1,0:T(8,128)(2,1)} %collective-permute-done.14.refs_1_), custom_call_target="tpu_custom_call" | custom-call | flops 999999995904 | tf_op jit(solution)/shard_map/pallas_call | solution.py:224
  96.1 2.7 %shard_map.63.refs_0_ = bf16[288,3072]{1,0:T(8,128)(2,1)} custom-call(bf16[96,3072]{1,0:T(8,128)(2,1)} %collective-permute-done.4.refs_0_, bf16[96,3072]{1,0:T(8,128)(2,1)} %collective-permute-done.9.refs_1_, bf16[48,3072]{1,0:T(8,128)(2,1)} %collective-permute-done.10.refs_2_, bf16[48,3072]{1,0:T(8,128)(2,1)} %collective-permute-done.11.refs_3_), custom_call_target="tpu_custom_call" | custom-call | tf_op jit(solution)/shard_map/pallas_call | solution.py:65
  98.8 0.1 collective-permute-start.12
  98.8 2.8 %shard_map.67.refs_5_ = bf16[1536,3072]{1,0:T(8,128)(2,1)S(1)} custom-call(bf16[480,3072]{1,0:T(8,128)(2,1)} %shard_map.66.refs_0_, bf16[480,3072]{1,0:T(8,128)(2,1)} %collective-permute-done.17.refs_1_, bf16[256,768]{1,0:T(8,128)(2,1)S(1)} %shard_map.65.refs_2_.refs_4_), custom_call_target="tpu_custom_call" | custom-call | flops 999999995904 | tf_op jit(solution)/shard_map/pallas_call | solution.py:258
  101.7 1.3 %collective-permute-done.13.refs_3_ = bf16[264,768]{1,0:T(8,128)(2,1)} collective-permute-done((bf16[264,768]{1,0:T(8,128)(2,1)}, bf16[264,768]{1,0:T(8,128)(2,1)}, u32[]{:S(2)}, u32[]{:S(2)}) %collective-permute-start.13) | collective-permute-done | bytes 405536 | tf_op jit(solution)/shard_map/ppermute | solution.py:412
  102.9 6.6 %shard_map.68 = (bf16[256,3072]{1,0:T(8,128)(2,1)}, bf16[1536,3072]{1,0:T(8,128)(2,1)S(1)}) custom-call(s32[1]{0:T(128)} %bitcast.partner_ref, bf16[288,3072]{1,0:T(8,128)(2,1)} %shard_map.63.refs_0_, bf16[288,3072]{1,0:T(8,128)(2,1)} %collective-permute-done.12.refs_1_, f32[264,768]{1,0:T(8,128)S(1)} %shard_map.62.refs_2_, ...), custom_call_target="tpu_custom_call", output_to_operand_aliasing={{1}: (6, {})} | custom-call | tf_op jit(solution)/shard_map/pallas_call | solution.py:301
  (31 shorter events, 0.1 us)
Async XLA Ops:
  1.7 17.9 %collective-permute-start.2 = (bf16[48,3072]{1,0:T(8,128)(2,1)}, bf16[48,3072]{1,0:T(8,128)(2,1)}, u32[]{:S(2)}, u32[]{:S(2)}) collective-permute-start(bf16[48,3072]{1,0:T(8,128)(2,1)} %constant_dynamic-slice_fusion), channel_id=1, source_target_pairs={{0,2},{1,3},{2,0},{3,1},{4,6},{5,7},{6,4},{7,5},{8,10},{9,11},{10,... | collective-permute-start | bytes 884744 | tf_op jit(solution)/shard_map/ppermute | solution.py:25
  4.7 17.5 %collective-permute-start.1 = (bf16[48,3072]{1,0:T(8,128)(2,1)}, bf16[48,3072]{1,0:T(8,128)(2,1)}, u32[]{:S(2)}, u32[]{:S(2)}) collective-permute-start(bf16[48,3072]{1,0:T(8,128)(2,1)} %constant_dynamic-slice_fusion), channel_id=1, source_target_pairs={{0,8},{1,9},{2,10},{3,11},{4,12},{5,13},{6,14},{7,15},{8,0},{9,1},... | collective-permute-start | bytes 884744 | tf_op jit(solution)/shard_map/ppermute | solution.py:25
  7.3 13.7 %collective-permute-start = (bf16[48,3072]{1,0:T(8,128)(2,1)}, bf16[48,3072]{1,0:T(8,128)(2,1)}, u32[]{:S(2)}, u32[]{:S(2)}) collective-permute-start(bf16[48,3072]{1,0:T(8,128)(2,1)} %constant_dynamic-slice_fusion), channel_id=1, source_target_pairs={{0,4},{1,5},{2,6},{3,7},{4,0},{5,1},{6,2},{7,3},{8,12},{9,13},{10,... | collective-permute-start | bytes 884744 | tf_op jit(solution)/shard_map/ppermute | solution.py:25
  8.8 1.1 %copy-start.1 = (bf16[256,1536]{1,0:T(8,128)(2,1)S(1)}, bf16[256,1536]{1,0:T(8,128)(2,1)}, u32[]{:S(2)}) copy-start(bf16[256,1536]{1,0:T(8,128)(2,1)} %k0.7) | copy-start | bytes 2359300
  10.0 1.1 %copy-start.3 = (bf16[256,1536]{1,0:T(8,128)(2,1)S(1)}, bf16[256,1536]{1,0:T(8,128)(2,1)}, u32[]{:S(2)}) copy-start(bf16[256,1536]{1,0:T(8,128)(2,1)} %v0.7) | copy-start | bytes 2359300
  11.1 6.9 %copy-start = (bf16[256,1536]{1,0:T(8,128)(2,1)S(1)}, bf16[256,1536]{1,0:T(8,128)(2,1)}, u32[]{:S(2)}) copy-start(bf16[256,1536]{1,0:T(8,128)(2,1)} %q_ref.1) | copy-start | bytes 2359300
  11.1 7.7 %copy-start.9 = (s32[2,27]{1,0:T(2,128)S(1)}, s32[2,27]{1,0:T(2,128)}, u32[]{:S(2)}) copy-start(s32[2,27]{1,0:T(2,128)} %param.8) | copy-start | bytes 652
  12.4 6.5 %slice-start = ((bf16[256,1536]{1,0:T(8,128)(2,1)}), bf16[256,768]{1,0:T(8,128)(2,1)S(1)}, s32[]{:S(2)}) async-start(bf16[256,1536]{1,0:T(8,128)(2,1)} %q_ref.1), calls=%async_computation | async-start | bytes 786432 | tf_op jit(solution)/shard_map/slice | solution.py:379
  12.4 42.0 %collective-permute-start.7 = (bf16[2,256,1536]{2,1,0:T(8,128)(2,1)}, bf16[2,256,1536]{2,1,0:T(8,128)(2,1)}, u32[]{:S(2)}, u32[]{:S(2)}) collective-permute-start(bf16[2,256,1536]{2,1,0:T(8,128)(2,1)} %bitcast.1), channel_id=1, source_target_pairs={{1,0},{2,1},{3,2},{4,3},{5,4},{6,5},{7,6},{9,8},{10,9},{11,10},{12... | collective-permute-start | bytes 4718600 | tf_op jit(solution)/shard_map/ppermute | solution.py:35
  13.8 40.6 %collective-permute-start.6 = (bf16[2,256,1536]{2,1,0:T(8,128)(2,1)}, bf16[2,256,1536]{2,1,0:T(8,128)(2,1)}, u32[]{:S(2)}, u32[]{:S(2)}) collective-permute-start(bf16[2,256,1536]{2,1,0:T(8,128)(2,1)} %bitcast.1), channel_id=1, source_target_pairs={{0,1},{1,2},{2,3},{3,4},{4,5},{5,6},{6,7},{8,9},{9,10},{10,11},{11... | collective-permute-start | bytes 4718600 | tf_op jit(solution)/shard_map/ppermute | solution.py:35
  18.8 2.1 %copy-start.8 = (bf16[8,128]{1,0:T(8,128)(2,1)}, bf16[8,128]{1,0:T(8,128)(2,1)S(1)}, u32[]{:S(2)}) copy-start(bf16[8,128]{1,0:T(8,128)(2,1)S(1)} %pad.4.in_ref) | copy-start | bytes 6148
  19.6 16.0 %collective-permute-start.3 = (bf16[264,768]{1,0:T(8,128)(2,1)}, bf16[264,768]{1,0:T(8,128)(2,1)}, u32[]{:S(2)}, u32[]{:S(2)}) collective-permute-start(bf16[264,768]{1,0:T(8,128)(2,1)} %pad_maximum_fusion), channel_id=1, source_target_pairs={{0,8},{1,9},{2,10},{3,11},{4,12},{5,13},{6,14},{7,15},{8,0},{9,1},... | collective-permute-start | bytes 1216520 | tf_op jit(solution)/shard_map/ppermute | solution.py:386
  22.2 32.3 %copy-start.2 = (bf16[256,1536]{1,0:T(8,128)(2,1)S(1)}, bf16[256,1536]{1,0:T(8,128)(2,1)}, u32[]{:S(2)}) copy-start(bf16[256,1536]{1,0:T(8,128)(2,1)} %k0.7) | copy-start | bytes 2359300
  22.2 32.3 %copy-start.4 = (bf16[256,1536]{1,0:T(8,128)(2,1)S(1)}, bf16[256,1536]{1,0:T(8,128)(2,1)}, u32[]{:S(2)}) copy-start(bf16[256,1536]{1,0:T(8,128)(2,1)} %v0.7) | copy-start | bytes 2359300
  24.4 48.9 %collective-permute-start.15 = (bf16[144,3072]{1,0:T(8,128)(2,1)}, bf16[144,3072]{1,0:T(8,128)(2,1)}, u32[]{:S(2)}, u32[]{:S(2)}) collective-permute-start(bf16[144,3072]{1,0:T(8,128)(2,1)} %shard_map.58.refs_1_), channel_id=1, source_target_pairs={{0,16},{16,0},{1,17},{17,1},{2,18},{18,2},{3,19},{19,3},{4,20},{20... | collective-permute-start | bytes 2654216 | tf_op jit(solution)/shard_map/ppermute | solution.py:29
  36.3 23.5 %collective-permute-start.8 = (bf16[48,3072]{1,0:T(8,128)(2,1)}, bf16[48,3072]{1,0:T(8,128)(2,1)}, u32[]{:S(2)}, u32[]{:S(2)}) collective-permute-start(bf16[48,3072]{1,0:T(8,128)(2,1)} %collective-permute-done.1.refs_1_.refs_2_), channel_id=1, source_target_pairs={{0,4},{1,5},{2,6},{3,7},{4,0},{5,1},{6,2},{7,3},{8,12},{9,13},{10,... | collective-permute-start | bytes 884744 | tf_op jit(solution)/shard_map/ppermute | solution.py:25
  52.4 13.2 %collective-permute-start.5 = (bf16[256,768]{1,0:T(8,128)(2,1)}, bf16[256,768]{1,0:T(8,128)(2,1)}, u32[]{:S(2)}, u32[]{:S(2)}) collective-permute-start(bf16[256,768]{1,0:T(8,128)(2,1)} %slice.12), channel_id=1, source_target_pairs={{0,8},{1,9},{2,10},{3,11},{4,12},{5,13},{6,14},{7,15},{8,0},{9,1},... | collective-permute-start | bytes 1179656 | tf_op jit(solution)/shard_map/ppermute | solution.py:398
  54.4 21.3 %collective-permute-start.4 = (bf16[96,3072]{1,0:T(8,128)(2,1)}, bf16[96,3072]{1,0:T(8,128)(2,1)}, u32[]{:S(2)}, u32[]{:S(2)}) collective-permute-start(bf16[96,3072]{1,0:T(8,128)(2,1)} %shard_map.57), channel_id=1, source_target_pairs={{0,2},{1,3},{2,0},{3,1},{4,6},{5,7},{6,4},{7,5},{8,10},{9,11},{10,... | collective-permute-start | bytes 1769480 | tf_op jit(solution)/shard_map/ppermute | solution.py:25
  59.1 0.8 copy-start.6
  59.8 21.8 %collective-permute-start.16 = (bf16[48,3072]{1,0:T(8,128)(2,1)}, bf16[48,3072]{1,0:T(8,128)(2,1)}, u32[]{:S(2)}, u32[]{:S(2)}) collective-permute-start(bf16[48,3072]{1,0:T(8,128)(2,1)} %collective-permute-done.8.refs_3_), channel_id=1, source_target_pairs={{0,16},{16,0},{1,17},{17,1},{2,18},{18,2},{3,19},{19,3},{4,20},{20... | collective-permute-start | bytes 884744 | tf_op jit(solution)/shard_map/ppermute | solution.py:29
  61.3 20.3 %collective-permute-start.10 = (bf16[48,3072]{1,0:T(8,128)(2,1)}, bf16[48,3072]{1,0:T(8,128)(2,1)}, u32[]{:S(2)}, u32[]{:S(2)}) collective-permute-start(bf16[48,3072]{1,0:T(8,128)(2,1)} %collective-permute-done.8.refs_3_), channel_id=1, source_target_pairs={{0,2},{1,3},{2,0},{3,1},{4,6},{5,7},{6,4},{7,5},{8,10},{9,11},{10,... | collective-permute-start | bytes 884744 | tf_op jit(solution)/shard_map/ppermute | solution.py:25
  67.4 26.9 %collective-permute-start.14 = (bf16[264,768]{1,0:T(8,128)(2,1)}, bf16[264,768]{1,0:T(8,128)(2,1)}, u32[]{:S(2)}, u32[]{:S(2)}) collective-permute-start(bf16[264,768]{1,0:T(8,128)(2,1)} %shard_map.64), channel_id=1, source_target_pairs={{0,8},{1,9},{2,10},{3,11},{4,12},{5,13},{6,14},{7,15},{8,0},{9,1},... | collective-permute-start | bytes 1216520 | tf_op jit(solution)/shard_map/ppermute | solution.py:412
  68.0 9.2 %copy-start.7 = (bf16[8,128]{1,0:T(8,128)(2,1)S(1)}, bf16[8,128]{1,0:T(8,128)(2,1)}, u32[]{:S(2)}) copy-start(bf16[8,128]{1,0:T(8,128)(2,1)} %shard_map.56.list_ref) | copy-start | bytes 6148
  73.3 9.0 %copy-start.5 = (bf16[96,3072]{1,0:T(8,128)(2,1)S(1)}, bf16[96,3072]{1,0:T(8,128)(2,1)}, u32[]{:S(2)}) copy-start(bf16[96,3072]{1,0:T(8,128)(2,1)} %refs_0_.2) | copy-start | bytes 1769476
  73.3 29.6 %collective-permute-start.13 = (bf16[264,768]{1,0:T(8,128)(2,1)}, bf16[264,768]{1,0:T(8,128)(2,1)}, u32[]{:S(2)}, u32[]{:S(2)}) collective-permute-start(bf16[264,768]{1,0:T(8,128)(2,1)} %shard_map.60), channel_id=1, source_target_pairs={{0,8},{1,9},{2,10},{3,11},{4,12},{5,13},{6,14},{7,15},{8,0},{9,1},... | collective-permute-start | bytes 1216520 | tf_op jit(solution)/shard_map/ppermute | solution.py:412
  75.7 20.4 %collective-permute-start.9 = (bf16[96,3072]{1,0:T(8,128)(2,1)}, bf16[96,3072]{1,0:T(8,128)(2,1)}, u32[]{:S(2)}, u32[]{:S(2)}) collective-permute-start(bf16[96,3072]{1,0:T(8,128)(2,1)} %collective-permute-done.4.refs_0_), channel_id=1, source_target_pairs={{0,16},{16,0},{1,17},{17,1},{2,18},{18,2},{3,19},{19,3},{4,20},{20... | collective-permute-start | bytes 1769480 | tf_op jit(solution)/shard_map/ppermute | solution.py:29
  81.7 14.4 %collective-permute-start.11 = (bf16[48,3072]{1,0:T(8,128)(2,1)}, bf16[48,3072]{1,0:T(8,128)(2,1)}, u32[]{:S(2)}, u32[]{:S(2)}) collective-permute-start(bf16[48,3072]{1,0:T(8,128)(2,1)} %collective-permute-done.10.refs_2_), channel_id=1, source_target_pairs={{0,16},{16,0},{1,17},{17,1},{2,18},{18,2},{3,19},{19,3},{4,20},{20... | collective-permute-start | bytes 884744 | tf_op jit(solution)/shard_map/ppermute | solution.py:29
  85.6 13.2 %collective-permute-start.17 = (bf16[480,3072]{1,0:T(8,128)(2,1)}, bf16[480,3072]{1,0:T(8,128)(2,1)}, u32[]{:S(2)}, u32[]{:S(2)}) collective-permute-start(bf16[480,3072]{1,0:T(8,128)(2,1)} %shard_map.66.refs_0_), channel_id=1, source_target_pairs={{0,1},{1,0},{2,3},{3,2},{4,5},{5,4},{6,7},{7,6},{8,9},{9,8},{10,11... | collective-permute-start | bytes 8847368 | tf_op jit(solution)/shard_map/ppermute | solution.py:25
  98.8 4.2 %collective-permute-start.12 = (bf16[288,3072]{1,0:T(8,128)(2,1)}, bf16[288,3072]{1,0:T(8,128)(2,1)}, u32[]{:S(2)}, u32[]{:S(2)}) collective-permute-start(bf16[288,3072]{1,0:T(8,128)(2,1)} %shard_map.63.refs_0_), channel_id=1, source_target_pairs={{0,1},{1,0},{2,3},{3,2},{4,5},{5,4},{6,7},{7,6},{8,9},{9,8},{10,11... | collective-permute-start | bytes 5308424 | tf_op jit(solution)/shard_map/ppermute | solution.py:25
